TPU v7x, 256 devices: a whole 4x4x8 slice. The times are simulated.
256 devices in a mesh: tm: 8 (over z), height: 4 (over x_hi, core), width: 8 (over y, x_lo).
Axes of the slice: x: 4 (x_hi: 2, x_lo: 2; x = x_hi * 2 + x_lo), y: 4, z: 8, core: 2. Of those that a mesh axis runs over, the one named last changes fastest.
Arguments:
- features: bfloat16 [16, 128, 512, 128], P('tm', 'height', 'width'), may hold values from -6 to 6
- gain_fine: float32 [128], replicated, may hold values from 0.25 to 1.75
- conv_fine: bfloat16 [3, 3, 3, 128, 128], replicated, may hold values from -0.109375 to 0.109375
- down_fine: bfloat16 [1024, 256], replicated, may hold values from -0.1875 to 0.1875
- gain_coarse: float32 [256], replicated, may hold values from 0.25 to 1.75
- conv_coarse: bfloat16 [3, 3, 3, 256, 256], replicated, may hold values from -0.078125 to 0.078125
- down_coarse: bfloat16 [1024, 512], replicated, may hold values from -0.1875 to 0.1875
- gain_latent: float32 [512], replicated, may hold values from 0.25 to 1.75
- w_query: bfloat16 [512, 512], replicated, as said below
- w_key: bfloat16 [512, 512], replicated, as said below
- w_value: bfloat16 [512, 512], replicated, may hold values from -0.25 to 0.25
- w_out: bfloat16 [512, 512], replicated, may hold values from -0.25 to 0.25
Outputs:
- latent: bfloat16 [8, 32, 128, 512], P('tm', 'height', 'width')
Inputs may be any that keep to these rules, and one draw needn't show every extreme that they name: `w_query`: a projection with entries of order 2.5 over the square root of 512. `w_key`: a projection.
All inputs are finite; a program needn't handle non-finite values.
Results may differ from a plain program's by a relative error of at most 0.015.
Values may be sent and summed in bfloat16 or wider, within the bound.
No kernel may reach another device: no remote copies, remote signals or barrier semaphores. Data moves between devices by JAX's collectives and lax.ppermute only.
A program may use at most 192 MiB of HBM per device.

v0:
```python
import math

import jax
import jax.numpy as jnp
from jax import lax
from jax.sharding import PartitionSpec as P

EPSILON = 1e-06


def passed_along(value, axis, steps):
    count = lax.axis_size(axis)
    initial, last = (max(0, -steps), min(count, count - steps))
    return lax.ppermute(value, axis, [(source, source + steps) for source in range(initial, last)])


def padded_2(block, sides, width):
    for axis, dim in sides:
        count = lax.axis_size(axis)
        forward = [(i, i + 1) for i in range(count - 1)]
        backward = [(target, source) for source, target in forward]
        low = lax.ppermute(
            lax.slice_in_dim(block, block.shape[dim] - width, None, axis=dim), axis, forward
        )
        high = lax.ppermute(lax.slice_in_dim(block, 0, width, axis=dim), axis, backward)
        block = jnp.concatenate([low, block, high], axis=dim)
    return block


def channel_norm(inputs, gain):
    values_f = inputs.astype(jnp.float32)
    return (
        values_f * lax.rsqrt(jnp.mean(values_f * values_f, axis=-1, keepdims=True) + EPSILON) * gain
    )


def project(inputs, weight):
    flat = inputs.reshape(-1, inputs.shape[-1])
    result = jnp.dot(flat, weight, preferred_element_type=jnp.float32)
    return result.reshape(inputs.shape[:-1] + (weight.shape[-1],))


def causal_conv(padded, weight, frames):
    height = padded.shape[1] - 2
    breadth = padded.shape[2] - 2
    summed = jnp.zeros((frames, height, breadth, weight.shape[-1]), jnp.float32)
    for shift_t in range(3):
        for shift_h in range(3):
            for shift_w in range(3):
                window = padded[
                    shift_t : shift_t + frames,
                    shift_h : shift_h + height,
                    shift_w : shift_w + breadth,
                ]
                summed = summed + jnp.einsum(
                    "fhwc,cd->fhwd",
                    window,
                    weight[shift_t, shift_h, shift_w],
                    preferred_element_type=jnp.float32,
                )
    return summed


def fold_space_time(hidden):
    frames, height, breadth, channels = hidden.shape
    grouped = hidden.reshape(frames // 2, 2, height // 2, 2, breadth // 2, 2, channels)
    grouped = grouped.transpose(0, 2, 4, 1, 3, 5, 6)
    return grouped.reshape(frames // 2, height // 2, breadth // 2, 8 * channels)


def fold_space(hidden):
    frames, height, breadth, channels = hidden.shape
    grouped = hidden.reshape(frames, height // 2, 2, breadth // 2, 2, channels)
    grouped = grouped.transpose(0, 1, 3, 2, 4, 5)
    return grouped.reshape(frames, height // 2, breadth // 2, 4 * channels)


def per_device(
    features,
    gain_fine,
    conv_fine,
    down_fine,
    gain_coarse,
    conv_coarse,
    down_coarse,
    gain_latent,
    w_query,
    w_key,
    w_value,
    w_out,
):
    position = lax.axis_index("tm")
    at_start = position == 0
    active = jax.nn.silu(channel_norm(features, gain_fine)).astype(jnp.bfloat16)
    earlier = passed_along(active, "tm", 1)
    first_frame = active[:1]
    earlier = jnp.where(at_start, jnp.concatenate([first_frame, first_frame], 0), earlier)
    stacked = jnp.concatenate([earlier, active], 0)
    padded = padded_2(stacked, (("height", 1), ("width", 2)), 1)
    hidden_fine = (
        features.astype(jnp.float32) + causal_conv(padded, conv_fine, active.shape[0])
    ).astype(jnp.bfloat16)
    reduced = project(fold_space_time(hidden_fine), down_fine).astype(jnp.bfloat16)
    active_coarse = jax.nn.silu(channel_norm(reduced, gain_coarse)).astype(jnp.bfloat16)
    prior_one = passed_along(active_coarse, "tm", 1)
    prior_one = jnp.where(at_start, active_coarse, prior_one)
    prior_two = passed_along(prior_one, "tm", 1)
    prior_two = jnp.where(at_start, active_coarse, prior_two)
    stacked_coarse = jnp.concatenate([prior_two, prior_one, active_coarse], 0)
    padded_coarse = padded_2(stacked_coarse, (("height", 1), ("width", 2)), 1)
    hidden_coarse = (
        reduced.astype(jnp.float32)
        + causal_conv(padded_coarse, conv_coarse, active_coarse.shape[0])
    ).astype(jnp.bfloat16)
    latent_in = project(fold_space(hidden_coarse), down_coarse).astype(jnp.bfloat16)
    normed = channel_norm(latent_in, gain_latent).astype(jnp.bfloat16)
    local_frames, tile_rows, tile_cols, channels = normed.shape
    tokens_flat = normed.reshape(local_frames, tile_rows * tile_cols, channels)
    queries = project(tokens_flat, w_query).astype(jnp.bfloat16)
    score_scale = 1.0 / math.sqrt(channels)
    key_rows = project(tokens_flat, w_key).astype(jnp.bfloat16)
    value_rows = project(tokens_flat, w_value).astype(jnp.bfloat16)
    attend_key_rows = lax.all_gather(key_rows, ("height", "width"), axis=1, tiled=True)
    attend_value_rows = lax.all_gather(value_rows, ("height", "width"), axis=1, tiled=True)
    running_max = jnp.full(queries.shape[:2], -1e30, jnp.float32)
    scores = (
        jnp.einsum("fqc,fkc->fqk", queries, attend_key_rows, preferred_element_type=jnp.float32)
        * score_scale
    )
    new_max = jnp.maximum(running_max, jnp.max(scores, axis=-1))
    expo = jnp.exp(scores - new_max[..., None])
    running_sum = jnp.sum(expo, axis=-1)
    weighted = jnp.einsum(
        "fqk,fkc->fqc",
        expo.astype(jnp.bfloat16),
        attend_value_rows,
        preferred_element_type=jnp.float32,
    )
    result = (new_max, running_sum, weighted)
    running_max, running_sum, weighted = result
    attended = (weighted / running_sum[..., None]).astype(jnp.bfloat16)
    combined = latent_in.astype(jnp.float32) + project(attended, w_out).reshape(latent_in.shape)
    return combined.astype(jnp.bfloat16)


def solution(mesh):
    placed = (
        P("tm", "height", "width", None),
        P(),
        P(),
        P(),
        P(),
        P(),
        P(),
        P(),
        P(),
        P(),
        P(),
        P(),
    )
    return jax.shard_map(
        per_device,
        mesh=mesh,
        in_specs=placed,
        out_specs=P("tm", "height", "width", None),
        check_vma=False,
    )
```

profile of v0, /device:TPU:96, one launch (start us, length us, event | category | flops | bytes accessed | tf_op | source)
XLA Modules:
  0.0 366.1 jit_solution(2168005981429754921)
XLA Ops:
  6.5 2.0 fusion
  8.5 1.9 fusion.7
  10.4 5.0 %collective-permute-start = (bf16[2,32,64,128]{3,2,1,0:T(8,128)(2,1)S(1)}, bf16[2,32,64,128]{3,2,1,0:T(8,128)(2,1)}, u32[]{:S(2)}, u32[]{:S(2)}) collective-permute-start(bf16[2,32,64,128]{3,2,1,0:T(8,128)(2,1)S(1)} %fusion.7), channel_id=1, source_target_pairs={{0,32},{32,64},{64,96},{96,128},{128,160},{160,192},{192,224},{1,3... | collective-permute-start | bytes 3145736 | tf_op jit(solution)/shard_map/ppermute | solution.py:14
  15.5 1.8 fusion.171
  17.3 20.6 %collective-permute-done = bf16[2,32,64,128]{3,2,1,0:T(8,128)(2,1)} collective-permute-done((bf16[2,32,64,128]{3,2,1,0:T(8,128)(2,1)S(1)}, bf16[2,32,64,128]{3,2,1,0:T(8,128)(2,1)}, u32[]{:S(2)}, u32[]{:S(2)}) %collective-permute-start) | collective-permute-done | bytes 1048608 | tf_op jit(solution)/shard_map/ppermute | solution.py:14
  37.9 1.4 maximum_select_fusion
  39.2 1.8 fusion.194
  43.6 1.8 fusion.9
  45.4 3.3 collective-permute-done.2
  48.8 2.5 collective-permute-start.3
  52.7 1.7 fusion.175
  54.4 1.8 fusion.179
  56.2 1.8 fusion.186
  57.9 1.8 fusion.190
  59.7 1.7 fusion.198
  61.4 1.8 fusion.167
  63.2 3.5 pad_maximum_fusion
  66.8 2.1 fusion.34
  68.8 1.8 fusion.38
  70.6 1.8 fusion.36
  72.4 1.7 fusion.40
  74.1 1.8 fusion.42
  75.9 1.8 fusion.44
  77.6 1.8 fusion.46
  79.4 1.8 fusion.48
  81.2 1.7 fusion.50
  82.9 1.8 fusion.52
  84.7 1.7 fusion.54
  86.4 1.8 fusion.56
  88.2 1.8 fusion.58
  90.0 1.8 fusion.60
  91.8 1.8 fusion.62
  93.6 1.8 fusion.64
  95.3 1.7 fusion.66
  97.1 19.7 %fusion.8 = bf16[2,32,64,128]{3,2,1,0:T(8,128)(2,1)S(1)} fusion(bf16[2,32,64,128]{3,2,1,0:T(8,128)(2,1)S(1)} %copy-done.2, f32[2,32,64,128]{3,2,1,0:T(8,128)} %fusion.167, f32[2,32,64,128]{3,2,1,0:T(8,128)} %fusion.34, f32[2,32,64,128]{3,2,1,0:T(8,128)} %fusion.36, f32[2,32,64,128]{3,2,1,0:T(8,128)} %fusion.171, f32[2,32,64,128]{3,2,1,0:T(8,128)} %fusion.38, ...), kind=kOutput, calls=%fused_computation.16 | convolution fusion | flops 149422080 | bytes 57704448 | tf_op jit(solution)/shard_map/fhwc,cd->fhwd/dot_general | solution.py:55
  118.3 1.6 multiply_reduce_fusion
  120.1 6.0 %collective-permute-start.5 = (bf16[1,16,32,256]{3,2,1,0:T(8,128)(2,1)S(1)}, bf16[1,16,32,256]{3,2,1,0:T(8,128)(2,1)S(1)}, u32[]{:S(2)}, u32[]{:S(2)}) collective-permute-start(bf16[1,16,32,256]{3,2,1,0:T(8,128)(2,1)S(1)} %fusion.250), channel_id=1, source_target_pairs={{0,32},{32,64},{64,96},{96,128},{128,160},{160,192},{192,224},{1,3... | collective-permute-start | bytes 786440 | tf_op jit(solution)/shard_map/ppermute | solution.py:14
  126.1 3.9 %collective-permute-done.5 = bf16[1,16,32,256]{3,2,1,0:T(8,128)(2,1)S(1)} collective-permute-done((bf16[1,16,32,256]{3,2,1,0:T(8,128)(2,1)S(1)}, bf16[1,16,32,256]{3,2,1,0:T(8,128)(2,1)S(1)}, u32[]{:S(2)}, u32[]{:S(2)}) %collective-permute-start.5) | collective-permute-done | bytes 262176 | tf_op jit(solution)/shard_map/ppermute | solution.py:14
  130.2 5.6 %collective-permute-start.6 = (bf16[1,16,32,256]{3,2,1,0:T(8,128)(2,1)S(1)}, bf16[1,16,32,256]{3,2,1,0:T(8,128)(2,1)S(1)}, u32[]{:S(2)}, u32[]{:S(2)}) collective-permute-start(bf16[1,16,32,256]{3,2,1,0:T(8,128)(2,1)S(1)} %broadcast_select_fusion.1), channel_id=1, source_target_pairs={{0,32},{32,64},{64,96},{96,128},{128,160},{160,192},{192,224},{1,3... | collective-permute-start | bytes 786440 | tf_op jit(solution)/shard_map/ppermute | solution.py:14
  135.8 4.6 %collective-permute-done.6 = bf16[1,16,32,256]{3,2,1,0:T(8,128)(2,1)S(1)} collective-permute-done((bf16[1,16,32,256]{3,2,1,0:T(8,128)(2,1)S(1)}, bf16[1,16,32,256]{3,2,1,0:T(8,128)(2,1)S(1)}, u32[]{:S(2)}, u32[]{:S(2)}) %collective-permute-start.6) | collective-permute-done | bytes 262176 | tf_op jit(solution)/shard_map/ppermute | solution.py:14
  140.7 4.3 %collective-permute-start.7 = (bf16[3,1,32,256]{3,2,1,0:T(8,128)(2,1)S(1)}, bf16[3,1,32,256]{3,2,1,0:T(8,128)(2,1)S(1)}, u32[]{:S(2)}, u32[]{:S(2)}) collective-permute-start(bf16[3,1,32,256]{3,2,1,0:T(8,128)(2,1)S(1)} %get-tuple-element.15), channel_id=1, source_target_pairs={{0,8},{8,16},{16,24},{1,9},{9,17},{17,25},{2,10},{10,18},{18,26},{... | collective-permute-start | bytes 147464 | tf_op jit(solution)/shard_map/ppermute | solution.py:22
  146.3 3.4 collective-permute-done.8
  151.1 4.6 %collective-permute-start.9 = (bf16[3,18,1,256]{3,2,1,0:T(2,128)(2,1)S(1)}, bf16[3,18,1,256]{3,2,1,0:T(2,128)(2,1)S(1)}, u32[]{:S(2)}, u32[]{:S(2)}) collective-permute-start(bf16[3,18,1,256]{3,2,1,0:T(2,128)(2,1)S(1)} %get-tuple-element.13), channel_id=1, source_target_pairs={{0,1},{1,2},{2,3},{3,4},{4,5},{5,6},{6,7},{8,9},{9,10},{10,11},{11... | collective-permute-start | bytes 82952 | tf_op jit(solution)/shard_map/ppermute | solution.py:22
  156.0 1.5 collective-permute-done.9
  167.5 95.4 %all-gather.5.cloned.1.call-done = bf16[4096,512]{1,0:T(8,128)(2,1)} async-done(((bf16[128,512]{1,0:T(8,128)(2,1)}), bf16[4096,512]{1,0:T(8,128)(2,1)}) %all-gather.5.cloned.1.call-update) | async-done | bytes 4194320 | tf_op jit(solution)/shard_map/all_gather | solution.py:123
  262.9 4.0 %fusion.235 = (f32[128]{0:T(128)S(1)}, f32[128,4096]{1,0:T(8,128)S(1)}) fusion(bf16[4096,512]{1,0:T(8,128)(2,1)} %all-gather.5.cloned.1.call-done, bf16[128,512]{1,0:T(8,128)(2,1)S(1)} %bitcast.444, bf16[512,512]{1,0:T(8,128)(2,1)} %param.20), kind=kOutput, calls=%fused_computation.320 | convolution fusion | flops 605093760 | bytes 6947328 | tf_op jit(solution)/shard_map/fqc,fkc->fqk/dot_general | solution.py:127
  267.4 87.9 %all-gather.7.cloned.1.call-done = bf16[4096,512]{1,0:T(8,128)(2,1)} async-done(((bf16[128,512]{1,0:T(8,128)(2,1)}), bf16[4096,512]{1,0:T(8,128)(2,1)}) %all-gather.7.cloned.1.call-update) | async-done | bytes 4194320 | tf_op jit(solution)/shard_map/all_gather | solution.py:124
  355.4 3.0 fusion.27
  (85 shorter events, 20.3 us)
Async XLA Ops:
  6.5 158.5 %copy-start = (bf16[1024,512]{1,0:T(8,128)(2,1)S(1)}, bf16[1024,512]{1,0:T(8,128)(2,1)}, u32[]{:S(2)}) copy-start(bf16[1024,512]{1,0:T(8,128)(2,1)} %param.18) | copy-start | bytes 3145732
  6.5 9.0 %copy-start.4 = (bf16[3,3,3,128,128]{4,3,2,1,0:T(8,128)(2,1)S(1)}, bf16[3,3,3,128,128]{4,3,2,1,0:T(8,128)(2,1)}, u32[]{:S(2)}) copy-start(bf16[3,3,3,128,128]{4,3,2,1,0:T(8,128)(2,1)} %param.14) | copy-start | bytes 2654212
  6.5 256.4 %all-gather.5.cloned.1.call-start = ((), (), s32[]{:S(2)}) async-start(), calls=%async_computation | async-start | bytes 4325376 | tf_op jit(solution)/shard_map/all_gather | solution.py:123
  10.4 27.4 %collective-permute-start = (bf16[2,32,64,128]{3,2,1,0:T(8,128)(2,1)S(1)}, bf16[2,32,64,128]{3,2,1,0:T(8,128)(2,1)}, u32[]{:S(2)}, u32[]{:S(2)}) collective-permute-start(bf16[2,32,64,128]{3,2,1,0:T(8,128)(2,1)S(1)} %fusion.7), channel_id=1, source_target_pairs={{0,32},{32,64},{64,96},{96,128},{128,160},{160,192},{192,224},{1,3... | collective-permute-start | bytes 3145736 | tf_op jit(solution)/shard_map/ppermute | solution.py:14
  41.0 4.4 %collective-permute-start.1 = (bf16[4,1,64,128]{3,2,1,0:T(8,128)(2,1)S(1)}, bf16[4,1,64,128]{3,2,1,0:T(8,128)(2,1)S(1)}, u32[]{:S(2)}, u32[]{:S(2)}) collective-permute-start(bf16[4,1,64,128]{3,2,1,0:T(8,128)(2,1)S(1)} %get-tuple-element.9), channel_id=1, source_target_pairs={{0,8},{8,16},{16,24},{1,9},{9,17},{17,25},{2,10},{10,18},{18,26},{... | collective-permute-start | bytes 196616 | tf_op jit(solution)/shard_map/ppermute | solution.py:22
  42.3 6.4 %collective-permute-start.2 = (bf16[4,1,64,128]{3,2,1,0:T(8,128)(2,1)S(1)}, bf16[4,1,64,128]{3,2,1,0:T(8,128)(2,1)S(1)}, u32[]{:S(2)}, u32[]{:S(2)}) collective-permute-start(bf16[4,1,64,128]{3,2,1,0:T(8,128)(2,1)S(1)} %get-tuple-element.10), channel_id=1, source_target_pairs={{8,0},{16,8},{24,16},{9,1},{17,9},{25,17},{10,2},{18,10},{26,18},{... | collective-permute-start | bytes 196616 | tf_op jit(solution)/shard_map/ppermute | solution.py:25
  48.8 14.4 %collective-permute-start.3 = (bf16[4,34,1,128]{3,2,1,0:T(2,128)(2,1)S(1)}, bf16[4,34,1,128]{3,2,1,0:T(2,128)(2,1)S(1)}, u32[]{:S(2)}, u32[]{:S(2)}) collective-permute-start(bf16[4,34,1,128]{3,2,1,0:T(2,128)(2,1)S(1)} %get-tuple-element.8), channel_id=1, source_target_pairs={{0,1},{1,2},{2,3},{3,4},{4,5},{5,6},{6,7},{8,9},{9,10},{10,11},{11... | collective-permute-start | bytes 104456 | tf_op jit(solution)/shard_map/ppermute | solution.py:22
  51.4 11.9 %collective-permute-start.4 = (bf16[4,34,1,128]{3,2,1,0:T(2,128)(2,1)S(1)}, bf16[4,34,1,128]{3,2,1,0:T(2,128)(2,1)S(1)}, u32[]{:S(2)}, u32[]{:S(2)}) collective-permute-start(bf16[4,34,1,128]{3,2,1,0:T(2,128)(2,1)S(1)} %get-tuple-element.7), channel_id=1, source_target_pairs={{1,0},{2,1},{3,2},{4,3},{5,4},{6,5},{7,6},{9,8},{10,9},{11,10},{12... | collective-permute-start | bytes 104456 | tf_op jit(solution)/shard_map/ppermute | solution.py:25
  66.7 26.8 %copy-start.1 = (bf16[4,34,65,128]{3,2,1,0:T(8,128)(2,1)}, bf16[4,34,65,128]{3,2,1,0:T(8,128)(2,1)S(1)}, u32[]{:S(2)}) copy-start(bf16[4,34,65,128]{3,2,1,0:T(8,128)(2,1)S(1)} %get-tuple-element.5) | copy-start | bytes 6789124
  95.3 1.8 copy-start.2
  117.5 2.4 copy-start.8
  120.1 35.6 %copy-start.3 = (bf16[3,3,3,256,256]{4,3,2,1,0:T(8,128)(2,1)S(1)}, bf16[3,3,3,256,256]{4,3,2,1,0:T(8,128)(2,1)}, u32[]{:S(2)}) copy-start(bf16[3,3,3,256,256]{4,3,2,1,0:T(8,128)(2,1)} %param.17) | copy-start | bytes 10616836
  120.1 9.8 %collective-permute-start.5 = (bf16[1,16,32,256]{3,2,1,0:T(8,128)(2,1)S(1)}, bf16[1,16,32,256]{3,2,1,0:T(8,128)(2,1)S(1)}, u32[]{:S(2)}, u32[]{:S(2)}) collective-permute-start(bf16[1,16,32,256]{3,2,1,0:T(8,128)(2,1)S(1)} %fusion.250), channel_id=1, source_target_pairs={{0,32},{32,64},{64,96},{96,128},{128,160},{160,192},{192,224},{1,3... | collective-permute-start | bytes 786440 | tf_op jit(solution)/shard_map/ppermute | solution.py:14
  130.2 10.2 %collective-permute-start.6 = (bf16[1,16,32,256]{3,2,1,0:T(8,128)(2,1)S(1)}, bf16[1,16,32,256]{3,2,1,0:T(8,128)(2,1)S(1)}, u32[]{:S(2)}, u32[]{:S(2)}) collective-permute-start(bf16[1,16,32,256]{3,2,1,0:T(8,128)(2,1)S(1)} %broadcast_select_fusion.1), channel_id=1, source_target_pairs={{0,32},{32,64},{64,96},{96,128},{128,160},{160,192},{192,224},{1,3... | collective-permute-start | bytes 786440 | tf_op jit(solution)/shard_map/ppermute | solution.py:14
  140.7 5.7 %collective-permute-start.7 = (bf16[3,1,32,256]{3,2,1,0:T(8,128)(2,1)S(1)}, bf16[3,1,32,256]{3,2,1,0:T(8,128)(2,1)S(1)}, u32[]{:S(2)}, u32[]{:S(2)}) collective-permute-start(bf16[3,1,32,256]{3,2,1,0:T(8,128)(2,1)S(1)} %get-tuple-element.15), channel_id=1, source_target_pairs={{0,8},{8,16},{16,24},{1,9},{9,17},{17,25},{2,10},{10,18},{18,26},{... | collective-permute-start | bytes 147464 | tf_op jit(solution)/shard_map/ppermute | solution.py:22
  145.0 4.7 %collective-permute-start.8 = (bf16[3,1,32,256]{3,2,1,0:T(8,128)(2,1)S(1)}, bf16[3,1,32,256]{3,2,1,0:T(8,128)(2,1)S(1)}, u32[]{:S(2)}, u32[]{:S(2)}) collective-permute-start(bf16[3,1,32,256]{3,2,1,0:T(8,128)(2,1)S(1)} %get-tuple-element.16), channel_id=1, source_target_pairs={{8,0},{16,8},{24,16},{9,1},{17,9},{25,17},{10,2},{18,10},{26,18},{... | collective-permute-start | bytes 147464 | tf_op jit(solution)/shard_map/ppermute | solution.py:25
  149.8 6.1 %collective-permute-start.10 = (bf16[3,18,1,256]{3,2,1,0:T(2,128)(2,1)S(1)}, bf16[3,18,1,256]{3,2,1,0:T(2,128)(2,1)S(1)}, u32[]{:S(2)}, u32[]{:S(2)}) collective-permute-start(bf16[3,18,1,256]{3,2,1,0:T(2,128)(2,1)S(1)} %get-tuple-element.14), channel_id=1, source_target_pairs={{1,0},{2,1},{3,2},{4,3},{5,4},{6,5},{7,6},{9,8},{10,9},{11,10},{12... | collective-permute-start | bytes 82952 | tf_op jit(solution)/shard_map/ppermute | solution.py:25
  151.1 6.4 %collective-permute-start.9 = (bf16[3,18,1,256]{3,2,1,0:T(2,128)(2,1)S(1)}, bf16[3,18,1,256]{3,2,1,0:T(2,128)(2,1)S(1)}, u32[]{:S(2)}, u32[]{:S(2)}) collective-permute-start(bf16[3,18,1,256]{3,2,1,0:T(2,128)(2,1)S(1)} %get-tuple-element.13), channel_id=1, source_target_pairs={{0,1},{1,2},{2,3},{3,4},{4,5},{5,6},{6,7},{8,9},{9,10},{10,11},{11... | collective-permute-start | bytes 82952 | tf_op jit(solution)/shard_map/ppermute | solution.py:22
  164.6 0.9 copy-start.9
  164.6 1.0 copy-start.5
  164.6 2.0 copy-start.6
  166.5 188.8 %all-gather.7.cloned.1.call-start = ((), (), s32[]{:S(2)}) async-start(), calls=%async_computation.1 | async-start | bytes 4325376 | tf_op jit(solution)/shard_map/all_gather | solution.py:124
  355.4 3.0 copy-start.7
Sparse Core Ops, SparseCore 0:
  166.7 96.2 all-gather.4
  264.7 90.5 all-gather.6
where the time goes:
time: 369 us; the launch traced here: 366 us
  waiting for transfers between devices  221 us (60%)
  matrix products  84 us (23%)
  starting transfers between devices  34.5 us (9%)
  between operations  14 us (4%)
  other arithmetic  11 us (3%)
    all_gather x1, waiting for transfers between devices, per_device(): lax.all_gather(key_rows, ('height', 'width'), axis=1, tiled=True)  95.4 us
    all_gather x1, waiting for transfers between devices, per_device(): lax.all_gather(value_rows, ('height', 'width'), axis=1, tiled=True)  87.9 us
    dot_general x54, matrix products, causal_conv(): jnp.einsum('fhwc,cd->fhwd', window, weight[shift_t, shift_h, shift_w], pr...  72.3 us
    ppermute x3, waiting for transfers between devices, passed_along(): lax.ppermute(value, axis, [(source, source + steps) for source in range(i...  29 us
    ppermute x3, starting transfers between devices, passed_along(): lax.ppermute(value, axis, [(source, source + steps) for source in range(i...  16.6 us
    ppermute x4, starting transfers between devices, padded_2(): lax.ppermute(lax.slice_in_dim(block, block.shape[dim] - width, None, axis...  12.7 us
  transfers between devices with their start and end apart: 13, of which 8 were waited for; matrix products, arithmetic and copies ran while one was open for 5% of the time, Pallas kernels for 0%

commit v1 on v0

v1 whole, which is shorter than its diff:
```python
import math

import jax
import jax.numpy as jnp
from jax import lax
from jax.sharding import Mesh, PartitionSpec as P

EPSILON = 1e-06
BF16 = jnp.bfloat16
F32 = jnp.float32
HEIGHT = ("hx", "core")
ALL_GATHER = ("hx", "width")


def swapped(value, axis, count, first):
    pairs = []
    for low in range(first, count - 1, 2):
        pairs += [(low, low + 1), (low + 1, low)]
    return lax.ppermute(value, axis, pairs)


def halo(block, axis, dim, width, count):
    even = lax.axis_index(axis) % 2 == 0
    low = lax.slice_in_dim(block, 0, width, axis=dim)
    high = lax.slice_in_dim(block, block.shape[dim] - width, None, axis=dim)
    got_inner = swapped(jnp.where(even, high, low), axis, count, 0)
    got_outer = swapped(jnp.where(even, low, high), axis, count, 1)
    before = jnp.where(even, got_outer, got_inner)
    after = jnp.where(even, got_inner, got_outer)
    return jnp.concatenate([before, block, after], axis=dim)


def channel_norm(inputs, gain):
    values = inputs.astype(F32)
    return values * lax.rsqrt(jnp.mean(values * values, axis=-1, keepdims=True) + EPSILON) * gain


def composed_fine(conv_fine, down_fine, at_start):
    taps = conv_fine.astype(F32)
    k0, k1, k2 = taps[0], taps[1], taps[2]
    both = k0 + k1
    k2s = jnp.where(at_start, both + k2, k2)
    k1s = jnp.where(at_start, both, k1)
    zero = jnp.zeros_like(k0)
    left = jnp.stack([k2s, zero, k0, k1], 0)
    right = jnp.stack([k1s, k2, zero, k0], 0)
    lhs = jnp.concatenate([left, right], -1).astype(BF16)
    lhs = lhs.transpose(0, 3, 1, 2, 4).reshape(512, 3, 3, 256)
    down = down_fine.reshape(2, 2, 2, 128, 256).transpose(1, 2, 0, 3, 4).reshape(2, 2, 256, 256)
    down = down[::-1, ::-1]
    out = lax.conv_general_dilated(
        lhs, down, (1, 1), ((1, 1), (1, 1)),
        dimension_numbers=("NHWC", "HWIO", "NHWC"), preferred_element_type=F32,
    ).astype(BF16)
    out = out.reshape(2, 256, 4, 4, 256).transpose(2, 3, 1, 0, 4)
    return out.reshape(4, 4, 256, 512)


def fold(field):
    rows, cols, channels = field.shape
    grouped = field.reshape(rows // 2, 2, cols // 2, 2, channels).transpose(0, 2, 1, 3, 4)
    return grouped.reshape(rows // 2 * (cols // 2), 4 * channels)


def dot(a, b):
    return jnp.dot(a, b, preferred_element_type=F32)


def per_device(
    features, gain_fine, conv_fine, down_fine, gain_coarse, conv_coarse, down_coarse,
    gain_latent, w_query, w_key, w_value, w_out,
):
    tm = lax.axis_index("tm")
    at_start = tm == 0
    h, w = lax.axis_index(HEIGHT), lax.axis_index("width")
    padded = halo(features, HEIGHT, 1, 3, 4)
    padded = halo(padded, "width", 2, 3, 8)
    weight = composed_fine(conv_fine, down_fine, at_start)
    scale = 1.0 / math.sqrt(512)
    w_score = (jnp.einsum("ab,cb->ac", w_query, w_key, preferred_element_type=F32) * scale).astype(BF16)
    w_mix = dot(w_value, w_out).astype(BF16)
    active = jax.nn.silu(channel_norm(padded, gain_fine)).astype(BF16)
    active = jnp.concatenate([active[0], active[1]], -1)
    out = lax.conv_general_dilated(
        active[None], weight, (2, 2), "VALID",
        dimension_numbers=("NHWC", "HWIO", "NHWC"), preferred_element_type=F32,
    )[0]
    sent = lax.ppermute(out[..., 256:].astype(BF16), "tm", [(i, i + 1) for i in range(7)])
    plain = jnp.concatenate([padded[0], padded[1]], -1)[1:37, 1:69]
    down = down_fine.reshape(2, 2, 2, 128, 256).transpose(1, 2, 0, 3, 4).reshape(1024, 256)
    own = out[..., :256] + dot(fold(plain), down).reshape(18, 34, 256)
    reduced = (own + sent.astype(F32)).astype(BF16)
    rows = jnp.arange(18)[:, None, None]
    cols = jnp.arange(34)[None, :, None]
    inside = ((rows > 0) | (h > 0)) & ((rows < 17) | (h < 3)) & ((cols > 0) | (w > 0)) & ((cols < 33) | (w < 7))
    active_coarse = jnp.where(inside, jax.nn.silu(channel_norm(reduced, gain_coarse)), 0.0).astype(BF16)
    kernel = conv_coarse.transpose(1, 2, 3, 0, 4).reshape(3, 3, 256, 768)
    conv = lax.conv_general_dilated(
        active_coarse[None], kernel, (1, 1), "VALID",
        dimension_numbers=("NHWC", "HWIO", "NHWC"), preferred_element_type=F32,
    )[0]
    c0, c1, c2 = conv[..., :256], conv[..., 256:512], conv[..., 512:]
    c1 = jnp.where(at_start, c1 + c0, c1)
    c2 = jnp.where(at_start, c2 + c1, c2)
    far = dot(fold(c0.astype(BF16)), down_coarse).astype(BF16)
    near = dot(fold(c1.astype(BF16)), down_coarse).astype(BF16)
    near = lax.ppermute(near, "tm", [(i, i + 1) for i in range(7)])
    far = lax.ppermute(far, "tm", [(i, i + 2) for i in range(6)])
    hidden = (reduced[1:17, 1:33].astype(F32) + c2).astype(BF16)
    latent_in = (dot(fold(hidden), down_coarse) + near.astype(F32) + far.astype(F32)).astype(BF16)
    normed = channel_norm(latent_in, gain_latent).astype(BF16)
    other = swapped(normed, "core", 2, 0)
    copies = jnp.broadcast_to(normed[None], (16,) + normed.shape)
    keys = lax.all_to_all(copies, ALL_GATHER, 0, 0, tiled=True).reshape(2048, 512)
    queries = dot(jnp.concatenate([normed, other], 0), w_score).astype(BF16)
    scores = jnp.einsum("qc,kc->qk", queries, keys, preferred_element_type=F32)
    top = jnp.max(scores, -1, keepdims=True)
    expo = jnp.exp(scores - top)
    total = jnp.sum(expo, -1, keepdims=True)
    mixed = dot(expo.astype(BF16), keys) / total
    level = top + jnp.log(total)
    theirs = swapped(mixed[128:].astype(BF16), "core", 2, 0)
    their_level = swapped(jnp.broadcast_to(level[128:], (128, 128)), "core", 2, 0)[:, :1]
    share = jax.nn.sigmoid(level[:128] - their_level)
    attended = (mixed[:128] * share + theirs.astype(F32) * (1.0 - share)).astype(BF16)
    return (latent_in.astype(F32) + dot(attended, w_mix)).astype(BF16).reshape(1, 8, 16, 512)


def solution(mesh):
    split = Mesh(mesh.devices.reshape(8, 2, 2, 8), ("tm", "hx", "core", "width"))
    placed = (P("tm", HEIGHT, "width", None),) + (P(),) * 11
    return jax.shard_map(
        per_device, mesh=split, in_specs=placed,
        out_specs=P("tm", HEIGHT, "width", None), check_vma=False,
    )
```

time: 369 us -> 127 us (0.34)
  waiting for transfers between devices: 221 us -> 34.2 us
  matrix products: 84 us -> 22.6 us
  local copies, waits for them, and re-layouts: 2.11 us -> 29.7 us
  between operations: 14 us -> 0.63 us
  starting transfers between devices: 34.5 us -> 28.9 us
    all_gather x2 -> x0, waiting for transfers between devices: 183 us -> none  [the longest x1 95.4 us: per_device(): lax.all_gather(key_rows, ('height', 'width'), axis=1, tiled=True)]
    dot_general x61 -> x8, matrix products: 84 us -> 11.1 us  [the longest x7 9.31 us: dot(): return jnp.dot(a, b, preferred_element_type=F32)]
    ppermute x11 -> x10, waiting for transfers between devices: 37.2 us -> 9 us  [the longest x1 4.55 us: per_device(): far = lax.ppermute(far, 'tm', [(i, i + 2) for i in range(6)])]
    all_to_all x0 -> x1, waiting for transfers between devices: none -> 25.2 us  [per_device(): lax.all_to_all(copies, ALL_GATHER, 0, 0, tiled=True).reshape(2048, 512)]
    ppermute x11 -> x10, starting transfers between devices: 34.5 us -> 20.8 us  [the longest x7 7.66 us: swapped(): return lax.ppermute(value, axis, pairs)]
    unnamed x20 -> x39, local copies, waits for them, and re-layouts: 0.07 us -> 12.8 us
    conv_general_dilated x0 -> x3, matrix products: none -> 11.6 us  [the longest x1 5.85 us: composed_fine(): lax.conv_general_dilated(lhs, down, (1, 1), ((1, 1), (1, 1)), dimension_n...]
    all_to_all x0 -> x1, starting transfers between devices: none -> 8.1 us  [per_device(): lax.all_to_all(copies, ALL_GATHER, 0, 0, tiled=True).reshape(2048, 512)]
  transfers between devices with their start and end apart: 13 -> 11, of which waited for: 8 -> 6; matrix products, arithmetic and copies ran while one was open for 5% -> 24% of each run, Pallas kernels for 0% -> 0%
where the time goes in v1:
time: 127 us; the launch traced here: 125 us
  waiting for transfers between devices  34.2 us (27%)
  local copies, waits for them, and re-layouts  29.7 us (23%)
  starting transfers between devices  28.9 us (23%)
  matrix products  22.6 us (18%)
  other arithmetic  9.22 us (7%)
    all_to_all x1, waiting for transfers between devices, per_device(): lax.all_to_all(copies, ALL_GATHER, 0, 0, tiled=True).reshape(2048, 512)  25.2 us
    unnamed x39, local copies, waits for them, and re-layouts  12.8 us
    dot_general x7, matrix products, dot(): return jnp.dot(a, b, preferred_element_type=F32)  9.31 us
    all_to_all x1, starting transfers between devices, per_device(): lax.all_to_all(copies, ALL_GATHER, 0, 0, tiled=True).reshape(2048, 512)  8.1 us
    ppermute x7, starting transfers between devices, swapped(): return lax.ppermute(value, axis, pairs)  7.66 us
    conv_general_dilated x1, matrix products, composed_fine(): lax.conv_general_dilated(lhs, down, (1, 1), ((1, 1), (1, 1)), dimension_n...  5.85 us
    ppermute x1, starting transfers between devices, per_device(): near = lax.ppermute(near, 'tm', [(i, i + 1) for i in range(7)])  5.7 us
    ppermute x1, starting transfers between devices, per_device(): lax.ppermute(out[..., 256:].astype(BF16), 'tm', [(i, i + 1) for i in rang...  5.25 us
  transfers between devices with their start and end apart: 11, of which 6 were waited for; matrix products, arithmetic and copies ran while one was open for 24% of the time, Pallas kernels for 0%

profile of v1, /device:TPU:96, one launch (start us, length us, event | category | flops | bytes accessed | tf_op | source)
XLA Modules:
  0.0 125.3 jit_solution(17851268360869384924)
XLA Ops:
  0.0 1.7 %broadcast_select_fusion.3 = (bf16[2,3,64,128]{3,2,1,0:T(8,128)(2,1)}, bf16[2,3,64,128]{3,2,1,0:T(8,128)(2,1)}) fusion(pred[]{:T(512)S(6)} %eq.13, bf16[2,32,64,128]{3,2,1,0:T(8,128)(2,1)} %param.12), kind=kLoop, calls=%fused_computation.105 | loop fusion | flops 98304 | bytes 393217 | tf_op jit(solution)/shard_map/jit(_where)/select_n | solution.py:27
  1.7 0.7 collective-permute-start
  2.4 4.5 %collective-permute-start.1 = (bf16[2,3,64,128]{3,2,1,0:T(8,128)(2,1)}, bf16[2,3,64,128]{3,2,1,0:T(8,128)(2,1)}, u32[]{:S(2)}, u32[]{:S(2)}) collective-permute-start(bf16[2,3,64,128]{3,2,1,0:T(8,128)(2,1)} %get-tuple-element.25), channel_id=1, source_target_pairs={{0,8},{8,0},{16,24},{24,16},{1,9},{9,1},{17,25},{25,17},{2,10},{10... | collective-permute-start | bytes 294920 | tf_op jit(solution)/shard_map/ppermute | solution.py:19
  6.8 1.4 %convert_element_type.84 = f32[3,3,3,128,128]{4,3,2,1,0:T(8,128)S(1)} convert(bf16[3,3,3,128,128]{4,3,2,1,0:T(8,128)(2,1)} %param.14) | non-fusion elementwise | flops 442368 | bytes 2654208 | tf_op jit(solution)/shard_map/convert_element_type | solution.py:39
  8.3 0.9 fusion.73
  9.4 1.0 slice-done
  11.0 0.8 copy-done.10
  11.8 0.9 copy.25
  12.7 5.8 %convolution_convert_fusion = bf16[512,4,4,256]{3,0,2,1:T(8,128)(2,1)S(1)} fusion(bf16[512,3,3,256]{3,0,2,1:T(8,128)(2,1)S(1)} %bitcast.89, bf16[2,2,256,256]{3,2,1,0:T(8,128)(2,1)} %bitcast.103), kind=kOutput, calls=%fused_computation.12 | convolution fusion | flops 2418016256 | bytes 7077888 | tf_op jit(solution)/shard_map/conv_general_dilated | solution.py:51
  18.6 0.9 broadcast_select_fusion.1
  19.7 0.7 collective-permute-start.3
  20.3 0.8 collective-permute-start.2
  21.2 2.3 %copy.44 = bf16[4,4,2,32,8,256]{5,4,2,3,1,0:T(8,128)(2,1)} copy(bf16[4,4,2,32,8,256]{5,4,3,2,1,0:T(8,128)(2,1)S(1)} %bitcast.90) | data formatting | bytes 8388608 | tf_op jit(solution)/shard_map/reshape | solution.py:56
  23.6 6.1 %copy.34 = bf16[3,3,3,256,256]{3,4,0,2,1:T(8,128)(2,1)} copy(bf16[3,3,3,256,256]{4,3,2,1,0:T(8,128)(2,1)} %param.17) | data formatting | bytes 7077888 | tf_op args[5]
  29.8 1.4 %fusion.1 = (f32[2,38,70]{2,1,0:T(8,128)S(1)}, bf16[2,38,70,128]{3,2,1,0:T(8,128)(2,1)S(1)}) fusion(bf16[2,38,3,128]{3,2,1,0:T(4,128)(2,1)S(1)} %get-tuple-element.31, bf16[2,3,64,128]{3,2,1,0:T(8,128)(2,1)S(1)} %get-tuple-element.29, bf16[2,32,64,128]{3,2,1,0:T(8,128)(2,1)S(1)} %copy-done.2, bf16[2,3,64,128]{3,2,1,0:T(8,128)(2,1)S(1)} %get-tuple-element.28, ...), kind=kLoop, calls=%fused_computation.4 | loop fusion | flops 8847160 | bytes 2745120 | tf_op jit(solution)/shard_map/reduce_sum | solution.py:35
  31.2 1.0 fusion.8
  33.0 0.5 copy.23
  33.6 1.4 %copy-done.4 = bf16[4,4,2,32,8,256]{5,4,2,3,1,0:T(8,128)(2,1)S(1)} copy-done((bf16[4,4,2,32,8,256]{5,4,2,3,1,0:T(8,128)(2,1)S(1)}, bf16[4,4,2,32,8,256]{5,4,2,3,1,0:T(8,128)(2,1)}, u32[]{:S(2)}) %copy-start.4) | copy-done | bytes 4194328
  35.0 3.2 %fusion.18 = f32[18,8,5,512]{3,1,2,0:T(8,128)S(1)} fusion(bf16[4,4,256,512]{3,2,1,0:T(8,128)(2,1)S(1)} %bitcast.99, bf16[38,1,7,3,256]{4,2,3,0,1:T(8,128)(2,1)S(1)} %slice.110, bf16[38,1,8,10,256]{4,2,3,0,1:T(8,128)(2,1)S(1)} %copy.23, pred[8,5]{0,1:T(8,128)(4,1)S(1)} %copy-done.16), kind=kOutput, calls=%fused_computation.28 | convolution fusion | flops 3026337792 | bytes 7633960 | tf_op jit(solution)/shard_map/conv_general_dilated | solution.py:84
  38.2 0.9 copy.27
  39.3 0.7 copy.52
  40.1 1.1 copy-done.6
  41.1 5.3 %collective-permute-start.4 = (bf16[18,34,256]{2,1,0:T(8,128)(2,1)S(1)}, bf16[18,34,256]{2,1,0:T(8,128)(2,1)}, u32[]{:S(2)}, u32[]{:S(2)}) collective-permute-start(bf16[18,34,256]{2,1,0:T(8,128)(2,1)S(1)} %slice.180), channel_id=1, source_target_pairs={{0,32},{32,64},{64,96},{96,128},{128,160},{160,192},{192,224},{1,3... | collective-permute-start | bytes 940040 | tf_op jit(solution)/shard_map/ppermute | solution.py:88
  46.5 0.7 pad_maximum_fusion.1
  47.2 1.7 %reshape.186 = bf16[18,2,34,2,256]{4,3,2,1,0:T(2,128)(2,1)} reshape(bf16[36,68,256]{2,1,0:T(8,128)(2,1)S(1)} %pad_maximum_fusion.1) | data formatting | bytes 2506752 | tf_op jit(solution)/shard_map/reshape | solution.py:61
  49.0 2.2 %copy.53 = bf16[18,2,34,2,256]{4,3,1,2,0:T(2,128)(2,1)S(1)} copy(bf16[18,2,34,2,256]{4,3,2,1,0:T(2,128)(2,1)} %reshape.186) | data formatting | bytes 2506752 | tf_op jit(solution)/shard_map/reshape | solution.py:61
  51.2 1.7 %dot_general.32 = bf16[18,34,1024]{2,1,0:T(8,128)(2,1)} reshape(bf16[18,34,2,2,256]{4,3,2,1,0:T(2,128)(2,1)S(1)} %bitcast.98) | data formatting | bytes 2506752 | tf_op jit(solution)/shard_map/dot_general | solution.py:66
  52.9 1.0 collective-permute-done.4
  53.9 2.3 %fusion.31 = (f32[18,34]{1,0:T(8,128)S(1)}, bf16[18,34,256]{2,1,0:T(8,128)(2,1)S(1)}) fusion(bf16[18,34,256]{2,1,0:T(8,128)(2,1)} %collective-permute-done.4, bf16[18,34,1024]{2,1,0:T(8,128)(2,1)} %dot_general.32, bf16[1024,256,1]{1,0,2:T(8,128)(2,1)S(1)} %bitcast.104, f32[18,34,512]{2,1,0:T(8,128)} %bitcast.102), kind=kOutput, calls=%fused_computation.52 | convolution fusion | flops 321960352 | bytes 3033488 | tf_op jit(solution)/shard_map/dot_general | solution.py:66
  56.9 1.4 %copy-done.5 = bf16[3,3,3,256,256]{3,4,0,2,1:T(8,128)(2,1)S(1)} copy-done((bf16[3,3,3,256,256]{3,4,0,2,1:T(8,128)(2,1)S(1)}, bf16[3,3,3,256,256]{3,4,0,2,1:T(8,128)(2,1)}, u32[]{:S(2)}) %copy-start.5) | copy-done | bytes 3538968
  58.3 2.5 %convolution_select_fusion = f32[16,8,5,768]{3,1,2,0:T(8,128)S(1)} fusion(bf16[3,3,256,768]{2,3,1,0:T(8,128)(2,1)S(1)} %bitcast.100, pred[8,5]{0,1:T(8,128)(4,1)S(1)} %copy-done.15, bf16[18,1,7,2,256]{4,2,3,0,1:T(8,128)(2,1)S(1)} %slice.120, bf16[18,1,8,5,256]{4,2,3,0,1:T(8,128)(2,1)S(1)} %copy.33), kind=kOutput, calls=%fused_computation.24 | convolution fusion | flops 2266963968 | bytes 6002728 | tf_op jit(solution)/shard_map/conv_general_dilated | solution.py:98
  60.8 0.6 copy.35
  61.5 0.9 copy.51
  63.5 5.7 %collective-permute-start.5 = (bf16[128,512]{1,0:T(8,128)(2,1)S(1)}, bf16[128,512]{1,0:T(8,128)(2,1)S(1)}, u32[]{:S(2)}, u32[]{:S(2)}) collective-permute-start(bf16[128,512]{1,0:T(8,128)(2,1)S(1)} %convolution_convert_fusion.3), channel_id=1, source_target_pairs={{0,32},{32,64},{64,96},{96,128},{128,160},{160,192},{192,224},{1,3... | collective-permute-start | bytes 393224 | tf_op jit(solution)/shard_map/ppermute | solution.py:107
  70.0 2.2 %collective-permute-start.6 = (bf16[128,512]{1,0:T(8,128)(2,1)S(1)}, bf16[128,512]{1,0:T(8,128)(2,1)S(1)}, u32[]{:S(2)}, u32[]{:S(2)}) collective-permute-start(bf16[128,512]{1,0:T(8,128)(2,1)S(1)} %convolution_convert_fusion.2), channel_id=1, source_target_pairs={{0,64},{32,96},{64,128},{96,160},{128,192},{160,224},{1,65},{33,97... | collective-permute-start | bytes 393224 | tf_op jit(solution)/shard_map/ppermute | solution.py:108
  72.7 1.1 collective-permute-done.5
  73.7 4.5 %collective-permute-done.6 = bf16[128,512]{1,0:T(8,128)(2,1)S(1)} collective-permute-done((bf16[128,512]{1,0:T(8,128)(2,1)S(1)}, bf16[128,512]{1,0:T(8,128)(2,1)S(1)}, u32[]{:S(2)}, u32[]{:S(2)}) %collective-permute-start.6) | collective-permute-done | bytes 131104 | tf_op jit(solution)/shard_map/ppermute | solution.py:108
  78.8 1.6 %broadcast_in_dim.24 = bf16[16,128,512]{2,1,0:T(8,128)(2,1)} broadcast(bf16[128,512]{1,0:T(8,128)(2,1)S(1)} %fusion.53), dimensions={1,2} | broadcast | bytes 2228224 | tf_op jit(solution)/shard_map/broadcast_in_dim | solution.py:113
  80.4 8.1 %all-to-all-start = ((bf16[16,128,512]{2,1,0:T(8,128)(2,1)}), bf16[16,128,512]{2,1,0:T(8,128)(2,1)S(1)}, u32[]{:S(2)}, u32[]{:S(2)}) async-start(bf16[16,128,512]{2,1,0:T(8,128)(2,1)} %broadcast_in_dim.24), calls=%async_computation | async-start | bytes 4194304 | tf_op jit(solution)/shard_map/all_to_all | solution.py:114
  88.9 1.3 %collective-permute-done.7 = bf16[128,512]{1,0:T(8,128)(2,1)S(1)} collective-permute-done((bf16[128,512]{1,0:T(8,128)(2,1)S(1)}, bf16[128,512]{1,0:T(8,128)(2,1)S(1)}, u32[]{:S(2)}, u32[]{:S(2)}) %collective-permute-start.7) | collective-permute-done | bytes 131104 | tf_op jit(solution)/shard_map/ppermute | solution.py:19
  90.2 2.6 %fusion.24 = bf16[256,512]{1,0:T(8,128)(2,1)} fusion(bf16[512,512]{1,0:T(8,128)(2,1)} %param.20, bf16[512,512]{1,0:T(8,128)(2,1)} %param.21, bf16[128,512]{1,0:T(8,128)(2,1)S(1)} %collective-permute-done.7, bf16[128,512]{1,0:T(8,128)(2,1)S(1)} %fusion.53), kind=kOutput, calls=%fused_computation.38 | convolution fusion | flops 403832832 | bytes 1572864 | tf_op jit(solution)/shard_map/dot_general | solution.py:66
  92.8 25.2 %all-to-all-done = bf16[16,128,512]{2,1,0:T(8,128)(2,1)S(1)} async-done(((bf16[16,128,512]{2,1,0:T(8,128)(2,1)}), bf16[16,128,512]{2,1,0:T(8,128)(2,1)S(1)}, u32[]{:S(2)}, u32[]{:S(2)}) %all-to-all-start) | async-done | bytes 2097184 | tf_op jit(solution)/shard_map/all_to_all | solution.py:114
  117.9 1.8 %fusion.74 = (f32[256]{0:T(256)S(1)}, f32[256,2048]{1,0:T(8,128)S(1)}) fusion(bf16[256,512]{1,0:T(8,128)(2,1)} %fusion.24, bf16[2048,512]{1,0:T(8,128)(2,1)S(1)} %bitcast.91), kind=kOutput, calls=%fused_computation.134 | convolution fusion | flops 537394944 | bytes 4457472 | tf_op jit(solution)/shard_map/qc,kc->qk/dot_general | solution.py:116
  119.7 0.4 fusion.16
  120.3 0.8 convolution_divide_fusion
  121.1 0.6 collective-permute-start.9
  121.7 1.0 collective-permute-done.9
  122.7 2.5 %fusion.26 = bf16[128,512]{1,0:T(8,128)(2,1)} fusion(bf16[512,512]{1,0:T(8,128)(2,1)} %param.22, bf16[512,512]{1,0:T(8,128)(2,1)} %param.23, bf16[128,512]{1,0:T(8,128)(2,1)S(1)} %get-tuple-element.8, f32[256,512]{1,0:T(8,128)} %copy-done.11, bf16[128,512]{1,0:T(8,128)(2,1)S(1)} %collective-permute-done.9, f32[128]{0:T(128)S(1)} %get-tuple-element.5, ...), kind=kOutput, calls=%fused_computation.42 | convolution fusion | flops 336330752 | bytes 1704960 | tf_op jit(solution)/shard_map/dot_general | solution.py:66
  (86 shorter events, 6.1 us)
Async XLA Ops:
  0.0 63.2 %copy-start = (bf16[1024,512]{1,0:T(8,128)(2,1)S(1)}, bf16[1024,512]{1,0:T(8,128)(2,1)}, u32[]{:S(2)}) copy-start(bf16[1024,512]{1,0:T(8,128)(2,1)} %param.18) | copy-start | bytes 3145732
  1.7 16.8 %collective-permute-start = (bf16[2,3,64,128]{3,2,1,0:T(8,128)(2,1)}, bf16[2,3,64,128]{3,2,1,0:T(8,128)(2,1)S(1)}, u32[]{:S(2)}, u32[]{:S(2)}) collective-permute-start(bf16[2,3,64,128]{3,2,1,0:T(8,128)(2,1)} %get-tuple-element.24), channel_id=1, source_target_pairs={{8,16},{16,8},{9,17},{17,9},{10,18},{18,10},{11,19},{19,11},{12,20... | collective-permute-start | bytes 294920 | tf_op jit(solution)/shard_map/ppermute | solution.py:19
  2.4 16.2 %collective-permute-start.1 = (bf16[2,3,64,128]{3,2,1,0:T(8,128)(2,1)}, bf16[2,3,64,128]{3,2,1,0:T(8,128)(2,1)}, u32[]{:S(2)}, u32[]{:S(2)}) collective-permute-start(bf16[2,3,64,128]{3,2,1,0:T(8,128)(2,1)} %get-tuple-element.25), channel_id=1, source_target_pairs={{0,8},{8,0},{16,24},{24,16},{1,9},{9,1},{17,25},{25,17},{2,10},{10... | collective-permute-start | bytes 294920 | tf_op jit(solution)/shard_map/ppermute | solution.py:19
  6.8 1.4 %copy-start.3 = (bf16[3,3,3,128,128]{4,3,2,1,0:T(8,128)(2,1)S(1)}, bf16[3,3,3,128,128]{4,3,2,1,0:T(8,128)(2,1)}, u32[]{:S(2)}) copy-start(bf16[3,3,3,128,128]{4,3,2,1,0:T(8,128)(2,1)} %param.14) | copy-start | bytes 2654212
  9.2 1.2 slice-start
  9.2 1.2 copy-start.8
  9.2 1.2 copy-start.9
  10.7 1.0 copy-start.10
  12.7 6.8 %copy-start.1 = (bf16[2,32,64,128]{3,2,1,0:T(8,128)(2,1)S(1)}, bf16[2,32,64,128]{3,2,1,0:T(8,128)(2,1)}, u32[]{:S(2)}) copy-start(bf16[2,32,64,128]{3,2,1,0:T(8,128)(2,1)} %param.12) | copy-start | bytes 3145732
  19.7 10.1 %collective-permute-start.3 = (bf16[2,38,3,128]{3,2,1,0:T(4,128)(2,1)S(1)}, bf16[2,38,3,128]{3,2,1,0:T(4,128)(2,1)S(1)}, u32[]{:S(2)}, u32[]{:S(2)}) collective-permute-start(bf16[2,38,3,128]{3,2,1,0:T(4,128)(2,1)S(1)} %broadcast_select_fusion.6), channel_id=1, source_target_pairs={{0,1},{1,0},{2,3},{3,2},{4,5},{5,4},{6,7},{7,6},{8,9},{9,8},{10,11... | collective-permute-start | bytes 175112 | tf_op jit(solution)/shard_map/ppermute | solution.py:19
  20.3 9.4 %collective-permute-start.2 = (bf16[2,38,3,128]{3,2,1,0:T(4,128)(2,1)S(1)}, bf16[2,38,3,128]{3,2,1,0:T(4,128)(2,1)S(1)}, u32[]{:S(2)}, u32[]{:S(2)}) collective-permute-start(bf16[2,38,3,128]{3,2,1,0:T(4,128)(2,1)S(1)} %get-tuple-element.13), channel_id=1, source_target_pairs={{1,2},{2,1},{3,4},{4,3},{5,6},{6,5},{9,10},{10,9},{11,12},{12,11},... | collective-permute-start | bytes 175112 | tf_op jit(solution)/shard_map/ppermute | solution.py:19
  23.6 6.2 %copy-start.2 = (bf16[2,32,64,128]{3,2,1,0:T(8,128)(2,1)S(1)}, bf16[2,32,64,128]{3,2,1,0:T(8,128)(2,1)}, u32[]{:S(2)}) copy-start(bf16[2,32,64,128]{3,2,1,0:T(8,128)(2,1)} %param.12) | copy-start | bytes 3145732
  29.7 1.5 %copy-start.14 = (f32[128]{0:T(128)S(1)}, f32[128]{0:T(128)}, u32[]{:S(2)}) copy-start(f32[128]{0:T(128)} %param.13) | copy-start | bytes 1540
  32.8 2.2 %copy-start.4 = (bf16[4,4,2,32,8,256]{5,4,2,3,1,0:T(8,128)(2,1)S(1)}, bf16[4,4,2,32,8,256]{5,4,2,3,1,0:T(8,128)(2,1)}, u32[]{:S(2)}) copy-start(bf16[4,4,2,32,8,256]{5,4,2,3,1,0:T(8,128)(2,1)} %copy.44) | copy-start | bytes 12582916
  33.0 2.1 %copy-start.16 = (pred[8,5]{0,1:T(8,128)(4,1)S(1)}, pred[8,5]{0,1:T(8,128)(4,1)}, u32[]{:S(2)}) copy-start(pred[8,5]{0,1:T(8,128)(4,1)} %constant.82) | copy-start | bytes 124
  40.0 1.1 copy-start.6
  41.1 12.8 %collective-permute-start.4 = (bf16[18,34,256]{2,1,0:T(8,128)(2,1)S(1)}, bf16[18,34,256]{2,1,0:T(8,128)(2,1)}, u32[]{:S(2)}, u32[]{:S(2)}) collective-permute-start(bf16[18,34,256]{2,1,0:T(8,128)(2,1)S(1)} %slice.180), channel_id=1, source_target_pairs={{0,32},{32,64},{64,96},{96,128},{128,160},{160,192},{192,224},{1,3... | collective-permute-start | bytes 940040 | tf_op jit(solution)/shard_map/ppermute | solution.py:88
  49.0 4.9 %copy-start.7 = (bf16[2,2,2,128,256]{4,3,2,1,0:T(8,128)(2,1)S(1)}, bf16[2,2,2,128,256]{4,3,2,1,0:T(8,128)(2,1)}, u32[]{:S(2)}) copy-start(bf16[2,2,2,128,256]{4,3,2,1,0:T(8,128)(2,1)} %copy.25) | copy-start | bytes 1572868
  52.9 3.4 %copy-start.13 = (f32[256]{0:T(256)S(1)}, f32[256]{0:T(256)}, u32[]{:S(2)}) copy-start(f32[256]{0:T(256)} %param.16) | copy-start | bytes 3076
  56.2 2.0 %copy-start.5 = (bf16[3,3,3,256,256]{3,4,0,2,1:T(8,128)(2,1)S(1)}, bf16[3,3,3,256,256]{3,4,0,2,1:T(8,128)(2,1)}, u32[]{:S(2)}) copy-start(bf16[3,3,3,256,256]{3,4,0,2,1:T(8,128)(2,1)} %copy.34) | copy-start | bytes 10616836
  56.3 2.0 %copy-start.15 = (pred[8,5]{0,1:T(8,128)(4,1)S(1)}, pred[8,5]{0,1:T(8,128)(4,1)}, u32[]{:S(2)}) copy-start(pred[8,5]{0,1:T(8,128)(4,1)} %constant.83) | copy-start | bytes 124
  63.5 10.3 %collective-permute-start.5 = (bf16[128,512]{1,0:T(8,128)(2,1)S(1)}, bf16[128,512]{1,0:T(8,128)(2,1)S(1)}, u32[]{:S(2)}, u32[]{:S(2)}) collective-permute-start(bf16[128,512]{1,0:T(8,128)(2,1)S(1)} %convolution_convert_fusion.3), channel_id=1, source_target_pairs={{0,32},{32,64},{64,96},{96,128},{128,160},{160,192},{192,224},{1,3... | collective-permute-start | bytes 393224 | tf_op jit(solution)/shard_map/ppermute | solution.py:107
  69.7 9.0 %copy-start.12 = (f32[512]{0:T(512)S(1)}, f32[512]{0:T(512)}, u32[]{:S(2)}) copy-start(f32[512]{0:T(512)} %param.19) | copy-start | bytes 6148
  70.0 8.3 %collective-permute-start.6 = (bf16[128,512]{1,0:T(8,128)(2,1)S(1)}, bf16[128,512]{1,0:T(8,128)(2,1)S(1)}, u32[]{:S(2)}, u32[]{:S(2)}) collective-permute-start(bf16[128,512]{1,0:T(8,128)(2,1)S(1)} %convolution_convert_fusion.2), channel_id=1, source_target_pairs={{0,64},{32,96},{64,128},{96,160},{128,192},{160,224},{1,65},{33,97... | collective-permute-start | bytes 393224 | tf_op jit(solution)/shard_map/ppermute | solution.py:108
  80.4 37.6 %all-to-all-start = ((bf16[16,128,512]{2,1,0:T(8,128)(2,1)}), bf16[16,128,512]{2,1,0:T(8,128)(2,1)S(1)}, u32[]{:S(2)}, u32[]{:S(2)}) async-start(bf16[16,128,512]{2,1,0:T(8,128)(2,1)} %broadcast_in_dim.24), calls=%async_computation | async-start | bytes 4194304 | tf_op jit(solution)/shard_map/all_to_all | solution.py:114
  88.5 1.7 %collective-permute-start.7 = (bf16[128,512]{1,0:T(8,128)(2,1)S(1)}, bf16[128,512]{1,0:T(8,128)(2,1)S(1)}, u32[]{:S(2)}, u32[]{:S(2)}) collective-permute-start(bf16[128,512]{1,0:T(8,128)(2,1)S(1)} %fusion.53), channel_id=1, source_target_pairs={{0,8},{8,0},{1,9},{9,1},{2,10},{10,2},{3,11},{11,3},{4,12},{12,4},... | collective-permute-start | bytes 393224 | tf_op jit(solution)/shard_map/ppermute | solution.py:19
  120.2 1.5 %collective-permute-start.8 = (f32[128,128]{0,1:T(8,128)S(1)}, f32[128,128]{0,1:T(8,128)S(1)}, u32[]{:S(2)}, u32[]{:S(2)}) collective-permute-start(f32[128,128]{0,1:T(8,128)S(1)} %broadcast_in_dim.25), channel_id=1, source_target_pairs={{0,8},{8,0},{1,9},{9,1},{2,10},{10,2},{3,11},{11,3},{4,12},{12,4},... | collective-permute-start | bytes 196616 | tf_op jit(solution)/shard_map/ppermute | solution.py:19
  121.1 1.6 %copy-start.11 = (f32[256,512]{1,0:T(8,128)}, f32[256,512]{1,0:T(8,128)S(1)}, u32[]{:S(2)}) copy-start(f32[256,512]{1,0:T(8,128)S(1)} %convolution_divide_fusion) | copy-start | bytes 1572868
  121.1 1.6 %collective-permute-start.9 = (bf16[128,512]{1,0:T(8,128)(2,1)S(1)}, bf16[128,512]{1,0:T(8,128)(2,1)S(1)}, u32[]{:S(2)}, u32[]{:S(2)}) collective-permute-start(bf16[128,512]{1,0:T(8,128)(2,1)S(1)} %slice.184), channel_id=1, source_target_pairs={{0,8},{8,0},{1,9},{9,1},{2,10},{10,2},{3,11},{11,3},{4,12},{12,4},... | collective-permute-start | bytes 393224 | tf_op jit(solution)/shard_map/ppermute | solution.py:19

commit v2 on v1

v2 whole, which is shorter than its diff:
```python
import functools
import math

import jax
import jax.numpy as jnp
from jax import lax
from jax.experimental import pallas as pl
from jax.experimental.pallas import tpu as pltpu
from jax.sharding import Mesh, PartitionSpec as P

EPSILON = 1e-06
BF16 = jnp.bfloat16
F32 = jnp.float32
HEIGHT = ("hx", "core")
GATHER = ("hx", "width")
VMEM_LIMIT = 48 * 1024 * 1024
VM = pl.BlockSpec(memory_space=pltpu.VMEM)
HB = pl.BlockSpec(memory_space=pl.ANY)
SM = pl.BlockSpec(memory_space=pltpu.SMEM)


def call(kernel, out, ins, scratch=(), flops=0, name=None):
    return pl.pallas_call(
        kernel,
        out_shape=out,
        in_specs=ins,
        out_specs=jax.tree.map(lambda _: VM, out),
        scratch_shapes=list(scratch),
        compiler_params=pltpu.CompilerParams(vmem_limit_bytes=VMEM_LIMIT),
        cost_estimate=pl.CostEstimate(flops=flops, bytes_accessed=4 << 20, transcendentals=0),
        name=name,
    )


def shape(dims, dtype):
    return jax.ShapeDtypeStruct(dims, dtype)


def dot(a, b):
    return jnp.dot(a, b, preferred_element_type=F32)


def scaled(values, gain):
    mean = jnp.mean(values * values, axis=-1, keepdims=True)
    return values * lax.rsqrt(mean + EPSILON) * gain


def silu(values):
    return values * jax.nn.sigmoid(values)


def compose_kernel(own, flag_ref, conv_ref, down_ref, out_ref, acc):
    acc[...] = jnp.zeros_like(acc)
    start = flag_ref[0] == 0
    for i in range(3):
        k0, k1, k2 = (conv_ref[s, i].reshape(384, 128) for s in range(3))
        if own:
            f0, f1, f2 = (k.astype(F32) for k in (k0, k1, k2))
            k2s = jnp.where(start, f0 + f1 + f2, f2).astype(BF16)
            k1s = jnp.where(start, f0 + f1, f1).astype(BF16)
            wide, narrow, wide_at, narrow_at, half = jnp.concatenate([k2s, k1s], -1), k2, 0, 1, 1
        else:
            wide, narrow, wide_at, narrow_at, half = jnp.concatenate([k1, k0], -1), k0, 1, 0, 0
        for r in range(2):
            for c in range(2):
                at = (r * 2 + c) * 128
                halves = [down_ref[f * 512 + at : f * 512 + at + 128, :] for f in range(2)]
                both = dot(wide, jnp.concatenate(halves, 0))
                one = dot(narrow, halves[half])
                for j in range(3):
                    tap = (i + r) * 4 + j + c
                    rows = slice(j * 128, j * 128 + 128)
                    acc[tap, wide_at * 128 : wide_at * 128 + 128, :] += both[rows]
                    acc[tap, narrow_at * 128 : narrow_at * 128 + 128, :] += one[rows]
    out_ref[...] = acc[...].astype(BF16)


def compose(own, tm, conv_fine, down_fine):
    return call(
        functools.partial(compose_kernel, own),
        shape((16, 256, 256), BF16),
        [SM, VM, VM],
        [pltpu.VMEM((16, 256, 256), F32)],
        flops=900_000_000,
        name="compose_own" if own else "compose_next",
    )(tm, conv_fine.reshape(3, 3, 3, 128, 128), down_fine)


COLS = 104
PITCH = 48
FLAT = 624


def fine_kernel(own, x_ref, up_ref, low_ref, left_ref, right_ref, gain_ref, weight_hbm, *rest):
    if own:
        down_ref, out_ref, act, planes, weight, sem, raw, raw_planes = rest
    else:
        out_ref, act, planes, weight, sem, flat = rest
    fetch = pltpu.make_async_copy(weight_hbm, weight, sem)
    fetch.start()
    gain = gain_ref[...].reshape(1, 1, 128)

    def put(values, f, rows, cols):
        values = values.astype(F32)
        act[f, rows, cols, :] = silu(scaled(values, gain))
        if own:
            raw[f, rows, cols, :] = values

    for f in range(2):
        put(up_ref[f], f, pl.ds(0, 3), pl.ds(8, 64))
        put(low_ref[f], f, pl.ds(35, 3), pl.ds(8, 64))
        put(left_ref[f], f, pl.ds(0, 38), pl.ds(4, 4))
        put(right_ref[f], f, pl.ds(0, 38), pl.ds(72, 4))

        def inner(step, carry, f=f):
            put(x_ref[f, pl.ds(step * 4, 4)], f, pl.ds(3 + step * 4, 4), pl.ds(8, 64))
            return carry

        lax.fori_loop(0, 8, inner, 0)

    def build(q, carry):
        for rp in range(2):
            for v in range(4):
                both = [act[f, 2 * q + rp, pl.ds(5 + v, 40, stride=2), :].astype(BF16) for f in range(2)]
                planes[rp, v, q, pl.ds(0, 40), :] = jnp.concatenate(both, -1)
        if own:
            for rp in range(2):
                for v in range(2):
                    both = [raw[f, 2 * q + rp, pl.ds(6 + v, 40, stride=2), :].astype(BF16) for f in range(2)]
                    raw_planes[rp, v, q, pl.ds(0, 40), :] = jnp.concatenate(both, -1)
        return carry

    lax.fori_loop(0, 19, build, 0)
    fetch.wait()
    group = 6
    size = group * PITCH
    for base in range(0, 18, group):
        parts = []
        for u in range(4):
            for v in range(4):
                parts.append(planes[u % 2, v, pl.ds(base + u // 2, group)].reshape(size, 256))
        total = dot(jnp.concatenate(parts, -1), weight[...].reshape(4096, 256))
        if own:
            parts, folds = [], []
            for r in range(2):
                for c in range(2):
                    parts.append(raw_planes[(r + 1) % 2, c, pl.ds(base + (r + 1) // 2, group)].reshape(size, 256))
                    for f in range(2):
                        at = (f * 4 + r * 2 + c) * 128
                        folds.append(down_ref[at : at + 128, :])
            total = total + dot(jnp.concatenate(parts, -1), jnp.concatenate(folds, 0))
            out_ref[base : base + group] = total.reshape(group, PITCH, 256)
        else:
            total = total.reshape(group, PITCH, 256)
            for k in range(group):
                flat[pl.ds((base + k) * 34, 34), :] = total[k, :34]
    if not own:
        flat[pl.ds(612, 12), :] = jnp.zeros((12, 256), F32)
        out_ref[...] = flat[...].astype(BF16)


def fine(own, pieces, gain, weight, down=None):
    scratch = [
        pltpu.VMEM((2, 38, COLS, 128), F32),
        pltpu.VMEM((2, 4, 19, PITCH, 256), BF16),
        pltpu.VMEM((16, 256, 256), BF16),
        pltpu.SemaphoreType.DMA(()),
    ]
    if own:
        scratch += [pltpu.VMEM((2, 38, COLS, 128), F32), pltpu.VMEM((2, 2, 19, PITCH, 256), BF16)]
        out = shape((18, PITCH, 256), F32)
    else:
        scratch += [pltpu.VMEM((FLAT, 256), F32)]
        out = shape((FLAT, 256), BF16)
    return call(
        functools.partial(fine_kernel, own),
        out,
        [VM] * 6 + [HB] + ([VM] if own else []),
        scratch,
        flops=2_000_000_000,
        name="fine_own" if own else "fine_next",
    )(*pieces, gain.reshape(1, 128), weight, *([down] if own else []))


def coarse_kernel(
    flag_ref, own_ref, got_ref, gain_ref, conv_hbm, down_hbm,
    near_ref, far_ref, latent_ref,
    got, reduced, act, shifted, conv, down, sems,
):
    fetch_conv = pltpu.make_async_copy(conv_hbm, conv, sems.at[0])
    fetch_down = pltpu.make_async_copy(down_hbm, down, sems.at[1])
    fetch_conv.start()
    fetch_down.start()
    gain = gain_ref[...]
    got[...] = got_ref[...].astype(F32)

    for row in range(18):
        value = own_ref[row, pl.ds(0, 40), :] + got[pl.ds(row * 34, 40), :]
        value = value.astype(BF16).astype(F32)
        active = silu(scaled(value, gain))
        for half in range(2):
            reduced[half, row, pl.ds(0, 40), :] = value[:, half * 128 : half * 128 + 128]
            act[half, row, pl.ds(0, 40), :] = active[:, half * 128 : half * 128 + 128]

    @pl.when(flag_ref[1] == 0)
    def _():
        act[:, 0] = jnp.zeros((2, PITCH, 128), F32)

    @pl.when(flag_ref[1] == 3)
    def _():
        act[:, 17] = jnp.zeros((2, PITCH, 128), F32)

    @pl.when(flag_ref[2] == 0)
    def _():
        act[:, :, pl.ds(0, 1), :] = jnp.zeros((2, 18, 1, 128), F32)

    @pl.when(flag_ref[2] == 7)
    def _():
        act[:, :, pl.ds(33, 1), :] = jnp.zeros((2, 18, 1, 128), F32)

    def build(row, carry):
        for v in range(4):
            halves = [act[half, row, pl.ds(v, 16, stride=2), :] for half in range(2)]
            shifted[v, row] = jnp.concatenate(halves, -1).astype(BF16)
        return carry

    lax.fori_loop(0, 18, build, 0)
    sides = []
    for p in range(2):
        parts = [shifted[p + j, i : i + 16].reshape(256, 256) for i in range(3) for j in range(3)]
        sides.append(jnp.concatenate(parts, -1))
    lhs = jnp.concatenate(sides, 0)
    fetch_conv.wait()
    start = (flag_ref[0] == 0).astype(F32)
    c0 = dot(lhs, conv[0].reshape(2304, 256))
    c1 = dot(lhs, conv[1].reshape(2304, 256)) + c0 * start
    c2 = dot(lhs, conv[2].reshape(2304, 256)) + c1 * start
    plain = []
    for p in range(2):
        for row in range(16):
            halves = [reduced[half, row + 1, pl.ds(1 + p, 16, stride=2), :] for half in range(2)]
            plain.append(jnp.concatenate(halves, -1))
    c2 = c2 + jnp.concatenate(plain, 0)
    fetch_down.wait()

    def folded(field):
        field = field.astype(BF16).reshape(2, 8, 2, 16, 256)
        parts = [field[p, :, r].reshape(128, 256) for r in range(2) for p in range(2)]
        return jnp.concatenate(parts, -1)

    far_ref[...] = dot(folded(c0), down[...]).astype(BF16)
    near_ref[...] = dot(folded(c1), down[...]).astype(BF16)
    latent_ref[...] = dot(folded(c2), down[...])


def coarse(flags, own, got, gain, conv, down):
    return call(
        coarse_kernel,
        (shape((128, 512), BF16), shape((128, 512), BF16), shape((128, 512), F32)),
        [SM, VM, VM, VM, HB, HB],
        [
            pltpu.VMEM((FLAT, 256), F32),
            pltpu.VMEM((2, 18, PITCH, 128), F32),
            pltpu.VMEM((2, 18, PITCH, 128), F32),
            pltpu.VMEM((4, 18, 16, 256), BF16),
            pltpu.VMEM((3, 9, 256, 256), BF16),
            pltpu.VMEM((1024, 512), BF16),
            pltpu.SemaphoreType.DMA((2,)),
        ],
        flops=2_200_000_000,
        name="coarse",
    )(flags, own, got, gain.reshape(1, 256), conv.reshape(3, 9, 256, 256), down)


def latent_kernel(own_ref, near_ref, far_ref, gain_ref, latent_ref, copies_ref):
    latent = (own_ref[...] + near_ref[...].astype(F32) + far_ref[...].astype(F32)).astype(BF16)
    latent_ref[...] = latent
    normed = scaled(latent.astype(F32), gain_ref[...]).astype(BF16)
    for k in range(copies_ref.shape[0]):
        copies_ref[k] = normed


def attend_kernel(mine_ref, other_ref, keys_ref, score_ref, mixed_ref, level_ref, sent_ref, sent_level_ref):
    tokens = jnp.concatenate([mine_ref[...], other_ref[...]], 0)
    queries = dot(tokens, score_ref[...]).astype(BF16)
    keys = keys_ref[...]
    scores = lax.dot_general(queries, keys, (((1,), (1,)), ((), ())), preferred_element_type=F32)
    top = jnp.max(scores, -1, keepdims=True)
    expo = jnp.exp(scores - top)
    total = jnp.sum(expo, -1, keepdims=True)
    mixed = dot(expo.astype(BF16), keys) / total
    level = top + jnp.log(total)
    mixed_ref[...] = mixed[:128]
    sent_ref[...] = mixed[128:].astype(BF16)
    level = jnp.broadcast_to(level, (256, 128))
    level_ref[...] = level[:128]
    sent_level_ref[...] = level[128:]


def merge_kernel(mixed_ref, level_ref, theirs_ref, their_level_ref, latent_ref, mix_ref, out_ref):
    share = jax.nn.sigmoid(level_ref[...] - their_level_ref[...])[:, :1]
    attended = mixed_ref[...] * share + theirs_ref[...].astype(F32) * (1.0 - share)
    out_ref[...] = (latent_ref[...].astype(F32) + dot(attended.astype(BF16), mix_ref[...])).astype(BF16)


def swapped(value, axis, count, first):
    pairs = []
    for low in range(first, count - 1, 2):
        pairs += [(low, low + 1), (low + 1, low)]
    return lax.ppermute(value, axis, pairs)


def sides(block, axis, dim, width, count):
    odd = lax.axis_index(axis) % 2
    last = block.shape[dim] - width
    inner = lax.dynamic_slice_in_dim(block, (1 - odd) * last, width, axis=dim)
    outer = lax.dynamic_slice_in_dim(block, odd * last, width, axis=dim)
    got_inner = swapped(inner, axis, count, 0)
    got_outer = swapped(outer, axis, count, 1)
    even = odd == 0
    return jnp.where(even, got_outer, got_inner), jnp.where(even, got_inner, got_outer)


def per_device(
    features, gain_fine, conv_fine, down_fine, gain_coarse, conv_coarse, down_coarse,
    gain_latent, w_query, w_key, w_value, w_out,
):
    tm = lax.axis_index("tm").astype(jnp.int32)
    flags = jnp.stack([tm, lax.axis_index(HEIGHT).astype(jnp.int32), lax.axis_index("width").astype(jnp.int32)])
    above, below = sides(features, HEIGHT, 1, 3, 4)
    edge = [lax.slice_in_dim(part, 0, 4, axis=2) for part in (above, features, below)]
    far_edge = [lax.slice_in_dim(part, 60, 64, axis=2) for part in (above, features, below)]
    odd = lax.axis_index("width") % 2 == 1
    first, last = jnp.concatenate(edge, 1), jnp.concatenate(far_edge, 1)
    got_inner = swapped(jnp.where(odd, first, last), "width", 8, 0)
    got_outer = swapped(jnp.where(odd, last, first), "width", 8, 1)
    left, right = jnp.where(odd, got_inner, got_outer), jnp.where(odd, got_outer, got_inner)
    pieces = (features, above, below, left, right)
    weight_next = compose(False, flags, conv_fine, down_fine)
    weight_own = compose(True, flags, conv_fine, down_fine)
    scale = 1.0 / math.sqrt(512)
    w_score = (jnp.einsum("ab,cb->ac", w_query, w_key, preferred_element_type=F32) * scale).astype(BF16)
    w_mix = dot(w_value, w_out).astype(BF16)
    sent = fine(False, pieces, gain_fine, weight_next)
    got = lax.ppermute(sent, "tm", [(i, i + 1) for i in range(7)])
    own = fine(True, pieces, gain_fine, weight_own, down_fine)
    near, far, latent_own = coarse(flags, own, got, gain_coarse, conv_coarse, down_coarse)
    near = lax.ppermute(near, "tm", [(i, i + 1) for i in range(7)])
    far = lax.ppermute(far, "tm", [(i, i + 2) for i in range(6)])
    latent_in, copies = call(
        latent_kernel,
        (shape((128, 512), BF16), shape((16, 128, 512), BF16)),
        [VM] * 4,
        flops=10_000_000,
        name="latent",
    )(latent_own, near, far, gain_latent.reshape(1, 512))
    other = swapped(copies[0], "core", 2, 0)
    keys = lax.all_to_all(copies, GATHER, 0, 0, tiled=True).reshape(2048, 512)
    wide = shape((128, 128), F32)
    mixed, level, theirs, their_level = call(
        attend_kernel,
        (shape((128, 512), F32), wide, shape((128, 512), BF16), wide),
        [VM] * 4,
        flops=1_200_000_000,
        name="attend",
    )(copies[0], other, keys, w_score)
    theirs = swapped(theirs, "core", 2, 0)
    their_level = swapped(their_level, "core", 2, 0)
    out = call(merge_kernel, shape((128, 512), BF16), [VM] * 6, flops=70_000_000, name="merge")(
        mixed, level, theirs, their_level, latent_in, w_mix
    )
    return out.reshape(1, 8, 16, 512)


def solution(mesh):
    split = Mesh(mesh.devices.reshape(8, 2, 2, 8), ("tm", "hx", "core", "width"))
    placed = (P("tm", HEIGHT, "width", None),) + (P(),) * 11
    return jax.shard_map(
        per_device, mesh=split, in_specs=placed,
        out_specs=P("tm", HEIGHT, "width", None), check_vma=False,
    )
```

time: 127 us -> 96.5 us (0.76)
  Pallas kernels: 0 us -> 25 us
  local copies, waits for them, and re-layouts: 29.7 us -> 5.23 us
  matrix products: 22.6 us -> 1.94 us
  other arithmetic: 9.22 us -> 0.24 us
    pallas_call x0 -> x8, Pallas kernels: none -> 25 us  [the longest x2 10.9 us: fine(): call(functools.partial(fine_kernel, own), out, [VM] * 6 + [HB] + ([VM] if...]
    conv_general_dilated x3 -> x0, matrix products: 11.6 us -> none  [the longest x1 5.85 us: composed_fine(): lax.conv_general_dilated(lhs, down, (1, 1), ((1, 1), (1, 1)), dimension_n...]
    unnamed x39 -> x24, local copies, waits for them, and re-layouts: 12.8 us -> 2.26 us
    dot_general x7 -> x1, matrix products: 9.31 us -> 0.43 us  [dot(): return jnp.dot(a, b, preferred_element_type=F32)]
    reshape x12 -> x0, local copies, waits for them, and re-layouts: 7.66 us -> none  [the longest x8 4.82 us: fold(): field.reshape(rows // 2, 2, cols // 2, 2, channels).transpose(0, 2, 1, 3, 4)]
    ppermute x7, starting transfers between devices: 7.66 us -> 11 us  [swapped(): return lax.ppermute(value, axis, pairs)]
    ppermute x1, waiting for transfers between devices: 1.09 us -> 4.12 us  [per_device(): near = lax.ppermute(near, 'tm', [(i, i + 1) for i in range(7)])]
    convert_element_type x4 -> x0, other arithmetic: 2.75 us -> none  [the longest x1 1.43 us: composed_fine(): taps = conv_fine.astype(F32)]
  transfers between devices with their start and end apart: 11 -> 11, of which waited for: 6 -> 5; matrix products, arithmetic and copies ran while one was open for 24% -> 4% of each run, Pallas kernels for 0% -> 10%
where the time goes in v2:
time: 96.5 us; the launch traced here: 95.2 us
  waiting for transfers between devices  33.8 us (35%)
  starting transfers between devices  28.7 us (30%)
  Pallas kernels  25 us (26%)
  local copies, waits for them, and re-layouts  5.23 us (5%)
  matrix products  1.94 us (2%)
    all_to_all x1, waiting for transfers between devices, per_device(): keys = lax.all_to_all(copies, GATHER, 0, 0, tiled=True).reshape(2048, 512)  25.9 us
    ppermute x7, starting transfers between devices, swapped(): return lax.ppermute(value, axis, pairs)  11 us
    pallas_call x2, Pallas kernels, fine(): call(functools.partial(fine_kernel, own), out, [VM] * 6 + [HB] + ([VM] if...  10.9 us
    pallas_call x1, Pallas kernels, coarse(): call(coarse_kernel, (shape((128, 512), BF16), shape((128, 512), BF16), sh...  5.93 us
    all_to_all x1, starting transfers between devices, per_device(): keys = lax.all_to_all(copies, GATHER, 0, 0, tiled=True).reshape(2048, 512)  5.57 us
    ppermute x1, starting transfers between devices, per_device(): got = lax.ppermute(sent, 'tm', [(i, i + 1) for i in range(7)])  5.04 us
    ppermute x1, starting transfers between devices, per_device(): near = lax.ppermute(near, 'tm', [(i, i + 1) for i in range(7)])  4.86 us
    ppermute x1, waiting for transfers between devices, per_device(): near = lax.ppermute(near, 'tm', [(i, i + 1) for i in range(7)])  4.12 us
  transfers between devices with their start and end apart: 11, of which 5 were waited for; matrix products, arithmetic and copies ran while one was open for 4% of the time, Pallas kernels for 10%

profile of v2, /device:TPU:96, one launch (start us, length us, event | category | flops | bytes accessed | tf_op | source)
XLA Modules:
  0.0 95.2 jit_solution(3300608941788983020)
XLA Ops:
  0.0 0.0 copy-start
  0.0 1.0 %constant_dynamic-slice_fusion = (bf16[2,3,64,128]{3,2,1,0:T(8,128)(2,1)S(1)}, bf16[2,3,64,128]{3,2,1,0:T(8,128)(2,1)S(1)}) fusion(bf16[2,32,64,128]{3,2,1,0:T(8,128)(2,1)} %x_ref.3, s32[]{:T(128)S(6)} %select_n.52, s32[]{:T(128)S(6)} %select_n.51), kind=kLoop, calls=%fused_computation.13 | loop fusion | bytes 393224 | tf_op jit(solution)/shard_map/dynamic_slice | solution.py:316
  1.0 0.7 collective-permute-start
  1.7 4.5 %collective-permute-start.1 = (bf16[2,3,64,128]{3,2,1,0:T(8,128)(2,1)S(1)}, bf16[2,3,64,128]{3,2,1,0:T(8,128)(2,1)S(1)}, u32[]{:S(2)}, u32[]{:S(2)}) collective-permute-start(bf16[2,3,64,128]{3,2,1,0:T(8,128)(2,1)S(1)} %get-tuple-element.25), channel_id=1, source_target_pairs={{0,8},{8,0},{16,24},{24,16},{1,9},{9,1},{17,25},{25,17},{2,10},{10... | collective-permute-start | bytes 294920 | tf_op jit(solution)/shard_map/ppermute | solution.py:310
  6.2 1.0 %fusion.1 = (bf16[2,32,4,128]{3,2,1,0:T(4,128)(2,1)S(1)}, bf16[2,32,4,128]{3,2,1,0:T(4,128)(2,1)S(1)}) fusion(bf16[2,32,64,128]{3,2,1,0:T(8,128)(2,1)} %x_ref.3), kind=kLoop, calls=%fused_computation.15 | loop fusion | bytes 262144 | tf_op jit(solution)/shard_map/slice | solution.py:331
  7.2 0.1 pad_add_fusion.flag_ref
  7.3 0.0 collective-permute-done
  7.3 0.0 collective-permute-done.1
  7.3 0.0 copy-start.9
  7.3 0.1 broadcast_select_fusion.4
  7.5 0.7 collective-permute-start.3
  8.2 4.4 %collective-permute-start.2 = (bf16[2,38,4,128]{3,2,1,0:T(4,128)(2,1)S(1)}, bf16[2,38,4,128]{3,2,1,0:T(4,128)(2,1)S(1)}, u32[]{:S(2)}, u32[]{:S(2)}) collective-permute-start(bf16[2,38,4,128]{3,2,1,0:T(4,128)(2,1)S(1)} %get-tuple-element.32), channel_id=1, source_target_pairs={{0,1},{1,0},{2,3},{3,2},{4,5},{5,4},{6,7},{7,6},{8,9},{9,8},{10,11... | collective-permute-start | bytes 233480 | tf_op jit(solution)/shard_map/ppermute | solution.py:310
  12.5 1.2 %copy-done.1 = bf16[3,3,3,128,128]{4,3,2,1,0:T(8,128)(2,1)S(1)} copy-done((bf16[3,3,3,128,128]{4,3,2,1,0:T(8,128)(2,1)S(1)}, bf16[3,3,3,128,128]{4,3,2,1,0:T(8,128)(2,1)}, u32[]{:S(2)}) %copy-start.1) | copy-done | bytes 884760
  13.7 1.0 %copy-done.3 = bf16[1024,256]{1,0:T(8,128)(2,1)S(1)} copy-done((bf16[1024,256]{1,0:T(8,128)(2,1)S(1)}, bf16[1024,256]{1,0:T(8,128)(2,1)}, u32[]{:S(2)}) %copy-start.3) | copy-done | bytes 524312
  14.7 1.9 %compose_next.1.weight_hbm = bf16[16,256,256]{2,1,0:T(8,128)(2,1)S(1)} custom-call(s32[3]{0:T(128)S(1)} %pad_add_fusion.flag_ref, bf16[3,3,3,128,128]{4,3,2,1,0:T(8,128)(2,1)S(1)} %copy-done.1, bf16[1024,256]{1,0:T(8,128)(2,1)S(1)} %copy-done.3), custom_call_target="tpu_custom_call" | custom-call | flops 900000000 | bytes 4194304 | tf_op jit(solution)/shard_map/compose_next/pallas_call | solution.py:79
  16.7 0.0 collective-permute-done.3
  16.7 0.5 collective-permute-done.2
  17.2 0.0 copy-done.9
  17.2 0.0 copy-start.2
  17.2 0.0 copy-start.4
  17.2 5.1 %fine_next.1 = bf16[624,256]{1,0:T(8,128)(2,1)S(1)} custom-call(bf16[2,32,64,128]{3,2,1,0:T(8,128)(2,1)S(1)} %copy-done.5, bf16[2,3,64,128]{3,2,1,0:T(8,128)(2,1)S(1)} %get-tuple-element.28.up_ref, bf16[2,3,64,128]{3,2,1,0:T(8,128)(2,1)S(1)} %get-tuple-element.27.low_ref, bf16[2,38,4,128]{3,2,1,0:T(4,128)(2,1)S(1)} %bitcast.22, ...), custom_call_target="tpu_custom_call" | custom-call | flops 2000000000 | bytes 4194304 | tf_op jit(solution)/shard_map/fine_next/pallas_call | solution.py:175
  22.4 5.0 %collective-permute-start.4 = (bf16[624,256]{1,0:T(8,128)(2,1)S(1)}, bf16[624,256]{1,0:T(8,128)(2,1)S(1)}, u32[]{:S(2)}, u32[]{:S(2)}) collective-permute-start(bf16[624,256]{1,0:T(8,128)(2,1)S(1)} %fine_next.1), channel_id=1, source_target_pairs={{0,32},{32,64},{64,96},{96,128},{128,160},{160,192},{192,224},{1,3... | collective-permute-start | bytes 958472 | tf_op jit(solution)/shard_map/ppermute | solution.py:345
  27.4 1.9 %compose_own.1.weight_hbm = bf16[16,256,256]{2,1,0:T(8,128)(2,1)S(1)} custom-call(s32[3]{0:T(128)S(1)} %pad_add_fusion.flag_ref, bf16[3,3,3,128,128]{4,3,2,1,0:T(8,128)(2,1)S(1)} %copy-done.2, bf16[1024,256]{1,0:T(8,128)(2,1)S(1)} %copy-done.4), custom_call_target="tpu_custom_call" | custom-call | flops 900000000 | bytes 4194304 | tf_op jit(solution)/shard_map/compose_own/pallas_call | solution.py:79
  29.4 0.0 copy-start.7
  29.4 0.0 copy-start.8
  29.4 5.8 %fine_own.1.own_ref = f32[18,48,256]{2,1,0:T(8,128)S(1)} custom-call(bf16[2,32,64,128]{3,2,1,0:T(8,128)(2,1)S(1)} %copy-done.5, bf16[2,3,64,128]{3,2,1,0:T(8,128)(2,1)S(1)} %get-tuple-element.28.up_ref, bf16[2,3,64,128]{3,2,1,0:T(8,128)(2,1)S(1)} %get-tuple-element.27.low_ref, bf16[2,38,4,128]{3,2,1,0:T(4,128)(2,1)S(1)} %bitcast.23, ...), custom_call_target="tpu_custom_call" | custom-call | flops 2000000000 | bytes 4194304 | tf_op jit(solution)/shard_map/fine_own/pallas_call | solution.py:175
  35.2 0.0 collective-permute-done.4.got_ref
  35.2 0.0 copy-start.6
  35.2 5.9 %coarse.1 = (bf16[128,512]{1,0:T(8,128)(2,1)S(1)}, bf16[128,512]{1,0:T(8,128)(2,1)S(1)}, f32[128,512]{1,0:T(8,128)S(1)}) custom-call(s32[3]{0:T(128)S(1)} %pad_add_fusion.flag_ref, f32[18,48,256]{2,1,0:T(8,128)S(1)} %fine_own.1.own_ref, bf16[624,256]{1,0:T(8,128)(2,1)S(1)} %collective-permute-done.4.got_ref, f32[1,256]{1,0:T(1,128)S(1)} %bitcast.25, ...), custom_call_target="tpu_custom_call" | custom-call | flops 2200000000 | bytes 4194304 | tf_op jit(solution)/shard_map/coarse/pallas_call | solution.py:257
  41.1 4.9 %collective-permute-start.5 = (bf16[128,512]{1,0:T(8,128)(2,1)S(1)}, bf16[128,512]{1,0:T(8,128)(2,1)S(1)}, u32[]{:S(2)}, u32[]{:S(2)}) collective-permute-start(bf16[128,512]{1,0:T(8,128)(2,1)S(1)} %get-tuple-element.15), channel_id=1, source_target_pairs={{0,32},{32,64},{64,96},{96,128},{128,160},{160,192},{192,224},{1,3... | collective-permute-start | bytes 393224 | tf_op jit(solution)/shard_map/ppermute | solution.py:348
  46.0 2.2 %collective-permute-start.6 = (bf16[128,512]{1,0:T(8,128)(2,1)S(1)}, bf16[128,512]{1,0:T(8,128)(2,1)S(1)}, u32[]{:S(2)}, u32[]{:S(2)}) collective-permute-start(bf16[128,512]{1,0:T(8,128)(2,1)S(1)} %get-tuple-element.16), channel_id=1, source_target_pairs={{0,64},{32,96},{64,128},{96,160},{128,192},{160,224},{1,65},{33,97... | collective-permute-start | bytes 393224 | tf_op jit(solution)/shard_map/ppermute | solution.py:349
  48.2 4.1 %collective-permute-done.5.near_ref = bf16[128,512]{1,0:T(8,128)(2,1)S(1)} collective-permute-done((bf16[128,512]{1,0:T(8,128)(2,1)S(1)}, bf16[128,512]{1,0:T(8,128)(2,1)S(1)}, u32[]{:S(2)}, u32[]{:S(2)}) %collective-permute-start.5) | collective-permute-done | bytes 131104 | tf_op jit(solution)/shard_map/ppermute | solution.py:348
  52.3 2.8 %collective-permute-done.6.far_ref = bf16[128,512]{1,0:T(8,128)(2,1)S(1)} collective-permute-done((bf16[128,512]{1,0:T(8,128)(2,1)S(1)}, bf16[128,512]{1,0:T(8,128)(2,1)S(1)}, u32[]{:S(2)}, u32[]{:S(2)}) %collective-permute-start.6) | collective-permute-done | bytes 131104 | tf_op jit(solution)/shard_map/ppermute | solution.py:349
  55.1 1.6 %latent.1 = (bf16[128,512]{1,0:T(8,128)(2,1)S(1)}, bf16[16,128,512]{2,1,0:T(8,128)(2,1)}) custom-call(f32[128,512]{1,0:T(8,128)S(1)} %get-tuple-element.14.own_ref, bf16[128,512]{1,0:T(8,128)(2,1)S(1)} %collective-permute-done.5.near_ref, bf16[128,512]{1,0:T(8,128)(2,1)S(1)} %collective-permute-done.6.far_ref, f32[1,512]{1,0:T(1,128)S(1)} %bitcast.24), custom_call_target="tpu_custom_call" | custom-call | flops 10000000 | bytes 4194304 | tf_op jit(solution)/shard_map/latent/pallas_call | solution.py:350
  56.7 5.6 %all-to-all-start = ((bf16[16,128,512]{2,1,0:T(8,128)(2,1)}), bf16[16,128,512]{2,1,0:T(8,128)(2,1)S(1)}, u32[]{:S(2)}, u32[]{:S(2)}) async-start(bf16[16,128,512]{2,1,0:T(8,128)(2,1)} %get-tuple-element.17), calls=%async_computation | async-start | bytes 4194304 | tf_op jit(solution)/shard_map/all_to_all | solution.py:358
  62.3 0.9 slice_bitcast_fusion.mine_ref
  63.2 0.3 collective-permute-start.7
  63.5 0.0 copy-done
  63.5 1.5 %fusion.score_ref = bf16[512,512]{1,0:T(8,128)(2,1)S(1)} fusion(bf16[512,512]{1,0:T(8,128)(2,1)S(1)} %copy-done, bf16[512,512]{1,0:T(8,128)(2,1)} %param.21), kind=kOutput, calls=%fused_computation.2 | convolution fusion | flops 268959744 | bytes 1572864 | tf_op jit(solution)/shard_map/ab,cb->ac/dot_general | solution.py:342
  65.0 0.0 collective-permute-done.7.other_ref
  65.0 25.9 %all-to-all-done = bf16[16,128,512]{2,1,0:T(8,128)(2,1)S(1)} async-done(((bf16[16,128,512]{2,1,0:T(8,128)(2,1)}), bf16[16,128,512]{2,1,0:T(8,128)(2,1)S(1)}, u32[]{:S(2)}, u32[]{:S(2)}) %all-to-all-start) | async-done | bytes 2097184 | tf_op jit(solution)/shard_map/all_to_all | solution.py:358
  90.9 1.8 %attend.1 = (f32[128,512]{1,0:T(8,128)S(1)}, f32[128,128]{1,0:T(8,128)S(1)}, bf16[128,512]{1,0:T(8,128)(2,1)S(1)}, f32[128,128]{1,0:T(8,128)S(1)}) custom-call(bf16[128,512]{1,0:T(8,128)(2,1)S(1)} %slice_bitcast_fusion.mine_ref, bf16[128,512]{1,0:T(8,128)(2,1)S(1)} %collective-permute-done.7.other_ref, bf16[2048,512]{1,0:T(8,128)(2,1)S(1)} %bitcast.19, ...), custom_call_target="tpu_custom_call" | custom-call | flops 1200000000 | bytes 4194304 | tf_op jit(solution)/shard_map/attend/pallas_call | solution.py:360
  92.7 0.1 collective-permute-start.8
  92.8 0.5 collective-permute-start.9
  93.3 0.4 convolution_convert_fusion.mix_ref
  93.8 0.5 collective-permute-done.9.their_level_ref
  94.3 0.0 collective-permute-done.8.theirs_ref
  94.3 0.9 merge.1
  (16 shorter events, 0.1 us)
Async XLA Ops:
  0.0 63.5 %copy-start = (bf16[512,512]{1,0:T(8,128)(2,1)S(1)}, bf16[512,512]{1,0:T(8,128)(2,1)}, u32[]{:S(2)}) copy-start(bf16[512,512]{1,0:T(8,128)(2,1)} %param.20) | copy-start | bytes 1572868
  1.0 6.3 %collective-permute-start = (bf16[2,3,64,128]{3,2,1,0:T(8,128)(2,1)S(1)}, bf16[2,3,64,128]{3,2,1,0:T(8,128)(2,1)S(1)}, u32[]{:S(2)}, u32[]{:S(2)}) collective-permute-start(bf16[2,3,64,128]{3,2,1,0:T(8,128)(2,1)S(1)} %get-tuple-element.26), channel_id=1, source_target_pairs={{8,16},{16,8},{9,17},{17,9},{10,18},{18,10},{11,19},{19,11},{12,20... | collective-permute-start | bytes 294920 | tf_op jit(solution)/shard_map/ppermute | solution.py:310
  1.7 5.6 %collective-permute-start.1 = (bf16[2,3,64,128]{3,2,1,0:T(8,128)(2,1)S(1)}, bf16[2,3,64,128]{3,2,1,0:T(8,128)(2,1)S(1)}, u32[]{:S(2)}, u32[]{:S(2)}) collective-permute-start(bf16[2,3,64,128]{3,2,1,0:T(8,128)(2,1)S(1)} %get-tuple-element.25), channel_id=1, source_target_pairs={{0,8},{8,0},{16,24},{24,16},{1,9},{9,1},{17,25},{25,17},{2,10},{10... | collective-permute-start | bytes 294920 | tf_op jit(solution)/shard_map/ppermute | solution.py:310
  7.3 9.9 %copy-start.9 = (f32[128]{0:T(128)S(1)}, f32[128]{0:T(128)}, u32[]{:S(2)}) copy-start(f32[128]{0:T(128)} %param.13) | copy-start | bytes 1540
  7.5 9.2 %collective-permute-start.3 = (bf16[2,38,4,128]{3,2,1,0:T(4,128)(2,1)S(1)}, bf16[2,38,4,128]{3,2,1,0:T(4,128)(2,1)S(1)}, u32[]{:S(2)}, u32[]{:S(2)}) collective-permute-start(bf16[2,38,4,128]{3,2,1,0:T(4,128)(2,1)S(1)} %get-tuple-element.31), channel_id=1, source_target_pairs={{1,2},{2,1},{3,4},{4,3},{5,6},{6,5},{9,10},{10,9},{11,12},{12,11},... | collective-permute-start | bytes 233480 | tf_op jit(solution)/shard_map/ppermute | solution.py:310
  8.2 9.0 %collective-permute-start.2 = (bf16[2,38,4,128]{3,2,1,0:T(4,128)(2,1)S(1)}, bf16[2,38,4,128]{3,2,1,0:T(4,128)(2,1)S(1)}, u32[]{:S(2)}, u32[]{:S(2)}) collective-permute-start(bf16[2,38,4,128]{3,2,1,0:T(4,128)(2,1)S(1)} %get-tuple-element.32), channel_id=1, source_target_pairs={{0,1},{1,0},{2,3},{3,2},{4,5},{5,4},{6,7},{7,6},{8,9},{9,8},{10,11... | collective-permute-start | bytes 233480 | tf_op jit(solution)/shard_map/ppermute | solution.py:310
  12.5 1.2 %copy-start.1 = (bf16[3,3,3,128,128]{4,3,2,1,0:T(8,128)(2,1)S(1)}, bf16[3,3,3,128,128]{4,3,2,1,0:T(8,128)(2,1)}, u32[]{:S(2)}) copy-start(bf16[3,3,3,128,128]{4,3,2,1,0:T(8,128)(2,1)} %conv_ref.3) | copy-start | bytes 2654212
  13.7 1.0 %copy-start.3 = (bf16[1024,256]{1,0:T(8,128)(2,1)S(1)}, bf16[1024,256]{1,0:T(8,128)(2,1)}, u32[]{:S(2)}) copy-start(bf16[1024,256]{1,0:T(8,128)(2,1)} %down_ref.3) | copy-start | bytes 1572868
  14.7 2.5 %copy-start.5 = (bf16[2,32,64,128]{3,2,1,0:T(8,128)(2,1)S(1)}, bf16[2,32,64,128]{3,2,1,0:T(8,128)(2,1)}, u32[]{:S(2)}) copy-start(bf16[2,32,64,128]{3,2,1,0:T(8,128)(2,1)} %x_ref.3) | copy-start | bytes 3145732
  17.2 10.2 %copy-start.2 = (bf16[3,3,3,128,128]{4,3,2,1,0:T(8,128)(2,1)S(1)}, bf16[3,3,3,128,128]{4,3,2,1,0:T(8,128)(2,1)}, u32[]{:S(2)}) copy-start(bf16[3,3,3,128,128]{4,3,2,1,0:T(8,128)(2,1)} %conv_ref.3) | copy-start | bytes 2654212
  17.2 10.2 %copy-start.4 = (bf16[1024,256]{1,0:T(8,128)(2,1)S(1)}, bf16[1024,256]{1,0:T(8,128)(2,1)}, u32[]{:S(2)}) copy-start(bf16[1024,256]{1,0:T(8,128)(2,1)} %down_ref.3) | copy-start | bytes 1572868
  22.4 12.8 %collective-permute-start.4 = (bf16[624,256]{1,0:T(8,128)(2,1)S(1)}, bf16[624,256]{1,0:T(8,128)(2,1)S(1)}, u32[]{:S(2)}, u32[]{:S(2)}) collective-permute-start(bf16[624,256]{1,0:T(8,128)(2,1)S(1)} %fine_next.1), channel_id=1, source_target_pairs={{0,32},{32,64},{64,96},{96,128},{128,160},{160,192},{192,224},{1,3... | collective-permute-start | bytes 958472 | tf_op jit(solution)/shard_map/ppermute | solution.py:345
  29.4 5.8 %copy-start.7 = (bf16[1024,512]{1,0:T(8,128)(2,1)S(1)}, bf16[1024,512]{1,0:T(8,128)(2,1)}, u32[]{:S(2)}) copy-start(bf16[1024,512]{1,0:T(8,128)(2,1)} %down_hbm.1) | copy-start | bytes 3145732
  29.4 5.8 %copy-start.8 = (f32[256]{0:T(256)S(1)}, f32[256]{0:T(256)}, u32[]{:S(2)}) copy-start(f32[256]{0:T(256)} %param.16) | copy-start | bytes 3076
  35.2 19.9 %copy-start.6 = (f32[512]{0:T(512)S(1)}, f32[512]{0:T(512)}, u32[]{:S(2)}) copy-start(f32[512]{0:T(512)} %param.19) | copy-start | bytes 6148
  41.1 11.2 %collective-permute-start.5 = (bf16[128,512]{1,0:T(8,128)(2,1)S(1)}, bf16[128,512]{1,0:T(8,128)(2,1)S(1)}, u32[]{:S(2)}, u32[]{:S(2)}) collective-permute-start(bf16[128,512]{1,0:T(8,128)(2,1)S(1)} %get-tuple-element.15), channel_id=1, source_target_pairs={{0,32},{32,64},{64,96},{96,128},{128,160},{160,192},{192,224},{1,3... | collective-permute-start | bytes 393224 | tf_op jit(solution)/shard_map/ppermute | solution.py:348
  46.0 9.1 %collective-permute-start.6 = (bf16[128,512]{1,0:T(8,128)(2,1)S(1)}, bf16[128,512]{1,0:T(8,128)(2,1)S(1)}, u32[]{:S(2)}, u32[]{:S(2)}) collective-permute-start(bf16[128,512]{1,0:T(8,128)(2,1)S(1)} %get-tuple-element.16), channel_id=1, source_target_pairs={{0,64},{32,96},{64,128},{96,160},{128,192},{160,224},{1,65},{33,97... | collective-permute-start | bytes 393224 | tf_op jit(solution)/shard_map/ppermute | solution.py:349
  56.7 34.2 %all-to-all-start = ((bf16[16,128,512]{2,1,0:T(8,128)(2,1)}), bf16[16,128,512]{2,1,0:T(8,128)(2,1)S(1)}, u32[]{:S(2)}, u32[]{:S(2)}) async-start(bf16[16,128,512]{2,1,0:T(8,128)(2,1)} %get-tuple-element.17), calls=%async_computation | async-start | bytes 4194304 | tf_op jit(solution)/shard_map/all_to_all | solution.py:358
  63.2 1.8 %collective-permute-start.7 = (bf16[128,512]{1,0:T(8,128)(2,1)S(1)}, bf16[128,512]{1,0:T(8,128)(2,1)S(1)}, u32[]{:S(2)}, u32[]{:S(2)}) collective-permute-start(bf16[128,512]{1,0:T(8,128)(2,1)S(1)} %slice_bitcast_fusion.mine_ref), channel_id=1, source_target_pairs={{0,8},{8,0},{1,9},{9,1},{2,10},{10,2},{3,11},{11,3},{4,12},{12,4},... | collective-permute-start | bytes 393224 | tf_op jit(solution)/shard_map/ppermute | solution.py:310
  90.9 2.4 %copy-start.10 = (bf16[512,512]{1,0:T(8,128)(2,1)S(1)}, bf16[512,512]{1,0:T(8,128)(2,1)}, u32[]{:S(2)}) copy-start(bf16[512,512]{1,0:T(8,128)(2,1)} %param.22) | copy-start | bytes 1572868
  90.9 2.4 %copy-start.11 = (bf16[512,512]{1,0:T(8,128)(2,1)S(1)}, bf16[512,512]{1,0:T(8,128)(2,1)}, u32[]{:S(2)}) copy-start(bf16[512,512]{1,0:T(8,128)(2,1)} %param.23) | copy-start | bytes 1572868
  92.7 1.5 %collective-permute-start.8 = (bf16[128,512]{1,0:T(8,128)(2,1)S(1)}, bf16[128,512]{1,0:T(8,128)(2,1)S(1)}, u32[]{:S(2)}, u32[]{:S(2)}) collective-permute-start(bf16[128,512]{1,0:T(8,128)(2,1)S(1)} %get-tuple-element.20), channel_id=1, source_target_pairs={{0,8},{8,0},{1,9},{9,1},{2,10},{10,2},{3,11},{11,3},{4,12},{12,4},... | collective-permute-start | bytes 393224 | tf_op jit(solution)/shard_map/ppermute | solution.py:310
  92.8 1.4 %collective-permute-start.9 = (f32[128,128]{1,0:T(8,128)S(1)}, f32[128,128]{1,0:T(8,128)S(1)}, u32[]{:S(2)}, u32[]{:S(2)}) collective-permute-start(f32[128,128]{1,0:T(8,128)S(1)} %get-tuple-element.21), channel_id=1, source_target_pairs={{0,8},{8,0},{1,9},{9,1},{2,10},{10,2},{3,11},{11,3},{4,12},{12,4},... | collective-permute-start | bytes 196616 | tf_op jit(solution)/shard_map/ppermute | solution.py:310

commit v3 on v2

--- a/solution.py
+++ b/solution.py
@@ -12,8 +12,8 @@
 BF16 = jnp.bfloat16
 F32 = jnp.float32
 HEIGHT = ("hx", "core")
-GATHER = ("hx", "width")
-VMEM_LIMIT = 48 * 1024 * 1024
+GATHER = "width"
+VMEM_LIMIT = 36 * 1024 * 1024
 VM = pl.BlockSpec(memory_space=pltpu.VMEM)
 HB = pl.BlockSpec(memory_space=pl.ANY)
 SM = pl.BlockSpec(memory_space=pltpu.SMEM)
@@ -183,14 +183,10 @@
 
 
 def coarse_kernel(
-    flag_ref, own_ref, got_ref, gain_ref, conv_hbm, down_hbm,
+    flag_ref, own_ref, got_ref, gain_ref, conv, down,
     near_ref, far_ref, latent_ref,
-    got, reduced, act, shifted, conv, down, sems,
+    got, reduced, act, shifted,
 ):
-    fetch_conv = pltpu.make_async_copy(conv_hbm, conv, sems.at[0])
-    fetch_down = pltpu.make_async_copy(down_hbm, down, sems.at[1])
-    fetch_conv.start()
-    fetch_down.start()
     gain = gain_ref[...]
     got[...] = got_ref[...].astype(F32)
 
@@ -230,7 +226,6 @@
         parts = [shifted[p + j, i : i + 16].reshape(256, 256) for i in range(3) for j in range(3)]
         sides.append(jnp.concatenate(parts, -1))
     lhs = jnp.concatenate(sides, 0)
-    fetch_conv.wait()
     start = (flag_ref[0] == 0).astype(F32)
     c0 = dot(lhs, conv[0].reshape(2304, 256))
     c1 = dot(lhs, conv[1].reshape(2304, 256)) + c0 * start
@@ -241,7 +236,6 @@
             halves = [reduced[half, row + 1, pl.ds(1 + p, 16, stride=2), :] for half in range(2)]
             plain.append(jnp.concatenate(halves, -1))
     c2 = c2 + jnp.concatenate(plain, 0)
-    fetch_down.wait()
 
     def folded(field):
         field = field.astype(BF16).reshape(2, 8, 2, 16, 256)
@@ -257,32 +251,61 @@
     return call(
         coarse_kernel,
         (shape((128, 512), BF16), shape((128, 512), BF16), shape((128, 512), F32)),
-        [SM, VM, VM, VM, HB, HB],
+        [SM] + [VM] * 5,
         [
             pltpu.VMEM((FLAT, 256), F32),
             pltpu.VMEM((2, 18, PITCH, 128), F32),
             pltpu.VMEM((2, 18, PITCH, 128), F32),
             pltpu.VMEM((4, 18, 16, 256), BF16),
-            pltpu.VMEM((3, 9, 256, 256), BF16),
-            pltpu.VMEM((1024, 512), BF16),
-            pltpu.SemaphoreType.DMA((2,)),
         ],
         flops=2_200_000_000,
         name="coarse",
     )(flags, own, got, gain.reshape(1, 256), conv.reshape(3, 9, 256, 256), down)
 
 
-def latent_kernel(own_ref, near_ref, far_ref, gain_ref, latent_ref, copies_ref):
+def mix_kernel(query_ref, key_ref, value_ref, out_ref, score_ref, mix_ref):
+    scores = lax.dot_general(query_ref[...], key_ref[...], (((1,), (1,)), ((), ())), preferred_element_type=F32)
+    score_ref[...] = (scores * (1.0 / math.sqrt(512))).astype(BF16)
+    mix_ref[...] = dot(value_ref[...], out_ref[...]).astype(BF16)
+
+
+def latent_kernel(own_ref, near_ref, far_ref, gain_ref, score_ref, latent_ref, query_ref, copies_ref):
     latent = (own_ref[...] + near_ref[...].astype(F32) + far_ref[...].astype(F32)).astype(BF16)
     latent_ref[...] = latent
     normed = scaled(latent.astype(F32), gain_ref[...]).astype(BF16)
     for k in range(copies_ref.shape[0]):
         copies_ref[k] = normed
-
-
-def attend_kernel(mine_ref, other_ref, keys_ref, score_ref, mixed_ref, level_ref, sent_ref, sent_level_ref):
-    tokens = jnp.concatenate([mine_ref[...], other_ref[...]], 0)
-    queries = dot(tokens, score_ref[...]).astype(BF16)
+    query_ref[...] = dot(normed, score_ref[...]).astype(BF16)
+
+
+def packed(values, level):
+    level = jnp.broadcast_to(level, (level.shape[0], 128))
+    high = level.astype(BF16)
+    rest = level - high.astype(F32)
+    middle = rest.astype(BF16)
+    low = (rest - middle.astype(F32)).astype(BF16)
+    lane = lax.broadcasted_iota(jnp.int32, level.shape, 1)
+    parts = jnp.where(lane == 0, high.astype(F32), jnp.where(lane == 1, middle.astype(F32), low.astype(F32)))
+    return jnp.concatenate([values.astype(BF16), parts.astype(BF16)], -1)
+
+
+def level_of(block):
+    parts = block[:, 512:].astype(F32)
+    lane = lax.broadcasted_iota(jnp.int32, parts.shape, 1)
+    return jnp.sum(jnp.where(lane < 3, parts, 0.0), -1, keepdims=True)
+
+
+def joined(values, level, block):
+    other = level_of(block)
+    top = jnp.maximum(level, other)
+    low = jnp.minimum(level, other)
+    share = jax.nn.sigmoid(level - other)
+    merged = values * share + block[:, :512].astype(F32) * (1.0 - share)
+    return merged, top + jnp.log(1.0 + jnp.exp(low - top))
+
+
+def attend_kernel(mine_ref, theirs_ref, keys_ref, mixed_ref, level_ref, sent_ref):
+    queries = jnp.concatenate([mine_ref[...], theirs_ref[...]], 0)
     keys = keys_ref[...]
     scores = lax.dot_general(queries, keys, (((1,), (1,)), ((), ())), preferred_element_type=F32)
     top = jnp.max(scores, -1, keepdims=True)
@@ -290,16 +313,20 @@
     total = jnp.sum(expo, -1, keepdims=True)
     mixed = dot(expo.astype(BF16), keys) / total
     level = top + jnp.log(total)
-    mixed_ref[...] = mixed[:128]
-    sent_ref[...] = mixed[128:].astype(BF16)
-    level = jnp.broadcast_to(level, (256, 128))
-    level_ref[...] = level[:128]
-    sent_level_ref[...] = level[128:]
-
-
-def merge_kernel(mixed_ref, level_ref, theirs_ref, their_level_ref, latent_ref, mix_ref, out_ref):
-    share = jax.nn.sigmoid(level_ref[...] - their_level_ref[...])[:, :1]
-    attended = mixed_ref[...] * share + theirs_ref[...].astype(F32) * (1.0 - share)
+    mixed_ref[...] = mixed[:256]
+    level_ref[...] = jnp.broadcast_to(level[:256], (256, 128))
+    sent_ref[...] = packed(mixed[256:], level[256:])
+
+
+def merge_kernel(mixed_ref, level_ref, got_ref, kept_ref, kept_level_ref, sent_ref):
+    merged, level = joined(mixed_ref[...], level_ref[:, :1], got_ref[...])
+    kept_ref[...] = merged[:128]
+    kept_level_ref[...] = jnp.broadcast_to(level[:128], (128, 128))
+    sent_ref[...] = packed(merged[128:], level[128:])
+
+
+def finish_kernel(mixed_ref, level_ref, got_ref, latent_ref, mix_ref, out_ref):
+    attended, _ = joined(mixed_ref[...], level_ref[:, :1], got_ref[...])
     out_ref[...] = (latent_ref[...].astype(F32) + dot(attended.astype(BF16), mix_ref[...])).astype(BF16)
 
 
@@ -328,6 +355,8 @@
     tm = lax.axis_index("tm").astype(jnp.int32)
     flags = jnp.stack([tm, lax.axis_index(HEIGHT).astype(jnp.int32), lax.axis_index("width").astype(jnp.int32)])
     above, below = sides(features, HEIGHT, 1, 3, 4)
+    weight_next = compose(False, flags, conv_fine, down_fine)
+    above, below, weight_next = lax.optimization_barrier((above, below, weight_next))
     edge = [lax.slice_in_dim(part, 0, 4, axis=2) for part in (above, features, below)]
     far_edge = [lax.slice_in_dim(part, 60, 64, axis=2) for part in (above, features, below)]
     odd = lax.axis_index("width") % 2 == 1
@@ -336,39 +365,44 @@
     got_outer = swapped(jnp.where(odd, last, first), "width", 8, 1)
     left, right = jnp.where(odd, got_inner, got_outer), jnp.where(odd, got_outer, got_inner)
     pieces = (features, above, below, left, right)
-    weight_next = compose(False, flags, conv_fine, down_fine)
     weight_own = compose(True, flags, conv_fine, down_fine)
-    scale = 1.0 / math.sqrt(512)
-    w_score = (jnp.einsum("ab,cb->ac", w_query, w_key, preferred_element_type=F32) * scale).astype(BF16)
-    w_mix = dot(w_value, w_out).astype(BF16)
+    left, right, weight_own = lax.optimization_barrier((left, right, weight_own))
+    pieces = (features, above, below, left, right)
     sent = fine(False, pieces, gain_fine, weight_next)
     got = lax.ppermute(sent, "tm", [(i, i + 1) for i in range(7)])
     own = fine(True, pieces, gain_fine, weight_own, down_fine)
     near, far, latent_own = coarse(flags, own, got, gain_coarse, conv_coarse, down_coarse)
     near = lax.ppermute(near, "tm", [(i, i + 1) for i in range(7)])
     far = lax.ppermute(far, "tm", [(i, i + 2) for i in range(6)])
-    latent_in, copies = call(
-        latent_kernel,
-        (shape((128, 512), BF16), shape((16, 128, 512), BF16)),
-        [VM] * 4,
-        flops=10_000_000,
-        name="latent",
-    )(latent_own, near, far, gain_latent.reshape(1, 512))
-    other = swapped(copies[0], "core", 2, 0)
-    keys = lax.all_to_all(copies, GATHER, 0, 0, tiled=True).reshape(2048, 512)
-    wide = shape((128, 128), F32)
-    mixed, level, theirs, their_level = call(
+    square = shape((512, 512), BF16)
+    w_score, w_mix = call(mix_kernel, (square, square), [VM] * 4, flops=540_000_000, name="mix")(
+        w_query, w_key, w_value, w_out
+    )
+    near, far, w_score, w_mix = lax.optimization_barrier((near, far, w_score, w_mix))
+    rows = shape((128, 512), BF16)
+    latent_in, query, copies = call(
+        latent_kernel, (rows, rows, shape((8, 128, 512), BF16)), [VM] * 5, flops=80_000_000, name="latent"
+    )(latent_own, near, far, gain_latent.reshape(1, 512), w_score)
+    queries = jnp.concatenate([query, swapped(query, "hx", 2, 0)], 0)
+    their_queries = swapped(queries, "core", 2, 0)
+    keys = lax.all_to_all(copies, GATHER, 0, 0, tiled=True).reshape(1024, 512)
+    mixed, level, sent = call(
         attend_kernel,
-        (shape((128, 512), F32), wide, shape((128, 512), BF16), wide),
-        [VM] * 4,
-        flops=1_200_000_000,
+        (shape((256, 512), F32), shape((256, 128), F32), shape((256, 640), BF16)),
+        [VM] * 3,
+        flops=1_100_000_000,
         name="attend",
-    )(copies[0], other, keys, w_score)
-    theirs = swapped(theirs, "core", 2, 0)
-    their_level = swapped(their_level, "core", 2, 0)
-    out = call(merge_kernel, shape((128, 512), BF16), [VM] * 6, flops=70_000_000, name="merge")(
-        mixed, level, theirs, their_level, latent_in, w_mix
-    )
+    )(queries, their_queries, keys)
+    got = swapped(sent, "core", 2, 0)
+    mixed, level, sent = call(
+        merge_kernel,
+        (shape((128, 512), F32), shape((128, 128), F32), shape((128, 640), BF16)),
+        [VM] * 3,
+        flops=1_000_000,
+        name="merge",
+    )(mixed, level, got)
+    got = swapped(sent, "hx", 2, 0)
+    out = call(finish_kernel, rows, [VM] * 5, flops=70_000_000, name="finish")(mixed, level, got, latent_in, w_mix)
     return out.reshape(1, 8, 16, 512)
 
 

time: 96.5 us -> 89.9 us (0.932)
  waiting for transfers between devices: 33.8 us -> 29.8 us
  starting transfers between devices: 28.7 us -> 31.2 us
  matrix products: 1.94 us -> 0 us
  Pallas kernels: 25 us -> 23.4 us
    all_to_all x1, waiting for transfers between devices: 25.9 us -> 0.01 us  [per_device(): keys = lax.all_to_all(copies, GATHER, 0, 0, tiled=True).reshape(1024, 512)]
    ppermute x7 -> x8, waiting for transfers between devices: 1.01 us -> 25 us  [swapped(): return lax.ppermute(value, axis, pairs)]
    all_to_all x1, starting transfers between devices: 5.57 us -> 8.42 us  [per_device(): keys = lax.all_to_all(copies, GATHER, 0, 0, tiled=True).reshape(1024, 512)]
    pallas_call x1, Pallas kernels: 5.93 us -> 3.84 us  [coarse(): call(coarse_kernel, (shape((128, 512), BF16), shape((128, 512), BF16), sh...]
    ppermute x1, waiting for transfers between devices: 4.12 us -> 2.07 us  [per_device(): near = lax.ppermute(near, 'tm', [(i, i + 1) for i in range(7)])]
    dot_general x2 -> x0, matrix products: 1.94 us -> none  [the longest x1 1.51 us: per_device(): jnp.einsum('ab,cb->ac', w_query, w_key, preferred_element_type=F32) * scale]
    ppermute x7 -> x8, starting transfers between devices: 11 us -> 9.76 us  [swapped(): return lax.ppermute(value, axis, pairs)]
    pallas_call x3 -> x5, Pallas kernels: 4.39 us -> 4.82 us  [the longest x1 1.52 us: per_device(): call(attend_kernel, (shape((256, 512), F32), shape((256, 128), F32), shap...]
  transfers between devices with their start and end apart: 11 -> 12, of which waited for: 5 -> 7; matrix products, arithmetic and copies ran while one was open for 4% -> 1% of each run, Pallas kernels for 10% -> 12%
where the time goes in v3:
time: 89.9 us; the launch traced here: 89.3 us
  starting transfers between devices  31.2 us (35%)
  waiting for transfers between devices  29.8 us (33%)
  Pallas kernels  23.4 us (26%)
  local copies, waits for them, and re-layouts  4.29 us (5%)
    ppermute x8, waiting for transfers between devices, swapped(): return lax.ppermute(value, axis, pairs)  25 us
    pallas_call x2, Pallas kernels, fine(): call(functools.partial(fine_kernel, own), out, [VM] * 6 + [HB] + ([VM] if...  10.9 us
    ppermute x8, starting transfers between devices, swapped(): return lax.ppermute(value, axis, pairs)  9.76 us
    all_to_all x1, starting transfers between devices, per_device(): keys = lax.all_to_all(copies, GATHER, 0, 0, tiled=True).reshape(1024, 512)  8.42 us
    ppermute x1, starting transfers between devices, per_device(): near = lax.ppermute(near, 'tm', [(i, i + 1) for i in range(7)])  5.6 us
    ppermute x1, starting transfers between devices, per_device(): got = lax.ppermute(sent, 'tm', [(i, i + 1) for i in range(7)])  5.3 us
    pallas_call x1, Pallas kernels, coarse(): call(coarse_kernel, (shape((128, 512), BF16), shape((128, 512), BF16), sh...  3.84 us
    pallas_call x2, Pallas kernels, compose(): call(functools.partial(compose_kernel, own), shape((16, 256, 256), BF16),...  3.83 us
  transfers between devices with their start and end apart: 12, of which 7 were waited for; matrix products, arithmetic and copies ran while one was open for 1% of the time, Pallas kernels for 12%

profile of v3, /device:TPU:96, one launch (start us, length us, event | category | flops | bytes accessed | tf_op | source)
XLA Modules:
  0.0 89.3 jit_solution(16901607978454014461)
XLA Ops:
  0.0 1.0 %constant_dynamic-slice_fusion = (bf16[2,3,64,128]{3,2,1,0:T(8,128)(2,1)S(1)}, bf16[2,3,64,128]{3,2,1,0:T(8,128)(2,1)S(1)}) fusion(bf16[2,32,64,128]{3,2,1,0:T(8,128)(2,1)} %x_ref.3, s32[]{:T(128)S(6)} %select_n.52, s32[]{:T(128)S(6)} %select_n.51), kind=kLoop, calls=%fused_computation.11 | loop fusion | bytes 393224 | tf_op jit(solution)/shard_map/dynamic_slice | solution.py:343
  1.0 0.7 collective-permute-start
  1.6 4.5 %collective-permute-start.1 = (bf16[2,3,64,128]{3,2,1,0:T(8,128)(2,1)S(1)}, bf16[2,3,64,128]{3,2,1,0:T(8,128)(2,1)S(1)}, u32[]{:S(2)}, u32[]{:S(2)}) collective-permute-start(bf16[2,3,64,128]{3,2,1,0:T(8,128)(2,1)S(1)} %get-tuple-element.55), channel_id=1, source_target_pairs={{0,8},{8,0},{16,24},{24,16},{1,9},{9,1},{17,25},{25,17},{2,10},{10... | collective-permute-start | bytes 294920 | tf_op jit(solution)/shard_map/ppermute | solution.py:337
  6.1 1.0 %fusion = (bf16[2,32,4,128]{3,2,1,0:T(4,128)(2,1)S(1)}, bf16[2,32,4,128]{3,2,1,0:T(4,128)(2,1)S(1)}) fusion(bf16[2,32,64,128]{3,2,1,0:T(8,128)(2,1)} %x_ref.3), kind=kLoop, calls=%fused_computation.13 | loop fusion | bytes 262144 | tf_op jit(solution)/shard_map/slice | solution.py:360
  7.1 0.1 pad_add_fusion.flag_ref
  7.2 1.2 %copy-done = bf16[3,3,3,128,128]{4,3,2,1,0:T(8,128)(2,1)S(1)} copy-done((bf16[3,3,3,128,128]{4,3,2,1,0:T(8,128)(2,1)S(1)}, bf16[3,3,3,128,128]{4,3,2,1,0:T(8,128)(2,1)}, u32[]{:S(2)}) %copy-start) | copy-done | bytes 884760
  8.4 1.0 %copy-done.1 = bf16[1024,256]{1,0:T(8,128)(2,1)S(1)} copy-done((bf16[1024,256]{1,0:T(8,128)(2,1)S(1)}, bf16[1024,256]{1,0:T(8,128)(2,1)}, u32[]{:S(2)}) %copy-start.1) | copy-done | bytes 524312
  9.4 1.9 %compose_next.1.weight_hbm = bf16[16,256,256]{2,1,0:T(8,128)(2,1)S(1)} custom-call(s32[3]{0:T(128)S(1)} %pad_add_fusion.flag_ref, bf16[3,3,3,128,128]{4,3,2,1,0:T(8,128)(2,1)S(1)} %copy-done, bf16[1024,256]{1,0:T(8,128)(2,1)S(1)} %copy-done.1), custom_call_target="tpu_custom_call" | custom-call | flops 900000000 | bytes 4194304 | tf_op jit(solution)/shard_map/compose_next/pallas_call | solution.py:79
  11.4 0.0 collective-permute-done.1
  11.4 0.0 copy-start.7
  11.4 0.0 copy-start.12
  11.4 0.1 broadcast_select_fusion.4
  11.6 0.7 collective-permute-start.2
  12.2 0.7 collective-permute-start.3
  12.9 1.9 %compose_own.1.weight_hbm = bf16[16,256,256]{2,1,0:T(8,128)(2,1)S(1)} custom-call(s32[3]{0:T(128)S(1)} %pad_add_fusion.flag_ref, bf16[3,3,3,128,128]{4,3,2,1,0:T(8,128)(2,1)S(1)} %copy-done, bf16[1024,256]{1,0:T(8,128)(2,1)S(1)} %copy-done.1), custom_call_target="tpu_custom_call" | custom-call | flops 900000000 | bytes 4194304 | tf_op jit(solution)/shard_map/compose_own/pallas_call | solution.py:79
  14.8 1.2 %collective-permute-done.2 = bf16[2,38,4,128]{3,2,1,0:T(4,128)(2,1)S(1)} collective-permute-done((bf16[2,38,4,128]{3,2,1,0:T(4,128)(2,1)S(1)}, bf16[2,38,4,128]{3,2,1,0:T(4,128)(2,1)S(1)}, u32[]{:S(2)}, u32[]{:S(2)}) %collective-permute-start.2) | collective-permute-done | bytes 77856 | tf_op jit(solution)/shard_map/ppermute | solution.py:337
  16.1 0.0 copy-start.2
  16.1 5.1 %fine_next.1 = bf16[624,256]{1,0:T(8,128)(2,1)S(1)} custom-call(bf16[2,32,64,128]{3,2,1,0:T(8,128)(2,1)S(1)} %copy-done.7, bf16[2,3,64,128]{3,2,1,0:T(8,128)(2,1)S(1)} %get-tuple-element.29.up_ref, bf16[2,3,64,128]{3,2,1,0:T(8,128)(2,1)S(1)} %get-tuple-element.30.low_ref, bf16[2,38,4,128]{3,2,1,0:T(4,128)(2,1)S(1)} %bitcast.16, ...), custom_call_target="tpu_custom_call" | custom-call | flops 2000000000 | bytes 4194304 | tf_op jit(solution)/shard_map/fine_next/pallas_call | solution.py:175
  21.2 0.0 copy-start.9
  21.2 0.0 copy-start.10
  21.3 0.0 copy-start.11
  21.3 5.3 %collective-permute-start.4 = (bf16[624,256]{1,0:T(8,128)(2,1)S(1)}, bf16[624,256]{1,0:T(8,128)(2,1)S(1)}, u32[]{:S(2)}, u32[]{:S(2)}) collective-permute-start(bf16[624,256]{1,0:T(8,128)(2,1)S(1)} %fine_next.1), channel_id=1, source_target_pairs={{0,32},{32,64},{64,96},{96,128},{128,160},{160,192},{192,224},{1,3... | collective-permute-start | bytes 958472 | tf_op jit(solution)/shard_map/ppermute | solution.py:372
  26.6 5.8 %fine_own.1.own_ref = f32[18,48,256]{2,1,0:T(8,128)S(1)} custom-call(bf16[2,32,64,128]{3,2,1,0:T(8,128)(2,1)S(1)} %copy-done.7, bf16[2,3,64,128]{3,2,1,0:T(8,128)(2,1)S(1)} %get-tuple-element.29.up_ref, bf16[2,3,64,128]{3,2,1,0:T(8,128)(2,1)S(1)} %get-tuple-element.30.low_ref, bf16[2,38,4,128]{3,2,1,0:T(4,128)(2,1)S(1)} %bitcast.17, ...), custom_call_target="tpu_custom_call" | custom-call | flops 2000000000 | bytes 4194304 | tf_op jit(solution)/shard_map/fine_own/pallas_call | solution.py:175
  32.4 0.0 collective-permute-done.4.got_ref
  32.4 0.0 copy-start.3
  32.4 0.0 copy-start.4
  32.4 0.0 copy-start.5
  32.4 0.0 copy-start.6
  32.4 3.8 %coarse.1 = (bf16[128,512]{1,0:T(8,128)(2,1)S(1)}, bf16[128,512]{1,0:T(8,128)(2,1)S(1)}, f32[128,512]{1,0:T(8,128)S(1)}) custom-call(s32[3]{0:T(128)S(1)} %pad_add_fusion.flag_ref, f32[18,48,256]{2,1,0:T(8,128)S(1)} %fine_own.1.own_ref, bf16[624,256]{1,0:T(8,128)(2,1)S(1)} %collective-permute-done.4.got_ref, f32[1,256]{1,0:T(1,128)S(1)} %bitcast.20, ...), custom_call_target="tpu_custom_call" | custom-call | flops 2200000000 | bytes 4194304 | tf_op jit(solution)/shard_map/coarse/pallas_call | solution.py:251
  36.3 0.0 copy-start.8
  36.3 5.6 %collective-permute-start.5 = (bf16[128,512]{1,0:T(8,128)(2,1)S(1)}, bf16[128,512]{1,0:T(8,128)(2,1)S(1)}, u32[]{:S(2)}, u32[]{:S(2)}) collective-permute-start(bf16[128,512]{1,0:T(8,128)(2,1)S(1)} %get-tuple-element.36), channel_id=1, source_target_pairs={{0,32},{32,64},{64,96},{96,128},{128,160},{160,192},{192,224},{1,3... | collective-permute-start | bytes 393224 | tf_op jit(solution)/shard_map/ppermute | solution.py:375
  41.9 2.2 %collective-permute-start.6 = (bf16[128,512]{1,0:T(8,128)(2,1)S(1)}, bf16[128,512]{1,0:T(8,128)(2,1)S(1)}, u32[]{:S(2)}, u32[]{:S(2)}) collective-permute-start(bf16[128,512]{1,0:T(8,128)(2,1)S(1)} %get-tuple-element.37), channel_id=1, source_target_pairs={{0,64},{32,96},{64,128},{96,160},{128,192},{160,224},{1,65},{33,97... | collective-permute-start | bytes 393224 | tf_op jit(solution)/shard_map/ppermute | solution.py:376
  44.1 0.7 mix.1
  44.9 2.1 %collective-permute-done.5.near_ref = bf16[128,512]{1,0:T(8,128)(2,1)S(1)} collective-permute-done((bf16[128,512]{1,0:T(8,128)(2,1)S(1)}, bf16[128,512]{1,0:T(8,128)(2,1)S(1)}, u32[]{:S(2)}, u32[]{:S(2)}) %collective-permute-start.5) | collective-permute-done | bytes 131104 | tf_op jit(solution)/shard_map/ppermute | solution.py:375
  47.0 2.7 %collective-permute-done.6.far_ref = bf16[128,512]{1,0:T(8,128)(2,1)S(1)} collective-permute-done((bf16[128,512]{1,0:T(8,128)(2,1)S(1)}, bf16[128,512]{1,0:T(8,128)(2,1)S(1)}, u32[]{:S(2)}, u32[]{:S(2)}) %collective-permute-start.6) | collective-permute-done | bytes 131104 | tf_op jit(solution)/shard_map/ppermute | solution.py:376
  49.7 1.2 %latent.1 = (bf16[128,512]{1,0:T(8,128)(2,1)S(1)}, bf16[128,512]{1,0:T(8,128)(2,1)S(1)}, bf16[8,128,512]{2,1,0:T(8,128)(2,1)}) custom-call(f32[128,512]{1,0:T(8,128)S(1)} %get-tuple-element.35.own_ref, bf16[128,512]{1,0:T(8,128)(2,1)S(1)} %collective-permute-done.5.near_ref, bf16[128,512]{1,0:T(8,128)(2,1)S(1)} %collective-permute-done.6.far_ref, ...), custom_call_target="tpu_custom_call" | custom-call | flops 80000000 | bytes 4194304 | tf_op jit(solution)/shard_map/latent/pallas_call | solution.py:383
  50.9 8.4 %all-to-all-start = ((bf16[8,128,512]{2,1,0:T(8,128)(2,1)}), bf16[8,128,512]{2,1,0:T(8,128)(2,1)S(1)}, u32[]{:S(2)}, u32[]{:S(2)}) async-start(bf16[8,128,512]{2,1,0:T(8,128)(2,1)} %get-tuple-element.44), calls=%async_computation | async-start | bytes 2097152 | tf_op jit(solution)/shard_map/all_to_all | solution.py:388
  59.3 2.1 %collective-permute-start.7 = (bf16[128,512]{1,0:T(8,128)(2,1)S(1)}, bf16[128,512]{1,0:T(8,128)(2,1)S(1)}, u32[]{:S(2)}, u32[]{:S(2)}) collective-permute-start(bf16[128,512]{1,0:T(8,128)(2,1)S(1)} %get-tuple-element.43), channel_id=1, source_target_pairs={{0,16},{16,0},{1,17},{17,1},{2,18},{18,2},{3,19},{19,3},{4,20},{20... | collective-permute-start | bytes 393224 | tf_op jit(solution)/shard_map/ppermute | solution.py:337
  61.4 13.8 %collective-permute-done.7 = bf16[128,512]{1,0:T(8,128)(2,1)S(1)} collective-permute-done((bf16[128,512]{1,0:T(8,128)(2,1)S(1)}, bf16[128,512]{1,0:T(8,128)(2,1)S(1)}, u32[]{:S(2)}, u32[]{:S(2)}) %collective-permute-start.7) | collective-permute-done | bytes 131104 | tf_op jit(solution)/shard_map/ppermute | solution.py:337
  75.2 0.1 collective-permute-start.8
  75.3 1.5 %collective-permute-done.8.theirs_ref = bf16[256,512]{1,0:T(8,128)(2,1)S(1)} collective-permute-done((bf16[256,512]{1,0:T(8,128)(2,1)S(1)}, bf16[256,512]{1,0:T(8,128)(2,1)S(1)}, u32[]{:S(2)}, u32[]{:S(2)}) %collective-permute-start.8) | collective-permute-done | bytes 262176 | tf_op jit(solution)/shard_map/ppermute | solution.py:337
  76.8 1.5 %attend.1 = (f32[256,512]{1,0:T(8,128)S(1)}, f32[256,128]{1,0:T(8,128)S(1)}, bf16[256,640]{1,0:T(8,128)(2,1)S(1)}) custom-call(bf16[256,512]{1,0:T(8,128)(2,1)S(1)} %constant_dynamic-update-slice_fusion.mine_ref, bf16[256,512]{1,0:T(8,128)(2,1)S(1)} %collective-permute-done.8.theirs_ref, bf16[1024,512]{1,0:T(8,128)(2,1)S(1)} %bitcast.13), custom_call_target="tpu_custom_call" | custom-call | flops 1100000000 | bytes 4194304 | tf_op jit(solution)/shard_map/attend/pallas_call | solution.py:389
  78.4 0.2 collective-permute-start.9
  78.6 1.5 %collective-permute-done.9.got_ref = bf16[256,640]{1,0:T(8,128)(2,1)S(1)} collective-permute-done((bf16[256,640]{1,0:T(8,128)(2,1)S(1)}, bf16[256,640]{1,0:T(8,128)(2,1)S(1)}, u32[]{:S(2)}, u32[]{:S(2)}) %collective-permute-start.9) | collective-permute-done | bytes 327712 | tf_op jit(solution)/shard_map/ppermute | solution.py:337
  80.1 0.3 merge.1
  80.4 0.9 %collective-permute-start.10 = (bf16[128,640]{1,0:T(8,128)(2,1)S(1)}, bf16[128,640]{1,0:T(8,128)(2,1)S(1)}, u32[]{:S(2)}, u32[]{:S(2)}) collective-permute-start(bf16[128,640]{1,0:T(8,128)(2,1)S(1)} %get-tuple-element.50), channel_id=1, source_target_pairs={{0,16},{16,0},{1,17},{17,1},{2,18},{18,2},{3,19},{19,3},{4,20},{20... | collective-permute-start | bytes 491528 | tf_op jit(solution)/shard_map/ppermute | solution.py:337
  81.3 6.9 %collective-permute-done.10.got_ref = bf16[128,640]{1,0:T(8,128)(2,1)S(1)} collective-permute-done((bf16[128,640]{1,0:T(8,128)(2,1)S(1)}, bf16[128,640]{1,0:T(8,128)(2,1)S(1)}, u32[]{:S(2)}, u32[]{:S(2)}) %collective-permute-start.10) | collective-permute-done | bytes 163872 | tf_op jit(solution)/shard_map/ppermute | solution.py:337
  88.2 1.0 %finish.1 = bf16[128,512]{1,0:T(8,128)(2,1)} custom-call(f32[128,512]{1,0:T(8,128)S(1)} %get-tuple-element.48.mixed_ref, f32[128,128]{1,0:T(8,128)S(1)} %get-tuple-element.49.level_ref, bf16[128,640]{1,0:T(8,128)(2,1)S(1)} %collective-permute-done.10.got_ref, bf16[128,512]{1,0:T(8,128)(2,1)S(1)} %get-tuple-element.51.latent_ref, ...), custom_call_target="tpu_custom_call" | custom-call | flops 70000000 | bytes 4194304 | tf_op jit(solution)/shard_map/finish/pallas_call | solution.py:405
  (21 shorter events, 0.1 us)
Async XLA Ops:
  1.0 10.4 %collective-permute-start = (bf16[2,3,64,128]{3,2,1,0:T(8,128)(2,1)S(1)}, bf16[2,3,64,128]{3,2,1,0:T(8,128)(2,1)S(1)}, u32[]{:S(2)}, u32[]{:S(2)}) collective-permute-start(bf16[2,3,64,128]{3,2,1,0:T(8,128)(2,1)S(1)} %get-tuple-element.56), channel_id=1, source_target_pairs={{8,16},{16,8},{9,17},{17,9},{10,18},{18,10},{11,19},{19,11},{12,20... | collective-permute-start | bytes 294920 | tf_op jit(solution)/shard_map/ppermute | solution.py:337
  1.6 9.7 %collective-permute-start.1 = (bf16[2,3,64,128]{3,2,1,0:T(8,128)(2,1)S(1)}, bf16[2,3,64,128]{3,2,1,0:T(8,128)(2,1)S(1)}, u32[]{:S(2)}, u32[]{:S(2)}) collective-permute-start(bf16[2,3,64,128]{3,2,1,0:T(8,128)(2,1)S(1)} %get-tuple-element.55), channel_id=1, source_target_pairs={{0,8},{8,0},{16,24},{24,16},{1,9},{9,1},{17,25},{25,17},{2,10},{10... | collective-permute-start | bytes 294920 | tf_op jit(solution)/shard_map/ppermute | solution.py:337
  7.2 1.2 %copy-start = (bf16[3,3,3,128,128]{4,3,2,1,0:T(8,128)(2,1)S(1)}, bf16[3,3,3,128,128]{4,3,2,1,0:T(8,128)(2,1)}, u32[]{:S(2)}) copy-start(bf16[3,3,3,128,128]{4,3,2,1,0:T(8,128)(2,1)} %conv_ref.3) | copy-start | bytes 2654212
  8.4 1.0 %copy-start.1 = (bf16[1024,256]{1,0:T(8,128)(2,1)S(1)}, bf16[1024,256]{1,0:T(8,128)(2,1)}, u32[]{:S(2)}) copy-start(bf16[1024,256]{1,0:T(8,128)(2,1)} %rest_0_.1) | copy-start | bytes 1572868
  11.4 4.7 %copy-start.7 = (bf16[2,32,64,128]{3,2,1,0:T(8,128)(2,1)S(1)}, bf16[2,32,64,128]{3,2,1,0:T(8,128)(2,1)}, u32[]{:S(2)}) copy-start(bf16[2,32,64,128]{3,2,1,0:T(8,128)(2,1)} %x_ref.3) | copy-start | bytes 3145732
  11.4 4.7 %copy-start.12 = (f32[128]{0:T(128)S(1)}, f32[128]{0:T(128)}, u32[]{:S(2)}) copy-start(f32[128]{0:T(128)} %param.13) | copy-start | bytes 1540
  11.6 4.5 %collective-permute-start.2 = (bf16[2,38,4,128]{3,2,1,0:T(4,128)(2,1)S(1)}, bf16[2,38,4,128]{3,2,1,0:T(4,128)(2,1)S(1)}, u32[]{:S(2)}, u32[]{:S(2)}) collective-permute-start(bf16[2,38,4,128]{3,2,1,0:T(4,128)(2,1)S(1)} %get-tuple-element.62), channel_id=1, source_target_pairs={{0,1},{1,0},{2,3},{3,2},{4,5},{5,4},{6,7},{7,6},{8,9},{9,8},{10,11... | collective-permute-start | bytes 233480 | tf_op jit(solution)/shard_map/ppermute | solution.py:337
  12.2 3.8 %collective-permute-start.3 = (bf16[2,38,4,128]{3,2,1,0:T(4,128)(2,1)S(1)}, bf16[2,38,4,128]{3,2,1,0:T(4,128)(2,1)S(1)}, u32[]{:S(2)}, u32[]{:S(2)}) collective-permute-start(bf16[2,38,4,128]{3,2,1,0:T(4,128)(2,1)S(1)} %get-tuple-element.61), channel_id=1, source_target_pairs={{1,2},{2,1},{3,4},{4,3},{5,6},{6,5},{9,10},{10,9},{11,12},{12,11},... | collective-permute-start | bytes 233480 | tf_op jit(solution)/shard_map/ppermute | solution.py:337
  16.1 10.5 %copy-start.2 = (bf16[1024,256]{1,0:T(8,128)(2,1)S(1)}, bf16[1024,256]{1,0:T(8,128)(2,1)}, u32[]{:S(2)}) copy-start(bf16[1024,256]{1,0:T(8,128)(2,1)} %rest_0_.1) | copy-start | bytes 1572868
  21.2 11.2 %copy-start.9 = (bf16[3,3,3,256,256]{4,3,2,1,0:T(8,128)(2,1)S(1)}, bf16[3,3,3,256,256]{4,3,2,1,0:T(8,128)(2,1)}, u32[]{:S(2)}) copy-start(bf16[3,3,3,256,256]{4,3,2,1,0:T(8,128)(2,1)} %param.17) | copy-start | bytes 10616836
  21.2 11.1 %copy-start.10 = (bf16[1024,512]{1,0:T(8,128)(2,1)S(1)}, bf16[1024,512]{1,0:T(8,128)(2,1)}, u32[]{:S(2)}) copy-start(bf16[1024,512]{1,0:T(8,128)(2,1)} %down.1) | copy-start | bytes 3145732
  21.3 11.1 %copy-start.11 = (f32[256]{0:T(256)S(1)}, f32[256]{0:T(256)}, u32[]{:S(2)}) copy-start(f32[256]{0:T(256)} %param.16) | copy-start | bytes 3076
  21.3 11.1 %collective-permute-start.4 = (bf16[624,256]{1,0:T(8,128)(2,1)S(1)}, bf16[624,256]{1,0:T(8,128)(2,1)S(1)}, u32[]{:S(2)}, u32[]{:S(2)}) collective-permute-start(bf16[624,256]{1,0:T(8,128)(2,1)S(1)} %fine_next.1), channel_id=1, source_target_pairs={{0,32},{32,64},{64,96},{96,128},{128,160},{160,192},{192,224},{1,3... | collective-permute-start | bytes 958472 | tf_op jit(solution)/shard_map/ppermute | solution.py:372
  32.4 11.7 %copy-start.3 = (bf16[512,512]{1,0:T(8,128)(2,1)S(1)}, bf16[512,512]{1,0:T(8,128)(2,1)}, u32[]{:S(2)}) copy-start(bf16[512,512]{1,0:T(8,128)(2,1)} %query_ref.1) | copy-start | bytes 1572868
  32.4 11.7 %copy-start.4 = (bf16[512,512]{1,0:T(8,128)(2,1)S(1)}, bf16[512,512]{1,0:T(8,128)(2,1)}, u32[]{:S(2)}) copy-start(bf16[512,512]{1,0:T(8,128)(2,1)} %key_ref.1) | copy-start | bytes 1572868
  32.4 11.7 %copy-start.5 = (bf16[512,512]{1,0:T(8,128)(2,1)S(1)}, bf16[512,512]{1,0:T(8,128)(2,1)}, u32[]{:S(2)}) copy-start(bf16[512,512]{1,0:T(8,128)(2,1)} %value_ref.1) | copy-start | bytes 1572868
  32.4 11.7 %copy-start.6 = (bf16[512,512]{1,0:T(8,128)(2,1)S(1)}, bf16[512,512]{1,0:T(8,128)(2,1)}, u32[]{:S(2)}) copy-start(bf16[512,512]{1,0:T(8,128)(2,1)} %out_ref.1) | copy-start | bytes 1572868
  36.3 13.4 %copy-start.8 = (f32[512]{0:T(512)S(1)}, f32[512]{0:T(512)}, u32[]{:S(2)}) copy-start(f32[512]{0:T(512)} %param.19) | copy-start | bytes 6148
  36.3 10.6 %collective-permute-start.5 = (bf16[128,512]{1,0:T(8,128)(2,1)S(1)}, bf16[128,512]{1,0:T(8,128)(2,1)S(1)}, u32[]{:S(2)}, u32[]{:S(2)}) collective-permute-start(bf16[128,512]{1,0:T(8,128)(2,1)S(1)} %get-tuple-element.36), channel_id=1, source_target_pairs={{0,32},{32,64},{64,96},{96,128},{128,160},{160,192},{192,224},{1,3... | collective-permute-start | bytes 393224 | tf_op jit(solution)/shard_map/ppermute | solution.py:375
  41.9 7.8 %collective-permute-start.6 = (bf16[128,512]{1,0:T(8,128)(2,1)S(1)}, bf16[128,512]{1,0:T(8,128)(2,1)S(1)}, u32[]{:S(2)}, u32[]{:S(2)}) collective-permute-start(bf16[128,512]{1,0:T(8,128)(2,1)S(1)} %get-tuple-element.37), channel_id=1, source_target_pairs={{0,64},{32,96},{64,128},{96,160},{128,192},{160,224},{1,65},{33,97... | collective-permute-start | bytes 393224 | tf_op jit(solution)/shard_map/ppermute | solution.py:376
  50.9 25.9 %all-to-all-start = ((bf16[8,128,512]{2,1,0:T(8,128)(2,1)}), bf16[8,128,512]{2,1,0:T(8,128)(2,1)S(1)}, u32[]{:S(2)}, u32[]{:S(2)}) async-start(bf16[8,128,512]{2,1,0:T(8,128)(2,1)} %get-tuple-element.44), calls=%async_computation | async-start | bytes 2097152 | tf_op jit(solution)/shard_map/all_to_all | solution.py:388
  59.3 15.9 %collective-permute-start.7 = (bf16[128,512]{1,0:T(8,128)(2,1)S(1)}, bf16[128,512]{1,0:T(8,128)(2,1)S(1)}, u32[]{:S(2)}, u32[]{:S(2)}) collective-permute-start(bf16[128,512]{1,0:T(8,128)(2,1)S(1)} %get-tuple-element.43), channel_id=1, source_target_pairs={{0,16},{16,0},{1,17},{17,1},{2,18},{18,2},{3,19},{19,3},{4,20},{20... | collective-permute-start | bytes 393224 | tf_op jit(solution)/shard_map/ppermute | solution.py:337
  75.2 1.6 %collective-permute-start.8 = (bf16[256,512]{1,0:T(8,128)(2,1)S(1)}, bf16[256,512]{1,0:T(8,128)(2,1)S(1)}, u32[]{:S(2)}, u32[]{:S(2)}) collective-permute-start(bf16[256,512]{1,0:T(8,128)(2,1)S(1)} %constant_dynamic-update-slice_fusion.mine_ref), channel_id=1, source_target_pairs={{0,8},{8,0},{1,9},{9,1},{2,10},{10,2},{3,11},{11,3},{4,12},{12,4},... | collective-permute-start | bytes 786440 | tf_op jit(solution)/shard_map/ppermute | solution.py:337
  78.4 1.7 %collective-permute-start.9 = (bf16[256,640]{1,0:T(8,128)(2,1)S(1)}, bf16[256,640]{1,0:T(8,128)(2,1)S(1)}, u32[]{:S(2)}, u32[]{:S(2)}) collective-permute-start(bf16[256,640]{1,0:T(8,128)(2,1)S(1)} %get-tuple-element.47), channel_id=1, source_target_pairs={{0,8},{8,0},{1,9},{9,1},{2,10},{10,2},{3,11},{11,3},{4,12},{12,4},... | collective-permute-start | bytes 983048 | tf_op jit(solution)/shard_map/ppermute | solution.py:337
  80.4 7.8 %collective-permute-start.10 = (bf16[128,640]{1,0:T(8,128)(2,1)S(1)}, bf16[128,640]{1,0:T(8,128)(2,1)S(1)}, u32[]{:S(2)}, u32[]{:S(2)}) collective-permute-start(bf16[128,640]{1,0:T(8,128)(2,1)S(1)} %get-tuple-element.50), channel_id=1, source_target_pairs={{0,16},{16,0},{1,17},{17,1},{2,18},{18,2},{3,19},{19,3},{4,20},{20... | collective-permute-start | bytes 491528 | tf_op jit(solution)/shard_map/ppermute | solution.py:337

commit v4 on v3

v4 whole, which is shorter than its diff:
```python
import functools
import math

import jax
import jax.numpy as jnp
from jax import lax
from jax.experimental import pallas as pl
from jax.experimental.pallas import tpu as pltpu
from jax.sharding import Mesh, PartitionSpec as P

EPSILON = 1e-06
BF16 = jnp.bfloat16
F32 = jnp.float32
HEIGHT = ("hx", "core")
GATHER = "width"
VMEM_LIMIT = 32 * 1024 * 1024
VM = pl.BlockSpec(memory_space=pltpu.VMEM)
HB = pl.BlockSpec(memory_space=pltpu.HBM)
SM = pl.BlockSpec(memory_space=pltpu.SMEM)


def call(kernel, out, ins, scratch=(), flops=0, moved=4 << 20, name=None):
    return pl.pallas_call(
        kernel,
        out_shape=out,
        in_specs=ins,
        out_specs=jax.tree.map(lambda _: VM, out),
        scratch_shapes=list(scratch),
        compiler_params=pltpu.CompilerParams(vmem_limit_bytes=VMEM_LIMIT),
        cost_estimate=pl.CostEstimate(flops=flops, bytes_accessed=moved, transcendentals=0),
        name=name,
    )


def kept(value):
    return pltpu.with_memory_space_constraint(value, pltpu.HBM)


def shape(dims, dtype):
    return jax.ShapeDtypeStruct(dims, dtype)


def dot(a, b):
    return jnp.dot(a, b, preferred_element_type=F32)


def scaled(values, gain):
    mean = jnp.mean(values * values, axis=-1, keepdims=True)
    return values * lax.rsqrt(mean + EPSILON) * gain


def silu(values):
    return values * jax.nn.sigmoid(values)


def compose_kernel(own, flag_ref, conv_hbm, down_hbm, out_ref, acc, conv, down, sems):
    taps = 3 if own else 2
    fetch_down = pltpu.make_async_copy(down_hbm, down, sems.at[3])
    fetch_down.start()
    fetches = []
    for i in range(3):
        fetches.append(pltpu.make_async_copy(conv_hbm.at[pl.ds(0, taps), i], conv.at[pl.ds(0, taps), i], sems.at[i]))
        fetches[i].start()
    acc[...] = jnp.zeros_like(acc)
    start = flag_ref[0] == 0
    fetch_down.wait()
    for i in range(3):
        fetches[i].wait()
        k0, k1 = (conv[s, i].reshape(384, 128) for s in range(2))
        if own:
            k2 = conv[2, i].reshape(384, 128)
            f0, f1, f2 = (k.astype(F32) for k in (k0, k1, k2))
            k2s = jnp.where(start, f0 + f1 + f2, f2).astype(BF16)
            k1s = jnp.where(start, f0 + f1, f1).astype(BF16)
            wide, narrow, wide_at, narrow_at, half = jnp.concatenate([k2s, k1s], -1), k2, 0, 1, 1
        else:
            wide, narrow, wide_at, narrow_at, half = jnp.concatenate([k1, k0], -1), k0, 1, 0, 0
        for r in range(2):
            for c in range(2):
                at = (r * 2 + c) * 128
                halves = [down[f * 512 + at : f * 512 + at + 128, :] for f in range(2)]
                both = dot(wide, jnp.concatenate(halves, 0))
                one = dot(narrow, halves[half])
                for j in range(3):
                    tap = (i + r) * 4 + j + c
                    rows = slice(j * 128, j * 128 + 128)
                    acc[tap, wide_at * 128 : wide_at * 128 + 128, :] += both[rows]
                    acc[tap, narrow_at * 128 : narrow_at * 128 + 128, :] += one[rows]
    out_ref[...] = acc[...].astype(BF16)


def compose(own, tm, conv_fine, down_fine):
    return call(
        functools.partial(compose_kernel, own),
        shape((16, 256, 256), BF16),
        [SM, HB, HB],
        [
            pltpu.VMEM((16, 256, 256), F32),
            pltpu.VMEM((3, 3, 3, 128, 128), BF16),
            pltpu.VMEM((1024, 256), BF16),
            pltpu.SemaphoreType.DMA((4,)),
        ],
        flops=900_000_000,
        name="compose_own" if own else "compose_next",
    )(tm, kept(conv_fine.reshape(3, 3, 3, 128, 128)), kept(down_fine))


COLS = 104
PITCH = 48
FLAT = 624


def prepare_kernel(x_hbm, gain_ref, act_ref, first_ref, last_ref, x, sems):
    fetches = []
    for k in range(4):
        rows = pl.ds(k * 8, 8)
        fetches.append(pltpu.make_async_copy(x_hbm.at[:, rows], x.at[:, rows], sems.at[k]))
        fetches[k].start()
    gain = gain_ref[...].reshape(1, 1, 128)
    for k in range(4):
        fetches[k].wait()
        for f in range(2):
            for half in range(2):
                rows = pl.ds(k * 8 + half * 4, 4)
                act_ref[f, rows] = silu(scaled(x[f, rows].astype(F32), gain))
    first_ref[...] = x[:, :, 0:4]
    last_ref[...] = x[:, :, 60:64]


def prepare(features, gain):
    edge = shape((2, 32, 4, 128), BF16)
    return call(
        prepare_kernel,
        (shape((2, 32, 64, 128), F32), edge, edge),
        [HB, VM],
        [pltpu.VMEM((2, 32, 64, 128), BF16), pltpu.SemaphoreType.DMA((4,))],
        flops=10_000_000,
        name="prepare",
    )(kept(features), gain.reshape(1, 128))


def spread(field, up_ref, low_ref, left_ref, right_ref, change):
    for f in range(2):
        field[f, pl.ds(0, 3), pl.ds(8, 64), :] = change(up_ref[f].astype(F32))
        field[f, pl.ds(35, 3), pl.ds(8, 64), :] = change(low_ref[f].astype(F32))
        field[f, :, pl.ds(4, 4), :] = change(left_ref[f].astype(F32))
        field[f, :, pl.ds(72, 4), :] = change(right_ref[f].astype(F32))


GROUP = 6


def next_kernel(act_ref, up_ref, low_ref, left_ref, right_ref, gain_ref, weight_ref, out_ref, planes, act, flat):
    gain = gain_ref[...].reshape(1, 1, 128)
    spread(act, up_ref, low_ref, left_ref, right_ref, lambda values: silu(scaled(values, gain)))
    act[:, pl.ds(3, 32), pl.ds(8, 64), :] = act_ref[...]

    def build(q, carry):
        for rp in range(2):
            for v in range(4):
                both = [act[f, 2 * q + rp, pl.ds(5 + v, 40, stride=2), :].astype(BF16) for f in range(2)]
                planes[rp, v, q, pl.ds(0, 40), :] = jnp.concatenate(both, -1)
        return carry

    lax.fori_loop(0, 19, build, 0)
    for base in range(0, 18, GROUP):
        total = dot(taps_at(planes, base), weight_ref[...].reshape(4096, 256)).reshape(GROUP, PITCH, 256)
        for k in range(GROUP):
            flat[pl.ds((base + k) * 34, 34), :] = total[k, :34]
    flat[pl.ds(612, 12), :] = jnp.zeros((12, 256), F32)
    out_ref[...] = flat[...].astype(BF16)


def taps_at(planes, base):
    parts = []
    for u in range(4):
        for v in range(4):
            parts.append(planes[u % 2, v, pl.ds(base + u // 2, GROUP)].reshape(GROUP * PITCH, 256))
    return jnp.concatenate(parts, -1)


def own_kernel(x_ref, up_ref, low_ref, left_ref, right_ref, weight_ref, planes, down_ref, out_ref, raw, raw_planes):
    spread(raw, up_ref, low_ref, left_ref, right_ref, lambda values: values)
    raw[:, pl.ds(3, 32), pl.ds(8, 64), :] = x_ref[...].astype(F32)

    def build(q, carry):
        for rp in range(2):
            for v in range(2):
                both = [raw[f, 2 * q + rp, pl.ds(6 + v, 40, stride=2), :].astype(BF16) for f in range(2)]
                raw_planes[rp, v, q, pl.ds(0, 40), :] = jnp.concatenate(both, -1)
        return carry

    lax.fori_loop(0, 19, build, 0)
    folds = []
    for r in range(2):
        for c in range(2):
            for f in range(2):
                at = (f * 4 + r * 2 + c) * 128
                folds.append(down_ref[at : at + 128, :])
    fold_weight = jnp.concatenate(folds, 0)
    for base in range(0, 18, GROUP):
        parts = []
        for r in range(2):
            for c in range(2):
                rows = pl.ds(base + (r + 1) // 2, GROUP)
                parts.append(raw_planes[(r + 1) % 2, c, rows].reshape(GROUP * PITCH, 256))
        total = dot(taps_at(planes, base), weight_ref[...].reshape(4096, 256))
        total = total + dot(jnp.concatenate(parts, -1), fold_weight)
        out_ref[base : base + GROUP] = total.reshape(GROUP, PITCH, 256)


def fine_next(act, halos, gain, weight):
    return call(
        next_kernel,
        (shape((FLAT, 256), BF16), shape((2, 4, 19, PITCH, 256), BF16)),
        [VM] * 7,
        [pltpu.VMEM((2, 38, COLS, 128), F32), pltpu.VMEM((FLAT, 256), F32)],
        flops=1_800_000_000,
        name="fine_next",
    )(act, *halos, gain.reshape(1, 128), weight)


def fine_own(features, halos, weight, planes, down):
    return call(
        own_kernel,
        shape((18, PITCH, 256), F32),
        [VM] * 8,
        [pltpu.VMEM((2, 38, COLS, 128), F32), pltpu.VMEM((2, 2, 19, PITCH, 256), BF16)],
        flops=2_200_000_000,
        name="fine_own",
    )(features, *halos, weight, planes, down)


def folded(field):
    field = field.astype(BF16).reshape(2, 8, 2, 16, 256)
    parts = [field[p, :, r].reshape(128, 256) for r in range(2) for p in range(2)]
    return jnp.concatenate(parts, -1)


def windows(shifted):
    sides = []
    for p in range(2):
        parts = [shifted[p + j, i : i + 16].reshape(256, 256) for i in range(3) for j in range(3)]
        sides.append(jnp.concatenate(parts, -1))
    return jnp.concatenate(sides, 0)


def far_kernel(flag_ref, own_ref, got_ref, gain_ref, conv_ref, down_ref, far_ref, c0_ref, shifted, reduced, got, act):
    gain = gain_ref[...]
    got[...] = got_ref[...].astype(F32)
    for row in range(18):
        value = own_ref[row, pl.ds(0, 40), :] + got[pl.ds(row * 34, 40), :]
        value = value.astype(BF16).astype(F32)
        active = silu(scaled(value, gain))
        for half in range(2):
            reduced[half, row, pl.ds(0, 40), :] = value[:, half * 128 : half * 128 + 128]
            act[half, row, pl.ds(0, 40), :] = active[:, half * 128 : half * 128 + 128]

    @pl.when(flag_ref[1] == 0)
    def _():
        act[:, 0] = jnp.zeros((2, PITCH, 128), F32)

    @pl.when(flag_ref[1] == 3)
    def _():
        act[:, 17] = jnp.zeros((2, PITCH, 128), F32)

    @pl.when(flag_ref[2] == 0)
    def _():
        act[:, :, pl.ds(0, 1), :] = jnp.zeros((2, 18, 1, 128), F32)

    @pl.when(flag_ref[2] == 7)
    def _():
        act[:, :, pl.ds(33, 1), :] = jnp.zeros((2, 18, 1, 128), F32)

    def build(row, carry):
        for v in range(4):
            halves = [act[half, row, pl.ds(v, 16, stride=2), :] for half in range(2)]
            shifted[v, row] = jnp.concatenate(halves, -1).astype(BF16)
        return carry

    lax.fori_loop(0, 18, build, 0)
    c0 = dot(windows(shifted), conv_ref[0].reshape(2304, 256))
    c0_ref[...] = c0
    far_ref[...] = dot(folded(c0), down_ref[...]).astype(BF16)


def near_kernel(flag_ref, shifted, c0_ref, conv_ref, down_ref, near_ref, c1_ref):
    start = (flag_ref[0] == 0).astype(F32)
    c1 = dot(windows(shifted), conv_ref[1].reshape(2304, 256)) + c0_ref[...] * start
    c1_ref[...] = c1
    near_ref[...] = dot(folded(c1), down_ref[...]).astype(BF16)


def here_kernel(flag_ref, shifted, reduced, c1_ref, conv_ref, down_ref, latent_ref):
    start = (flag_ref[0] == 0).astype(F32)
    plain = []
    for p in range(2):
        for row in range(16):
            halves = [reduced[half, row + 1, pl.ds(1 + p, 16, stride=2), :] for half in range(2)]
            plain.append(jnp.concatenate(halves, -1))
    c2 = dot(windows(shifted), conv_ref[2].reshape(2304, 256)) + c1_ref[...] * start
    latent_ref[...] = dot(folded(c2 + jnp.concatenate(plain, 0)), down_ref[...])


def coarse(flags, own, got, gain, conv, down):
    conv = conv.reshape(3, 9, 256, 256)
    rows = shape((128, 512), BF16)
    field = shape((512, 256), F32)
    far, c0, shifted, reduced = call(
        far_kernel,
        (rows, field, shape((4, 18, 16, 256), BF16), shape((2, 18, PITCH, 128), F32)),
        [SM] + [VM] * 5,
        [pltpu.VMEM((FLAT, 256), F32), pltpu.VMEM((2, 18, PITCH, 128), F32)],
        flops=800_000_000,
        name="coarse_far",
    )(flags, own, got, gain.reshape(1, 256), conv, down)
    near, c1 = call(near_kernel, (rows, field), [SM] + [VM] * 4, flops=1000, moved=1000, name="coarse_near")(
        flags, shifted, c0, conv, down
    )
    latent = call(here_kernel, shape((128, 512), F32), [SM] + [VM] * 5, flops=1000, moved=1000, name="coarse_here")(
        flags, shifted, reduced, c1, conv, down
    )
    return near, far, latent


def mix_kernel(query_ref, key_ref, value_ref, out_ref, score_ref, mix_ref):
    scores = lax.dot_general(query_ref[...], key_ref[...], (((1,), (1,)), ((), ())), preferred_element_type=F32)
    score_ref[...] = (scores * (1.0 / math.sqrt(512))).astype(BF16)
    mix_ref[...] = dot(value_ref[...], out_ref[...]).astype(BF16)


def latent_kernel(own_ref, near_ref, far_ref, gain_ref, score_ref, latent_ref, query_ref, normed_ref):
    latent = (own_ref[...] + near_ref[...].astype(F32) + far_ref[...].astype(F32)).astype(BF16)
    latent_ref[...] = latent
    normed = scaled(latent.astype(F32), gain_ref[...]).astype(BF16)
    normed_ref[...] = normed
    query_ref[...] = dot(normed, score_ref[...]).astype(BF16)


def copies_kernel(normed_ref, copies_ref):
    for k in range(copies_ref.shape[0]):
        copies_ref[k] = normed_ref[...]


def packed(values, level):
    level = jnp.broadcast_to(level, (level.shape[0], 128))
    high = level.astype(BF16)
    rest = level - high.astype(F32)
    middle = rest.astype(BF16)
    low = (rest - middle.astype(F32)).astype(BF16)
    lane = lax.broadcasted_iota(jnp.int32, level.shape, 1)
    parts = jnp.where(lane == 0, high.astype(F32), jnp.where(lane == 1, middle.astype(F32), low.astype(F32)))
    return jnp.concatenate([values.astype(BF16), parts.astype(BF16)], -1)


def level_of(block):
    parts = block[:, 512:].astype(F32)
    lane = lax.broadcasted_iota(jnp.int32, parts.shape, 1)
    return jnp.sum(jnp.where(lane < 3, parts, 0.0), -1, keepdims=True)


def joined(values, level, block):
    other = level_of(block)
    top = jnp.maximum(level, other)
    low = jnp.minimum(level, other)
    share = jax.nn.sigmoid(level - other)
    merged = values * share + block[:, :512].astype(F32) * (1.0 - share)
    return merged, top + jnp.log(1.0 + jnp.exp(low - top))


def attend_kernel(mine_ref, theirs_ref, keys_ref, mixed_ref, level_ref, sent_ref):
    queries = jnp.concatenate([mine_ref[...], theirs_ref[...]], 0)
    keys = keys_ref[...]
    scores = lax.dot_general(queries, keys, (((1,), (1,)), ((), ())), preferred_element_type=F32)
    top = jnp.max(scores, -1, keepdims=True)
    expo = jnp.exp(scores - top)
    total = jnp.sum(expo, -1, keepdims=True)
    mixed = dot(expo.astype(BF16), keys) / total
    level = top + jnp.log(total)
    mixed_ref[...] = mixed[:256]
    level_ref[...] = jnp.broadcast_to(level[:256], (256, 128))
    sent_ref[...] = packed(mixed[256:], level[256:])


def merge_kernel(mixed_ref, level_ref, got_ref, kept_ref, kept_level_ref, sent_ref):
    merged, level = joined(mixed_ref[...], level_ref[:, :1], got_ref[...])
    kept_ref[...] = merged[:128]
    kept_level_ref[...] = jnp.broadcast_to(level[:128], (128, 128))
    sent_ref[...] = packed(merged[128:], level[128:])


def finish_kernel(mixed_ref, level_ref, got_ref, latent_ref, mix_ref, out_ref):
    attended, _ = joined(mixed_ref[...], level_ref[:, :1], got_ref[...])
    out_ref[...] = (latent_ref[...].astype(F32) + dot(attended.astype(BF16), mix_ref[...])).astype(BF16)


def swapped(value, axis, count, first):
    pairs = []
    for low in range(first, count - 1, 2):
        pairs += [(low, low + 1), (low + 1, low)]
    return lax.ppermute(value, axis, pairs)


def sides(block, axis, dim, width, count):
    odd = lax.axis_index(axis) % 2
    last = block.shape[dim] - width
    inner = lax.dynamic_slice_in_dim(block, (1 - odd) * last, width, axis=dim)
    outer = lax.dynamic_slice_in_dim(block, odd * last, width, axis=dim)
    got_inner = swapped(inner, axis, count, 0)
    got_outer = swapped(outer, axis, count, 1)
    even = odd == 0
    return jnp.where(even, got_outer, got_inner), jnp.where(even, got_inner, got_outer)


def per_device(
    features, gain_fine, conv_fine, down_fine, gain_coarse, conv_coarse, down_coarse,
    gain_latent, w_query, w_key, w_value, w_out,
):
    tm = lax.axis_index("tm").astype(jnp.int32)
    flags = jnp.stack([tm, lax.axis_index(HEIGHT).astype(jnp.int32), lax.axis_index("width").astype(jnp.int32)])
    above, below = sides(features, HEIGHT, 1, 3, 4)
    act, first, last = prepare(features, gain_fine)
    above, below, act, first, last = lax.optimization_barrier((above, below, act, first, last))
    first = jnp.concatenate([above[:, :, :4], first, below[:, :, :4]], 1)
    last = jnp.concatenate([above[:, :, 60:], last, below[:, :, 60:]], 1)
    odd = lax.axis_index("width") % 2 == 1
    got_inner = swapped(jnp.where(odd, first, last), "width", 8, 0)
    got_outer = swapped(jnp.where(odd, last, first), "width", 8, 1)
    weight_next = compose(False, flags, conv_fine, down_fine)
    got_inner, got_outer, weight_next = lax.optimization_barrier((got_inner, got_outer, weight_next))
    left, right = jnp.where(odd, got_inner, got_outer), jnp.where(odd, got_outer, got_inner)
    halos = (above, below, left, right)
    sent, planes = fine_next(act, halos, gain_fine, weight_next)
    got = lax.ppermute(sent, "tm", [(i, i + 1) for i in range(7)])
    weight_own = compose(True, flags, conv_fine, down_fine)
    own = fine_own(features, halos, weight_own, planes, down_fine)
    near, far, latent_own = coarse(flags, own, got, gain_coarse, conv_coarse, down_coarse)
    far = lax.ppermute(far, "tm", [(i, i + 2) for i in range(6)])
    near = lax.ppermute(near, "tm", [(i, i + 1) for i in range(7)])
    square = shape((512, 512), BF16)
    w_score, w_mix = call(mix_kernel, (square, square), [VM] * 4, flops=1000, moved=1000, name="mix")(
        w_query, w_key, w_value, w_out
    )
    near, far, latent_own, w_score, w_mix = lax.optimization_barrier((near, far, latent_own, w_score, w_mix))
    rows = shape((128, 512), BF16)
    latent_in, query, normed = call(
        latent_kernel, (rows, rows, rows), [VM] * 5, flops=80_000_000, name="latent"
    )(latent_own, near, far, gain_latent.reshape(1, 512), w_score)
    copies = call(copies_kernel, shape((8, 128, 512), BF16), [VM], name="copies")(normed)
    queries = jnp.concatenate([query, swapped(query, "hx", 2, 0)], 0)
    their_queries = swapped(queries, "core", 2, 0)
    keys = lax.all_to_all(copies, GATHER, 0, 0, tiled=True).reshape(1024, 512)
    mixed, level, sent = call(
        attend_kernel,
        (shape((256, 512), F32), shape((256, 128), F32), shape((256, 640), BF16)),
        [VM] * 3,
        flops=1_100_000_000,
        name="attend",
    )(queries, their_queries, keys)
    got = swapped(sent, "core", 2, 0)
    mixed, level, sent = call(
        merge_kernel,
        (shape((128, 512), F32), shape((128, 128), F32), shape((128, 640), BF16)),
        [VM] * 3,
        flops=1_000_000,
        name="merge",
    )(mixed, level, got)
    got = swapped(sent, "hx", 2, 0)
    out = call(finish_kernel, rows, [VM] * 5, flops=70_000_000, name="finish")(mixed, level, got, latent_in, w_mix)
    return out.reshape(1, 8, 16, 512)


def solution(mesh):
    split = Mesh(mesh.devices.reshape(8, 2, 2, 8), ("tm", "hx", "core", "width"))
    placed = (P("tm", HEIGHT, "width", None),) + (P(),) * 11
    return jax.shard_map(
        per_device, mesh=split, in_specs=placed,
        out_specs=P("tm", HEIGHT, "width", None), check_vma=False,
    )
```

time: 89.9 us -> 84.7 us (0.942)
  waiting for transfers between devices: 29.8 us -> 24.3 us
  local copies, waits for them, and re-layouts: 4.29 us -> 1.71 us
  Pallas kernels: 23.4 us -> 25.2 us
    ppermute x8, waiting for transfers between devices: 25 us -> 19.4 us  [swapped(): return lax.ppermute(value, axis, pairs)]
    pallas_call x2, Pallas kernels: 3.83 us -> 6.51 us  [compose(): call(functools.partial(compose_kernel, own), shape((16, 256, 256), BF16),...]
    ppermute x8, starting transfers between devices: 9.76 us -> 11.6 us  [swapped(): return lax.ppermute(value, axis, pairs)]
    unnamed x27 -> x25, local copies, waits for them, and re-layouts: 2.29 us -> 0.73 us
    all_to_all x1, starting transfers between devices: 8.42 us -> 6.94 us  [per_device(): keys = lax.all_to_all(copies, GATHER, 0, 0, tiled=True).reshape(1024, 512)]
    ppermute x1, waiting for transfers between devices: 2.07 us -> 0.78 us  [per_device(): near = lax.ppermute(near, 'tm', [(i, i + 1) for i in range(7)])]
    slice x2 -> x1, local copies, waits for them, and re-layouts: 1.04 us -> 0.02 us  [per_device(): first = jnp.concatenate([above[:, :, :4], first, below[:, :, :4]], 1)]
    pallas_call x5 -> x9, Pallas kernels: 16.7 us -> 15.8 us  [the longest x1 2.95 us: fine_next(): call(next_kernel, (shape((FLAT, 256), BF16), shape((2, 4, 19, PITCH, 256)...]
  transfers between devices with their start and end apart: 12 -> 12, of which waited for: 7 -> 8; matrix products, arithmetic and copies ran while one was open for 1% -> 0% of each run, Pallas kernels for 12% -> 17%
where the time goes in v4:
time: 84.7 us; the launch traced here: 83.4 us
  starting transfers between devices  31.6 us (37%)
  Pallas kernels  25.2 us (30%)
  waiting for transfers between devices  24.3 us (29%)
  local copies, waits for them, and re-layouts  1.71 us (2%)
    ppermute x8, waiting for transfers between devices, swapped(): return lax.ppermute(value, axis, pairs)  19.4 us
    ppermute x8, starting transfers between devices, swapped(): return lax.ppermute(value, axis, pairs)  11.6 us
    all_to_all x1, starting transfers between devices, per_device(): keys = lax.all_to_all(copies, GATHER, 0, 0, tiled=True).reshape(1024, 512)  6.94 us
    pallas_call x2, Pallas kernels, compose(): call(functools.partial(compose_kernel, own), shape((16, 256, 256), BF16),...  6.51 us
    ppermute x1, starting transfers between devices, per_device(): near = lax.ppermute(near, 'tm', [(i, i + 1) for i in range(7)])  5.61 us
    ppermute x1, starting transfers between devices, per_device(): got = lax.ppermute(sent, 'tm', [(i, i + 1) for i in range(7)])  5.17 us
    pallas_call x1, Pallas kernels, fine_next(): call(next_kernel, (shape((FLAT, 256), BF16), shape((2, 4, 19, PITCH, 256)...  2.95 us
    pallas_call x1, Pallas kernels, fine_own(): call(own_kernel, shape((18, PITCH, 256), F32), [VM] * 8, [pltpu.VMEM((2,...  2.92 us
  transfers between devices with their start and end apart: 12, of which 8 were waited for; matrix products, arithmetic and copies ran while one was open for 0% of the time, Pallas kernels for 17%

profile of v4, /device:TPU:96, one launch (start us, length us, event | category | flops | bytes accessed | tf_op | source)
XLA Modules:
  0.0 83.4 jit_solution(16434769437624756109)
XLA Ops:
  0.0 1.0 %constant_dynamic-slice_fusion = (bf16[2,3,64,128]{3,2,1,0:T(8,128)(2,1)S(1)}, bf16[2,3,64,128]{3,2,1,0:T(8,128)(2,1)S(1)}) fusion(bf16[2,32,64,128]{3,2,1,0:T(8,128)(2,1)} %x_ref.1, s32[]{:T(128)S(6)} %select_n.52, s32[]{:T(128)S(6)} %select_n.51), kind=kLoop, calls=%fused_computation.11 | loop fusion | bytes 393224 | tf_op jit(solution)/shard_map/dynamic_slice | solution.py:407
  1.0 0.7 collective-permute-start
  1.6 4.5 %collective-permute-start.1 = (bf16[2,3,64,128]{3,2,1,0:T(8,128)(2,1)S(1)}, bf16[2,3,64,128]{3,2,1,0:T(8,128)(2,1)S(1)}, u32[]{:S(2)}, u32[]{:S(2)}) collective-permute-start(bf16[2,3,64,128]{3,2,1,0:T(8,128)(2,1)S(1)} %get-tuple-element.75), channel_id=1, source_target_pairs={{0,8},{8,0},{16,24},{24,16},{1,9},{9,1},{17,25},{25,17},{2,10},{10... | collective-permute-start | bytes 294920 | tf_op jit(solution)/shard_map/ppermute | solution.py:401
  6.1 0.7 copy-done.10
  6.8 1.9 %prepare.1 = (f32[2,32,64,128]{3,2,1,0:T(8,128)S(1)}, bf16[2,32,4,128]{3,2,1,0:T(4,128)(2,1)S(1)}, bf16[2,32,4,128]{3,2,1,0:T(4,128)(2,1)S(1)}) custom-call(bf16[2,32,64,128]{3,2,1,0:T(8,128)(2,1)} %x_ref.1, f32[1,128]{1,0:T(1,128)S(1)} %bitcast.23), custom_call_target="tpu_custom_call" | custom-call | flops 10000000 | bytes 4194304 | tf_op jit(solution)/shard_map/prepare/pallas_call | solution.py:132
  8.7 0.1 pad_add_fusion.flag_ref
  8.8 0.0 copy-start.11
  8.9 0.1 broadcast_select_fusion.4
  9.0 0.7 collective-permute-start.2
  9.7 0.7 collective-permute-start.3
  10.3 3.2 %compose_next.1.weight_ref = bf16[16,256,256]{2,1,0:T(8,128)(2,1)S(1)} custom-call(s32[3]{0:T(128)S(1)} %pad_add_fusion.flag_ref, bf16[3,3,3,128,128]{4,3,2,1,0:T(8,128)(2,1)} %conv_hbm.3, bf16[1024,256]{1,0:T(8,128)(2,1)} %down_ref.4), custom_call_target="tpu_custom_call" | custom-call | flops 900000000 | bytes 4194304 | tf_op jit(solution)/shard_map/compose_next/pallas_call | solution.py:93
  13.6 3.0 %fine_next.1 = (bf16[624,256]{1,0:T(8,128)(2,1)S(1)}, bf16[2,4,19,48,256]{4,3,2,1,0:T(8,128)(2,1)S(1)}) custom-call(f32[2,32,64,128]{3,2,1,0:T(8,128)S(1)} %get-tuple-element.49.act_ref, bf16[2,3,64,128]{3,2,1,0:T(8,128)(2,1)S(1)} %get-tuple-element.43.up_ref, bf16[2,3,64,128]{3,2,1,0:T(8,128)(2,1)S(1)} %get-tuple-element.44.low_ref, ...), custom_call_target="tpu_custom_call" | custom-call | flops 1800000000 | bytes 4194304 | tf_op jit(solution)/shard_map/fine_next/pallas_call | solution.py:213
  16.6 0.0 copy-start.2
  16.6 0.0 copy-start.3
  16.6 5.2 %collective-permute-start.4 = (bf16[624,256]{1,0:T(8,128)(2,1)S(1)}, bf16[624,256]{1,0:T(8,128)(2,1)S(1)}, u32[]{:S(2)}, u32[]{:S(2)}) collective-permute-start(bf16[624,256]{1,0:T(8,128)(2,1)S(1)} %get-tuple-element.52), channel_id=1, source_target_pairs={{0,32},{32,64},{64,96},{96,128},{128,160},{160,192},{192,224},{1,3... | collective-permute-start | bytes 958472 | tf_op jit(solution)/shard_map/ppermute | solution.py:434
  21.8 3.3 %compose_own.1.weight_ref = bf16[16,256,256]{2,1,0:T(8,128)(2,1)S(1)} custom-call(s32[3]{0:T(128)S(1)} %pad_add_fusion.flag_ref, bf16[3,3,3,128,128]{4,3,2,1,0:T(8,128)(2,1)} %conv_hbm.3, bf16[1024,256]{1,0:T(8,128)(2,1)} %down_ref.4), custom_call_target="tpu_custom_call" | custom-call | flops 900000000 | bytes 4194304 | tf_op jit(solution)/shard_map/compose_own/pallas_call | solution.py:93
  25.1 0.0 copy-start
  25.1 0.0 copy-start.1
  25.1 0.0 copy-start.9
  25.1 2.9 %fine_own.1.own_ref = f32[18,48,256]{2,1,0:T(8,128)S(1)} custom-call(bf16[2,32,64,128]{3,2,1,0:T(8,128)(2,1)S(1)} %copy-done.2, bf16[2,3,64,128]{3,2,1,0:T(8,128)(2,1)S(1)} %get-tuple-element.43.up_ref, bf16[2,3,64,128]{3,2,1,0:T(8,128)(2,1)S(1)} %get-tuple-element.44.low_ref, bf16[2,38,4,128]{3,2,1,0:T(4,128)(2,1)S(1)} %bitcast.20, ...), custom_call_target="tpu_custom_call" | custom-call | flops 2200000000 | bytes 4194304 | tf_op jit(solution)/shard_map/fine_own/pallas_call | solution.py:224
  28.1 0.7 collective-permute-done.4.got_ref
  28.8 2.3 %coarse_far.1 = (bf16[128,512]{1,0:T(8,128)(2,1)S(1)}, f32[512,256]{1,0:T(8,128)S(1)}, bf16[4,18,16,256]{3,2,1,0:T(8,128)(2,1)S(1)}, f32[2,18,48,128]{3,2,1,0:T(8,128)S(1)}) custom-call(s32[3]{0:T(128)S(1)} %pad_add_fusion.flag_ref, f32[18,48,256]{2,1,0:T(8,128)S(1)} %fine_own.1.own_ref, bf16[624,256]{1,0:T(8,128)(2,1)S(1)} %collective-permute-done.4.got_ref, ...), custom_call_target="tpu_custom_call" | custom-call | flops 800000000 | bytes 4194304 | tf_op jit(solution)/shard_map/coarse_far/pallas_call | solution.py:309
  31.1 0.0 copy-start.4
  31.1 0.0 copy-start.5
  31.1 0.0 copy-start.7
  31.1 1.8 %coarse_near.1 = (bf16[128,512]{1,0:T(8,128)(2,1)S(1)}, f32[512,256]{1,0:T(8,128)S(1)}) custom-call(s32[3]{0:T(128)S(1)} %pad_add_fusion.flag_ref, bf16[4,18,16,256]{3,2,1,0:T(8,128)(2,1)S(1)} %get-tuple-element.53.shifted, f32[512,256]{1,0:T(8,128)S(1)} %get-tuple-element.54.c0_ref, bf16[3,9,256,256]{3,2,1,0:T(8,128)(2,1)S(1)} %bitcast.14, ...), custom_call_target="tpu_custom_call" | custom-call | flops 1000 | bytes 1000 | tf_op jit(solution)/shard_map/coarse_near/pallas_call | solution.py:317
  32.9 5.6 %collective-permute-start.5 = (bf16[128,512]{1,0:T(8,128)(2,1)S(1)}, bf16[128,512]{1,0:T(8,128)(2,1)S(1)}, u32[]{:S(2)}, u32[]{:S(2)}) collective-permute-start(bf16[128,512]{1,0:T(8,128)(2,1)S(1)} %get-tuple-element.55), channel_id=1, source_target_pairs={{0,32},{32,64},{64,96},{96,128},{128,160},{160,192},{192,224},{1,3... | collective-permute-start | bytes 393224 | tf_op jit(solution)/shard_map/ppermute | solution.py:439
  38.5 2.4 %collective-permute-start.6 = (bf16[128,512]{1,0:T(8,128)(2,1)S(1)}, bf16[128,512]{1,0:T(8,128)(2,1)S(1)}, u32[]{:S(2)}, u32[]{:S(2)}) collective-permute-start(bf16[128,512]{1,0:T(8,128)(2,1)S(1)} %get-tuple-element.56), channel_id=1, source_target_pairs={{0,64},{32,96},{64,128},{96,160},{128,192},{160,224},{1,65},{33,97... | collective-permute-start | bytes 393224 | tf_op jit(solution)/shard_map/ppermute | solution.py:438
  40.9 0.7 mix.1
  41.7 0.0 copy-start.8
  41.7 1.8 %coarse_here.1.own_ref = f32[128,512]{1,0:T(8,128)S(1)} custom-call(s32[3]{0:T(128)S(1)} %pad_add_fusion.flag_ref, bf16[4,18,16,256]{3,2,1,0:T(8,128)(2,1)S(1)} %get-tuple-element.53.shifted, f32[2,18,48,128]{3,2,1,0:T(8,128)S(1)} %get-tuple-element.57.reduced, f32[512,256]{1,0:T(8,128)S(1)} %get-tuple-element.58.c1_ref, ...), custom_call_target="tpu_custom_call" | custom-call | flops 1000 | bytes 1000 | tf_op jit(solution)/shard_map/coarse_here/pallas_call | solution.py:320
  43.5 0.8 collective-permute-done.5.near_ref
  44.3 2.7 %collective-permute-done.6.far_ref = bf16[128,512]{1,0:T(8,128)(2,1)S(1)} collective-permute-done((bf16[128,512]{1,0:T(8,128)(2,1)S(1)}, bf16[128,512]{1,0:T(8,128)(2,1)S(1)}, u32[]{:S(2)}, u32[]{:S(2)}) %collective-permute-start.6) | collective-permute-done | bytes 131104 | tf_op jit(solution)/shard_map/ppermute | solution.py:438
  47.0 0.3 latent.1
  47.3 1.0 %copies.1 = bf16[8,128,512]{2,1,0:T(8,128)(2,1)} custom-call(bf16[128,512]{1,0:T(8,128)(2,1)S(1)} %get-tuple-element.66.normed_ref), custom_call_target="tpu_custom_call" | custom-call | bytes 4194304 | tf_op jit(solution)/shard_map/copies/pallas_call | solution.py:449
  48.4 6.9 %all-to-all-start = ((bf16[8,128,512]{2,1,0:T(8,128)(2,1)}), bf16[8,128,512]{2,1,0:T(8,128)(2,1)S(1)}, u32[]{:S(2)}, u32[]{:S(2)}) async-start(bf16[8,128,512]{2,1,0:T(8,128)(2,1)} %copies.1), calls=%async_computation | async-start | bytes 2097152 | tf_op jit(solution)/shard_map/all_to_all | solution.py:452
  55.3 2.1 %collective-permute-start.7 = (bf16[128,512]{1,0:T(8,128)(2,1)S(1)}, bf16[128,512]{1,0:T(8,128)(2,1)S(1)}, u32[]{:S(2)}, u32[]{:S(2)}) collective-permute-start(bf16[128,512]{1,0:T(8,128)(2,1)S(1)} %get-tuple-element.65), channel_id=1, source_target_pairs={{0,16},{16,0},{1,17},{17,1},{2,18},{18,2},{3,19},{19,3},{4,20},{20... | collective-permute-start | bytes 393224 | tf_op jit(solution)/shard_map/ppermute | solution.py:401
  57.4 11.2 %collective-permute-done.7 = bf16[128,512]{1,0:T(8,128)(2,1)S(1)} collective-permute-done((bf16[128,512]{1,0:T(8,128)(2,1)S(1)}, bf16[128,512]{1,0:T(8,128)(2,1)S(1)}, u32[]{:S(2)}, u32[]{:S(2)}) %collective-permute-start.7) | collective-permute-done | bytes 131104 | tf_op jit(solution)/shard_map/ppermute | solution.py:401
  68.7 0.1 collective-permute-start.8
  68.8 1.5 %collective-permute-done.8.theirs_ref = bf16[256,512]{1,0:T(8,128)(2,1)S(1)} collective-permute-done((bf16[256,512]{1,0:T(8,128)(2,1)S(1)}, bf16[256,512]{1,0:T(8,128)(2,1)S(1)}, u32[]{:S(2)}, u32[]{:S(2)}) %collective-permute-start.8) | collective-permute-done | bytes 262176 | tf_op jit(solution)/shard_map/ppermute | solution.py:401
  70.3 0.7 all-to-all-done
  71.0 1.5 %attend.1 = (f32[256,512]{1,0:T(8,128)S(1)}, f32[256,128]{1,0:T(8,128)S(1)}, bf16[256,640]{1,0:T(8,128)(2,1)S(1)}) custom-call(bf16[256,512]{1,0:T(8,128)(2,1)S(1)} %constant_dynamic-update-slice_fusion.mine_ref, bf16[256,512]{1,0:T(8,128)(2,1)S(1)} %collective-permute-done.8.theirs_ref, bf16[1024,512]{1,0:T(8,128)(2,1)S(1)} %bitcast.16), custom_call_target="tpu_custom_call" | custom-call | flops 1100000000 | bytes 4194304 | tf_op jit(solution)/shard_map/attend/pallas_call | solution.py:453
  72.5 0.1 collective-permute-start.9
  72.6 1.6 %collective-permute-done.9.got_ref = bf16[256,640]{1,0:T(8,128)(2,1)S(1)} collective-permute-done((bf16[256,640]{1,0:T(8,128)(2,1)S(1)}, bf16[256,640]{1,0:T(8,128)(2,1)S(1)}, u32[]{:S(2)}, u32[]{:S(2)}) %collective-permute-start.9) | collective-permute-done | bytes 327712 | tf_op jit(solution)/shard_map/ppermute | solution.py:401
  74.3 0.3 merge.1
  74.6 2.8 %collective-permute-start.10 = (bf16[128,640]{1,0:T(8,128)(2,1)S(1)}, bf16[128,640]{1,0:T(8,128)(2,1)S(1)}, u32[]{:S(2)}, u32[]{:S(2)}) collective-permute-start(bf16[128,640]{1,0:T(8,128)(2,1)S(1)} %get-tuple-element.72), channel_id=1, source_target_pairs={{0,16},{16,0},{1,17},{17,1},{2,18},{18,2},{3,19},{19,3},{4,20},{20... | collective-permute-start | bytes 491528 | tf_op jit(solution)/shard_map/ppermute | solution.py:401
  77.4 5.0 %collective-permute-done.10.got_ref = bf16[128,640]{1,0:T(8,128)(2,1)S(1)} collective-permute-done((bf16[128,640]{1,0:T(8,128)(2,1)S(1)}, bf16[128,640]{1,0:T(8,128)(2,1)S(1)}, u32[]{:S(2)}, u32[]{:S(2)}) %collective-permute-start.10) | collective-permute-done | bytes 163872 | tf_op jit(solution)/shard_map/ppermute | solution.py:401
  82.4 1.0 %finish.1 = bf16[128,512]{1,0:T(8,128)(2,1)} custom-call(f32[128,512]{1,0:T(8,128)S(1)} %get-tuple-element.70.mixed_ref, f32[128,128]{1,0:T(8,128)S(1)} %get-tuple-element.71.level_ref, bf16[128,640]{1,0:T(8,128)(2,1)S(1)} %collective-permute-done.10.got_ref, bf16[128,512]{1,0:T(8,128)(2,1)S(1)} %get-tuple-element.73.latent_ref, ...), custom_call_target="tpu_custom_call" | custom-call | flops 70000000 | bytes 4194304 | tf_op jit(solution)/shard_map/finish/pallas_call | solution.py:469
  (22 shorter events, 0.1 us)
Async XLA Ops:
  1.0 7.8 %collective-permute-start = (bf16[2,3,64,128]{3,2,1,0:T(8,128)(2,1)S(1)}, bf16[2,3,64,128]{3,2,1,0:T(8,128)(2,1)S(1)}, u32[]{:S(2)}, u32[]{:S(2)}) collective-permute-start(bf16[2,3,64,128]{3,2,1,0:T(8,128)(2,1)S(1)} %get-tuple-element.76), channel_id=1, source_target_pairs={{8,16},{16,8},{9,17},{17,9},{10,18},{18,10},{11,19},{19,11},{12,20... | collective-permute-start | bytes 294920 | tf_op jit(solution)/shard_map/ppermute | solution.py:401
  1.6 7.2 %collective-permute-start.1 = (bf16[2,3,64,128]{3,2,1,0:T(8,128)(2,1)S(1)}, bf16[2,3,64,128]{3,2,1,0:T(8,128)(2,1)S(1)}, u32[]{:S(2)}, u32[]{:S(2)}) collective-permute-start(bf16[2,3,64,128]{3,2,1,0:T(8,128)(2,1)S(1)} %get-tuple-element.75), channel_id=1, source_target_pairs={{0,8},{8,0},{16,24},{24,16},{1,9},{9,1},{17,25},{25,17},{2,10},{10... | collective-permute-start | bytes 294920 | tf_op jit(solution)/shard_map/ppermute | solution.py:401
  6.1 0.7 copy-start.10
  8.8 4.8 %copy-start.11 = (f32[128]{0:T(128)S(1)}, f32[128]{0:T(128)}, u32[]{:S(2)}) copy-start(f32[128]{0:T(128)} %param.13) | copy-start | bytes 1540
  9.0 4.6 %collective-permute-start.2 = (bf16[2,38,4,128]{3,2,1,0:T(4,128)(2,1)S(1)}, bf16[2,38,4,128]{3,2,1,0:T(4,128)(2,1)S(1)}, u32[]{:S(2)}, u32[]{:S(2)}) collective-permute-start(bf16[2,38,4,128]{3,2,1,0:T(4,128)(2,1)S(1)} %get-tuple-element.82), channel_id=1, source_target_pairs={{0,1},{1,0},{2,3},{3,2},{4,5},{5,4},{6,7},{7,6},{8,9},{9,8},{10,11... | collective-permute-start | bytes 233480 | tf_op jit(solution)/shard_map/ppermute | solution.py:401
  9.7 3.9 %collective-permute-start.3 = (bf16[2,38,4,128]{3,2,1,0:T(4,128)(2,1)S(1)}, bf16[2,38,4,128]{3,2,1,0:T(4,128)(2,1)S(1)}, u32[]{:S(2)}, u32[]{:S(2)}) collective-permute-start(bf16[2,38,4,128]{3,2,1,0:T(4,128)(2,1)S(1)} %get-tuple-element.81), channel_id=1, source_target_pairs={{1,2},{2,1},{3,4},{4,3},{5,6},{6,5},{9,10},{10,9},{11,12},{12,11},... | collective-permute-start | bytes 233480 | tf_op jit(solution)/shard_map/ppermute | solution.py:401
  16.6 8.5 %copy-start.2 = (bf16[2,32,64,128]{3,2,1,0:T(8,128)(2,1)S(1)}, bf16[2,32,64,128]{3,2,1,0:T(8,128)(2,1)}, u32[]{:S(2)}) copy-start(bf16[2,32,64,128]{3,2,1,0:T(8,128)(2,1)} %x_ref.1) | copy-start | bytes 3145732
  16.6 8.5 %copy-start.3 = (bf16[1024,256]{1,0:T(8,128)(2,1)S(1)}, bf16[1024,256]{1,0:T(8,128)(2,1)}, u32[]{:S(2)}) copy-start(bf16[1024,256]{1,0:T(8,128)(2,1)} %down_ref.4) | copy-start | bytes 1572868
  16.6 12.2 %collective-permute-start.4 = (bf16[624,256]{1,0:T(8,128)(2,1)S(1)}, bf16[624,256]{1,0:T(8,128)(2,1)S(1)}, u32[]{:S(2)}, u32[]{:S(2)}) collective-permute-start(bf16[624,256]{1,0:T(8,128)(2,1)S(1)} %get-tuple-element.52), channel_id=1, source_target_pairs={{0,32},{32,64},{64,96},{96,128},{128,160},{160,192},{192,224},{1,3... | collective-permute-start | bytes 958472 | tf_op jit(solution)/shard_map/ppermute | solution.py:434
  25.1 3.7 %copy-start = (bf16[3,3,3,256,256]{4,3,2,1,0:T(8,128)(2,1)S(1)}, bf16[3,3,3,256,256]{4,3,2,1,0:T(8,128)(2,1)}, u32[]{:S(2)}) copy-start(bf16[3,3,3,256,256]{4,3,2,1,0:T(8,128)(2,1)} %param.17) | copy-start | bytes 10616836
  25.1 3.7 %copy-start.1 = (bf16[1024,512]{1,0:T(8,128)(2,1)S(1)}, bf16[1024,512]{1,0:T(8,128)(2,1)}, u32[]{:S(2)}) copy-start(bf16[1024,512]{1,0:T(8,128)(2,1)} %down_ref.7) | copy-start | bytes 3145732
  25.1 3.7 %copy-start.9 = (f32[256]{0:T(256)S(1)}, f32[256]{0:T(256)}, u32[]{:S(2)}) copy-start(f32[256]{0:T(256)} %param.16) | copy-start | bytes 3076
  31.1 9.8 %copy-start.4 = (bf16[512,512]{1,0:T(8,128)(2,1)S(1)}, bf16[512,512]{1,0:T(8,128)(2,1)}, u32[]{:S(2)}) copy-start(bf16[512,512]{1,0:T(8,128)(2,1)} %query_ref.1) | copy-start | bytes 1572868
  31.1 9.8 %copy-start.5 = (bf16[512,512]{1,0:T(8,128)(2,1)S(1)}, bf16[512,512]{1,0:T(8,128)(2,1)}, u32[]{:S(2)}) copy-start(bf16[512,512]{1,0:T(8,128)(2,1)} %key_ref.1) | copy-start | bytes 1572868
  31.1 9.8 %copy-start.6 = (bf16[512,512]{1,0:T(8,128)(2,1)S(1)}, bf16[512,512]{1,0:T(8,128)(2,1)}, u32[]{:S(2)}) copy-start(bf16[512,512]{1,0:T(8,128)(2,1)} %value_ref.1) | copy-start | bytes 1572868
  31.1 9.8 %copy-start.7 = (bf16[512,512]{1,0:T(8,128)(2,1)S(1)}, bf16[512,512]{1,0:T(8,128)(2,1)}, u32[]{:S(2)}) copy-start(bf16[512,512]{1,0:T(8,128)(2,1)} %out_ref.1) | copy-start | bytes 1572868
  32.9 11.4 %collective-permute-start.5 = (bf16[128,512]{1,0:T(8,128)(2,1)S(1)}, bf16[128,512]{1,0:T(8,128)(2,1)S(1)}, u32[]{:S(2)}, u32[]{:S(2)}) collective-permute-start(bf16[128,512]{1,0:T(8,128)(2,1)S(1)} %get-tuple-element.55), channel_id=1, source_target_pairs={{0,32},{32,64},{64,96},{96,128},{128,160},{160,192},{192,224},{1,3... | collective-permute-start | bytes 393224 | tf_op jit(solution)/shard_map/ppermute | solution.py:439
  38.5 8.4 %collective-permute-start.6 = (bf16[128,512]{1,0:T(8,128)(2,1)S(1)}, bf16[128,512]{1,0:T(8,128)(2,1)S(1)}, u32[]{:S(2)}, u32[]{:S(2)}) collective-permute-start(bf16[128,512]{1,0:T(8,128)(2,1)S(1)} %get-tuple-element.56), channel_id=1, source_target_pairs={{0,64},{32,96},{64,128},{96,160},{128,192},{160,224},{1,65},{33,97... | collective-permute-start | bytes 393224 | tf_op jit(solution)/shard_map/ppermute | solution.py:438
  41.7 5.3 %copy-start.8 = (f32[512]{0:T(512)S(1)}, f32[512]{0:T(512)}, u32[]{:S(2)}) copy-start(f32[512]{0:T(512)} %param.19) | copy-start | bytes 6148
  48.4 22.6 %all-to-all-start = ((bf16[8,128,512]{2,1,0:T(8,128)(2,1)}), bf16[8,128,512]{2,1,0:T(8,128)(2,1)S(1)}, u32[]{:S(2)}, u32[]{:S(2)}) async-start(bf16[8,128,512]{2,1,0:T(8,128)(2,1)} %copies.1), calls=%async_computation | async-start | bytes 2097152 | tf_op jit(solution)/shard_map/all_to_all | solution.py:452
  55.3 13.3 %collective-permute-start.7 = (bf16[128,512]{1,0:T(8,128)(2,1)S(1)}, bf16[128,512]{1,0:T(8,128)(2,1)S(1)}, u32[]{:S(2)}, u32[]{:S(2)}) collective-permute-start(bf16[128,512]{1,0:T(8,128)(2,1)S(1)} %get-tuple-element.65), channel_id=1, source_target_pairs={{0,16},{16,0},{1,17},{17,1},{2,18},{18,2},{3,19},{19,3},{4,20},{20... | collective-permute-start | bytes 393224 | tf_op jit(solution)/shard_map/ppermute | solution.py:401
  68.7 1.6 %collective-permute-start.8 = (bf16[256,512]{1,0:T(8,128)(2,1)S(1)}, bf16[256,512]{1,0:T(8,128)(2,1)S(1)}, u32[]{:S(2)}, u32[]{:S(2)}) collective-permute-start(bf16[256,512]{1,0:T(8,128)(2,1)S(1)} %constant_dynamic-update-slice_fusion.mine_ref), channel_id=1, source_target_pairs={{0,8},{8,0},{1,9},{9,1},{2,10},{10,2},{3,11},{11,3},{4,12},{12,4},... | collective-permute-start | bytes 786440 | tf_op jit(solution)/shard_map/ppermute | solution.py:401
  72.5 1.7 %collective-permute-start.9 = (bf16[256,640]{1,0:T(8,128)(2,1)S(1)}, bf16[256,640]{1,0:T(8,128)(2,1)S(1)}, u32[]{:S(2)}, u32[]{:S(2)}) collective-permute-start(bf16[256,640]{1,0:T(8,128)(2,1)S(1)} %get-tuple-element.69), channel_id=1, source_target_pairs={{0,8},{8,0},{1,9},{9,1},{2,10},{10,2},{3,11},{11,3},{4,12},{12,4},... | collective-permute-start | bytes 983048 | tf_op jit(solution)/shard_map/ppermute | solution.py:401
  74.6 7.8 %collective-permute-start.10 = (bf16[128,640]{1,0:T(8,128)(2,1)S(1)}, bf16[128,640]{1,0:T(8,128)(2,1)S(1)}, u32[]{:S(2)}, u32[]{:S(2)}) collective-permute-start(bf16[128,640]{1,0:T(8,128)(2,1)S(1)} %get-tuple-element.72), channel_id=1, source_target_pairs={{0,16},{16,0},{1,17},{17,1},{2,18},{18,2},{3,19},{19,3},{4,20},{20... | collective-permute-start | bytes 491528 | tf_op jit(solution)/shard_map/ppermute | solution.py:401

commit v5 on v4

--- a/solution.py
+++ b/solution.py
@@ -12,7 +12,8 @@
 BF16 = jnp.bfloat16
 F32 = jnp.float32
 HEIGHT = ("hx", "core")
-GATHER = "width"
+WIDTH = ("y", "lx")
+RING = ("hx", "lx")
 VMEM_LIMIT = 32 * 1024 * 1024
 VM = pl.BlockSpec(memory_space=pltpu.VMEM)
 HB = pl.BlockSpec(memory_space=pltpu.HBM)
@@ -110,12 +111,15 @@
 FLAT = 624
 
 
-def prepare_kernel(x_hbm, gain_ref, act_ref, first_ref, last_ref, x, sems):
+def prepare_kernel(x_hbm, gain_hbm, act_ref, first_ref, last_ref, x, gain_ref, sems):
     fetches = []
     for k in range(4):
         rows = pl.ds(k * 8, 8)
         fetches.append(pltpu.make_async_copy(x_hbm.at[:, rows], x.at[:, rows], sems.at[k]))
         fetches[k].start()
+    fetch_gain = pltpu.make_async_copy(gain_hbm, gain_ref, sems.at[4])
+    fetch_gain.start()
+    fetch_gain.wait()
     gain = gain_ref[...].reshape(1, 1, 128)
     for k in range(4):
         fetches[k].wait()
@@ -132,11 +136,11 @@
     return call(
         prepare_kernel,
         (shape((2, 32, 64, 128), F32), edge, edge),
-        [HB, VM],
-        [pltpu.VMEM((2, 32, 64, 128), BF16), pltpu.SemaphoreType.DMA((4,))],
+        [HB, HB],
+        [pltpu.VMEM((2, 32, 64, 128), BF16), pltpu.VMEM((1, 128), F32), pltpu.SemaphoreType.DMA((5,))],
         flops=10_000_000,
         name="prepare",
-    )(kept(features), gain.reshape(1, 128))
+    )(kept(features), kept(gain.reshape(1, 128)))
 
 
 def spread(field, up_ref, low_ref, left_ref, right_ref, change):
@@ -237,15 +241,9 @@
     return jnp.concatenate(parts, -1)
 
 
-def windows(shifted):
-    sides = []
-    for p in range(2):
-        parts = [shifted[p + j, i : i + 16].reshape(256, 256) for i in range(3) for j in range(3)]
-        sides.append(jnp.concatenate(parts, -1))
-    return jnp.concatenate(sides, 0)
-
-
-def far_kernel(flag_ref, own_ref, got_ref, gain_ref, conv_ref, down_ref, far_ref, c0_ref, shifted, reduced, got, act):
+def sent_kernel(
+    flag_ref, own_ref, got_ref, gain_ref, conv_ref, down_ref, far_ref, near_ref, c1_ref, windows, reduced, got, act
+):
     gain = gain_ref[...]
     got[...] = got_ref[...].astype(F32)
     for row in range(18):
@@ -272,33 +270,33 @@
     def _():
         act[:, :, pl.ds(33, 1), :] = jnp.zeros((2, 18, 1, 128), F32)
 
-    def build(row, carry):
+    for row in range(18):
         for v in range(4):
             halves = [act[half, row, pl.ds(v, 16, stride=2), :] for half in range(2)]
-            shifted[v, row] = jnp.concatenate(halves, -1).astype(BF16)
-        return carry
-
-    lax.fori_loop(0, 18, build, 0)
-    c0 = dot(windows(shifted), conv_ref[0].reshape(2304, 256))
-    c0_ref[...] = c0
-    far_ref[...] = dot(folded(c0), down_ref[...]).astype(BF16)
-
-
-def near_kernel(flag_ref, shifted, c0_ref, conv_ref, down_ref, near_ref, c1_ref):
+            cells = jnp.concatenate(halves, -1).astype(BF16)
+            for p in range(2):
+                for i in range(3):
+                    if 0 <= v - p < 3 and 0 <= row - i < 16:
+                        tap = i * 3 + v - p
+                        windows[pl.ds((p * 16 + row - i) * 16, 16), pl.ds(tap * 256, 256)] = cells
     start = (flag_ref[0] == 0).astype(F32)
-    c1 = dot(windows(shifted), conv_ref[1].reshape(2304, 256)) + c0_ref[...] * start
+    lhs = windows[...]
+    c0 = dot(lhs, conv_ref[0].reshape(2304, 256))
+    c1 = dot(lhs, conv_ref[1].reshape(2304, 256)) + c0 * start
     c1_ref[...] = c1
-    near_ref[...] = dot(folded(c1), down_ref[...]).astype(BF16)
-
-
-def here_kernel(flag_ref, shifted, reduced, c1_ref, conv_ref, down_ref, latent_ref):
+    both = dot(jnp.concatenate([folded(c0), folded(c1)], 0), down_ref[...]).astype(BF16)
+    far_ref[...] = both[:128]
+    near_ref[...] = both[128:]
+
+
+def here_kernel(flag_ref, windows, reduced, c1_ref, conv_ref, down_ref, latent_ref):
     start = (flag_ref[0] == 0).astype(F32)
     plain = []
     for p in range(2):
         for row in range(16):
             halves = [reduced[half, row + 1, pl.ds(1 + p, 16, stride=2), :] for half in range(2)]
             plain.append(jnp.concatenate(halves, -1))
-    c2 = dot(windows(shifted), conv_ref[2].reshape(2304, 256)) + c1_ref[...] * start
+    c2 = dot(windows[...], conv_ref[2].reshape(2304, 256)) + c1_ref[...] * start
     latent_ref[...] = dot(folded(c2 + jnp.concatenate(plain, 0)), down_ref[...])
 
 
@@ -306,19 +304,16 @@
     conv = conv.reshape(3, 9, 256, 256)
     rows = shape((128, 512), BF16)
     field = shape((512, 256), F32)
-    far, c0, shifted, reduced = call(
-        far_kernel,
-        (rows, field, shape((4, 18, 16, 256), BF16), shape((2, 18, PITCH, 128), F32)),
+    far, near, c1, windows, reduced = call(
+        sent_kernel,
+        (rows, rows, field, shape((512, 2304), BF16), shape((2, 18, PITCH, 128), F32)),
         [SM] + [VM] * 5,
         [pltpu.VMEM((FLAT, 256), F32), pltpu.VMEM((2, 18, PITCH, 128), F32)],
-        flops=800_000_000,
-        name="coarse_far",
+        flops=1_500_000_000,
+        name="coarse_sent",
     )(flags, own, got, gain.reshape(1, 256), conv, down)
-    near, c1 = call(near_kernel, (rows, field), [SM] + [VM] * 4, flops=1000, moved=1000, name="coarse_near")(
-        flags, shifted, c0, conv, down
-    )
     latent = call(here_kernel, shape((128, 512), F32), [SM] + [VM] * 5, flops=1000, moved=1000, name="coarse_here")(
-        flags, shifted, reduced, c1, conv, down
+        flags, windows, reduced, c1, conv, down
     )
     return near, far, latent
 
@@ -329,68 +324,63 @@
     mix_ref[...] = dot(value_ref[...], out_ref[...]).astype(BF16)
 
 
-def latent_kernel(own_ref, near_ref, far_ref, gain_ref, score_ref, latent_ref, query_ref, normed_ref):
+def latent_kernel(own_ref, near_ref, far_ref, gain_ref, score_ref, latent_ref, query_ref, copies_ref):
     latent = (own_ref[...] + near_ref[...].astype(F32) + far_ref[...].astype(F32)).astype(BF16)
     latent_ref[...] = latent
     normed = scaled(latent.astype(F32), gain_ref[...]).astype(BF16)
-    normed_ref[...] = normed
+    for k in range(copies_ref.shape[0]):
+        copies_ref[k] = normed
     query_ref[...] = dot(normed, score_ref[...]).astype(BF16)
 
 
-def copies_kernel(normed_ref, copies_ref):
-    for k in range(copies_ref.shape[0]):
-        copies_ref[k] = normed_ref[...]
-
-
 def packed(values, level):
-    level = jnp.broadcast_to(level, (level.shape[0], 128))
-    high = level.astype(BF16)
-    rest = level - high.astype(F32)
-    middle = rest.astype(BF16)
-    low = (rest - middle.astype(F32)).astype(BF16)
-    lane = lax.broadcasted_iota(jnp.int32, level.shape, 1)
-    parts = jnp.where(lane == 0, high.astype(F32), jnp.where(lane == 1, middle.astype(F32), low.astype(F32)))
-    return jnp.concatenate([values.astype(BF16), parts.astype(BF16)], -1)
+    across = jnp.broadcast_to(level, (128, 128)).T[:16]
+    high = across.astype(BF16).astype(F32)
+    middle = (across - high).astype(BF16).astype(F32)
+    low = across - high - middle
+    row = lax.broadcasted_iota(jnp.int32, (16, 128), 0)
+    parts = jnp.where(row == 0, high, jnp.where(row == 1, middle, jnp.where(row == 2, low, 0.0)))
+    last = jnp.concatenate([parts, jnp.zeros((16, 384), F32)], -1)
+    return jnp.concatenate([values, last], 0).astype(BF16)
 
 
 def level_of(block):
-    parts = block[:, 512:].astype(F32)
-    lane = lax.broadcasted_iota(jnp.int32, parts.shape, 1)
-    return jnp.sum(jnp.where(lane < 3, parts, 0.0), -1, keepdims=True)
-
-
-def joined(values, level, block):
-    other = level_of(block)
-    top = jnp.maximum(level, other)
-    low = jnp.minimum(level, other)
-    share = jax.nn.sigmoid(level - other)
-    merged = values * share + block[:, :512].astype(F32) * (1.0 - share)
-    return merged, top + jnp.log(1.0 + jnp.exp(low - top))
-
-
-def attend_kernel(mine_ref, theirs_ref, keys_ref, mixed_ref, level_ref, sent_ref):
-    queries = jnp.concatenate([mine_ref[...], theirs_ref[...]], 0)
-    keys = keys_ref[...]
+    across = jnp.sum(block[128:, :128].astype(F32), 0, keepdims=True)
+    return jnp.broadcast_to(across, (128, 128)).T[:, :1]
+
+
+def softmax_part(queries, keys):
     scores = lax.dot_general(queries, keys, (((1,), (1,)), ((), ())), preferred_element_type=F32)
     top = jnp.max(scores, -1, keepdims=True)
     expo = jnp.exp(scores - top)
     total = jnp.sum(expo, -1, keepdims=True)
-    mixed = dot(expo.astype(BF16), keys) / total
-    level = top + jnp.log(total)
-    mixed_ref[...] = mixed[:256]
-    level_ref[...] = jnp.broadcast_to(level[:256], (256, 128))
-    sent_ref[...] = packed(mixed[256:], level[256:])
-
-
-def merge_kernel(mixed_ref, level_ref, got_ref, kept_ref, kept_level_ref, sent_ref):
-    merged, level = joined(mixed_ref[...], level_ref[:, :1], got_ref[...])
-    kept_ref[...] = merged[:128]
-    kept_level_ref[...] = jnp.broadcast_to(level[:128], (128, 128))
-    sent_ref[...] = packed(merged[128:], level[128:])
-
-
-def finish_kernel(mixed_ref, level_ref, got_ref, latent_ref, mix_ref, out_ref):
-    attended, _ = joined(mixed_ref[...], level_ref[:, :1], got_ref[...])
+    return dot(expo.astype(BF16), keys) / total, top + jnp.log(total)
+
+
+def attend_theirs_kernel(q1_ref, q2_ref, q3_ref, keys_ref, other_keys_ref, *sent):
+    queries = jnp.concatenate([q1_ref[...], q2_ref[...], q3_ref[...]], 0)
+    keys = jnp.concatenate([keys_ref[...], other_keys_ref[...]], 0)
+    mixed, level = softmax_part(queries, keys)
+    for k in range(3):
+        rows = slice(128 * k, 128 * (k + 1))
+        sent[k][...] = packed(mixed[rows], level[rows])
+
+
+def attend_mine_kernel(queries_ref, keys_ref, other_keys_ref, mixed_ref, level_ref):
+    keys = jnp.concatenate([keys_ref[...], other_keys_ref[...]], 0)
+    mixed, level = softmax_part(queries_ref[...], keys)
+    mixed_ref[...] = mixed
+    level_ref[...] = jnp.broadcast_to(level, (128, 128))
+
+
+def finish_kernel(mixed_ref, level_ref, got1_ref, got2_ref, got3_ref, latent_ref, mix_ref, out_ref):
+    blocks = [ref[...] for ref in (got1_ref, got2_ref, got3_ref)]
+    levels = [level_ref[:, :1]] + [level_of(block) for block in blocks]
+    values = [mixed_ref[...]] + [block[:128].astype(F32) for block in blocks]
+    top = functools.reduce(jnp.maximum, levels)
+    shares = [jnp.exp(level - top) for level in levels]
+    summed = sum(value * share for value, share in zip(values, shares))
+    attended = summed / sum(shares)
     out_ref[...] = (latent_ref[...].astype(F32) + dot(attended.astype(BF16), mix_ref[...])).astype(BF16)
 
 
@@ -399,6 +389,10 @@
     for low in range(first, count - 1, 2):
         pairs += [(low, low + 1), (low + 1, low)]
     return lax.ppermute(value, axis, pairs)
+
+
+def turned(value, step):
+    return lax.ppermute(value, RING, [(i, (i + step) % 4) for i in range(4)])
 
 
 def sides(block, axis, dim, width, count):
@@ -416,16 +410,17 @@
     features, gain_fine, conv_fine, down_fine, gain_coarse, conv_coarse, down_coarse,
     gain_latent, w_query, w_key, w_value, w_out,
 ):
+    rows = shape((128, 512), BF16)
     tm = lax.axis_index("tm").astype(jnp.int32)
-    flags = jnp.stack([tm, lax.axis_index(HEIGHT).astype(jnp.int32), lax.axis_index("width").astype(jnp.int32)])
+    flags = jnp.stack([tm, lax.axis_index(HEIGHT).astype(jnp.int32), lax.axis_index(WIDTH).astype(jnp.int32)])
     above, below = sides(features, HEIGHT, 1, 3, 4)
     act, first, last = prepare(features, gain_fine)
     above, below, act, first, last = lax.optimization_barrier((above, below, act, first, last))
     first = jnp.concatenate([above[:, :, :4], first, below[:, :, :4]], 1)
     last = jnp.concatenate([above[:, :, 60:], last, below[:, :, 60:]], 1)
-    odd = lax.axis_index("width") % 2 == 1
-    got_inner = swapped(jnp.where(odd, first, last), "width", 8, 0)
-    got_outer = swapped(jnp.where(odd, last, first), "width", 8, 1)
+    odd = lax.axis_index(WIDTH) % 2 == 1
+    got_inner = swapped(jnp.where(odd, first, last), WIDTH, 8, 0)
+    got_outer = swapped(jnp.where(odd, last, first), WIDTH, 8, 1)
     weight_next = compose(False, flags, conv_fine, down_fine)
     got_inner, got_outer, weight_next = lax.optimization_barrier((got_inner, got_outer, weight_next))
     left, right = jnp.where(odd, got_inner, got_outer), jnp.where(odd, got_outer, got_inner)
@@ -434,46 +429,41 @@
     got = lax.ppermute(sent, "tm", [(i, i + 1) for i in range(7)])
     weight_own = compose(True, flags, conv_fine, down_fine)
     own = fine_own(features, halos, weight_own, planes, down_fine)
-    near, far, latent_own = coarse(flags, own, got, gain_coarse, conv_coarse, down_coarse)
-    far = lax.ppermute(far, "tm", [(i, i + 2) for i in range(6)])
-    near = lax.ppermute(near, "tm", [(i, i + 1) for i in range(7)])
     square = shape((512, 512), BF16)
     w_score, w_mix = call(mix_kernel, (square, square), [VM] * 4, flops=1000, moved=1000, name="mix")(
         w_query, w_key, w_value, w_out
     )
-    near, far, latent_own, w_score, w_mix = lax.optimization_barrier((near, far, latent_own, w_score, w_mix))
-    rows = shape((128, 512), BF16)
-    latent_in, query, normed = call(
-        latent_kernel, (rows, rows, rows), [VM] * 5, flops=80_000_000, name="latent"
+    got, own, w_score, w_mix = lax.optimization_barrier((got, own, w_score, w_mix))
+    near, far, latent_own = coarse(flags, own, got, gain_coarse, conv_coarse, down_coarse)
+    far = lax.ppermute(far, "tm", [(i, i + 2) for i in range(6)])
+    near = lax.ppermute(near, "tm", [(i, i + 1) for i in range(7)])
+    near, far, latent_own = lax.optimization_barrier((near, far, latent_own))
+    latent_in, query, copies = call(
+        latent_kernel, (rows, rows, shape((4, 128, 512), BF16)), [VM] * 5, flops=80_000_000, name="latent"
     )(latent_own, near, far, gain_latent.reshape(1, 512), w_score)
-    copies = call(copies_kernel, shape((8, 128, 512), BF16), [VM], name="copies")(normed)
-    queries = jnp.concatenate([query, swapped(query, "hx", 2, 0)], 0)
-    their_queries = swapped(queries, "core", 2, 0)
-    keys = lax.all_to_all(copies, GATHER, 0, 0, tiled=True).reshape(1024, 512)
-    mixed, level, sent = call(
-        attend_kernel,
-        (shape((256, 512), F32), shape((256, 128), F32), shape((256, 640), BF16)),
+    keys = lax.all_to_all(copies, "y", 0, 0, tiled=True).reshape(512, 512)
+    asked = [turned(query, step) for step in (1, 2, 3)]
+    keys, *asked = lax.optimization_barrier((keys, *asked))
+    other_keys = swapped(keys, "core", 2, 0)
+    sent = call(
+        attend_theirs_kernel, (shape((144, 512), BF16),) * 3, [VM] * 5, flops=800_000_000, name="attend_theirs"
+    )(*asked, keys, other_keys)
+    mixed, level = call(
+        attend_mine_kernel,
+        (shape((128, 512), F32), shape((128, 128), F32)),
         [VM] * 3,
-        flops=1_100_000_000,
-        name="attend",
-    )(queries, their_queries, keys)
-    got = swapped(sent, "core", 2, 0)
-    mixed, level, sent = call(
-        merge_kernel,
-        (shape((128, 512), F32), shape((128, 128), F32), shape((128, 640), BF16)),
-        [VM] * 3,
-        flops=1_000_000,
-        name="merge",
-    )(mixed, level, got)
-    got = swapped(sent, "hx", 2, 0)
-    out = call(finish_kernel, rows, [VM] * 5, flops=70_000_000, name="finish")(mixed, level, got, latent_in, w_mix)
+        flops=300_000_000,
+        name="attend_mine",
+    )(query, keys, other_keys)
+    got = [turned(block, -step) for step, block in zip((1, 2, 3), sent)]
+    out = call(finish_kernel, rows, [VM] * 7, flops=70_000_000, name="finish")(mixed, level, *got, latent_in, w_mix)
     return out.reshape(1, 8, 16, 512)
 
 
 def solution(mesh):
-    split = Mesh(mesh.devices.reshape(8, 2, 2, 8), ("tm", "hx", "core", "width"))
-    placed = (P("tm", HEIGHT, "width", None),) + (P(),) * 11
+    split = Mesh(mesh.devices.reshape(8, 2, 2, 4, 2), ("tm", "hx", "core", "y", "lx"))
+    placed = (P("tm", HEIGHT, WIDTH, None),) + (P(),) * 11
     return jax.shard_map(
         per_device, mesh=split, in_specs=placed,
-        out_specs=P("tm", HEIGHT, "width", None), check_vma=False,
+        out_specs=P("tm", HEIGHT, WIDTH, None), check_vma=False,
     )

time: 84.7 us -> 80.5 us (0.950)
  waiting for transfers between devices: 24.3 us -> 19.6 us
  starting transfers between devices: 31.6 us -> 34.9 us
  Pallas kernels: 25.2 us -> 23.6 us
    ppermute x8 -> x5, waiting for transfers between devices: 19.4 us -> 1.92 us  [swapped(): return lax.ppermute(value, axis, pairs)]
    ppermute x0 -> x6, waiting for transfers between devices: none -> 12.7 us  [turned(): return lax.ppermute(value, RING, [(i, (i + step) % 4) for i in range(4)])]
    ppermute x0 -> x6, starting transfers between devices: none -> 8.1 us  [turned(): return lax.ppermute(value, RING, [(i, (i + step) % 4) for i in range(4)])]
    ppermute x8 -> x5, starting transfers between devices: 11.6 us -> 6.47 us  [swapped(): return lax.ppermute(value, axis, pairs)]
    pallas_call x8 -> x6, Pallas kernels: 10.3 us -> 8.8 us  [the longest x1 2.61 us: coarse(): call(sent_kernel, (rows, rows, field, shape((512, 2304), BF16), shape((2,...]
  transfers between devices with their start and end apart: 12 -> 15, of which waited for: 8 -> 9; matrix products, arithmetic and copies ran while one was open for 0% -> 0% of each run, Pallas kernels for 17% -> 18%
where the time goes in v5:
time: 80.5 us; the launch traced here: 79.8 us
  starting transfers between devices  34.9 us (43%)
  Pallas kernels  23.6 us (29%)
  waiting for transfers between devices  19.6 us (24%)
  local copies, waits for them, and re-layouts  1.04 us (1%)
    ppermute x6, waiting for transfers between devices, turned(): return lax.ppermute(value, RING, [(i, (i + step) % 4) for i in range(4)])  12.7 us
    ppermute x6, starting transfers between devices, turned(): return lax.ppermute(value, RING, [(i, (i + step) % 4) for i in range(4)])  8.1 us
    all_to_all x1, starting transfers between devices, per_device(): keys = lax.all_to_all(copies, 'y', 0, 0, tiled=True).reshape(512, 512)  7.38 us
    pallas_call x2, Pallas kernels, compose(): call(functools.partial(compose_kernel, own), shape((16, 256, 256), BF16),...  6.5 us
    ppermute x5, starting transfers between devices, swapped(): return lax.ppermute(value, axis, pairs)  6.47 us
    ppermute x1, starting transfers between devices, per_device(): near = lax.ppermute(near, 'tm', [(i, i + 1) for i in range(7)])  5.61 us
    ppermute x1, starting transfers between devices, per_device(): got = lax.ppermute(sent, 'tm', [(i, i + 1) for i in range(7)])  5.17 us
    ppermute x1, waiting for transfers between devices, per_device(): far = lax.ppermute(far, 'tm', [(i, i + 2) for i in range(6)])  3.12 us
  transfers between devices with their start and end apart: 15, of which 9 were waited for; matrix products, arithmetic and copies ran while one was open for 0% of the time, Pallas kernels for 18%

profile of v5, /device:TPU:96, one launch (start us, length us, event | category | flops | bytes accessed | tf_op | source)
XLA Modules:
  0.0 79.8 jit_solution(8551756647882369286)
XLA Ops:
  0.0 1.0 %constant_dynamic-slice_fusion = (bf16[2,3,64,128]{3,2,1,0:T(8,128)(2,1)S(1)}, bf16[2,3,64,128]{3,2,1,0:T(8,128)(2,1)S(1)}) fusion(bf16[2,32,64,128]{3,2,1,0:T(8,128)(2,1)} %x_ref.1, s32[]{:T(128)S(6)} %select_n.52, s32[]{:T(128)S(6)} %select_n.51), kind=kLoop, calls=%fused_computation.9 | loop fusion | bytes 393224 | tf_op jit(solution)/shard_map/dynamic_slice | solution.py:401
  1.0 0.7 collective-permute-start
  1.6 4.5 %collective-permute-start.1 = (bf16[2,3,64,128]{3,2,1,0:T(8,128)(2,1)S(1)}, bf16[2,3,64,128]{3,2,1,0:T(8,128)(2,1)S(1)}, u32[]{:S(2)}, u32[]{:S(2)}) collective-permute-start(bf16[2,3,64,128]{3,2,1,0:T(8,128)(2,1)S(1)} %get-tuple-element.83), channel_id=1, source_target_pairs={{0,8},{8,0},{16,24},{24,16},{1,9},{9,1},{17,25},{25,17},{2,10},{10... | collective-permute-start | bytes 294920 | tf_op jit(solution)/shard_map/ppermute | solution.py:391
  6.1 2.0 %prepare.1 = (f32[2,32,64,128]{3,2,1,0:T(8,128)S(1)}, bf16[2,32,4,128]{3,2,1,0:T(4,128)(2,1)S(1)}, bf16[2,32,4,128]{3,2,1,0:T(4,128)(2,1)S(1)}) custom-call(bf16[2,32,64,128]{3,2,1,0:T(8,128)(2,1)} %x_ref.1, f32[1,128]{1,0:T(1,128)} %bitcast.24), custom_call_target="tpu_custom_call" | custom-call | flops 10000000 | bytes 4194304 | tf_op jit(solution)/shard_map/prepare/pallas_call | solution.py:136
  8.1 0.0 copy-start.10
  8.1 0.1 pad_add_fusion.flag_ref
  8.2 0.1 broadcast_select_fusion.4
  8.4 0.7 collective-permute-start.2
  9.1 0.7 collective-permute-start.3
  9.7 3.2 %compose_next.1.weight_ref = bf16[16,256,256]{2,1,0:T(8,128)(2,1)S(1)} custom-call(s32[3]{0:T(128)S(1)} %pad_add_fusion.flag_ref, bf16[3,3,3,128,128]{4,3,2,1,0:T(8,128)(2,1)} %conv_hbm.3, bf16[1024,256]{1,0:T(8,128)(2,1)} %down_ref.3), custom_call_target="tpu_custom_call" | custom-call | flops 900000000 | bytes 4194304 | tf_op jit(solution)/shard_map/compose_next/pallas_call | solution.py:94
  13.0 0.0 copy-start.4
  13.0 0.0 copy-start.5
  13.0 0.0 copy-start.6
  13.0 0.0 copy-start.7
  13.1 3.0 %fine_next.1 = (bf16[624,256]{1,0:T(8,128)(2,1)S(1)}, bf16[2,4,19,48,256]{4,3,2,1,0:T(8,128)(2,1)S(1)}) custom-call(f32[2,32,64,128]{3,2,1,0:T(8,128)S(1)} %get-tuple-element.47.act_ref, bf16[2,3,64,128]{3,2,1,0:T(8,128)(2,1)S(1)} %get-tuple-element.48.up_ref, bf16[2,3,64,128]{3,2,1,0:T(8,128)(2,1)S(1)} %get-tuple-element.49.low_ref, ...), custom_call_target="tpu_custom_call" | custom-call | flops 1800000000 | bytes 4194304 | tf_op jit(solution)/shard_map/fine_next/pallas_call | solution.py:217
  16.0 0.0 copy-start.1
  16.0 0.0 copy-start.2
  16.0 5.2 %collective-permute-start.4 = (bf16[624,256]{1,0:T(8,128)(2,1)S(1)}, bf16[624,256]{1,0:T(8,128)(2,1)S(1)}, u32[]{:S(2)}, u32[]{:S(2)}) collective-permute-start(bf16[624,256]{1,0:T(8,128)(2,1)S(1)} %get-tuple-element.55), channel_id=1, source_target_pairs={{0,32},{32,64},{64,96},{96,128},{128,160},{160,192},{192,224},{1,3... | collective-permute-start | bytes 958472 | tf_op jit(solution)/shard_map/ppermute | solution.py:429
  21.2 0.7 mix.1
  22.0 3.3 %compose_own.1.weight_ref = bf16[16,256,256]{2,1,0:T(8,128)(2,1)S(1)} custom-call(s32[3]{0:T(128)S(1)} %pad_add_fusion.flag_ref, bf16[3,3,3,128,128]{4,3,2,1,0:T(8,128)(2,1)} %conv_hbm.3, bf16[1024,256]{1,0:T(8,128)(2,1)} %down_ref.3), custom_call_target="tpu_custom_call" | custom-call | flops 900000000 | bytes 4194304 | tf_op jit(solution)/shard_map/compose_own/pallas_call | solution.py:94
  25.3 0.0 copy-start
  25.3 0.0 copy-start.9
  25.3 2.9 %fine_own.1.own_ref = f32[18,48,256]{2,1,0:T(8,128)S(1)} custom-call(bf16[2,32,64,128]{3,2,1,0:T(8,128)(2,1)S(1)} %copy-done.1, bf16[2,3,64,128]{3,2,1,0:T(8,128)(2,1)S(1)} %get-tuple-element.48.up_ref, bf16[2,3,64,128]{3,2,1,0:T(8,128)(2,1)S(1)} %get-tuple-element.49.low_ref, bf16[2,38,4,128]{3,2,1,0:T(4,128)(2,1)S(1)} %bitcast.21, ...), custom_call_target="tpu_custom_call" | custom-call | flops 2200000000 | bytes 4194304 | tf_op jit(solution)/shard_map/fine_own/pallas_call | solution.py:228
  28.2 0.6 collective-permute-done.4.got_ref
  28.8 2.6 %coarse_sent.1 = (bf16[128,512]{1,0:T(8,128)(2,1)S(1)}, bf16[128,512]{1,0:T(8,128)(2,1)S(1)}, f32[512,256]{1,0:T(8,128)S(1)}, bf16[512,2304]{1,0:T(8,128)(2,1)S(1)}, f32[2,18,48,128]{3,2,1,0:T(8,128)S(1)}) custom-call(s32[3]{0:T(128)S(1)} %pad_add_fusion.flag_ref, f32[18,48,256]{2,1,0:T(8,128)S(1)} %fine_own.1.own_ref, ...), custom_call_target="tpu_custom_call" | custom-call | flops 1500000000 | bytes 4194304 | tf_op jit(solution)/shard_map/coarse_sent/pallas_call | solution.py:307
  31.4 5.6 %collective-permute-start.5 = (bf16[128,512]{1,0:T(8,128)(2,1)S(1)}, bf16[128,512]{1,0:T(8,128)(2,1)S(1)}, u32[]{:S(2)}, u32[]{:S(2)}) collective-permute-start(bf16[128,512]{1,0:T(8,128)(2,1)S(1)} %get-tuple-element.61), channel_id=1, source_target_pairs={{0,32},{32,64},{64,96},{96,128},{128,160},{160,192},{192,224},{1,3... | collective-permute-start | bytes 393224 | tf_op jit(solution)/shard_map/ppermute | solution.py:439
  37.0 2.2 %collective-permute-start.6 = (bf16[128,512]{1,0:T(8,128)(2,1)S(1)}, bf16[128,512]{1,0:T(8,128)(2,1)S(1)}, u32[]{:S(2)}, u32[]{:S(2)}) collective-permute-start(bf16[128,512]{1,0:T(8,128)(2,1)S(1)} %get-tuple-element.62), channel_id=1, source_target_pairs={{0,64},{32,96},{64,128},{96,160},{128,192},{160,224},{1,65},{33,97... | collective-permute-start | bytes 393224 | tf_op jit(solution)/shard_map/ppermute | solution.py:438
  39.2 0.0 copy-start.8
  39.2 1.8 %coarse_here.1.own_ref = f32[128,512]{1,0:T(8,128)S(1)} custom-call(s32[3]{0:T(128)S(1)} %pad_add_fusion.flag_ref, bf16[512,2304]{1,0:T(8,128)(2,1)S(1)} %get-tuple-element.63.windows, f32[2,18,48,128]{3,2,1,0:T(8,128)S(1)} %get-tuple-element.64.reduced, f32[512,256]{1,0:T(8,128)S(1)} %get-tuple-element.65.c1_ref, bf16[3,9,256,256]{3,2,1,0:T(8,128)(2,1)S(1)} %bitcast.14, ...), custom_call_target="tpu_custom_call" | custom-call | flops 1000 | bytes 1000 | tf_op jit(solution)/shard_map/coarse_here/pallas_call | solution.py:315
  41.0 1.4 %collective-permute-done.5.near_ref = bf16[128,512]{1,0:T(8,128)(2,1)S(1)} collective-permute-done((bf16[128,512]{1,0:T(8,128)(2,1)S(1)}, bf16[128,512]{1,0:T(8,128)(2,1)S(1)}, u32[]{:S(2)}, u32[]{:S(2)}) %collective-permute-start.5) | collective-permute-done | bytes 131104 | tf_op jit(solution)/shard_map/ppermute | solution.py:439
  42.4 3.1 %collective-permute-done.6.far_ref = bf16[128,512]{1,0:T(8,128)(2,1)S(1)} collective-permute-done((bf16[128,512]{1,0:T(8,128)(2,1)S(1)}, bf16[128,512]{1,0:T(8,128)(2,1)S(1)}, u32[]{:S(2)}, u32[]{:S(2)}) %collective-permute-start.6) | collective-permute-done | bytes 131104 | tf_op jit(solution)/shard_map/ppermute | solution.py:438
  45.5 1.0 %latent.1 = (bf16[128,512]{1,0:T(8,128)(2,1)S(1)}, bf16[128,512]{1,0:T(8,128)(2,1)S(1)}, bf16[4,128,512]{2,1,0:T(8,128)(2,1)}) custom-call(f32[128,512]{1,0:T(8,128)S(1)} %coarse_here.1.own_ref, bf16[128,512]{1,0:T(8,128)(2,1)S(1)} %collective-permute-done.5.near_ref, bf16[128,512]{1,0:T(8,128)(2,1)S(1)} %collective-permute-done.6.far_ref, ...), custom_call_target="tpu_custom_call" | custom-call | flops 80000000 | bytes 4194304 | tf_op jit(solution)/shard_map/latent/pallas_call | solution.py:441
  46.5 7.4 %all-to-all-start = ((bf16[4,128,512]{2,1,0:T(8,128)(2,1)}), bf16[4,128,512]{2,1,0:T(8,128)(2,1)S(1)}, u32[]{:S(2)}, u32[]{:S(2)}) async-start(bf16[4,128,512]{2,1,0:T(8,128)(2,1)} %get-tuple-element.71), calls=%async_computation | async-start | bytes 1048576 | tf_op jit(solution)/shard_map/all_to_all | solution.py:444
  53.9 0.8 collective-permute-start.7
  54.7 1.8 %collective-permute-start.8 = (bf16[128,512]{1,0:T(8,128)(2,1)S(1)}, bf16[128,512]{1,0:T(8,128)(2,1)S(1)}, u32[]{:S(2)}, u32[]{:S(2)}) collective-permute-start(bf16[128,512]{1,0:T(8,128)(2,1)S(1)} %get-tuple-element.70.queries_ref), channel_id=1, source_target_pairs={{0,16},{1,17},{16,0},{17,1},{2,18},{3,19},{18,2},{19,3},{4,20},{5,... | collective-permute-start | bytes 393224 | tf_op jit(solution)/shard_map/ppermute | solution.py:395
  56.5 1.8 %collective-permute-start.9 = (bf16[128,512]{1,0:T(8,128)(2,1)S(1)}, bf16[128,512]{1,0:T(8,128)(2,1)S(1)}, u32[]{:S(2)}, u32[]{:S(2)}) collective-permute-start(bf16[128,512]{1,0:T(8,128)(2,1)S(1)} %get-tuple-element.70.queries_ref), channel_id=1, source_target_pairs={{0,17},{1,0},{16,1},{17,16},{2,19},{3,2},{18,3},{19,18},{4,21},{5,... | collective-permute-start | bytes 393224 | tf_op jit(solution)/shard_map/ppermute | solution.py:395
  58.3 3.9 %collective-permute-done.7.q1_ref = bf16[128,512]{1,0:T(8,128)(2,1)S(1)} collective-permute-done((bf16[128,512]{1,0:T(8,128)(2,1)S(1)}, bf16[128,512]{1,0:T(8,128)(2,1)S(1)}, u32[]{:S(2)}, u32[]{:S(2)}) %collective-permute-start.7) | collective-permute-done | bytes 131104 | tf_op jit(solution)/shard_map/ppermute | solution.py:395
  62.2 0.6 collective-permute-done.9.q3_ref
  62.8 1.9 %collective-permute-done.10.other_keys_ref = bf16[512,512]{1,0:T(8,128)(2,1)S(1)} collective-permute-done((bf16[512,512]{1,0:T(8,128)(2,1)S(1)}, bf16[512,512]{1,0:T(8,128)(2,1)S(1)}, u32[]{:S(2)}, u32[]{:S(2)}) %collective-permute-start.10) | collective-permute-done | bytes 524320 | tf_op jit(solution)/shard_map/ppermute | solution.py:391
  64.7 1.2 %attend_theirs.1 = (bf16[144,512]{1,0:T(8,128)(2,1)S(1)}, bf16[144,512]{1,0:T(8,128)(2,1)S(1)}, bf16[144,512]{1,0:T(8,128)(2,1)S(1)}) custom-call(bf16[128,512]{1,0:T(8,128)(2,1)S(1)} %collective-permute-done.7.q1_ref, bf16[128,512]{1,0:T(8,128)(2,1)S(1)} %collective-permute-done.8.q2_ref, bf16[128,512]{1,0:T(8,128)(2,1)S(1)} %collective-permute-done.9.q3_ref, ...), custom_call_target="tpu_custom_call" | custom-call | flops 800000000 | bytes 4194304 | tf_op jit(solution)/shard_map/attend_theirs/pallas_call | solution.py:448
  65.9 2.7 %collective-permute-start.11 = (bf16[144,512]{1,0:T(8,128)(2,1)S(1)}, bf16[144,512]{1,0:T(8,128)(2,1)S(1)}, u32[]{:S(2)}, u32[]{:S(2)}) collective-permute-start(bf16[144,512]{1,0:T(8,128)(2,1)S(1)} %get-tuple-element.78), channel_id=1, source_target_pairs={{0,17},{1,0},{16,1},{17,16},{2,19},{3,2},{18,3},{19,18},{4,21},{5,... | collective-permute-start | bytes 442376 | tf_op jit(solution)/shard_map/ppermute | solution.py:395
  68.7 0.1 collective-permute-start.12
  68.8 0.8 %collective-permute-start.13 = (bf16[144,512]{1,0:T(8,128)(2,1)S(1)}, bf16[144,512]{1,0:T(8,128)(2,1)S(1)}, u32[]{:S(2)}, u32[]{:S(2)}) collective-permute-start(bf16[144,512]{1,0:T(8,128)(2,1)S(1)} %get-tuple-element.80), channel_id=1, source_target_pairs={{0,1},{1,16},{16,17},{17,0},{2,3},{3,18},{18,19},{19,2},{4,5},{5,2... | collective-permute-start | bytes 442376 | tf_op jit(solution)/shard_map/ppermute | solution.py:395
  69.6 0.8 %attend_mine.1 = (f32[128,512]{1,0:T(8,128)S(1)}, f32[128,128]{1,0:T(8,128)S(1)}) custom-call(bf16[128,512]{1,0:T(8,128)(2,1)S(1)} %get-tuple-element.70.queries_ref, bf16[512,512]{1,0:T(8,128)(2,1)S(1)} %bitcast.17, bf16[512,512]{1,0:T(8,128)(2,1)S(1)} %collective-permute-done.10.other_keys_ref), custom_call_target="tpu_custom_call" | custom-call | flops 300000000 | bytes 4194304 | tf_op jit(solution)/shard_map/attend_mine/pallas_call | solution.py:451
  70.5 4.8 %collective-permute-done.11.got1_ref = bf16[144,512]{1,0:T(8,128)(2,1)S(1)} collective-permute-done((bf16[144,512]{1,0:T(8,128)(2,1)S(1)}, bf16[144,512]{1,0:T(8,128)(2,1)S(1)}, u32[]{:S(2)}, u32[]{:S(2)}) %collective-permute-start.11) | collective-permute-done | bytes 147488 | tf_op jit(solution)/shard_map/ppermute | solution.py:395
  75.3 1.6 %collective-permute-done.12.got2_ref = bf16[144,512]{1,0:T(8,128)(2,1)S(1)} collective-permute-done((bf16[144,512]{1,0:T(8,128)(2,1)S(1)}, bf16[144,512]{1,0:T(8,128)(2,1)S(1)}, u32[]{:S(2)}, u32[]{:S(2)}) %collective-permute-start.12) | collective-permute-done | bytes 147488 | tf_op jit(solution)/shard_map/ppermute | solution.py:395
  76.9 1.7 %collective-permute-done.13.got3_ref = bf16[144,512]{1,0:T(8,128)(2,1)S(1)} collective-permute-done((bf16[144,512]{1,0:T(8,128)(2,1)S(1)}, bf16[144,512]{1,0:T(8,128)(2,1)S(1)}, u32[]{:S(2)}, u32[]{:S(2)}) %collective-permute-start.13) | collective-permute-done | bytes 147488 | tf_op jit(solution)/shard_map/ppermute | solution.py:395
  78.7 1.1 %finish.1 = bf16[128,512]{1,0:T(8,128)(2,1)} custom-call(f32[128,512]{1,0:T(8,128)S(1)} %get-tuple-element.73.mixed_ref, f32[128,128]{1,0:T(8,128)S(1)} %get-tuple-element.74.level_ref, bf16[144,512]{1,0:T(8,128)(2,1)S(1)} %collective-permute-done.11.got1_ref, bf16[144,512]{1,0:T(8,128)(2,1)S(1)} %collective-permute-done.12.got2_ref, ...), custom_call_target="tpu_custom_call" | custom-call | flops 70000000 | bytes 4194304 | tf_op jit(solution)/shard_map/finish/pallas_call | solution.py:459
  (22 shorter events, 0.1 us)
Async XLA Ops:
  1.0 7.2 %collective-permute-start = (bf16[2,3,64,128]{3,2,1,0:T(8,128)(2,1)S(1)}, bf16[2,3,64,128]{3,2,1,0:T(8,128)(2,1)S(1)}, u32[]{:S(2)}, u32[]{:S(2)}) collective-permute-start(bf16[2,3,64,128]{3,2,1,0:T(8,128)(2,1)S(1)} %get-tuple-element.84), channel_id=1, source_target_pairs={{8,16},{16,8},{9,17},{17,9},{10,18},{18,10},{11,19},{19,11},{12,20... | collective-permute-start | bytes 294920 | tf_op jit(solution)/shard_map/ppermute | solution.py:391
  1.6 6.6 %collective-permute-start.1 = (bf16[2,3,64,128]{3,2,1,0:T(8,128)(2,1)S(1)}, bf16[2,3,64,128]{3,2,1,0:T(8,128)(2,1)S(1)}, u32[]{:S(2)}, u32[]{:S(2)}) collective-permute-start(bf16[2,3,64,128]{3,2,1,0:T(8,128)(2,1)S(1)} %get-tuple-element.83), channel_id=1, source_target_pairs={{0,8},{8,0},{16,24},{24,16},{1,9},{9,1},{17,25},{25,17},{2,10},{10... | collective-permute-start | bytes 294920 | tf_op jit(solution)/shard_map/ppermute | solution.py:391
  8.1 4.9 %copy-start.10 = (f32[128]{0:T(128)S(1)}, f32[128]{0:T(128)}, u32[]{:S(2)}) copy-start(f32[128]{0:T(128)} %param.13) | copy-start | bytes 1540
  8.4 4.6 %collective-permute-start.2 = (bf16[2,38,4,128]{3,2,1,0:T(4,128)(2,1)S(1)}, bf16[2,38,4,128]{3,2,1,0:T(4,128)(2,1)S(1)}, u32[]{:S(2)}, u32[]{:S(2)}) collective-permute-start(bf16[2,38,4,128]{3,2,1,0:T(4,128)(2,1)S(1)} %get-tuple-element.90), channel_id=1, source_target_pairs={{0,1},{1,0},{2,3},{3,2},{4,5},{5,4},{6,7},{7,6},{8,9},{9,8},{10,11... | collective-permute-start | bytes 233480 | tf_op jit(solution)/shard_map/ppermute | solution.py:391
  9.1 3.9 %collective-permute-start.3 = (bf16[2,38,4,128]{3,2,1,0:T(4,128)(2,1)S(1)}, bf16[2,38,4,128]{3,2,1,0:T(4,128)(2,1)S(1)}, u32[]{:S(2)}, u32[]{:S(2)}) collective-permute-start(bf16[2,38,4,128]{3,2,1,0:T(4,128)(2,1)S(1)} %get-tuple-element.89), channel_id=1, source_target_pairs={{1,2},{2,1},{3,4},{4,3},{5,6},{6,5},{9,10},{10,9},{11,12},{12,11},... | collective-permute-start | bytes 233480 | tf_op jit(solution)/shard_map/ppermute | solution.py:391
  13.0 8.2 %copy-start.4 = (bf16[512,512]{1,0:T(8,128)(2,1)S(1)}, bf16[512,512]{1,0:T(8,128)(2,1)}, u32[]{:S(2)}) copy-start(bf16[512,512]{1,0:T(8,128)(2,1)} %query_ref.1) | copy-start | bytes 1572868
  13.0 8.2 %copy-start.5 = (bf16[512,512]{1,0:T(8,128)(2,1)S(1)}, bf16[512,512]{1,0:T(8,128)(2,1)}, u32[]{:S(2)}) copy-start(bf16[512,512]{1,0:T(8,128)(2,1)} %key_ref.1) | copy-start | bytes 1572868
  13.0 8.2 %copy-start.6 = (bf16[512,512]{1,0:T(8,128)(2,1)S(1)}, bf16[512,512]{1,0:T(8,128)(2,1)}, u32[]{:S(2)}) copy-start(bf16[512,512]{1,0:T(8,128)(2,1)} %value_ref.1) | copy-start | bytes 1572868
  13.0 8.2 %copy-start.7 = (bf16[512,512]{1,0:T(8,128)(2,1)S(1)}, bf16[512,512]{1,0:T(8,128)(2,1)}, u32[]{:S(2)}) copy-start(bf16[512,512]{1,0:T(8,128)(2,1)} %out_ref.1) | copy-start | bytes 1572868
  16.0 9.3 %copy-start.1 = (bf16[2,32,64,128]{3,2,1,0:T(8,128)(2,1)S(1)}, bf16[2,32,64,128]{3,2,1,0:T(8,128)(2,1)}, u32[]{:S(2)}) copy-start(bf16[2,32,64,128]{3,2,1,0:T(8,128)(2,1)} %x_ref.1) | copy-start | bytes 3145732
  16.0 9.3 %copy-start.2 = (bf16[1024,256]{1,0:T(8,128)(2,1)S(1)}, bf16[1024,256]{1,0:T(8,128)(2,1)}, u32[]{:S(2)}) copy-start(bf16[1024,256]{1,0:T(8,128)(2,1)} %down_ref.3) | copy-start | bytes 1572868
  16.0 12.8 %collective-permute-start.4 = (bf16[624,256]{1,0:T(8,128)(2,1)S(1)}, bf16[624,256]{1,0:T(8,128)(2,1)S(1)}, u32[]{:S(2)}, u32[]{:S(2)}) collective-permute-start(bf16[624,256]{1,0:T(8,128)(2,1)S(1)} %get-tuple-element.55), channel_id=1, source_target_pairs={{0,32},{32,64},{64,96},{96,128},{128,160},{160,192},{192,224},{1,3... | collective-permute-start | bytes 958472 | tf_op jit(solution)/shard_map/ppermute | solution.py:429
  25.3 3.5 %copy-start = (bf16[3,3,3,256,256]{4,3,2,1,0:T(8,128)(2,1)S(1)}, bf16[3,3,3,256,256]{4,3,2,1,0:T(8,128)(2,1)}, u32[]{:S(2)}) copy-start(bf16[3,3,3,256,256]{4,3,2,1,0:T(8,128)(2,1)} %param.17) | copy-start | bytes 10616836
  25.3 3.5 %copy-start.3 = (bf16[1024,512]{1,0:T(8,128)(2,1)S(1)}, bf16[1024,512]{1,0:T(8,128)(2,1)}, u32[]{:S(2)}) copy-start(bf16[1024,512]{1,0:T(8,128)(2,1)} %down_ref.5) | copy-start | bytes 3145732
  25.3 3.5 %copy-start.9 = (f32[256]{0:T(256)S(1)}, f32[256]{0:T(256)}, u32[]{:S(2)}) copy-start(f32[256]{0:T(256)} %param.16) | copy-start | bytes 3076
  31.4 10.9 %collective-permute-start.5 = (bf16[128,512]{1,0:T(8,128)(2,1)S(1)}, bf16[128,512]{1,0:T(8,128)(2,1)S(1)}, u32[]{:S(2)}, u32[]{:S(2)}) collective-permute-start(bf16[128,512]{1,0:T(8,128)(2,1)S(1)} %get-tuple-element.61), channel_id=1, source_target_pairs={{0,32},{32,64},{64,96},{96,128},{128,160},{160,192},{192,224},{1,3... | collective-permute-start | bytes 393224 | tf_op jit(solution)/shard_map/ppermute | solution.py:439
  37.0 8.4 %collective-permute-start.6 = (bf16[128,512]{1,0:T(8,128)(2,1)S(1)}, bf16[128,512]{1,0:T(8,128)(2,1)S(1)}, u32[]{:S(2)}, u32[]{:S(2)}) collective-permute-start(bf16[128,512]{1,0:T(8,128)(2,1)S(1)} %get-tuple-element.62), channel_id=1, source_target_pairs={{0,64},{32,96},{64,128},{96,160},{128,192},{160,224},{1,65},{33,97... | collective-permute-start | bytes 393224 | tf_op jit(solution)/shard_map/ppermute | solution.py:438
  39.2 6.3 %copy-start.8 = (f32[512]{0:T(512)S(1)}, f32[512]{0:T(512)}, u32[]{:S(2)}) copy-start(f32[512]{0:T(512)} %param.19) | copy-start | bytes 6148
  46.5 16.3 %all-to-all-start = ((bf16[4,128,512]{2,1,0:T(8,128)(2,1)}), bf16[4,128,512]{2,1,0:T(8,128)(2,1)S(1)}, u32[]{:S(2)}, u32[]{:S(2)}) async-start(bf16[4,128,512]{2,1,0:T(8,128)(2,1)} %get-tuple-element.71), calls=%async_computation | async-start | bytes 1048576 | tf_op jit(solution)/shard_map/all_to_all | solution.py:444
  53.9 8.3 %collective-permute-start.7 = (bf16[128,512]{1,0:T(8,128)(2,1)S(1)}, bf16[128,512]{1,0:T(8,128)(2,1)S(1)}, u32[]{:S(2)}, u32[]{:S(2)}) collective-permute-start(bf16[128,512]{1,0:T(8,128)(2,1)S(1)} %get-tuple-element.70.queries_ref), channel_id=1, source_target_pairs={{0,1},{1,16},{16,17},{17,0},{2,3},{3,18},{18,19},{19,2},{4,5},{5,2... | collective-permute-start | bytes 393224 | tf_op jit(solution)/shard_map/ppermute | solution.py:395
  54.7 7.5 %collective-permute-start.8 = (bf16[128,512]{1,0:T(8,128)(2,1)S(1)}, bf16[128,512]{1,0:T(8,128)(2,1)S(1)}, u32[]{:S(2)}, u32[]{:S(2)}) collective-permute-start(bf16[128,512]{1,0:T(8,128)(2,1)S(1)} %get-tuple-element.70.queries_ref), channel_id=1, source_target_pairs={{0,16},{1,17},{16,0},{17,1},{2,18},{3,19},{18,2},{19,3},{4,20},{5,... | collective-permute-start | bytes 393224 | tf_op jit(solution)/shard_map/ppermute | solution.py:395
  56.5 6.3 %collective-permute-start.9 = (bf16[128,512]{1,0:T(8,128)(2,1)S(1)}, bf16[128,512]{1,0:T(8,128)(2,1)S(1)}, u32[]{:S(2)}, u32[]{:S(2)}) collective-permute-start(bf16[128,512]{1,0:T(8,128)(2,1)S(1)} %get-tuple-element.70.queries_ref), channel_id=1, source_target_pairs={{0,17},{1,0},{16,1},{17,16},{2,19},{3,2},{18,3},{19,18},{4,21},{5,... | collective-permute-start | bytes 393224 | tf_op jit(solution)/shard_map/ppermute | solution.py:395
  62.8 1.9 %collective-permute-start.10 = (bf16[512,512]{1,0:T(8,128)(2,1)S(1)}, bf16[512,512]{1,0:T(8,128)(2,1)S(1)}, u32[]{:S(2)}, u32[]{:S(2)}) collective-permute-start(bf16[512,512]{1,0:T(8,128)(2,1)S(1)} %bitcast.15), channel_id=1, source_target_pairs={{0,8},{8,0},{1,9},{9,1},{2,10},{10,2},{3,11},{11,3},{4,12},{12,4},... | collective-permute-start | bytes 1572872 | tf_op jit(solution)/shard_map/ppermute | solution.py:391
  65.9 9.3 %collective-permute-start.11 = (bf16[144,512]{1,0:T(8,128)(2,1)S(1)}, bf16[144,512]{1,0:T(8,128)(2,1)S(1)}, u32[]{:S(2)}, u32[]{:S(2)}) collective-permute-start(bf16[144,512]{1,0:T(8,128)(2,1)S(1)} %get-tuple-element.78), channel_id=1, source_target_pairs={{0,17},{1,0},{16,1},{17,16},{2,19},{3,2},{18,3},{19,18},{4,21},{5,... | collective-permute-start | bytes 442376 | tf_op jit(solution)/shard_map/ppermute | solution.py:395
  68.7 8.2 %collective-permute-start.12 = (bf16[144,512]{1,0:T(8,128)(2,1)S(1)}, bf16[144,512]{1,0:T(8,128)(2,1)S(1)}, u32[]{:S(2)}, u32[]{:S(2)}) collective-permute-start(bf16[144,512]{1,0:T(8,128)(2,1)S(1)} %get-tuple-element.79), channel_id=1, source_target_pairs={{0,16},{1,17},{16,0},{17,1},{2,18},{3,19},{18,2},{19,3},{4,20},{5,... | collective-permute-start | bytes 442376 | tf_op jit(solution)/shard_map/ppermute | solution.py:395
  68.8 9.9 %collective-permute-start.13 = (bf16[144,512]{1,0:T(8,128)(2,1)S(1)}, bf16[144,512]{1,0:T(8,128)(2,1)S(1)}, u32[]{:S(2)}, u32[]{:S(2)}) collective-permute-start(bf16[144,512]{1,0:T(8,128)(2,1)S(1)} %get-tuple-element.80), channel_id=1, source_target_pairs={{0,1},{1,16},{16,17},{17,0},{2,3},{3,18},{18,19},{19,2},{4,5},{5,2... | collective-permute-start | bytes 442376 | tf_op jit(solution)/shard_map/ppermute | solution.py:395

commit v6 on v5

--- a/solution.py
+++ b/solution.py
@@ -54,19 +54,10 @@
     return values * jax.nn.sigmoid(values)
 
 
-def compose_kernel(own, flag_ref, conv_hbm, down_hbm, out_ref, acc, conv, down, sems):
-    taps = 3 if own else 2
-    fetch_down = pltpu.make_async_copy(down_hbm, down, sems.at[3])
-    fetch_down.start()
-    fetches = []
-    for i in range(3):
-        fetches.append(pltpu.make_async_copy(conv_hbm.at[pl.ds(0, taps), i], conv.at[pl.ds(0, taps), i], sems.at[i]))
-        fetches[i].start()
+def compose_kernel(own, flag_ref, conv, down, out_ref, acc):
     acc[...] = jnp.zeros_like(acc)
     start = flag_ref[0] == 0
-    fetch_down.wait()
     for i in range(3):
-        fetches[i].wait()
         k0, k1 = (conv[s, i].reshape(384, 128) for s in range(2))
         if own:
             k2 = conv[2, i].reshape(384, 128)
@@ -94,16 +85,11 @@
     return call(
         functools.partial(compose_kernel, own),
         shape((16, 256, 256), BF16),
-        [SM, HB, HB],
-        [
-            pltpu.VMEM((16, 256, 256), F32),
-            pltpu.VMEM((3, 3, 3, 128, 128), BF16),
-            pltpu.VMEM((1024, 256), BF16),
-            pltpu.SemaphoreType.DMA((4,)),
-        ],
+        [SM, VM, VM],
+        [pltpu.VMEM((16, 256, 256), F32)],
         flops=900_000_000,
         name="compose_own" if own else "compose_next",
-    )(tm, kept(conv_fine.reshape(3, 3, 3, 128, 128)), kept(down_fine))
+    )(tm, conv_fine, down_fine)
 
 
 COLS = 104
@@ -111,7 +97,19 @@
 FLAT = 624
 
 
-def prepare_kernel(x_hbm, gain_hbm, act_ref, first_ref, last_ref, x, gain_ref, sems):
+def edges_kernel(odd_ref, x_hbm, inner_ref, outer_ref, sems):
+    odd = odd_ref[0]
+    inner = pltpu.make_async_copy(x_hbm.at[:, pl.ds((1 - odd) * 29, 3)], inner_ref, sems.at[0])
+    outer = pltpu.make_async_copy(x_hbm.at[:, pl.ds(odd * 29, 3)], outer_ref, sems.at[1])
+    inner.start()
+    outer.start()
+    inner.wait()
+    outer.wait()
+
+
+def prepare_kernel(
+    x_hbm, gain_hbm, conv_hbm, down_hbm, act_ref, first_ref, last_ref, conv_ref, down_ref, x, gain_ref, sems
+):
     fetches = []
     for k in range(4):
         rows = pl.ds(k * 8, 8)
@@ -119,6 +117,9 @@
         fetches[k].start()
     fetch_gain = pltpu.make_async_copy(gain_hbm, gain_ref, sems.at[4])
     fetch_gain.start()
+    weights = [pltpu.make_async_copy(conv_hbm, conv_ref, sems.at[5]), pltpu.make_async_copy(down_hbm, down_ref, sems.at[6])]
+    for fetch in weights:
+        fetch.start()
     fetch_gain.wait()
     gain = gain_ref[...].reshape(1, 1, 128)
     for k in range(4):
@@ -129,18 +130,20 @@
                 act_ref[f, rows] = silu(scaled(x[f, rows].astype(F32), gain))
     first_ref[...] = x[:, :, 0:4]
     last_ref[...] = x[:, :, 60:64]
-
-
-def prepare(features, gain):
+    for fetch in weights:
+        fetch.wait()
+
+
+def prepare(features, gain, conv, down):
     edge = shape((2, 32, 4, 128), BF16)
     return call(
         prepare_kernel,
-        (shape((2, 32, 64, 128), F32), edge, edge),
-        [HB, HB],
-        [pltpu.VMEM((2, 32, 64, 128), BF16), pltpu.VMEM((1, 128), F32), pltpu.SemaphoreType.DMA((5,))],
+        (shape((2, 32, 64, 128), F32), edge, edge, shape((3, 3, 3, 128, 128), BF16), shape((1024, 256), BF16)),
+        [HB] * 4,
+        [pltpu.VMEM((2, 32, 64, 128), BF16), pltpu.VMEM((1, 128), F32), pltpu.SemaphoreType.DMA((7,))],
         flops=10_000_000,
         name="prepare",
-    )(kept(features), kept(gain.reshape(1, 128)))
+    )(kept(features), kept(gain.reshape(1, 128)), kept(conv.reshape(3, 3, 3, 128, 128)), kept(down))
 
 
 def spread(field, up_ref, low_ref, left_ref, right_ref, change):
@@ -159,15 +162,17 @@
     spread(act, up_ref, low_ref, left_ref, right_ref, lambda values: silu(scaled(values, gain)))
     act[:, pl.ds(3, 32), pl.ds(8, 64), :] = act_ref[...]
 
-    def build(q, carry):
+    def build(q):
         for rp in range(2):
             for v in range(4):
                 both = [act[f, 2 * q + rp, pl.ds(5 + v, 40, stride=2), :].astype(BF16) for f in range(2)]
                 planes[rp, v, q, pl.ds(0, 40), :] = jnp.concatenate(both, -1)
-        return carry
-
-    lax.fori_loop(0, 19, build, 0)
+
+    built = 0
     for base in range(0, 18, GROUP):
+        while built < base + GROUP + 1:
+            build(built)
+            built += 1
         total = dot(taps_at(planes, base), weight_ref[...].reshape(4096, 256)).reshape(GROUP, PITCH, 256)
         for k in range(GROUP):
             flat[pl.ds((base + k) * 34, 34), :] = total[k, :34]
@@ -187,14 +192,12 @@
     spread(raw, up_ref, low_ref, left_ref, right_ref, lambda values: values)
     raw[:, pl.ds(3, 32), pl.ds(8, 64), :] = x_ref[...].astype(F32)
 
-    def build(q, carry):
+    def build(q):
         for rp in range(2):
             for v in range(2):
                 both = [raw[f, 2 * q + rp, pl.ds(6 + v, 40, stride=2), :].astype(BF16) for f in range(2)]
                 raw_planes[rp, v, q, pl.ds(0, 40), :] = jnp.concatenate(both, -1)
-        return carry
-
-    lax.fori_loop(0, 19, build, 0)
+
     folds = []
     for r in range(2):
         for c in range(2):
@@ -202,7 +205,11 @@
                 at = (f * 4 + r * 2 + c) * 128
                 folds.append(down_ref[at : at + 128, :])
     fold_weight = jnp.concatenate(folds, 0)
+    built = 0
     for base in range(0, 18, GROUP):
+        while built < base + GROUP + 1:
+            build(built)
+            built += 1
         parts = []
         for r in range(2):
             for c in range(2):
@@ -236,8 +243,8 @@
 
 
 def folded(field):
-    field = field.astype(BF16).reshape(2, 8, 2, 16, 256)
-    parts = [field[p, :, r].reshape(128, 256) for r in range(2) for p in range(2)]
+    field = field.astype(BF16).reshape(2, 2, 4, 2, 16, 256)
+    parts = [field[:, p, :, r].reshape(128, 256) for r in range(2) for p in range(2)]
     return jnp.concatenate(parts, -1)
 
 
@@ -246,43 +253,37 @@
 ):
     gain = gain_ref[...]
     got[...] = got_ref[...].astype(F32)
-    for row in range(18):
-        value = own_ref[row, pl.ds(0, 40), :] + got[pl.ds(row * 34, 40), :]
-        value = value.astype(BF16).astype(F32)
-        active = silu(scaled(value, gain))
-        for half in range(2):
-            reduced[half, row, pl.ds(0, 40), :] = value[:, half * 128 : half * 128 + 128]
-            act[half, row, pl.ds(0, 40), :] = active[:, half * 128 : half * 128 + 128]
-
-    @pl.when(flag_ref[1] == 0)
-    def _():
-        act[:, 0] = jnp.zeros((2, PITCH, 128), F32)
-
-    @pl.when(flag_ref[1] == 3)
-    def _():
-        act[:, 17] = jnp.zeros((2, PITCH, 128), F32)
-
-    @pl.when(flag_ref[2] == 0)
-    def _():
-        act[:, :, pl.ds(0, 1), :] = jnp.zeros((2, 18, 1, 128), F32)
-
-    @pl.when(flag_ref[2] == 7)
-    def _():
-        act[:, :, pl.ds(33, 1), :] = jnp.zeros((2, 18, 1, 128), F32)
-
-    for row in range(18):
-        for v in range(4):
-            halves = [act[half, row, pl.ds(v, 16, stride=2), :] for half in range(2)]
-            cells = jnp.concatenate(halves, -1).astype(BF16)
-            for p in range(2):
-                for i in range(3):
-                    if 0 <= v - p < 3 and 0 <= row - i < 16:
-                        tap = i * 3 + v - p
-                        windows[pl.ds((p * 16 + row - i) * 16, 16), pl.ds(tap * 256, 256)] = cells
     start = (flag_ref[0] == 0).astype(F32)
-    lhs = windows[...]
-    c0 = dot(lhs, conv_ref[0].reshape(2304, 256))
-    c1 = dot(lhs, conv_ref[1].reshape(2304, 256)) + c0 * start
+    col = lax.broadcasted_iota(jnp.int32, (40, 128), 0)
+    inside = ((col > 0) | (flag_ref[2] > 0)) & ((col < 33) | (flag_ref[2] < 7))
+    inside = inside.astype(F32)
+    ends = {0: (flag_ref[1] > 0).astype(F32), 17: (flag_ref[1] < 3).astype(F32)}
+    fields = []
+    done = 0
+    for part in range(2):
+        for row in range(done, 10 + 8 * part):
+            value = own_ref[row, pl.ds(0, 40), :] + got[pl.ds(row * 34, 40), :]
+            value = value.astype(BF16).astype(F32)
+            active = silu(scaled(value, gain))
+            keep = inside * ends[row] if row in ends else inside
+            for half in range(2):
+                reduced[half, row, pl.ds(0, 40), :] = value[:, half * 128 : half * 128 + 128]
+                act[half, row, pl.ds(0, 40), :] = active[:, half * 128 : half * 128 + 128] * keep
+        done = 10 + 8 * part
+        for row in range(8 * part, 8 * part + 10):
+            for v in range(4):
+                halves = [act[half, row, pl.ds(v, 16, stride=2), :] for half in range(2)]
+                cells = jnp.concatenate(halves, -1).astype(BF16)
+                for p in range(2):
+                    for i in range(3):
+                        at = row - i - 8 * part
+                        if 0 <= v - p < 3 and 0 <= at < 8:
+                            tap = i * 3 + v - p
+                            windows[pl.ds(((part * 2 + p) * 8 + at) * 16, 16), pl.ds(tap * 256, 256)] = cells
+        lhs = windows[pl.ds(part * 256, 256), :]
+        fields.append([dot(lhs, conv_ref[s].reshape(2304, 256)) for s in range(2)])
+    c0 = jnp.concatenate([fields[0][0], fields[1][0]], 0)
+    c1 = jnp.concatenate([fields[0][1], fields[1][1]], 0) + c0 * start
     c1_ref[...] = c1
     both = dot(jnp.concatenate([folded(c0), folded(c1)], 0), down_ref[...]).astype(BF16)
     far_ref[...] = both[:128]
@@ -292,10 +293,11 @@
 def here_kernel(flag_ref, windows, reduced, c1_ref, conv_ref, down_ref, latent_ref):
     start = (flag_ref[0] == 0).astype(F32)
     plain = []
-    for p in range(2):
-        for row in range(16):
-            halves = [reduced[half, row + 1, pl.ds(1 + p, 16, stride=2), :] for half in range(2)]
-            plain.append(jnp.concatenate(halves, -1))
+    for part in range(2):
+        for p in range(2):
+            for row in range(8 * part, 8 * part + 8):
+                halves = [reduced[half, row + 1, pl.ds(1 + p, 16, stride=2), :] for half in range(2)]
+                plain.append(jnp.concatenate(halves, -1))
     c2 = dot(windows[...], conv_ref[2].reshape(2304, 256)) + c1_ref[...] * start
     latent_ref[...] = dot(folded(c2 + jnp.concatenate(plain, 0)), down_ref[...])
 
@@ -395,11 +397,12 @@
     return lax.ppermute(value, RING, [(i, (i + step) % 4) for i in range(4)])
 
 
-def sides(block, axis, dim, width, count):
+def sides(block, axis, count):
     odd = lax.axis_index(axis) % 2
-    last = block.shape[dim] - width
-    inner = lax.dynamic_slice_in_dim(block, (1 - odd) * last, width, axis=dim)
-    outer = lax.dynamic_slice_in_dim(block, odd * last, width, axis=dim)
+    rows = shape((2, 3, 64, 128), BF16)
+    inner, outer = call(
+        edges_kernel, (rows, rows), [SM, HB], [pltpu.SemaphoreType.DMA((2,))], flops=1000, name="edges"
+    )(odd.astype(jnp.int32).reshape(1), kept(block))
     got_inner = swapped(inner, axis, count, 0)
     got_outer = swapped(outer, axis, count, 1)
     even = odd == 0
@@ -413,22 +416,23 @@
     rows = shape((128, 512), BF16)
     tm = lax.axis_index("tm").astype(jnp.int32)
     flags = jnp.stack([tm, lax.axis_index(HEIGHT).astype(jnp.int32), lax.axis_index(WIDTH).astype(jnp.int32)])
-    above, below = sides(features, HEIGHT, 1, 3, 4)
-    act, first, last = prepare(features, gain_fine)
+    above, below = sides(features, HEIGHT, 4)
+    act, first, last, conv_here, down_here = prepare(features, gain_fine, conv_fine, down_fine)
     above, below, act, first, last = lax.optimization_barrier((above, below, act, first, last))
     first = jnp.concatenate([above[:, :, :4], first, below[:, :, :4]], 1)
     last = jnp.concatenate([above[:, :, 60:], last, below[:, :, 60:]], 1)
     odd = lax.axis_index(WIDTH) % 2 == 1
     got_inner = swapped(jnp.where(odd, first, last), WIDTH, 8, 0)
     got_outer = swapped(jnp.where(odd, last, first), WIDTH, 8, 1)
-    weight_next = compose(False, flags, conv_fine, down_fine)
+    weight_next = compose(False, flags, conv_here, down_here)
     got_inner, got_outer, weight_next = lax.optimization_barrier((got_inner, got_outer, weight_next))
     left, right = jnp.where(odd, got_inner, got_outer), jnp.where(odd, got_outer, got_inner)
     halos = (above, below, left, right)
     sent, planes = fine_next(act, halos, gain_fine, weight_next)
+    sent, conv_here, down_here = lax.optimization_barrier((sent, conv_here, down_here))
     got = lax.ppermute(sent, "tm", [(i, i + 1) for i in range(7)])
-    weight_own = compose(True, flags, conv_fine, down_fine)
-    own = fine_own(features, halos, weight_own, planes, down_fine)
+    weight_own = compose(True, flags, conv_here, down_here)
+    own = fine_own(features, halos, weight_own, planes, down_here)
     square = shape((512, 512), BF16)
     w_score, w_mix = call(mix_kernel, (square, square), [VM] * 4, flops=1000, moved=1000, name="mix")(
         w_query, w_key, w_value, w_out
@@ -437,7 +441,6 @@
     near, far, latent_own = coarse(flags, own, got, gain_coarse, conv_coarse, down_coarse)
     far = lax.ppermute(far, "tm", [(i, i + 2) for i in range(6)])
     near = lax.ppermute(near, "tm", [(i, i + 1) for i in range(7)])
-    near, far, latent_own = lax.optimization_barrier((near, far, latent_own))
     latent_in, query, copies = call(
         latent_kernel, (rows, rows, shape((4, 128, 512), BF16)), [VM] * 5, flops=80_000_000, name="latent"
     )(latent_own, near, far, gain_latent.reshape(1, 512), w_score)

time: 80.5 us -> 79.3 us (0.985)
  Pallas kernels: 23.6 us -> 21 us
  waiting for transfers between devices: 19.6 us -> 21.9 us
  local copies, waits for them, and re-layouts: 1.04 us -> 0.08 us
    pallas_call x2, Pallas kernels: 6.5 us -> 3.83 us  [compose(): call(functools.partial(compose_kernel, own), shape((16, 256, 256), BF16),...]
    all_to_all x1, starting transfers between devices: 7.38 us -> 9.09 us  [per_device(): keys = lax.all_to_all(copies, 'y', 0, 0, tiled=True).reshape(512, 512)]
    ppermute x6, starting transfers between devices: 8.1 us -> 6.61 us  [turned(): return lax.ppermute(value, RING, [(i, (i + step) % 4) for i in range(4)])]
    ppermute x5, waiting for transfers between devices: 1.92 us -> 3.14 us  [swapped(): return lax.ppermute(value, axis, pairs)]
    ppermute x6, waiting for transfers between devices: 12.7 us -> 13.8 us  [turned(): return lax.ppermute(value, RING, [(i, (i + step) % 4) for i in range(4)])]
    pallas_call x1 -> x2, Pallas kernels: 1.97 us -> 2.95 us  [the longest x1 1.99 us: prepare(): call(prepare_kernel, (shape((2, 32, 64, 128), F32), edge, edge, shape((3,...]
    dynamic_slice x1 -> x0, local copies, waits for them, and re-layouts: 0.95 us -> none  [sides(): inner = lax.dynamic_slice_in_dim(block, (1 - odd) * last, width, axis=dim)]
  transfers between devices with their start and end apart: 15 -> 15, of which waited for: 9 -> 10; matrix products, arithmetic and copies ran while one was open for 0% -> 0% of each run, Pallas kernels for 18% -> 15%
where the time goes in v6:
time: 79.3 us; the launch traced here: 78.6 us
  starting transfers between devices  35.1 us (44%)
  waiting for transfers between devices  21.9 us (28%)
  Pallas kernels  21 us (26%)
    ppermute x6, waiting for transfers between devices, turned(): return lax.ppermute(value, RING, [(i, (i + step) % 4) for i in range(4)])  13.8 us
    all_to_all x1, starting transfers between devices, per_device(): keys = lax.all_to_all(copies, 'y', 0, 0, tiled=True).reshape(512, 512)  9.09 us
    ppermute x6, starting transfers between devices, turned(): return lax.ppermute(value, RING, [(i, (i + step) % 4) for i in range(4)])  6.61 us
    ppermute x5, starting transfers between devices, swapped(): return lax.ppermute(value, axis, pairs)  6.47 us
    ppermute x1, starting transfers between devices, per_device(): near = lax.ppermute(near, 'tm', [(i, i + 1) for i in range(7)])  5.6 us
    ppermute x1, starting transfers between devices, per_device(): got = lax.ppermute(sent, 'tm', [(i, i + 1) for i in range(7)])  5.17 us
    pallas_call x2, Pallas kernels, compose(): call(functools.partial(compose_kernel, own), shape((16, 256, 256), BF16),...  3.83 us
    ppermute x5, waiting for transfers between devices, swapped(): return lax.ppermute(value, axis, pairs)  3.14 us
  transfers between devices with their start and end apart: 15, of which 10 were waited for; matrix products, arithmetic and copies ran while one was open for 0% of the time, Pallas kernels for 15%

profile of v6, /device:TPU:96, one launch (start us, length us, event | category | flops | bytes accessed | tf_op | source)
XLA Modules:
  0.0 78.6 jit_solution(6731037894078757194)
XLA Ops:
  0.0 1.0 %edges.1 = (bf16[2,3,64,128]{3,2,1,0:T(8,128)(2,1)S(1)}, bf16[2,3,64,128]{3,2,1,0:T(8,128)(2,1)S(1)}) custom-call(s32[1]{0:T(128)} %bitcast.3.odd_ref, bf16[2,32,64,128]{3,2,1,0:T(8,128)(2,1)} %x_ref.1), custom_call_target="tpu_custom_call" | custom-call | flops 1000 | bytes 4194304 | tf_op jit(solution)/shard_map/edges/pallas_call | solution.py:403
  1.0 0.7 collective-permute-start
  1.6 4.5 %collective-permute-start.1 = (bf16[2,3,64,128]{3,2,1,0:T(8,128)(2,1)S(1)}, bf16[2,3,64,128]{3,2,1,0:T(8,128)(2,1)S(1)}, u32[]{:S(2)}, u32[]{:S(2)}) collective-permute-start(bf16[2,3,64,128]{3,2,1,0:T(8,128)(2,1)S(1)} %get-tuple-element.49), channel_id=1, source_target_pairs={{0,8},{8,0},{16,24},{24,16},{1,9},{9,1},{17,25},{25,17},{2,10},{10... | collective-permute-start | bytes 294920 | tf_op jit(solution)/shard_map/ppermute | solution.py:393
  6.1 2.0 %prepare.1 = (f32[2,32,64,128]{3,2,1,0:T(8,128)S(1)}, bf16[2,32,4,128]{3,2,1,0:T(4,128)(2,1)S(1)}, bf16[2,32,4,128]{3,2,1,0:T(4,128)(2,1)S(1)}, bf16[3,3,3,128,1...) custom-call(bf16[2,32,64,128]{3,2,1,0:T(8,128)(2,1)} %x_ref.1, f32[1,128]{1,0:T(1,128)} %bitcast.25, ...), custom_call_target="tpu_custom_call" | custom-call | flops 10000000 | bytes 4194304 | tf_op jit(solution)/shard_map/prepare/pallas_call | solution.py:139
  8.1 0.0 copy-start.9
  8.1 0.1 pad_add_fusion.flag_ref
  8.3 0.1 broadcast_select_fusion.4
  8.4 0.7 collective-permute-start.2
  9.1 0.7 collective-permute-start.3
  9.7 1.9 %compose_next.1.weight_ref = bf16[16,256,256]{2,1,0:T(8,128)(2,1)S(1)} custom-call(s32[3]{0:T(128)S(1)} %pad_add_fusion.flag_ref, bf16[3,3,3,128,128]{4,3,2,1,0:T(8,128)(2,1)S(1)} %get-tuple-element.65.conv, bf16[1024,256]{1,0:T(8,128)(2,1)S(1)} %get-tuple-element.66.down.down_ref), custom_call_target="tpu_custom_call" | custom-call | flops 900000000 | bytes 4194304 | tf_op jit(solution)/shard_map/compose_next/pallas_call | solution.py:85
  11.6 1.2 %collective-permute-done.2 = bf16[2,38,4,128]{3,2,1,0:T(4,128)(2,1)S(1)} collective-permute-done((bf16[2,38,4,128]{3,2,1,0:T(4,128)(2,1)S(1)}, bf16[2,38,4,128]{3,2,1,0:T(4,128)(2,1)S(1)}, u32[]{:S(2)}, u32[]{:S(2)}) %collective-permute-start.2) | collective-permute-done | bytes 77856 | tf_op jit(solution)/shard_map/ppermute | solution.py:393
  12.9 0.0 copy-start.3
  12.9 0.0 copy-start.4
  12.9 0.0 copy-start.5
  12.9 0.0 copy-start.6
  13.0 2.4 %fine_next.1 = (bf16[624,256]{1,0:T(8,128)(2,1)S(1)}, bf16[2,4,19,48,256]{4,3,2,1,0:T(8,128)(2,1)S(1)}) custom-call(f32[2,32,64,128]{3,2,1,0:T(8,128)S(1)} %get-tuple-element.53.act_ref, bf16[2,3,64,128]{3,2,1,0:T(8,128)(2,1)S(1)} %get-tuple-element.54.up_ref, bf16[2,3,64,128]{3,2,1,0:T(8,128)(2,1)S(1)} %get-tuple-element.55.low_ref, ...), custom_call_target="tpu_custom_call" | custom-call | flops 1800000000 | bytes 4194304 | tf_op jit(solution)/shard_map/fine_next/pallas_call | solution.py:224
  15.4 0.0 copy-start.1
  15.4 5.2 %collective-permute-start.4 = (bf16[624,256]{1,0:T(8,128)(2,1)S(1)}, bf16[624,256]{1,0:T(8,128)(2,1)S(1)}, u32[]{:S(2)}, u32[]{:S(2)}) collective-permute-start(bf16[624,256]{1,0:T(8,128)(2,1)S(1)} %get-tuple-element.64), channel_id=1, source_target_pairs={{0,32},{32,64},{64,96},{96,128},{128,160},{160,192},{192,224},{1,3... | collective-permute-start | bytes 958472 | tf_op jit(solution)/shard_map/ppermute | solution.py:433
  20.6 0.7 mix.1
  21.4 1.9 %compose_own.1.weight_ref = bf16[16,256,256]{2,1,0:T(8,128)(2,1)S(1)} custom-call(s32[3]{0:T(128)S(1)} %pad_add_fusion.flag_ref, bf16[3,3,3,128,128]{4,3,2,1,0:T(8,128)(2,1)S(1)} %get-tuple-element.65.conv, bf16[1024,256]{1,0:T(8,128)(2,1)S(1)} %get-tuple-element.66.down.down_ref), custom_call_target="tpu_custom_call" | custom-call | flops 900000000 | bytes 4194304 | tf_op jit(solution)/shard_map/compose_own/pallas_call | solution.py:85
  23.3 0.0 copy-start
  23.3 0.0 copy-start.2
  23.3 0.0 copy-start.8
  23.3 2.6 %fine_own.1.own_ref = f32[18,48,256]{2,1,0:T(8,128)S(1)} custom-call(bf16[2,32,64,128]{3,2,1,0:T(8,128)(2,1)S(1)} %copy-done.1, bf16[2,3,64,128]{3,2,1,0:T(8,128)(2,1)S(1)} %get-tuple-element.54.up_ref, bf16[2,3,64,128]{3,2,1,0:T(8,128)(2,1)S(1)} %get-tuple-element.55.low_ref, bf16[2,38,4,128]{3,2,1,0:T(4,128)(2,1)S(1)} %bitcast.22, ...), custom_call_target="tpu_custom_call" | custom-call | flops 2200000000 | bytes 4194304 | tf_op jit(solution)/shard_map/fine_own/pallas_call | solution.py:235
  26.0 1.0 %collective-permute-done.4.got_ref = bf16[624,256]{1,0:T(8,128)(2,1)S(1)} collective-permute-done((bf16[624,256]{1,0:T(8,128)(2,1)S(1)}, bf16[624,256]{1,0:T(8,128)(2,1)S(1)}, u32[]{:S(2)}, u32[]{:S(2)}) %collective-permute-start.4) | collective-permute-done | bytes 319520 | tf_op jit(solution)/shard_map/ppermute | solution.py:433
  27.0 2.5 %coarse_sent.1 = (bf16[128,512]{1,0:T(8,128)(2,1)S(1)}, bf16[128,512]{1,0:T(8,128)(2,1)S(1)}, f32[512,256]{1,0:T(8,128)S(1)}, bf16[512,2304]{1,0:T(8,128)(2,1)S(1)}, f32[2,18,48,128]{3,2,1,0:T(8,128)S(1)}) custom-call(s32[3]{0:T(128)S(1)} %pad_add_fusion.flag_ref, f32[18,48,256]{2,1,0:T(8,128)S(1)} %fine_own.1.own_ref, ...), custom_call_target="tpu_custom_call" | custom-call | flops 1500000000 | bytes 4194304 | tf_op jit(solution)/shard_map/coarse_sent/pallas_call | solution.py:309
  29.5 5.6 %collective-permute-start.5 = (bf16[128,512]{1,0:T(8,128)(2,1)S(1)}, bf16[128,512]{1,0:T(8,128)(2,1)S(1)}, u32[]{:S(2)}, u32[]{:S(2)}) collective-permute-start(bf16[128,512]{1,0:T(8,128)(2,1)S(1)} %get-tuple-element.75), channel_id=1, source_target_pairs={{0,32},{32,64},{64,96},{96,128},{128,160},{160,192},{192,224},{1,3... | collective-permute-start | bytes 393224 | tf_op jit(solution)/shard_map/ppermute | solution.py:443
  35.1 2.2 %collective-permute-start.6 = (bf16[128,512]{1,0:T(8,128)(2,1)S(1)}, bf16[128,512]{1,0:T(8,128)(2,1)S(1)}, u32[]{:S(2)}, u32[]{:S(2)}) collective-permute-start(bf16[128,512]{1,0:T(8,128)(2,1)S(1)} %get-tuple-element.76), channel_id=1, source_target_pairs={{0,64},{32,96},{64,128},{96,160},{128,192},{160,224},{1,65},{33,97... | collective-permute-start | bytes 393224 | tf_op jit(solution)/shard_map/ppermute | solution.py:442
  37.3 0.0 copy-start.7
  37.3 1.8 %coarse_here.1.own_ref = f32[128,512]{1,0:T(8,128)S(1)} custom-call(s32[3]{0:T(128)S(1)} %pad_add_fusion.flag_ref, bf16[512,2304]{1,0:T(8,128)(2,1)S(1)} %get-tuple-element.72.windows, f32[2,18,48,128]{3,2,1,0:T(8,128)S(1)} %get-tuple-element.73.reduced, f32[512,256]{1,0:T(8,128)S(1)} %get-tuple-element.74.c1_ref, bf16[3,9,256,256]{3,2,1,0:T(8,128)(2,1)S(1)} %bitcast.15, ...), custom_call_target="tpu_custom_call" | custom-call | flops 1000 | bytes 1000 | tf_op jit(solution)/shard_map/coarse_here/pallas_call | solution.py:317
  39.0 1.7 %collective-permute-done.5.near_ref = bf16[128,512]{1,0:T(8,128)(2,1)S(1)} collective-permute-done((bf16[128,512]{1,0:T(8,128)(2,1)S(1)}, bf16[128,512]{1,0:T(8,128)(2,1)S(1)}, u32[]{:S(2)}, u32[]{:S(2)}) %collective-permute-start.5) | collective-permute-done | bytes 131104 | tf_op jit(solution)/shard_map/ppermute | solution.py:443
  40.7 2.3 %collective-permute-done.6.far_ref = bf16[128,512]{1,0:T(8,128)(2,1)S(1)} collective-permute-done((bf16[128,512]{1,0:T(8,128)(2,1)S(1)}, bf16[128,512]{1,0:T(8,128)(2,1)S(1)}, u32[]{:S(2)}, u32[]{:S(2)}) %collective-permute-start.6) | collective-permute-done | bytes 131104 | tf_op jit(solution)/shard_map/ppermute | solution.py:442
  43.0 1.0 %latent.1 = (bf16[128,512]{1,0:T(8,128)(2,1)S(1)}, bf16[128,512]{1,0:T(8,128)(2,1)S(1)}, bf16[4,128,512]{2,1,0:T(8,128)(2,1)}) custom-call(f32[128,512]{1,0:T(8,128)S(1)} %coarse_here.1.own_ref, bf16[128,512]{1,0:T(8,128)(2,1)S(1)} %collective-permute-done.5.near_ref, bf16[128,512]{1,0:T(8,128)(2,1)S(1)} %collective-permute-done.6.far_ref, ...), custom_call_target="tpu_custom_call" | custom-call | flops 80000000 | bytes 4194304 | tf_op jit(solution)/shard_map/latent/pallas_call | solution.py:444
  44.0 9.1 %all-to-all-start = ((bf16[4,128,512]{2,1,0:T(8,128)(2,1)}), bf16[4,128,512]{2,1,0:T(8,128)(2,1)S(1)}, u32[]{:S(2)}, u32[]{:S(2)}) async-start(bf16[4,128,512]{2,1,0:T(8,128)(2,1)} %get-tuple-element.79), calls=%async_computation | async-start | bytes 1048576 | tf_op jit(solution)/shard_map/all_to_all | solution.py:447
  53.1 1.4 %collective-permute-start.8 = (bf16[128,512]{1,0:T(8,128)(2,1)S(1)}, bf16[128,512]{1,0:T(8,128)(2,1)S(1)}, u32[]{:S(2)}, u32[]{:S(2)}) collective-permute-start(bf16[128,512]{1,0:T(8,128)(2,1)S(1)} %get-tuple-element.78.queries_ref), channel_id=1, source_target_pairs={{0,16},{1,17},{16,0},{17,1},{2,18},{3,19},{18,2},{19,3},{4,20},{5,... | collective-permute-start | bytes 393224 | tf_op jit(solution)/shard_map/ppermute | solution.py:397
  54.5 1.8 %collective-permute-start.9 = (bf16[128,512]{1,0:T(8,128)(2,1)S(1)}, bf16[128,512]{1,0:T(8,128)(2,1)S(1)}, u32[]{:S(2)}, u32[]{:S(2)}) collective-permute-start(bf16[128,512]{1,0:T(8,128)(2,1)S(1)} %get-tuple-element.78.queries_ref), channel_id=1, source_target_pairs={{0,17},{1,0},{16,1},{17,16},{2,19},{3,2},{18,3},{19,18},{4,21},{5,... | collective-permute-start | bytes 393224 | tf_op jit(solution)/shard_map/ppermute | solution.py:397
  56.4 5.0 %collective-permute-done.7.q1_ref = bf16[128,512]{1,0:T(8,128)(2,1)S(1)} collective-permute-done((bf16[128,512]{1,0:T(8,128)(2,1)S(1)}, bf16[128,512]{1,0:T(8,128)(2,1)S(1)}, u32[]{:S(2)}, u32[]{:S(2)}) %collective-permute-start.7) | collective-permute-done | bytes 131104 | tf_op jit(solution)/shard_map/ppermute | solution.py:397
  61.3 0.6 collective-permute-done.9.q3_ref
  61.9 1.9 %collective-permute-done.10.other_keys_ref = bf16[512,512]{1,0:T(8,128)(2,1)S(1)} collective-permute-done((bf16[512,512]{1,0:T(8,128)(2,1)S(1)}, bf16[512,512]{1,0:T(8,128)(2,1)S(1)}, u32[]{:S(2)}, u32[]{:S(2)}) %collective-permute-start.10) | collective-permute-done | bytes 524320 | tf_op jit(solution)/shard_map/ppermute | solution.py:393
  63.9 1.2 %attend_theirs.1 = (bf16[144,512]{1,0:T(8,128)(2,1)S(1)}, bf16[144,512]{1,0:T(8,128)(2,1)S(1)}, bf16[144,512]{1,0:T(8,128)(2,1)S(1)}) custom-call(bf16[128,512]{1,0:T(8,128)(2,1)S(1)} %collective-permute-done.7.q1_ref, bf16[128,512]{1,0:T(8,128)(2,1)S(1)} %collective-permute-done.8.q2_ref, bf16[128,512]{1,0:T(8,128)(2,1)S(1)} %collective-permute-done.9.q3_ref, ...), custom_call_target="tpu_custom_call" | custom-call | flops 800000000 | bytes 4194304 | tf_op jit(solution)/shard_map/attend_theirs/pallas_call | solution.py:451
  65.1 2.4 %collective-permute-start.11 = (bf16[144,512]{1,0:T(8,128)(2,1)S(1)}, bf16[144,512]{1,0:T(8,128)(2,1)S(1)}, u32[]{:S(2)}, u32[]{:S(2)}) collective-permute-start(bf16[144,512]{1,0:T(8,128)(2,1)S(1)} %get-tuple-element.86), channel_id=1, source_target_pairs={{0,17},{1,0},{16,1},{17,16},{2,19},{3,2},{18,3},{19,18},{4,21},{5,... | collective-permute-start | bytes 442376 | tf_op jit(solution)/shard_map/ppermute | solution.py:397
  67.5 0.0 collective-permute-start.12
  67.5 0.9 %collective-permute-start.13 = (bf16[144,512]{1,0:T(8,128)(2,1)S(1)}, bf16[144,512]{1,0:T(8,128)(2,1)S(1)}, u32[]{:S(2)}, u32[]{:S(2)}) collective-permute-start(bf16[144,512]{1,0:T(8,128)(2,1)S(1)} %get-tuple-element.88), channel_id=1, source_target_pairs={{0,1},{1,16},{16,17},{17,0},{2,3},{3,18},{18,19},{19,2},{4,5},{5,2... | collective-permute-start | bytes 442376 | tf_op jit(solution)/shard_map/ppermute | solution.py:397
  68.5 0.8 %attend_mine.1 = (f32[128,512]{1,0:T(8,128)S(1)}, f32[128,128]{1,0:T(8,128)S(1)}) custom-call(bf16[128,512]{1,0:T(8,128)(2,1)S(1)} %get-tuple-element.78.queries_ref, bf16[512,512]{1,0:T(8,128)(2,1)S(1)} %bitcast.18, bf16[512,512]{1,0:T(8,128)(2,1)S(1)} %collective-permute-done.10.other_keys_ref), custom_call_target="tpu_custom_call" | custom-call | flops 300000000 | bytes 4194304 | tf_op jit(solution)/shard_map/attend_mine/pallas_call | solution.py:454
  69.3 4.8 %collective-permute-done.11.got1_ref = bf16[144,512]{1,0:T(8,128)(2,1)S(1)} collective-permute-done((bf16[144,512]{1,0:T(8,128)(2,1)S(1)}, bf16[144,512]{1,0:T(8,128)(2,1)S(1)}, u32[]{:S(2)}, u32[]{:S(2)}) %collective-permute-start.11) | collective-permute-done | bytes 147488 | tf_op jit(solution)/shard_map/ppermute | solution.py:397
  74.1 1.6 %collective-permute-done.12.got2_ref = bf16[144,512]{1,0:T(8,128)(2,1)S(1)} collective-permute-done((bf16[144,512]{1,0:T(8,128)(2,1)S(1)}, bf16[144,512]{1,0:T(8,128)(2,1)S(1)}, u32[]{:S(2)}, u32[]{:S(2)}) %collective-permute-start.12) | collective-permute-done | bytes 147488 | tf_op jit(solution)/shard_map/ppermute | solution.py:397
  75.8 1.7 %collective-permute-done.13.got3_ref = bf16[144,512]{1,0:T(8,128)(2,1)S(1)} collective-permute-done((bf16[144,512]{1,0:T(8,128)(2,1)S(1)}, bf16[144,512]{1,0:T(8,128)(2,1)S(1)}, u32[]{:S(2)}, u32[]{:S(2)}) %collective-permute-start.13) | collective-permute-done | bytes 147488 | tf_op jit(solution)/shard_map/ppermute | solution.py:397
  77.5 1.1 %finish.1 = bf16[128,512]{1,0:T(8,128)(2,1)} custom-call(f32[128,512]{1,0:T(8,128)S(1)} %get-tuple-element.81.mixed_ref, f32[128,128]{1,0:T(8,128)S(1)} %get-tuple-element.82.level_ref, bf16[144,512]{1,0:T(8,128)(2,1)S(1)} %collective-permute-done.11.got1_ref, bf16[144,512]{1,0:T(8,128)(2,1)S(1)} %collective-permute-done.12.got2_ref, ...), custom_call_target="tpu_custom_call" | custom-call | flops 70000000 | bytes 4194304 | tf_op jit(solution)/shard_map/finish/pallas_call | solution.py:462
  (20 shorter events, 0.1 us)
Async XLA Ops:
  1.0 7.2 %collective-permute-start = (bf16[2,3,64,128]{3,2,1,0:T(8,128)(2,1)S(1)}, bf16[2,3,64,128]{3,2,1,0:T(8,128)(2,1)S(1)}, u32[]{:S(2)}, u32[]{:S(2)}) collective-permute-start(bf16[2,3,64,128]{3,2,1,0:T(8,128)(2,1)S(1)} %get-tuple-element.48), channel_id=1, source_target_pairs={{8,16},{16,8},{9,17},{17,9},{10,18},{18,10},{11,19},{19,11},{12,20... | collective-permute-start | bytes 294920 | tf_op jit(solution)/shard_map/ppermute | solution.py:393
  1.6 6.6 %collective-permute-start.1 = (bf16[2,3,64,128]{3,2,1,0:T(8,128)(2,1)S(1)}, bf16[2,3,64,128]{3,2,1,0:T(8,128)(2,1)S(1)}, u32[]{:S(2)}, u32[]{:S(2)}) collective-permute-start(bf16[2,3,64,128]{3,2,1,0:T(8,128)(2,1)S(1)} %get-tuple-element.49), channel_id=1, source_target_pairs={{0,8},{8,0},{16,24},{24,16},{1,9},{9,1},{17,25},{25,17},{2,10},{10... | collective-permute-start | bytes 294920 | tf_op jit(solution)/shard_map/ppermute | solution.py:393
  8.1 4.8 %copy-start.9 = (f32[128]{0:T(128)S(1)}, f32[128]{0:T(128)}, u32[]{:S(2)}) copy-start(f32[128]{0:T(128)} %param.13) | copy-start | bytes 1540
  8.4 4.5 %collective-permute-start.2 = (bf16[2,38,4,128]{3,2,1,0:T(4,128)(2,1)S(1)}, bf16[2,38,4,128]{3,2,1,0:T(4,128)(2,1)S(1)}, u32[]{:S(2)}, u32[]{:S(2)}) collective-permute-start(bf16[2,38,4,128]{3,2,1,0:T(4,128)(2,1)S(1)} %get-tuple-element.96), channel_id=1, source_target_pairs={{0,1},{1,0},{2,3},{3,2},{4,5},{5,4},{6,7},{7,6},{8,9},{9,8},{10,11... | collective-permute-start | bytes 233480 | tf_op jit(solution)/shard_map/ppermute | solution.py:393
  9.1 3.8 %collective-permute-start.3 = (bf16[2,38,4,128]{3,2,1,0:T(4,128)(2,1)S(1)}, bf16[2,38,4,128]{3,2,1,0:T(4,128)(2,1)S(1)}, u32[]{:S(2)}, u32[]{:S(2)}) collective-permute-start(bf16[2,38,4,128]{3,2,1,0:T(4,128)(2,1)S(1)} %get-tuple-element.95), channel_id=1, source_target_pairs={{1,2},{2,1},{3,4},{4,3},{5,6},{6,5},{9,10},{10,9},{11,12},{12,11},... | collective-permute-start | bytes 233480 | tf_op jit(solution)/shard_map/ppermute | solution.py:393
  12.9 7.7 %copy-start.3 = (bf16[512,512]{1,0:T(8,128)(2,1)S(1)}, bf16[512,512]{1,0:T(8,128)(2,1)}, u32[]{:S(2)}) copy-start(bf16[512,512]{1,0:T(8,128)(2,1)} %query_ref.1) | copy-start | bytes 1572868
  12.9 7.7 %copy-start.4 = (bf16[512,512]{1,0:T(8,128)(2,1)S(1)}, bf16[512,512]{1,0:T(8,128)(2,1)}, u32[]{:S(2)}) copy-start(bf16[512,512]{1,0:T(8,128)(2,1)} %key_ref.1) | copy-start | bytes 1572868
  12.9 7.7 %copy-start.5 = (bf16[512,512]{1,0:T(8,128)(2,1)S(1)}, bf16[512,512]{1,0:T(8,128)(2,1)}, u32[]{:S(2)}) copy-start(bf16[512,512]{1,0:T(8,128)(2,1)} %value_ref.1) | copy-start | bytes 1572868
  12.9 7.7 %copy-start.6 = (bf16[512,512]{1,0:T(8,128)(2,1)S(1)}, bf16[512,512]{1,0:T(8,128)(2,1)}, u32[]{:S(2)}) copy-start(bf16[512,512]{1,0:T(8,128)(2,1)} %out_ref.1) | copy-start | bytes 1572868
  15.4 7.9 %copy-start.1 = (bf16[2,32,64,128]{3,2,1,0:T(8,128)(2,1)S(1)}, bf16[2,32,64,128]{3,2,1,0:T(8,128)(2,1)}, u32[]{:S(2)}) copy-start(bf16[2,32,64,128]{3,2,1,0:T(8,128)(2,1)} %x_ref.1) | copy-start | bytes 3145732
  15.4 11.6 %collective-permute-start.4 = (bf16[624,256]{1,0:T(8,128)(2,1)S(1)}, bf16[624,256]{1,0:T(8,128)(2,1)S(1)}, u32[]{:S(2)}, u32[]{:S(2)}) collective-permute-start(bf16[624,256]{1,0:T(8,128)(2,1)S(1)} %get-tuple-element.64), channel_id=1, source_target_pairs={{0,32},{32,64},{64,96},{96,128},{128,160},{160,192},{192,224},{1,3... | collective-permute-start | bytes 958472 | tf_op jit(solution)/shard_map/ppermute | solution.py:433
  23.3 3.7 %copy-start = (bf16[3,3,3,256,256]{4,3,2,1,0:T(8,128)(2,1)S(1)}, bf16[3,3,3,256,256]{4,3,2,1,0:T(8,128)(2,1)}, u32[]{:S(2)}) copy-start(bf16[3,3,3,256,256]{4,3,2,1,0:T(8,128)(2,1)} %param.17) | copy-start | bytes 10616836
  23.3 3.7 %copy-start.2 = (bf16[1024,512]{1,0:T(8,128)(2,1)S(1)}, bf16[1024,512]{1,0:T(8,128)(2,1)}, u32[]{:S(2)}) copy-start(bf16[1024,512]{1,0:T(8,128)(2,1)} %down_ref.3) | copy-start | bytes 3145732
  23.3 3.6 %copy-start.8 = (f32[256]{0:T(256)S(1)}, f32[256]{0:T(256)}, u32[]{:S(2)}) copy-start(f32[256]{0:T(256)} %param.16) | copy-start | bytes 3076
  29.5 11.2 %collective-permute-start.5 = (bf16[128,512]{1,0:T(8,128)(2,1)S(1)}, bf16[128,512]{1,0:T(8,128)(2,1)S(1)}, u32[]{:S(2)}, u32[]{:S(2)}) collective-permute-start(bf16[128,512]{1,0:T(8,128)(2,1)S(1)} %get-tuple-element.75), channel_id=1, source_target_pairs={{0,32},{32,64},{64,96},{96,128},{128,160},{160,192},{192,224},{1,3... | collective-permute-start | bytes 393224 | tf_op jit(solution)/shard_map/ppermute | solution.py:443
  35.1 8.0 %collective-permute-start.6 = (bf16[128,512]{1,0:T(8,128)(2,1)S(1)}, bf16[128,512]{1,0:T(8,128)(2,1)S(1)}, u32[]{:S(2)}, u32[]{:S(2)}) collective-permute-start(bf16[128,512]{1,0:T(8,128)(2,1)S(1)} %get-tuple-element.76), channel_id=1, source_target_pairs={{0,64},{32,96},{64,128},{96,160},{128,192},{160,224},{1,65},{33,97... | collective-permute-start | bytes 393224 | tf_op jit(solution)/shard_map/ppermute | solution.py:442
  37.3 5.8 %copy-start.7 = (f32[512]{0:T(512)S(1)}, f32[512]{0:T(512)}, u32[]{:S(2)}) copy-start(f32[512]{0:T(512)} %param.19) | copy-start | bytes 6148
  44.0 17.9 %all-to-all-start = ((bf16[4,128,512]{2,1,0:T(8,128)(2,1)}), bf16[4,128,512]{2,1,0:T(8,128)(2,1)S(1)}, u32[]{:S(2)}, u32[]{:S(2)}) async-start(bf16[4,128,512]{2,1,0:T(8,128)(2,1)} %get-tuple-element.79), calls=%async_computation | async-start | bytes 1048576 | tf_op jit(solution)/shard_map/all_to_all | solution.py:447
  53.1 8.2 %collective-permute-start.7 = (bf16[128,512]{1,0:T(8,128)(2,1)S(1)}, bf16[128,512]{1,0:T(8,128)(2,1)S(1)}, u32[]{:S(2)}, u32[]{:S(2)}) collective-permute-start(bf16[128,512]{1,0:T(8,128)(2,1)S(1)} %get-tuple-element.78.queries_ref), channel_id=1, source_target_pairs={{0,1},{1,16},{16,17},{17,0},{2,3},{3,18},{18,19},{19,2},{4,5},{5,2... | collective-permute-start | bytes 393224 | tf_op jit(solution)/shard_map/ppermute | solution.py:397
  53.1 8.2 %collective-permute-start.8 = (bf16[128,512]{1,0:T(8,128)(2,1)S(1)}, bf16[128,512]{1,0:T(8,128)(2,1)S(1)}, u32[]{:S(2)}, u32[]{:S(2)}) collective-permute-start(bf16[128,512]{1,0:T(8,128)(2,1)S(1)} %get-tuple-element.78.queries_ref), channel_id=1, source_target_pairs={{0,16},{1,17},{16,0},{17,1},{2,18},{3,19},{18,2},{19,3},{4,20},{5,... | collective-permute-start | bytes 393224 | tf_op jit(solution)/shard_map/ppermute | solution.py:397
  54.5 7.4 %collective-permute-start.9 = (bf16[128,512]{1,0:T(8,128)(2,1)S(1)}, bf16[128,512]{1,0:T(8,128)(2,1)S(1)}, u32[]{:S(2)}, u32[]{:S(2)}) collective-permute-start(bf16[128,512]{1,0:T(8,128)(2,1)S(1)} %get-tuple-element.78.queries_ref), channel_id=1, source_target_pairs={{0,17},{1,0},{16,1},{17,16},{2,19},{3,2},{18,3},{19,18},{4,21},{5,... | collective-permute-start | bytes 393224 | tf_op jit(solution)/shard_map/ppermute | solution.py:397
  61.9 1.9 %collective-permute-start.10 = (bf16[512,512]{1,0:T(8,128)(2,1)S(1)}, bf16[512,512]{1,0:T(8,128)(2,1)S(1)}, u32[]{:S(2)}, u32[]{:S(2)}) collective-permute-start(bf16[512,512]{1,0:T(8,128)(2,1)S(1)} %bitcast.16), channel_id=1, source_target_pairs={{0,8},{8,0},{1,9},{9,1},{2,10},{10,2},{3,11},{11,3},{4,12},{12,4},... | collective-permute-start | bytes 1572872 | tf_op jit(solution)/shard_map/ppermute | solution.py:393
  65.1 9.0 %collective-permute-start.11 = (bf16[144,512]{1,0:T(8,128)(2,1)S(1)}, bf16[144,512]{1,0:T(8,128)(2,1)S(1)}, u32[]{:S(2)}, u32[]{:S(2)}) collective-permute-start(bf16[144,512]{1,0:T(8,128)(2,1)S(1)} %get-tuple-element.86), channel_id=1, source_target_pairs={{0,17},{1,0},{16,1},{17,16},{2,19},{3,2},{18,3},{19,18},{4,21},{5,... | collective-permute-start | bytes 442376 | tf_op jit(solution)/shard_map/ppermute | solution.py:397
  67.5 8.2 %collective-permute-start.12 = (bf16[144,512]{1,0:T(8,128)(2,1)S(1)}, bf16[144,512]{1,0:T(8,128)(2,1)S(1)}, u32[]{:S(2)}, u32[]{:S(2)}) collective-permute-start(bf16[144,512]{1,0:T(8,128)(2,1)S(1)} %get-tuple-element.87), channel_id=1, source_target_pairs={{0,16},{1,17},{16,0},{17,1},{2,18},{3,19},{18,2},{19,3},{4,20},{5,... | collective-permute-start | bytes 442376 | tf_op jit(solution)/shard_map/ppermute | solution.py:397
  67.5 10.0 %collective-permute-start.13 = (bf16[144,512]{1,0:T(8,128)(2,1)S(1)}, bf16[144,512]{1,0:T(8,128)(2,1)S(1)}, u32[]{:S(2)}, u32[]{:S(2)}) collective-permute-start(bf16[144,512]{1,0:T(8,128)(2,1)S(1)} %get-tuple-element.88), channel_id=1, source_target_pairs={{0,1},{1,16},{16,17},{17,0},{2,3},{3,18},{18,19},{19,2},{4,5},{5,2... | collective-permute-start | bytes 442376 | tf_op jit(solution)/shard_map/ppermute | solution.py:397

commit v7 on v6

--- a/solution.py
+++ b/solution.py
@@ -359,20 +359,19 @@
     return dot(expo.astype(BF16), keys) / total, top + jnp.log(total)
 
 
-def attend_theirs_kernel(q1_ref, q2_ref, q3_ref, keys_ref, other_keys_ref, *sent):
-    queries = jnp.concatenate([q1_ref[...], q2_ref[...], q3_ref[...]], 0)
+def attend_two_kernel(q1_ref, q2_ref, keys_ref, other_keys_ref, sent1_ref, sent2_ref):
     keys = jnp.concatenate([keys_ref[...], other_keys_ref[...]], 0)
-    mixed, level = softmax_part(queries, keys)
-    for k in range(3):
-        rows = slice(128 * k, 128 * (k + 1))
-        sent[k][...] = packed(mixed[rows], level[rows])
-
-
-def attend_mine_kernel(queries_ref, keys_ref, other_keys_ref, mixed_ref, level_ref):
+    mixed, level = softmax_part(jnp.concatenate([q1_ref[...], q2_ref[...]], 0), keys)
+    sent1_ref[...] = packed(mixed[:128], level[:128])
+    sent2_ref[...] = packed(mixed[128:], level[128:])
+
+
+def attend_last_kernel(q3_ref, mine_ref, keys_ref, other_keys_ref, sent3_ref, mixed_ref, level_ref):
     keys = jnp.concatenate([keys_ref[...], other_keys_ref[...]], 0)
-    mixed, level = softmax_part(queries_ref[...], keys)
-    mixed_ref[...] = mixed
-    level_ref[...] = jnp.broadcast_to(level, (128, 128))
+    mixed, level = softmax_part(jnp.concatenate([q3_ref[...], mine_ref[...]], 0), keys)
+    sent3_ref[...] = packed(mixed[:128], level[:128])
+    mixed_ref[...] = mixed[128:]
+    level_ref[...] = jnp.broadcast_to(level[128:], (128, 128))
 
 
 def finish_kernel(mixed_ref, level_ref, got1_ref, got2_ref, got3_ref, latent_ref, mix_ref, out_ref):
@@ -446,18 +445,20 @@
     )(latent_own, near, far, gain_latent.reshape(1, 512), w_score)
     keys = lax.all_to_all(copies, "y", 0, 0, tiled=True).reshape(512, 512)
     asked = [turned(query, step) for step in (1, 2, 3)]
-    keys, *asked = lax.optimization_barrier((keys, *asked))
+    keys, asked[0], asked[1] = lax.optimization_barrier((keys, asked[0], asked[1]))
     other_keys = swapped(keys, "core", 2, 0)
-    sent = call(
-        attend_theirs_kernel, (shape((144, 512), BF16),) * 3, [VM] * 5, flops=800_000_000, name="attend_theirs"
-    )(*asked, keys, other_keys)
-    mixed, level = call(
-        attend_mine_kernel,
-        (shape((128, 512), F32), shape((128, 128), F32)),
-        [VM] * 3,
-        flops=300_000_000,
-        name="attend_mine",
-    )(query, keys, other_keys)
+    block = shape((144, 512), BF16)
+    sent1, sent2 = call(attend_two_kernel, (block, block), [VM] * 4, flops=550_000_000, name="attend_two")(
+        asked[0], asked[1], keys, other_keys
+    )
+    sent3, mixed, level = call(
+        attend_last_kernel,
+        (block, shape((128, 512), F32), shape((128, 128), F32)),
+        [VM] * 4,
+        flops=550_000_000,
+        name="attend_last",
+    )(asked[2], query, keys, other_keys)
+    sent = (sent1, sent2, sent3)
     got = [turned(block, -step) for step, block in zip((1, 2, 3), sent)]
     out = call(finish_kernel, rows, [VM] * 7, flops=70_000_000, name="finish")(mixed, level, *got, latent_in, w_mix)
     return out.reshape(1, 8, 16, 512)

time: 79.3 us -> 78.3 us (0.987)
  starting transfers between devices: 35.1 us -> 33.3 us
    ppermute x6, starting transfers between devices: 6.61 us -> 4.79 us  [turned(): return lax.ppermute(value, RING, [(i, (i + step) % 4) for i in range(4)])]
    ppermute x6, waiting for transfers between devices: 13.8 us -> 14.8 us  [turned(): return lax.ppermute(value, RING, [(i, (i + step) % 4) for i in range(4)])]
    ppermute x5, waiting for transfers between devices: 3.14 us -> 2.13 us  [swapped(): return lax.ppermute(value, axis, pairs)]
  transfers between devices with their start and end apart: 15 -> 15, of which waited for: 10 -> 11; matrix products, arithmetic and copies ran while one was open for 0% -> 0% of each run, Pallas kernels for 15% -> 17%
where the time goes in v7:
time: 78.3 us; the launch traced here: 77.2 us
  starting transfers between devices  33.3 us (43%)
  waiting for transfers between devices  22.4 us (29%)
  Pallas kernels  20.9 us (27%)
    ppermute x6, waiting for transfers between devices, turned(): return lax.ppermute(value, RING, [(i, (i + step) % 4) for i in range(4)])  14.8 us
    all_to_all x1, starting transfers between devices, per_device(): keys = lax.all_to_all(copies, 'y', 0, 0, tiled=True).reshape(512, 512)  9.09 us
    ppermute x5, starting transfers between devices, swapped(): return lax.ppermute(value, axis, pairs)  6.47 us
    ppermute x1, starting transfers between devices, per_device(): near = lax.ppermute(near, 'tm', [(i, i + 1) for i in range(7)])  5.6 us
    ppermute x1, starting transfers between devices, per_device(): got = lax.ppermute(sent, 'tm', [(i, i + 1) for i in range(7)])  5.17 us
    ppermute x6, starting transfers between devices, turned(): return lax.ppermute(value, RING, [(i, (i + step) % 4) for i in range(4)])  4.79 us
    pallas_call x2, Pallas kernels, compose(): call(functools.partial(compose_kernel, own), shape((16, 256, 256), BF16),...  3.83 us
    pallas_call x1, Pallas kernels, fine_own(): call(own_kernel, shape((18, PITCH, 256), F32), [VM] * 8, [pltpu.VMEM((2,...  2.62 us
  transfers between devices with their start and end apart: 15, of which 11 were waited for; matrix products, arithmetic and copies ran while one was open for 0% of the time, Pallas kernels for 17%

profile of v7, /device:TPU:96, one launch (start us, length us, event | category | flops | bytes accessed | tf_op | source)
XLA Modules:
  0.0 77.2 jit_solution(7043151392601820583)
XLA Ops:
  0.0 1.0 %edges.1 = (bf16[2,3,64,128]{3,2,1,0:T(8,128)(2,1)S(1)}, bf16[2,3,64,128]{3,2,1,0:T(8,128)(2,1)S(1)}) custom-call(s32[1]{0:T(128)} %bitcast.3.odd_ref, bf16[2,32,64,128]{3,2,1,0:T(8,128)(2,1)} %x_ref.1), custom_call_target="tpu_custom_call" | custom-call | flops 1000 | bytes 4194304 | tf_op jit(solution)/shard_map/edges/pallas_call | solution.py:402
  1.0 0.7 collective-permute-start
  1.6 4.5 %collective-permute-start.1 = (bf16[2,3,64,128]{3,2,1,0:T(8,128)(2,1)S(1)}, bf16[2,3,64,128]{3,2,1,0:T(8,128)(2,1)S(1)}, u32[]{:S(2)}, u32[]{:S(2)}) collective-permute-start(bf16[2,3,64,128]{3,2,1,0:T(8,128)(2,1)S(1)} %get-tuple-element.48), channel_id=1, source_target_pairs={{0,8},{8,0},{16,24},{24,16},{1,9},{9,1},{17,25},{25,17},{2,10},{10... | collective-permute-start | bytes 294920 | tf_op jit(solution)/shard_map/ppermute | solution.py:392
  6.1 2.0 %prepare.1 = (f32[2,32,64,128]{3,2,1,0:T(8,128)S(1)}, bf16[2,32,4,128]{3,2,1,0:T(4,128)(2,1)S(1)}, bf16[2,32,4,128]{3,2,1,0:T(4,128)(2,1)S(1)}, bf16[3,3,3,128,1...) custom-call(bf16[2,32,64,128]{3,2,1,0:T(8,128)(2,1)} %x_ref.1, f32[1,128]{1,0:T(1,128)} %bitcast.25, ...), custom_call_target="tpu_custom_call" | custom-call | flops 10000000 | bytes 4194304 | tf_op jit(solution)/shard_map/prepare/pallas_call | solution.py:139
  8.1 0.0 copy-start.9
  8.1 0.1 pad_add_fusion.flag_ref
  8.3 0.1 broadcast_select_fusion.4
  8.4 0.7 collective-permute-start.2
  9.1 0.7 collective-permute-start.3
  9.7 1.9 %compose_next.1.weight_ref = bf16[16,256,256]{2,1,0:T(8,128)(2,1)S(1)} custom-call(s32[3]{0:T(128)S(1)} %pad_add_fusion.flag_ref, bf16[3,3,3,128,128]{4,3,2,1,0:T(8,128)(2,1)S(1)} %get-tuple-element.64.conv, bf16[1024,256]{1,0:T(8,128)(2,1)S(1)} %get-tuple-element.65.down.down_ref), custom_call_target="tpu_custom_call" | custom-call | flops 900000000 | bytes 4194304 | tf_op jit(solution)/shard_map/compose_next/pallas_call | solution.py:85
  11.6 1.2 %collective-permute-done.2 = bf16[2,38,4,128]{3,2,1,0:T(4,128)(2,1)S(1)} collective-permute-done((bf16[2,38,4,128]{3,2,1,0:T(4,128)(2,1)S(1)}, bf16[2,38,4,128]{3,2,1,0:T(4,128)(2,1)S(1)}, u32[]{:S(2)}, u32[]{:S(2)}) %collective-permute-start.2) | collective-permute-done | bytes 77856 | tf_op jit(solution)/shard_map/ppermute | solution.py:392
  12.9 0.0 copy-start.3
  12.9 0.0 copy-start.4
  12.9 0.0 copy-start.5
  12.9 0.0 copy-start.6
  13.0 2.4 %fine_next.1 = (bf16[624,256]{1,0:T(8,128)(2,1)S(1)}, bf16[2,4,19,48,256]{4,3,2,1,0:T(8,128)(2,1)S(1)}) custom-call(f32[2,32,64,128]{3,2,1,0:T(8,128)S(1)} %get-tuple-element.52.act_ref, bf16[2,3,64,128]{3,2,1,0:T(8,128)(2,1)S(1)} %get-tuple-element.53.up_ref, bf16[2,3,64,128]{3,2,1,0:T(8,128)(2,1)S(1)} %get-tuple-element.54.low_ref, ...), custom_call_target="tpu_custom_call" | custom-call | flops 1800000000 | bytes 4194304 | tf_op jit(solution)/shard_map/fine_next/pallas_call | solution.py:224
  15.4 0.0 copy-start.1
  15.4 5.2 %collective-permute-start.4 = (bf16[624,256]{1,0:T(8,128)(2,1)S(1)}, bf16[624,256]{1,0:T(8,128)(2,1)S(1)}, u32[]{:S(2)}, u32[]{:S(2)}) collective-permute-start(bf16[624,256]{1,0:T(8,128)(2,1)S(1)} %get-tuple-element.63), channel_id=1, source_target_pairs={{0,32},{32,64},{64,96},{96,128},{128,160},{160,192},{192,224},{1,3... | collective-permute-start | bytes 958472 | tf_op jit(solution)/shard_map/ppermute | solution.py:432
  20.6 0.7 mix.1
  21.4 1.9 %compose_own.1.weight_ref = bf16[16,256,256]{2,1,0:T(8,128)(2,1)S(1)} custom-call(s32[3]{0:T(128)S(1)} %pad_add_fusion.flag_ref, bf16[3,3,3,128,128]{4,3,2,1,0:T(8,128)(2,1)S(1)} %get-tuple-element.64.conv, bf16[1024,256]{1,0:T(8,128)(2,1)S(1)} %get-tuple-element.65.down.down_ref), custom_call_target="tpu_custom_call" | custom-call | flops 900000000 | bytes 4194304 | tf_op jit(solution)/shard_map/compose_own/pallas_call | solution.py:85
  23.3 0.0 copy-start
  23.3 0.0 copy-start.2
  23.3 0.0 copy-start.8
  23.3 2.6 %fine_own.1.own_ref = f32[18,48,256]{2,1,0:T(8,128)S(1)} custom-call(bf16[2,32,64,128]{3,2,1,0:T(8,128)(2,1)S(1)} %copy-done.1, bf16[2,3,64,128]{3,2,1,0:T(8,128)(2,1)S(1)} %get-tuple-element.53.up_ref, bf16[2,3,64,128]{3,2,1,0:T(8,128)(2,1)S(1)} %get-tuple-element.54.low_ref, bf16[2,38,4,128]{3,2,1,0:T(4,128)(2,1)S(1)} %bitcast.22, ...), custom_call_target="tpu_custom_call" | custom-call | flops 2200000000 | bytes 4194304 | tf_op jit(solution)/shard_map/fine_own/pallas_call | solution.py:235
  26.0 1.0 %collective-permute-done.4.got_ref = bf16[624,256]{1,0:T(8,128)(2,1)S(1)} collective-permute-done((bf16[624,256]{1,0:T(8,128)(2,1)S(1)}, bf16[624,256]{1,0:T(8,128)(2,1)S(1)}, u32[]{:S(2)}, u32[]{:S(2)}) %collective-permute-start.4) | collective-permute-done | bytes 319520 | tf_op jit(solution)/shard_map/ppermute | solution.py:432
  27.0 2.5 %coarse_sent.1 = (bf16[128,512]{1,0:T(8,128)(2,1)S(1)}, bf16[128,512]{1,0:T(8,128)(2,1)S(1)}, f32[512,256]{1,0:T(8,128)S(1)}, bf16[512,2304]{1,0:T(8,128)(2,1)S(1)}, f32[2,18,48,128]{3,2,1,0:T(8,128)S(1)}) custom-call(s32[3]{0:T(128)S(1)} %pad_add_fusion.flag_ref, f32[18,48,256]{2,1,0:T(8,128)S(1)} %fine_own.1.own_ref, ...), custom_call_target="tpu_custom_call" | custom-call | flops 1500000000 | bytes 4194304 | tf_op jit(solution)/shard_map/coarse_sent/pallas_call | solution.py:309
  29.5 5.6 %collective-permute-start.5 = (bf16[128,512]{1,0:T(8,128)(2,1)S(1)}, bf16[128,512]{1,0:T(8,128)(2,1)S(1)}, u32[]{:S(2)}, u32[]{:S(2)}) collective-permute-start(bf16[128,512]{1,0:T(8,128)(2,1)S(1)} %get-tuple-element.74), channel_id=1, source_target_pairs={{0,32},{32,64},{64,96},{96,128},{128,160},{160,192},{192,224},{1,3... | collective-permute-start | bytes 393224 | tf_op jit(solution)/shard_map/ppermute | solution.py:442
  35.1 2.2 %collective-permute-start.6 = (bf16[128,512]{1,0:T(8,128)(2,1)S(1)}, bf16[128,512]{1,0:T(8,128)(2,1)S(1)}, u32[]{:S(2)}, u32[]{:S(2)}) collective-permute-start(bf16[128,512]{1,0:T(8,128)(2,1)S(1)} %get-tuple-element.75), channel_id=1, source_target_pairs={{0,64},{32,96},{64,128},{96,160},{128,192},{160,224},{1,65},{33,97... | collective-permute-start | bytes 393224 | tf_op jit(solution)/shard_map/ppermute | solution.py:441
  37.3 1.8 %coarse_here.1.own_ref = f32[128,512]{1,0:T(8,128)S(1)} custom-call(s32[3]{0:T(128)S(1)} %pad_add_fusion.flag_ref, bf16[512,2304]{1,0:T(8,128)(2,1)S(1)} %get-tuple-element.71.windows, f32[2,18,48,128]{3,2,1,0:T(8,128)S(1)} %get-tuple-element.72.reduced, f32[512,256]{1,0:T(8,128)S(1)} %get-tuple-element.73.c1_ref, bf16[3,9,256,256]{3,2,1,0:T(8,128)(2,1)S(1)} %bitcast.15, ...), custom_call_target="tpu_custom_call" | custom-call | flops 1000 | bytes 1000 | tf_op jit(solution)/shard_map/coarse_here/pallas_call | solution.py:317
  39.0 1.7 %collective-permute-done.5.near_ref = bf16[128,512]{1,0:T(8,128)(2,1)S(1)} collective-permute-done((bf16[128,512]{1,0:T(8,128)(2,1)S(1)}, bf16[128,512]{1,0:T(8,128)(2,1)S(1)}, u32[]{:S(2)}, u32[]{:S(2)}) %collective-permute-start.5) | collective-permute-done | bytes 131104 | tf_op jit(solution)/shard_map/ppermute | solution.py:442
  40.7 2.3 %collective-permute-done.6.far_ref = bf16[128,512]{1,0:T(8,128)(2,1)S(1)} collective-permute-done((bf16[128,512]{1,0:T(8,128)(2,1)S(1)}, bf16[128,512]{1,0:T(8,128)(2,1)S(1)}, u32[]{:S(2)}, u32[]{:S(2)}) %collective-permute-start.6) | collective-permute-done | bytes 131104 | tf_op jit(solution)/shard_map/ppermute | solution.py:441
  43.0 1.0 %latent.1 = (bf16[128,512]{1,0:T(8,128)(2,1)S(1)}, bf16[128,512]{1,0:T(8,128)(2,1)S(1)}, bf16[4,128,512]{2,1,0:T(8,128)(2,1)}) custom-call(f32[128,512]{1,0:T(8,128)S(1)} %coarse_here.1.own_ref, bf16[128,512]{1,0:T(8,128)(2,1)S(1)} %collective-permute-done.5.near_ref, bf16[128,512]{1,0:T(8,128)(2,1)S(1)} %collective-permute-done.6.far_ref, ...), custom_call_target="tpu_custom_call" | custom-call | flops 80000000 | bytes 4194304 | tf_op jit(solution)/shard_map/latent/pallas_call | solution.py:443
  44.0 9.1 %all-to-all-start = ((bf16[4,128,512]{2,1,0:T(8,128)(2,1)}), bf16[4,128,512]{2,1,0:T(8,128)(2,1)S(1)}, u32[]{:S(2)}, u32[]{:S(2)}) async-start(bf16[4,128,512]{2,1,0:T(8,128)(2,1)} %get-tuple-element.78), calls=%async_computation | async-start | bytes 1048576 | tf_op jit(solution)/shard_map/all_to_all | solution.py:446
  53.1 1.4 %collective-permute-start.9 = (bf16[128,512]{1,0:T(8,128)(2,1)S(1)}, bf16[128,512]{1,0:T(8,128)(2,1)S(1)}, u32[]{:S(2)}, u32[]{:S(2)}) collective-permute-start(bf16[128,512]{1,0:T(8,128)(2,1)S(1)} %get-tuple-element.77.mine_ref), channel_id=1, source_target_pairs={{0,16},{1,17},{16,0},{17,1},{2,18},{3,19},{18,2},{19,3},{4,20},{5,... | collective-permute-start | bytes 393224 | tf_op jit(solution)/shard_map/ppermute | solution.py:396
  54.5 6.8 %collective-permute-done.8.q1_ref = bf16[128,512]{1,0:T(8,128)(2,1)S(1)} collective-permute-done((bf16[128,512]{1,0:T(8,128)(2,1)S(1)}, bf16[128,512]{1,0:T(8,128)(2,1)S(1)}, u32[]{:S(2)}, u32[]{:S(2)}) %collective-permute-start.8) | collective-permute-done | bytes 131104 | tf_op jit(solution)/shard_map/ppermute | solution.py:396
  61.3 0.5 all-to-all-done
  61.8 1.0 %collective-permute-start.7 = (bf16[128,512]{1,0:T(8,128)(2,1)S(1)}, bf16[128,512]{1,0:T(8,128)(2,1)S(1)}, u32[]{:S(2)}, u32[]{:S(2)}) collective-permute-start(bf16[128,512]{1,0:T(8,128)(2,1)S(1)} %get-tuple-element.77.mine_ref), channel_id=1, source_target_pairs={{0,17},{1,0},{16,1},{17,16},{2,19},{3,2},{18,3},{19,18},{4,21},{5,... | collective-permute-start | bytes 393224 | tf_op jit(solution)/shard_map/ppermute | solution.py:396
  62.8 0.9 %collective-permute-done.10.other_keys_ref = bf16[512,512]{1,0:T(8,128)(2,1)S(1)} collective-permute-done((bf16[512,512]{1,0:T(8,128)(2,1)S(1)}, bf16[512,512]{1,0:T(8,128)(2,1)S(1)}, u32[]{:S(2)}, u32[]{:S(2)}) %collective-permute-start.10) | collective-permute-done | bytes 524320 | tf_op jit(solution)/shard_map/ppermute | solution.py:392
  63.7 1.0 %attend_two.1 = (bf16[144,512]{1,0:T(8,128)(2,1)S(1)}, bf16[144,512]{1,0:T(8,128)(2,1)S(1)}) custom-call(bf16[128,512]{1,0:T(8,128)(2,1)S(1)} %collective-permute-done.8.q1_ref, bf16[128,512]{1,0:T(8,128)(2,1)S(1)} %collective-permute-done.9.q2_ref, bf16[512,512]{1,0:T(8,128)(2,1)S(1)} %bitcast.17, bf16[512,512]{1,0:T(8,128)(2,1)S(1)} %collective-permute-done.10.other_keys_ref), custom_call_target="tpu_custom_call" | custom-call | flops 550000000 | bytes 4194304 | tf_op jit(solution)/shard_map/attend_two/pallas_call | solution.py:451
  64.7 1.1 %collective-permute-start.11 = (bf16[144,512]{1,0:T(8,128)(2,1)S(1)}, bf16[144,512]{1,0:T(8,128)(2,1)S(1)}, u32[]{:S(2)}, u32[]{:S(2)}) collective-permute-start(bf16[144,512]{1,0:T(8,128)(2,1)S(1)} %get-tuple-element.84), channel_id=1, source_target_pairs={{0,17},{1,0},{16,1},{17,16},{2,19},{3,2},{18,3},{19,18},{4,21},{5,... | collective-permute-start | bytes 442376 | tf_op jit(solution)/shard_map/ppermute | solution.py:396
  65.8 1.2 %collective-permute-start.12 = (bf16[144,512]{1,0:T(8,128)(2,1)S(1)}, bf16[144,512]{1,0:T(8,128)(2,1)S(1)}, u32[]{:S(2)}, u32[]{:S(2)}) collective-permute-start(bf16[144,512]{1,0:T(8,128)(2,1)S(1)} %get-tuple-element.85), channel_id=1, source_target_pairs={{0,16},{1,17},{16,0},{17,1},{2,18},{3,19},{18,2},{19,3},{4,20},{5,... | collective-permute-start | bytes 442376 | tf_op jit(solution)/shard_map/ppermute | solution.py:396
  67.0 0.9 %collective-permute-done.7.q3_ref = bf16[128,512]{1,0:T(8,128)(2,1)S(1)} collective-permute-done((bf16[128,512]{1,0:T(8,128)(2,1)S(1)}, bf16[128,512]{1,0:T(8,128)(2,1)S(1)}, u32[]{:S(2)}, u32[]{:S(2)}) %collective-permute-start.7) | collective-permute-done | bytes 131104 | tf_op jit(solution)/shard_map/ppermute | solution.py:396
  67.9 1.0 %attend_last.1 = (bf16[144,512]{1,0:T(8,128)(2,1)S(1)}, f32[128,512]{1,0:T(8,128)S(1)}, f32[128,128]{1,0:T(8,128)S(1)}) custom-call(bf16[128,512]{1,0:T(8,128)(2,1)S(1)} %collective-permute-done.7.q3_ref, bf16[128,512]{1,0:T(8,128)(2,1)S(1)} %get-tuple-element.77.mine_ref, bf16[512,512]{1,0:T(8,128)(2,1)S(1)} %bitcast.18, ...), custom_call_target="tpu_custom_call" | custom-call | flops 550000000 | bytes 4194304 | tf_op jit(solution)/shard_map/attend_last/pallas_call | solution.py:454
  68.9 0.1 collective-permute-start.13
  68.9 2.5 %collective-permute-done.11.got1_ref = bf16[144,512]{1,0:T(8,128)(2,1)S(1)} collective-permute-done((bf16[144,512]{1,0:T(8,128)(2,1)S(1)}, bf16[144,512]{1,0:T(8,128)(2,1)S(1)}, u32[]{:S(2)}, u32[]{:S(2)}) %collective-permute-start.11) | collective-permute-done | bytes 147488 | tf_op jit(solution)/shard_map/ppermute | solution.py:396
  71.5 1.5 %collective-permute-done.12.got2_ref = bf16[144,512]{1,0:T(8,128)(2,1)S(1)} collective-permute-done((bf16[144,512]{1,0:T(8,128)(2,1)S(1)}, bf16[144,512]{1,0:T(8,128)(2,1)S(1)}, u32[]{:S(2)}, u32[]{:S(2)}) %collective-permute-start.12) | collective-permute-done | bytes 147488 | tf_op jit(solution)/shard_map/ppermute | solution.py:396
  73.0 3.1 %collective-permute-done.13.got3_ref = bf16[144,512]{1,0:T(8,128)(2,1)S(1)} collective-permute-done((bf16[144,512]{1,0:T(8,128)(2,1)S(1)}, bf16[144,512]{1,0:T(8,128)(2,1)S(1)}, u32[]{:S(2)}, u32[]{:S(2)}) %collective-permute-start.13) | collective-permute-done | bytes 147488 | tf_op jit(solution)/shard_map/ppermute | solution.py:396
  76.1 1.1 %finish.1 = bf16[128,512]{1,0:T(8,128)(2,1)} custom-call(f32[128,512]{1,0:T(8,128)S(1)} %get-tuple-element.80.mixed_ref, f32[128,128]{1,0:T(8,128)S(1)} %get-tuple-element.81.level_ref, bf16[144,512]{1,0:T(8,128)(2,1)S(1)} %collective-permute-done.11.got1_ref, bf16[144,512]{1,0:T(8,128)(2,1)S(1)} %collective-permute-done.12.got2_ref, ...), custom_call_target="tpu_custom_call" | custom-call | flops 70000000 | bytes 4194304 | tf_op jit(solution)/shard_map/finish/pallas_call | solution.py:463
  (20 shorter events, 0.1 us)
Async XLA Ops:
  1.0 7.2 %collective-permute-start = (bf16[2,3,64,128]{3,2,1,0:T(8,128)(2,1)S(1)}, bf16[2,3,64,128]{3,2,1,0:T(8,128)(2,1)S(1)}, u32[]{:S(2)}, u32[]{:S(2)}) collective-permute-start(bf16[2,3,64,128]{3,2,1,0:T(8,128)(2,1)S(1)} %get-tuple-element.47), channel_id=1, source_target_pairs={{8,16},{16,8},{9,17},{17,9},{10,18},{18,10},{11,19},{19,11},{12,20... | collective-permute-start | bytes 294920 | tf_op jit(solution)/shard_map/ppermute | solution.py:392
  1.6 6.6 %collective-permute-start.1 = (bf16[2,3,64,128]{3,2,1,0:T(8,128)(2,1)S(1)}, bf16[2,3,64,128]{3,2,1,0:T(8,128)(2,1)S(1)}, u32[]{:S(2)}, u32[]{:S(2)}) collective-permute-start(bf16[2,3,64,128]{3,2,1,0:T(8,128)(2,1)S(1)} %get-tuple-element.48), channel_id=1, source_target_pairs={{0,8},{8,0},{16,24},{24,16},{1,9},{9,1},{17,25},{25,17},{2,10},{10... | collective-permute-start | bytes 294920 | tf_op jit(solution)/shard_map/ppermute | solution.py:392
  8.1 4.8 %copy-start.9 = (f32[128]{0:T(128)S(1)}, f32[128]{0:T(128)}, u32[]{:S(2)}) copy-start(f32[128]{0:T(128)} %param.13) | copy-start | bytes 1540
  8.4 4.5 %collective-permute-start.2 = (bf16[2,38,4,128]{3,2,1,0:T(4,128)(2,1)S(1)}, bf16[2,38,4,128]{3,2,1,0:T(4,128)(2,1)S(1)}, u32[]{:S(2)}, u32[]{:S(2)}) collective-permute-start(bf16[2,38,4,128]{3,2,1,0:T(4,128)(2,1)S(1)} %get-tuple-element.94), channel_id=1, source_target_pairs={{0,1},{1,0},{2,3},{3,2},{4,5},{5,4},{6,7},{7,6},{8,9},{9,8},{10,11... | collective-permute-start | bytes 233480 | tf_op jit(solution)/shard_map/ppermute | solution.py:392
  9.1 3.8 %collective-permute-start.3 = (bf16[2,38,4,128]{3,2,1,0:T(4,128)(2,1)S(1)}, bf16[2,38,4,128]{3,2,1,0:T(4,128)(2,1)S(1)}, u32[]{:S(2)}, u32[]{:S(2)}) collective-permute-start(bf16[2,38,4,128]{3,2,1,0:T(4,128)(2,1)S(1)} %get-tuple-element.93), channel_id=1, source_target_pairs={{1,2},{2,1},{3,4},{4,3},{5,6},{6,5},{9,10},{10,9},{11,12},{12,11},... | collective-permute-start | bytes 233480 | tf_op jit(solution)/shard_map/ppermute | solution.py:392
  12.9 7.7 %copy-start.3 = (bf16[512,512]{1,0:T(8,128)(2,1)S(1)}, bf16[512,512]{1,0:T(8,128)(2,1)}, u32[]{:S(2)}) copy-start(bf16[512,512]{1,0:T(8,128)(2,1)} %query_ref.1) | copy-start | bytes 1572868
  12.9 7.7 %copy-start.4 = (bf16[512,512]{1,0:T(8,128)(2,1)S(1)}, bf16[512,512]{1,0:T(8,128)(2,1)}, u32[]{:S(2)}) copy-start(bf16[512,512]{1,0:T(8,128)(2,1)} %key_ref.1) | copy-start | bytes 1572868
  12.9 7.7 %copy-start.5 = (bf16[512,512]{1,0:T(8,128)(2,1)S(1)}, bf16[512,512]{1,0:T(8,128)(2,1)}, u32[]{:S(2)}) copy-start(bf16[512,512]{1,0:T(8,128)(2,1)} %value_ref.1) | copy-start | bytes 1572868
  12.9 7.7 %copy-start.6 = (bf16[512,512]{1,0:T(8,128)(2,1)S(1)}, bf16[512,512]{1,0:T(8,128)(2,1)}, u32[]{:S(2)}) copy-start(bf16[512,512]{1,0:T(8,128)(2,1)} %out_ref.1) | copy-start | bytes 1572868
  15.4 7.9 %copy-start.1 = (bf16[2,32,64,128]{3,2,1,0:T(8,128)(2,1)S(1)}, bf16[2,32,64,128]{3,2,1,0:T(8,128)(2,1)}, u32[]{:S(2)}) copy-start(bf16[2,32,64,128]{3,2,1,0:T(8,128)(2,1)} %x_ref.1) | copy-start | bytes 3145732
  15.4 11.6 %collective-permute-start.4 = (bf16[624,256]{1,0:T(8,128)(2,1)S(1)}, bf16[624,256]{1,0:T(8,128)(2,1)S(1)}, u32[]{:S(2)}, u32[]{:S(2)}) collective-permute-start(bf16[624,256]{1,0:T(8,128)(2,1)S(1)} %get-tuple-element.63), channel_id=1, source_target_pairs={{0,32},{32,64},{64,96},{96,128},{128,160},{160,192},{192,224},{1,3... | collective-permute-start | bytes 958472 | tf_op jit(solution)/shard_map/ppermute | solution.py:432
  23.3 3.7 %copy-start = (bf16[3,3,3,256,256]{4,3,2,1,0:T(8,128)(2,1)S(1)}, bf16[3,3,3,256,256]{4,3,2,1,0:T(8,128)(2,1)}, u32[]{:S(2)}) copy-start(bf16[3,3,3,256,256]{4,3,2,1,0:T(8,128)(2,1)} %param.17) | copy-start | bytes 10616836
  23.3 3.7 %copy-start.2 = (bf16[1024,512]{1,0:T(8,128)(2,1)S(1)}, bf16[1024,512]{1,0:T(8,128)(2,1)}, u32[]{:S(2)}) copy-start(bf16[1024,512]{1,0:T(8,128)(2,1)} %down_ref.3) | copy-start | bytes 3145732
  23.3 3.6 %copy-start.8 = (f32[256]{0:T(256)S(1)}, f32[256]{0:T(256)}, u32[]{:S(2)}) copy-start(f32[256]{0:T(256)} %param.16) | copy-start | bytes 3076
  29.5 11.2 %collective-permute-start.5 = (bf16[128,512]{1,0:T(8,128)(2,1)S(1)}, bf16[128,512]{1,0:T(8,128)(2,1)S(1)}, u32[]{:S(2)}, u32[]{:S(2)}) collective-permute-start(bf16[128,512]{1,0:T(8,128)(2,1)S(1)} %get-tuple-element.74), channel_id=1, source_target_pairs={{0,32},{32,64},{64,96},{96,128},{128,160},{160,192},{192,224},{1,3... | collective-permute-start | bytes 393224 | tf_op jit(solution)/shard_map/ppermute | solution.py:442
  35.1 8.0 %collective-permute-start.6 = (bf16[128,512]{1,0:T(8,128)(2,1)S(1)}, bf16[128,512]{1,0:T(8,128)(2,1)S(1)}, u32[]{:S(2)}, u32[]{:S(2)}) collective-permute-start(bf16[128,512]{1,0:T(8,128)(2,1)S(1)} %get-tuple-element.75), channel_id=1, source_target_pairs={{0,64},{32,96},{64,128},{96,160},{128,192},{160,224},{1,65},{33,97... | collective-permute-start | bytes 393224 | tf_op jit(solution)/shard_map/ppermute | solution.py:441
  37.3 5.8 %copy-start.7 = (f32[512]{0:T(512)S(1)}, f32[512]{0:T(512)}, u32[]{:S(2)}) copy-start(f32[512]{0:T(512)} %param.19) | copy-start | bytes 6148
  44.0 17.8 %all-to-all-start = ((bf16[4,128,512]{2,1,0:T(8,128)(2,1)}), bf16[4,128,512]{2,1,0:T(8,128)(2,1)S(1)}, u32[]{:S(2)}, u32[]{:S(2)}) async-start(bf16[4,128,512]{2,1,0:T(8,128)(2,1)} %get-tuple-element.78), calls=%async_computation | async-start | bytes 1048576 | tf_op jit(solution)/shard_map/all_to_all | solution.py:446
  53.1 8.2 %collective-permute-start.8 = (bf16[128,512]{1,0:T(8,128)(2,1)S(1)}, bf16[128,512]{1,0:T(8,128)(2,1)S(1)}, u32[]{:S(2)}, u32[]{:S(2)}) collective-permute-start(bf16[128,512]{1,0:T(8,128)(2,1)S(1)} %get-tuple-element.77.mine_ref), channel_id=1, source_target_pairs={{0,1},{1,16},{16,17},{17,0},{2,3},{3,18},{18,19},{19,2},{4,5},{5,2... | collective-permute-start | bytes 393224 | tf_op jit(solution)/shard_map/ppermute | solution.py:396
  53.1 8.2 %collective-permute-start.9 = (bf16[128,512]{1,0:T(8,128)(2,1)S(1)}, bf16[128,512]{1,0:T(8,128)(2,1)S(1)}, u32[]{:S(2)}, u32[]{:S(2)}) collective-permute-start(bf16[128,512]{1,0:T(8,128)(2,1)S(1)} %get-tuple-element.77.mine_ref), channel_id=1, source_target_pairs={{0,16},{1,17},{16,0},{17,1},{2,18},{3,19},{18,2},{19,3},{4,20},{5,... | collective-permute-start | bytes 393224 | tf_op jit(solution)/shard_map/ppermute | solution.py:396
  61.8 1.9 %collective-permute-start.10 = (bf16[512,512]{1,0:T(8,128)(2,1)S(1)}, bf16[512,512]{1,0:T(8,128)(2,1)S(1)}, u32[]{:S(2)}, u32[]{:S(2)}) collective-permute-start(bf16[512,512]{1,0:T(8,128)(2,1)S(1)} %bitcast.16), channel_id=1, source_target_pairs={{0,8},{8,0},{1,9},{9,1},{2,10},{10,2},{3,11},{11,3},{4,12},{12,4},... | collective-permute-start | bytes 1572872 | tf_op jit(solution)/shard_map/ppermute | solution.py:392
  61.8 6.1 %collective-permute-start.7 = (bf16[128,512]{1,0:T(8,128)(2,1)S(1)}, bf16[128,512]{1,0:T(8,128)(2,1)S(1)}, u32[]{:S(2)}, u32[]{:S(2)}) collective-permute-start(bf16[128,512]{1,0:T(8,128)(2,1)S(1)} %get-tuple-element.77.mine_ref), channel_id=1, source_target_pairs={{0,17},{1,0},{16,1},{17,16},{2,19},{3,2},{18,3},{19,18},{4,21},{5,... | collective-permute-start | bytes 393224 | tf_op jit(solution)/shard_map/ppermute | solution.py:396
  64.7 6.8 %collective-permute-start.11 = (bf16[144,512]{1,0:T(8,128)(2,1)S(1)}, bf16[144,512]{1,0:T(8,128)(2,1)S(1)}, u32[]{:S(2)}, u32[]{:S(2)}) collective-permute-start(bf16[144,512]{1,0:T(8,128)(2,1)S(1)} %get-tuple-element.84), channel_id=1, source_target_pairs={{0,17},{1,0},{16,1},{17,16},{2,19},{3,2},{18,3},{19,18},{4,21},{5,... | collective-permute-start | bytes 442376 | tf_op jit(solution)/shard_map/ppermute | solution.py:396
  65.8 7.2 %collective-permute-start.12 = (bf16[144,512]{1,0:T(8,128)(2,1)S(1)}, bf16[144,512]{1,0:T(8,128)(2,1)S(1)}, u32[]{:S(2)}, u32[]{:S(2)}) collective-permute-start(bf16[144,512]{1,0:T(8,128)(2,1)S(1)} %get-tuple-element.85), channel_id=1, source_target_pairs={{0,16},{1,17},{16,0},{17,1},{2,18},{3,19},{18,2},{19,3},{4,20},{5,... | collective-permute-start | bytes 442376 | tf_op jit(solution)/shard_map/ppermute | solution.py:396
  68.9 7.2 %collective-permute-start.13 = (bf16[144,512]{1,0:T(8,128)(2,1)S(1)}, bf16[144,512]{1,0:T(8,128)(2,1)S(1)}, u32[]{:S(2)}, u32[]{:S(2)}) collective-permute-start(bf16[144,512]{1,0:T(8,128)(2,1)S(1)} %get-tuple-element.86), channel_id=1, source_target_pairs={{0,1},{1,16},{16,17},{17,0},{2,3},{3,18},{18,19},{19,2},{4,5},{5,2... | collective-permute-start | bytes 442376 | tf_op jit(solution)/shard_map/ppermute | solution.py:396

commit v8 on v7

--- a/solution.py
+++ b/solution.py
@@ -444,22 +444,21 @@
         latent_kernel, (rows, rows, shape((4, 128, 512), BF16)), [VM] * 5, flops=80_000_000, name="latent"
     )(latent_own, near, far, gain_latent.reshape(1, 512), w_score)
     keys = lax.all_to_all(copies, "y", 0, 0, tiled=True).reshape(512, 512)
-    asked = [turned(query, step) for step in (1, 2, 3)]
-    keys, asked[0], asked[1] = lax.optimization_barrier((keys, asked[0], asked[1]))
+    two, back, ahead = (turned(query, step) for step in (2, 3, 1))
+    keys, two, back = lax.optimization_barrier((keys, two, back))
     other_keys = swapped(keys, "core", 2, 0)
     block = shape((144, 512), BF16)
-    sent1, sent2 = call(attend_two_kernel, (block, block), [VM] * 4, flops=550_000_000, name="attend_two")(
-        asked[0], asked[1], keys, other_keys
+    sent_two, sent_back = call(attend_two_kernel, (block, block), [VM] * 4, flops=550_000_000, name="attend_two")(
+        two, back, keys, other_keys
     )
-    sent3, mixed, level = call(
+    sent_ahead, mixed, level = call(
         attend_last_kernel,
         (block, shape((128, 512), F32), shape((128, 128), F32)),
         [VM] * 4,
         flops=550_000_000,
         name="attend_last",
-    )(asked[2], query, keys, other_keys)
-    sent = (sent1, sent2, sent3)
-    got = [turned(block, -step) for step, block in zip((1, 2, 3), sent)]
+    )(ahead, query, keys, other_keys)
+    got = [turned(part, -step) for step, part in ((2, sent_two), (3, sent_back), (1, sent_ahead))]
     out = call(finish_kernel, rows, [VM] * 7, flops=70_000_000, name="finish")(mixed, level, *got, latent_in, w_mix)
     return out.reshape(1, 8, 16, 512)
 

time: 78.3 us -> 76.9 us (0.982); the launches traced: 77.2 us -> 76.6 us
    ppermute x6, waiting for transfers between devices: 14.8 us -> 12 us  [turned(): return lax.ppermute(value, RING, [(i, (i + step) % 4) for i in range(4)])]
    all_to_all x1, waiting for transfers between devices: 0.5 us -> 2.23 us  [per_device(): keys = lax.all_to_all(copies, 'y', 0, 0, tiled=True).reshape(512, 512)]
    ppermute x5, waiting for transfers between devices: 2.13 us -> 3.13 us  [swapped(): return lax.ppermute(value, axis, pairs)]
where the time goes in v8:
time: 76.9 us; the launch traced here: 76.6 us
  starting transfers between devices  32.8 us (43%)
  waiting for transfers between devices  22.3 us (29%)
  Pallas kernels  20.9 us (27%)
    ppermute x6, waiting for transfers between devices, turned(): return lax.ppermute(value, RING, [(i, (i + step) % 4) for i in range(4)])  12 us
    all_to_all x1, starting transfers between devices, per_device(): keys = lax.all_to_all(copies, 'y', 0, 0, tiled=True).reshape(512, 512)  9.09 us
    ppermute x5, starting transfers between devices, swapped(): return lax.ppermute(value, axis, pairs)  6.47 us
    ppermute x1, starting transfers between devices, per_device(): near = lax.ppermute(near, 'tm', [(i, i + 1) for i in range(7)])  5.6 us
    ppermute x1, starting transfers between devices, per_device(): got = lax.ppermute(sent, 'tm', [(i, i + 1) for i in range(7)])  5.17 us
    ppermute x6, starting transfers between devices, turned(): return lax.ppermute(value, RING, [(i, (i + step) % 4) for i in range(4)])  4.29 us
    pallas_call x2, Pallas kernels, compose(): call(functools.partial(compose_kernel, own), shape((16, 256, 256), BF16),...  3.83 us
    ppermute x5, waiting for transfers between devices, swapped(): return lax.ppermute(value, axis, pairs)  3.13 us
  transfers between devices with their start and end apart: 15, of which 11 were waited for; matrix products, arithmetic and copies ran while one was open for 0% of the time, Pallas kernels for 17%

profile of v8, /device:TPU:96, one launch (start us, length us, event | category | flops | bytes accessed | tf_op | source)
XLA Modules:
  0.0 76.6 jit_solution(12180274683322009305)
XLA Ops:
  0.0 1.0 %edges.1 = (bf16[2,3,64,128]{3,2,1,0:T(8,128)(2,1)S(1)}, bf16[2,3,64,128]{3,2,1,0:T(8,128)(2,1)S(1)}) custom-call(s32[1]{0:T(128)} %bitcast.3.odd_ref, bf16[2,32,64,128]{3,2,1,0:T(8,128)(2,1)} %x_ref.1), custom_call_target="tpu_custom_call" | custom-call | flops 1000 | bytes 4194304 | tf_op jit(solution)/shard_map/edges/pallas_call | solution.py:402
  1.0 0.7 collective-permute-start
  1.6 4.5 %collective-permute-start.1 = (bf16[2,3,64,128]{3,2,1,0:T(8,128)(2,1)S(1)}, bf16[2,3,64,128]{3,2,1,0:T(8,128)(2,1)S(1)}, u32[]{:S(2)}, u32[]{:S(2)}) collective-permute-start(bf16[2,3,64,128]{3,2,1,0:T(8,128)(2,1)S(1)} %get-tuple-element.48), channel_id=1, source_target_pairs={{0,8},{8,0},{16,24},{24,16},{1,9},{9,1},{17,25},{25,17},{2,10},{10... | collective-permute-start | bytes 294920 | tf_op jit(solution)/shard_map/ppermute | solution.py:392
  6.1 2.0 %prepare.1 = (f32[2,32,64,128]{3,2,1,0:T(8,128)S(1)}, bf16[2,32,4,128]{3,2,1,0:T(4,128)(2,1)S(1)}, bf16[2,32,4,128]{3,2,1,0:T(4,128)(2,1)S(1)}, bf16[3,3,3,128,1...) custom-call(bf16[2,32,64,128]{3,2,1,0:T(8,128)(2,1)} %x_ref.1, f32[1,128]{1,0:T(1,128)} %bitcast.25, ...), custom_call_target="tpu_custom_call" | custom-call | flops 10000000 | bytes 4194304 | tf_op jit(solution)/shard_map/prepare/pallas_call | solution.py:139
  8.1 0.0 copy-start.9
  8.1 0.1 pad_add_fusion.flag_ref
  8.3 0.1 broadcast_select_fusion.4
  8.4 0.7 collective-permute-start.2
  9.1 0.7 collective-permute-start.3
  9.7 1.9 %compose_next.1.weight_ref = bf16[16,256,256]{2,1,0:T(8,128)(2,1)S(1)} custom-call(s32[3]{0:T(128)S(1)} %pad_add_fusion.flag_ref, bf16[3,3,3,128,128]{4,3,2,1,0:T(8,128)(2,1)S(1)} %get-tuple-element.64.conv, bf16[1024,256]{1,0:T(8,128)(2,1)S(1)} %get-tuple-element.65.down.down_ref), custom_call_target="tpu_custom_call" | custom-call | flops 900000000 | bytes 4194304 | tf_op jit(solution)/shard_map/compose_next/pallas_call | solution.py:85
  11.6 1.2 %collective-permute-done.2 = bf16[2,38,4,128]{3,2,1,0:T(4,128)(2,1)S(1)} collective-permute-done((bf16[2,38,4,128]{3,2,1,0:T(4,128)(2,1)S(1)}, bf16[2,38,4,128]{3,2,1,0:T(4,128)(2,1)S(1)}, u32[]{:S(2)}, u32[]{:S(2)}) %collective-permute-start.2) | collective-permute-done | bytes 77856 | tf_op jit(solution)/shard_map/ppermute | solution.py:392
  12.9 0.0 copy-start.3
  12.9 0.0 copy-start.4
  12.9 0.0 copy-start.5
  12.9 0.0 copy-start.6
  13.0 2.4 %fine_next.1 = (bf16[624,256]{1,0:T(8,128)(2,1)S(1)}, bf16[2,4,19,48,256]{4,3,2,1,0:T(8,128)(2,1)S(1)}) custom-call(f32[2,32,64,128]{3,2,1,0:T(8,128)S(1)} %get-tuple-element.52.act_ref, bf16[2,3,64,128]{3,2,1,0:T(8,128)(2,1)S(1)} %get-tuple-element.53.up_ref, bf16[2,3,64,128]{3,2,1,0:T(8,128)(2,1)S(1)} %get-tuple-element.54.low_ref, ...), custom_call_target="tpu_custom_call" | custom-call | flops 1800000000 | bytes 4194304 | tf_op jit(solution)/shard_map/fine_next/pallas_call | solution.py:224
  15.4 0.0 copy-start.1
  15.4 5.2 %collective-permute-start.4 = (bf16[624,256]{1,0:T(8,128)(2,1)S(1)}, bf16[624,256]{1,0:T(8,128)(2,1)S(1)}, u32[]{:S(2)}, u32[]{:S(2)}) collective-permute-start(bf16[624,256]{1,0:T(8,128)(2,1)S(1)} %get-tuple-element.63), channel_id=1, source_target_pairs={{0,32},{32,64},{64,96},{96,128},{128,160},{160,192},{192,224},{1,3... | collective-permute-start | bytes 958472 | tf_op jit(solution)/shard_map/ppermute | solution.py:432
  20.6 0.7 mix.1
  21.4 1.9 %compose_own.1.weight_ref = bf16[16,256,256]{2,1,0:T(8,128)(2,1)S(1)} custom-call(s32[3]{0:T(128)S(1)} %pad_add_fusion.flag_ref, bf16[3,3,3,128,128]{4,3,2,1,0:T(8,128)(2,1)S(1)} %get-tuple-element.64.conv, bf16[1024,256]{1,0:T(8,128)(2,1)S(1)} %get-tuple-element.65.down.down_ref), custom_call_target="tpu_custom_call" | custom-call | flops 900000000 | bytes 4194304 | tf_op jit(solution)/shard_map/compose_own/pallas_call | solution.py:85
  23.3 0.0 copy-start
  23.3 0.0 copy-start.8
  23.3 2.6 %fine_own.1.own_ref = f32[18,48,256]{2,1,0:T(8,128)S(1)} custom-call(bf16[2,32,64,128]{3,2,1,0:T(8,128)(2,1)S(1)} %copy-done.1, bf16[2,3,64,128]{3,2,1,0:T(8,128)(2,1)S(1)} %get-tuple-element.53.up_ref, bf16[2,3,64,128]{3,2,1,0:T(8,128)(2,1)S(1)} %get-tuple-element.54.low_ref, bf16[2,38,4,128]{3,2,1,0:T(4,128)(2,1)S(1)} %bitcast.22, ...), custom_call_target="tpu_custom_call" | custom-call | flops 2200000000 | bytes 4194304 | tf_op jit(solution)/shard_map/fine_own/pallas_call | solution.py:235
  26.0 1.0 %collective-permute-done.4.got_ref = bf16[624,256]{1,0:T(8,128)(2,1)S(1)} collective-permute-done((bf16[624,256]{1,0:T(8,128)(2,1)S(1)}, bf16[624,256]{1,0:T(8,128)(2,1)S(1)}, u32[]{:S(2)}, u32[]{:S(2)}) %collective-permute-start.4) | collective-permute-done | bytes 319520 | tf_op jit(solution)/shard_map/ppermute | solution.py:432
  27.0 2.5 %coarse_sent.1 = (bf16[128,512]{1,0:T(8,128)(2,1)S(1)}, bf16[128,512]{1,0:T(8,128)(2,1)S(1)}, f32[512,256]{1,0:T(8,128)S(1)}, bf16[512,2304]{1,0:T(8,128)(2,1)S(1)}, f32[2,18,48,128]{3,2,1,0:T(8,128)S(1)}) custom-call(s32[3]{0:T(128)S(1)} %pad_add_fusion.flag_ref, f32[18,48,256]{2,1,0:T(8,128)S(1)} %fine_own.1.own_ref, ...), custom_call_target="tpu_custom_call" | custom-call | flops 1500000000 | bytes 4194304 | tf_op jit(solution)/shard_map/coarse_sent/pallas_call | solution.py:309
  29.5 5.6 %collective-permute-start.5 = (bf16[128,512]{1,0:T(8,128)(2,1)S(1)}, bf16[128,512]{1,0:T(8,128)(2,1)S(1)}, u32[]{:S(2)}, u32[]{:S(2)}) collective-permute-start(bf16[128,512]{1,0:T(8,128)(2,1)S(1)} %get-tuple-element.74), channel_id=1, source_target_pairs={{0,32},{32,64},{64,96},{96,128},{128,160},{160,192},{192,224},{1,3... | collective-permute-start | bytes 393224 | tf_op jit(solution)/shard_map/ppermute | solution.py:442
  35.1 2.2 %collective-permute-start.6 = (bf16[128,512]{1,0:T(8,128)(2,1)S(1)}, bf16[128,512]{1,0:T(8,128)(2,1)S(1)}, u32[]{:S(2)}, u32[]{:S(2)}) collective-permute-start(bf16[128,512]{1,0:T(8,128)(2,1)S(1)} %get-tuple-element.75), channel_id=1, source_target_pairs={{0,64},{32,96},{64,128},{96,160},{128,192},{160,224},{1,65},{33,97... | collective-permute-start | bytes 393224 | tf_op jit(solution)/shard_map/ppermute | solution.py:441
  37.3 0.0 copy-start.7
  37.3 1.8 %coarse_here.1.own_ref = f32[128,512]{1,0:T(8,128)S(1)} custom-call(s32[3]{0:T(128)S(1)} %pad_add_fusion.flag_ref, bf16[512,2304]{1,0:T(8,128)(2,1)S(1)} %get-tuple-element.71.windows, f32[2,18,48,128]{3,2,1,0:T(8,128)S(1)} %get-tuple-element.72.reduced, f32[512,256]{1,0:T(8,128)S(1)} %get-tuple-element.73.c1_ref, bf16[3,9,256,256]{3,2,1,0:T(8,128)(2,1)S(1)} %bitcast.15, ...), custom_call_target="tpu_custom_call" | custom-call | flops 1000 | bytes 1000 | tf_op jit(solution)/shard_map/coarse_here/pallas_call | solution.py:317
  39.0 1.7 %collective-permute-done.5.near_ref = bf16[128,512]{1,0:T(8,128)(2,1)S(1)} collective-permute-done((bf16[128,512]{1,0:T(8,128)(2,1)S(1)}, bf16[128,512]{1,0:T(8,128)(2,1)S(1)}, u32[]{:S(2)}, u32[]{:S(2)}) %collective-permute-start.5) | collective-permute-done | bytes 131104 | tf_op jit(solution)/shard_map/ppermute | solution.py:442
  40.7 2.3 %collective-permute-done.6.far_ref = bf16[128,512]{1,0:T(8,128)(2,1)S(1)} collective-permute-done((bf16[128,512]{1,0:T(8,128)(2,1)S(1)}, bf16[128,512]{1,0:T(8,128)(2,1)S(1)}, u32[]{:S(2)}, u32[]{:S(2)}) %collective-permute-start.6) | collective-permute-done | bytes 131104 | tf_op jit(solution)/shard_map/ppermute | solution.py:441
  43.0 1.0 %latent.1 = (bf16[128,512]{1,0:T(8,128)(2,1)S(1)}, bf16[128,512]{1,0:T(8,128)(2,1)S(1)}, bf16[4,128,512]{2,1,0:T(8,128)(2,1)}) custom-call(f32[128,512]{1,0:T(8,128)S(1)} %coarse_here.1.own_ref, bf16[128,512]{1,0:T(8,128)(2,1)S(1)} %collective-permute-done.5.near_ref, bf16[128,512]{1,0:T(8,128)(2,1)S(1)} %collective-permute-done.6.far_ref, ...), custom_call_target="tpu_custom_call" | custom-call | flops 80000000 | bytes 4194304 | tf_op jit(solution)/shard_map/latent/pallas_call | solution.py:443
  44.0 9.1 %all-to-all-start = ((bf16[4,128,512]{2,1,0:T(8,128)(2,1)}), bf16[4,128,512]{2,1,0:T(8,128)(2,1)S(1)}, u32[]{:S(2)}, u32[]{:S(2)}) async-start(bf16[4,128,512]{2,1,0:T(8,128)(2,1)} %get-tuple-element.78), calls=%async_computation | async-start | bytes 1048576 | tf_op jit(solution)/shard_map/all_to_all | solution.py:446
  53.1 0.6 collective-permute-start.8
  53.7 1.3 %collective-permute-start.9 = (bf16[128,512]{1,0:T(8,128)(2,1)S(1)}, bf16[128,512]{1,0:T(8,128)(2,1)S(1)}, u32[]{:S(2)}, u32[]{:S(2)}) collective-permute-start(bf16[128,512]{1,0:T(8,128)(2,1)S(1)} %get-tuple-element.77.mine_ref), channel_id=1, source_target_pairs={{0,17},{1,0},{16,1},{17,16},{2,19},{3,2},{18,3},{19,18},{4,21},{5,... | collective-permute-start | bytes 393224 | tf_op jit(solution)/shard_map/ppermute | solution.py:396
  55.0 4.5 %collective-permute-done.8.q1_ref = bf16[128,512]{1,0:T(8,128)(2,1)S(1)} collective-permute-done((bf16[128,512]{1,0:T(8,128)(2,1)S(1)}, bf16[128,512]{1,0:T(8,128)(2,1)S(1)}, u32[]{:S(2)}, u32[]{:S(2)}) %collective-permute-start.8) | collective-permute-done | bytes 131104 | tf_op jit(solution)/shard_map/ppermute | solution.py:396
  59.6 2.2 %all-to-all-done = bf16[4,128,512]{2,1,0:T(8,128)(2,1)S(1)} async-done(((bf16[4,128,512]{2,1,0:T(8,128)(2,1)}), bf16[4,128,512]{2,1,0:T(8,128)(2,1)S(1)}, u32[]{:S(2)}, u32[]{:S(2)}) %all-to-all-start) | async-done | bytes 524320 | tf_op jit(solution)/shard_map/all_to_all | solution.py:446
  61.8 1.9 %collective-permute-done.10.other_keys_ref = bf16[512,512]{1,0:T(8,128)(2,1)S(1)} collective-permute-done((bf16[512,512]{1,0:T(8,128)(2,1)S(1)}, bf16[512,512]{1,0:T(8,128)(2,1)S(1)}, u32[]{:S(2)}, u32[]{:S(2)}) %collective-permute-start.10) | collective-permute-done | bytes 524320 | tf_op jit(solution)/shard_map/ppermute | solution.py:392
  63.7 1.0 %attend_two.1 = (bf16[144,512]{1,0:T(8,128)(2,1)S(1)}, bf16[144,512]{1,0:T(8,128)(2,1)S(1)}) custom-call(bf16[128,512]{1,0:T(8,128)(2,1)S(1)} %collective-permute-done.8.q1_ref, bf16[128,512]{1,0:T(8,128)(2,1)S(1)} %collective-permute-done.9.q2_ref, bf16[512,512]{1,0:T(8,128)(2,1)S(1)} %bitcast.17, bf16[512,512]{1,0:T(8,128)(2,1)S(1)} %collective-permute-done.10.other_keys_ref), custom_call_target="tpu_custom_call" | custom-call | flops 550000000 | bytes 4194304 | tf_op jit(solution)/shard_map/attend_two/pallas_call | solution.py:451
  64.7 0.2 collective-permute-start.11
  64.9 2.1 %collective-permute-start.12 = (bf16[144,512]{1,0:T(8,128)(2,1)S(1)}, bf16[144,512]{1,0:T(8,128)(2,1)S(1)}, u32[]{:S(2)}, u32[]{:S(2)}) collective-permute-start(bf16[144,512]{1,0:T(8,128)(2,1)S(1)} %get-tuple-element.85), channel_id=1, source_target_pairs={{0,1},{1,16},{16,17},{17,0},{2,3},{3,18},{18,19},{19,2},{4,5},{5,2... | collective-permute-start | bytes 442376 | tf_op jit(solution)/shard_map/ppermute | solution.py:396
  67.0 2.0 %collective-permute-done.7.q3_ref = bf16[128,512]{1,0:T(8,128)(2,1)S(1)} collective-permute-done((bf16[128,512]{1,0:T(8,128)(2,1)S(1)}, bf16[128,512]{1,0:T(8,128)(2,1)S(1)}, u32[]{:S(2)}, u32[]{:S(2)}) %collective-permute-start.7) | collective-permute-done | bytes 131104 | tf_op jit(solution)/shard_map/ppermute | solution.py:396
  69.0 1.0 %attend_last.1 = (bf16[144,512]{1,0:T(8,128)(2,1)S(1)}, f32[128,512]{1,0:T(8,128)S(1)}, f32[128,128]{1,0:T(8,128)S(1)}) custom-call(bf16[128,512]{1,0:T(8,128)(2,1)S(1)} %collective-permute-done.7.q3_ref, bf16[128,512]{1,0:T(8,128)(2,1)S(1)} %get-tuple-element.77.mine_ref, bf16[512,512]{1,0:T(8,128)(2,1)S(1)} %bitcast.18, ...), custom_call_target="tpu_custom_call" | custom-call | flops 550000000 | bytes 4194304 | tf_op jit(solution)/shard_map/attend_last/pallas_call | solution.py:454
  70.0 0.1 collective-permute-start.13
  70.1 3.0 %collective-permute-done.11.got1_ref = bf16[144,512]{1,0:T(8,128)(2,1)S(1)} collective-permute-done((bf16[144,512]{1,0:T(8,128)(2,1)S(1)}, bf16[144,512]{1,0:T(8,128)(2,1)S(1)}, u32[]{:S(2)}, u32[]{:S(2)}) %collective-permute-start.11) | collective-permute-done | bytes 147488 | tf_op jit(solution)/shard_map/ppermute | solution.py:396
  73.0 2.2 %collective-permute-done.12.got2_ref = bf16[144,512]{1,0:T(8,128)(2,1)S(1)} collective-permute-done((bf16[144,512]{1,0:T(8,128)(2,1)S(1)}, bf16[144,512]{1,0:T(8,128)(2,1)S(1)}, u32[]{:S(2)}, u32[]{:S(2)}) %collective-permute-start.12) | collective-permute-done | bytes 147488 | tf_op jit(solution)/shard_map/ppermute | solution.py:396
  75.3 0.2 collective-permute-done.13.got3_ref
  75.5 1.1 %finish.1 = bf16[128,512]{1,0:T(8,128)(2,1)} custom-call(f32[128,512]{1,0:T(8,128)S(1)} %get-tuple-element.80.mixed_ref, f32[128,128]{1,0:T(8,128)S(1)} %get-tuple-element.81.level_ref, bf16[144,512]{1,0:T(8,128)(2,1)S(1)} %collective-permute-done.11.got1_ref, bf16[144,512]{1,0:T(8,128)(2,1)S(1)} %collective-permute-done.12.got2_ref, ...), custom_call_target="tpu_custom_call" | custom-call | flops 70000000 | bytes 4194304 | tf_op jit(solution)/shard_map/finish/pallas_call | solution.py:462
  (20 shorter events, 0.1 us)
Async XLA Ops:
  1.0 7.2 %collective-permute-start = (bf16[2,3,64,128]{3,2,1,0:T(8,128)(2,1)S(1)}, bf16[2,3,64,128]{3,2,1,0:T(8,128)(2,1)S(1)}, u32[]{:S(2)}, u32[]{:S(2)}) collective-permute-start(bf16[2,3,64,128]{3,2,1,0:T(8,128)(2,1)S(1)} %get-tuple-element.47), channel_id=1, source_target_pairs={{8,16},{16,8},{9,17},{17,9},{10,18},{18,10},{11,19},{19,11},{12,20... | collective-permute-start | bytes 294920 | tf_op jit(solution)/shard_map/ppermute | solution.py:392
  1.6 6.6 %collective-permute-start.1 = (bf16[2,3,64,128]{3,2,1,0:T(8,128)(2,1)S(1)}, bf16[2,3,64,128]{3,2,1,0:T(8,128)(2,1)S(1)}, u32[]{:S(2)}, u32[]{:S(2)}) collective-permute-start(bf16[2,3,64,128]{3,2,1,0:T(8,128)(2,1)S(1)} %get-tuple-element.48), channel_id=1, source_target_pairs={{0,8},{8,0},{16,24},{24,16},{1,9},{9,1},{17,25},{25,17},{2,10},{10... | collective-permute-start | bytes 294920 | tf_op jit(solution)/shard_map/ppermute | solution.py:392
  8.1 4.8 %copy-start.9 = (f32[128]{0:T(128)S(1)}, f32[128]{0:T(128)}, u32[]{:S(2)}) copy-start(f32[128]{0:T(128)} %param.13) | copy-start | bytes 1540
  8.4 4.5 %collective-permute-start.2 = (bf16[2,38,4,128]{3,2,1,0:T(4,128)(2,1)S(1)}, bf16[2,38,4,128]{3,2,1,0:T(4,128)(2,1)S(1)}, u32[]{:S(2)}, u32[]{:S(2)}) collective-permute-start(bf16[2,38,4,128]{3,2,1,0:T(4,128)(2,1)S(1)} %get-tuple-element.94), channel_id=1, source_target_pairs={{0,1},{1,0},{2,3},{3,2},{4,5},{5,4},{6,7},{7,6},{8,9},{9,8},{10,11... | collective-permute-start | bytes 233480 | tf_op jit(solution)/shard_map/ppermute | solution.py:392
  9.1 3.8 %collective-permute-start.3 = (bf16[2,38,4,128]{3,2,1,0:T(4,128)(2,1)S(1)}, bf16[2,38,4,128]{3,2,1,0:T(4,128)(2,1)S(1)}, u32[]{:S(2)}, u32[]{:S(2)}) collective-permute-start(bf16[2,38,4,128]{3,2,1,0:T(4,128)(2,1)S(1)} %get-tuple-element.93), channel_id=1, source_target_pairs={{1,2},{2,1},{3,4},{4,3},{5,6},{6,5},{9,10},{10,9},{11,12},{12,11},... | collective-permute-start | bytes 233480 | tf_op jit(solution)/shard_map/ppermute | solution.py:392
  12.9 7.7 %copy-start.3 = (bf16[512,512]{1,0:T(8,128)(2,1)S(1)}, bf16[512,512]{1,0:T(8,128)(2,1)}, u32[]{:S(2)}) copy-start(bf16[512,512]{1,0:T(8,128)(2,1)} %query_ref.1) | copy-start | bytes 1572868
  12.9 7.7 %copy-start.4 = (bf16[512,512]{1,0:T(8,128)(2,1)S(1)}, bf16[512,512]{1,0:T(8,128)(2,1)}, u32[]{:S(2)}) copy-start(bf16[512,512]{1,0:T(8,128)(2,1)} %key_ref.1) | copy-start | bytes 1572868
  12.9 7.7 %copy-start.5 = (bf16[512,512]{1,0:T(8,128)(2,1)S(1)}, bf16[512,512]{1,0:T(8,128)(2,1)}, u32[]{:S(2)}) copy-start(bf16[512,512]{1,0:T(8,128)(2,1)} %value_ref.1) | copy-start | bytes 1572868
  12.9 7.7 %copy-start.6 = (bf16[512,512]{1,0:T(8,128)(2,1)S(1)}, bf16[512,512]{1,0:T(8,128)(2,1)}, u32[]{:S(2)}) copy-start(bf16[512,512]{1,0:T(8,128)(2,1)} %out_ref.1) | copy-start | bytes 1572868
  15.4 7.9 %copy-start.1 = (bf16[2,32,64,128]{3,2,1,0:T(8,128)(2,1)S(1)}, bf16[2,32,64,128]{3,2,1,0:T(8,128)(2,1)}, u32[]{:S(2)}) copy-start(bf16[2,32,64,128]{3,2,1,0:T(8,128)(2,1)} %x_ref.1) | copy-start | bytes 3145732
  15.4 11.6 %collective-permute-start.4 = (bf16[624,256]{1,0:T(8,128)(2,1)S(1)}, bf16[624,256]{1,0:T(8,128)(2,1)S(1)}, u32[]{:S(2)}, u32[]{:S(2)}) collective-permute-start(bf16[624,256]{1,0:T(8,128)(2,1)S(1)} %get-tuple-element.63), channel_id=1, source_target_pairs={{0,32},{32,64},{64,96},{96,128},{128,160},{160,192},{192,224},{1,3... | collective-permute-start | bytes 958472 | tf_op jit(solution)/shard_map/ppermute | solution.py:432
  23.3 3.7 %copy-start = (bf16[3,3,3,256,256]{4,3,2,1,0:T(8,128)(2,1)S(1)}, bf16[3,3,3,256,256]{4,3,2,1,0:T(8,128)(2,1)}, u32[]{:S(2)}) copy-start(bf16[3,3,3,256,256]{4,3,2,1,0:T(8,128)(2,1)} %param.17) | copy-start | bytes 10616836
  23.3 3.7 %copy-start.2 = (bf16[1024,512]{1,0:T(8,128)(2,1)S(1)}, bf16[1024,512]{1,0:T(8,128)(2,1)}, u32[]{:S(2)}) copy-start(bf16[1024,512]{1,0:T(8,128)(2,1)} %down_ref.3) | copy-start | bytes 3145732
  23.3 3.6 %copy-start.8 = (f32[256]{0:T(256)S(1)}, f32[256]{0:T(256)}, u32[]{:S(2)}) copy-start(f32[256]{0:T(256)} %param.16) | copy-start | bytes 3076
  29.5 11.2 %collective-permute-start.5 = (bf16[128,512]{1,0:T(8,128)(2,1)S(1)}, bf16[128,512]{1,0:T(8,128)(2,1)S(1)}, u32[]{:S(2)}, u32[]{:S(2)}) collective-permute-start(bf16[128,512]{1,0:T(8,128)(2,1)S(1)} %get-tuple-element.74), channel_id=1, source_target_pairs={{0,32},{32,64},{64,96},{96,128},{128,160},{160,192},{192,224},{1,3... | collective-permute-start | bytes 393224 | tf_op jit(solution)/shard_map/ppermute | solution.py:442
  35.1 8.0 %collective-permute-start.6 = (bf16[128,512]{1,0:T(8,128)(2,1)S(1)}, bf16[128,512]{1,0:T(8,128)(2,1)S(1)}, u32[]{:S(2)}, u32[]{:S(2)}) collective-permute-start(bf16[128,512]{1,0:T(8,128)(2,1)S(1)} %get-tuple-element.75), channel_id=1, source_target_pairs={{0,64},{32,96},{64,128},{96,160},{128,192},{160,224},{1,65},{33,97... | collective-permute-start | bytes 393224 | tf_op jit(solution)/shard_map/ppermute | solution.py:441
  37.3 5.8 %copy-start.7 = (f32[512]{0:T(512)S(1)}, f32[512]{0:T(512)}, u32[]{:S(2)}) copy-start(f32[512]{0:T(512)} %param.19) | copy-start | bytes 6148
  44.0 17.8 %all-to-all-start = ((bf16[4,128,512]{2,1,0:T(8,128)(2,1)}), bf16[4,128,512]{2,1,0:T(8,128)(2,1)S(1)}, u32[]{:S(2)}, u32[]{:S(2)}) async-start(bf16[4,128,512]{2,1,0:T(8,128)(2,1)} %get-tuple-element.78), calls=%async_computation | async-start | bytes 1048576 | tf_op jit(solution)/shard_map/all_to_all | solution.py:446
  53.1 6.5 %collective-permute-start.8 = (bf16[128,512]{1,0:T(8,128)(2,1)S(1)}, bf16[128,512]{1,0:T(8,128)(2,1)S(1)}, u32[]{:S(2)}, u32[]{:S(2)}) collective-permute-start(bf16[128,512]{1,0:T(8,128)(2,1)S(1)} %get-tuple-element.77.mine_ref), channel_id=1, source_target_pairs={{0,16},{1,17},{16,0},{17,1},{2,18},{3,19},{18,2},{19,3},{4,20},{5,... | collective-permute-start | bytes 393224 | tf_op jit(solution)/shard_map/ppermute | solution.py:396
  53.7 5.9 %collective-permute-start.9 = (bf16[128,512]{1,0:T(8,128)(2,1)S(1)}, bf16[128,512]{1,0:T(8,128)(2,1)S(1)}, u32[]{:S(2)}, u32[]{:S(2)}) collective-permute-start(bf16[128,512]{1,0:T(8,128)(2,1)S(1)} %get-tuple-element.77.mine_ref), channel_id=1, source_target_pairs={{0,17},{1,0},{16,1},{17,16},{2,19},{3,2},{18,3},{19,18},{4,21},{5,... | collective-permute-start | bytes 393224 | tf_op jit(solution)/shard_map/ppermute | solution.py:396
  61.8 1.9 %collective-permute-start.10 = (bf16[512,512]{1,0:T(8,128)(2,1)S(1)}, bf16[512,512]{1,0:T(8,128)(2,1)S(1)}, u32[]{:S(2)}, u32[]{:S(2)}) collective-permute-start(bf16[512,512]{1,0:T(8,128)(2,1)S(1)} %bitcast.16), channel_id=1, source_target_pairs={{0,8},{8,0},{1,9},{9,1},{2,10},{10,2},{3,11},{11,3},{4,12},{12,4},... | collective-permute-start | bytes 1572872 | tf_op jit(solution)/shard_map/ppermute | solution.py:392
  61.8 7.2 %collective-permute-start.7 = (bf16[128,512]{1,0:T(8,128)(2,1)S(1)}, bf16[128,512]{1,0:T(8,128)(2,1)S(1)}, u32[]{:S(2)}, u32[]{:S(2)}) collective-permute-start(bf16[128,512]{1,0:T(8,128)(2,1)S(1)} %get-tuple-element.77.mine_ref), channel_id=1, source_target_pairs={{0,1},{1,16},{16,17},{17,0},{2,3},{3,18},{18,19},{19,2},{4,5},{5,2... | collective-permute-start | bytes 393224 | tf_op jit(solution)/shard_map/ppermute | solution.py:396
  64.7 8.3 %collective-permute-start.11 = (bf16[144,512]{1,0:T(8,128)(2,1)S(1)}, bf16[144,512]{1,0:T(8,128)(2,1)S(1)}, u32[]{:S(2)}, u32[]{:S(2)}) collective-permute-start(bf16[144,512]{1,0:T(8,128)(2,1)S(1)} %get-tuple-element.84), channel_id=1, source_target_pairs={{0,16},{1,17},{16,0},{17,1},{2,18},{3,19},{18,2},{19,3},{4,20},{5,... | collective-permute-start | bytes 442376 | tf_op jit(solution)/shard_map/ppermute | solution.py:396
  64.9 10.3 %collective-permute-start.12 = (bf16[144,512]{1,0:T(8,128)(2,1)S(1)}, bf16[144,512]{1,0:T(8,128)(2,1)S(1)}, u32[]{:S(2)}, u32[]{:S(2)}) collective-permute-start(bf16[144,512]{1,0:T(8,128)(2,1)S(1)} %get-tuple-element.85), channel_id=1, source_target_pairs={{0,1},{1,16},{16,17},{17,0},{2,3},{3,18},{18,19},{19,2},{4,5},{5,2... | collective-permute-start | bytes 442376 | tf_op jit(solution)/shard_map/ppermute | solution.py:396
  70.0 5.5 %collective-permute-start.13 = (bf16[144,512]{1,0:T(8,128)(2,1)S(1)}, bf16[144,512]{1,0:T(8,128)(2,1)S(1)}, u32[]{:S(2)}, u32[]{:S(2)}) collective-permute-start(bf16[144,512]{1,0:T(8,128)(2,1)S(1)} %get-tuple-element.86), channel_id=1, source_target_pairs={{0,17},{1,0},{16,1},{17,16},{2,19},{3,2},{18,3},{19,18},{4,21},{5,... | collective-permute-start | bytes 442376 | tf_op jit(solution)/shard_map/ppermute | solution.py:396

commit v9 on v8

--- a/solution.py
+++ b/solution.py
@@ -351,24 +351,27 @@
     return jnp.broadcast_to(across, (128, 128)).T[:, :1]
 
 
-def softmax_part(queries, keys):
-    scores = lax.dot_general(queries, keys, (((1,), (1,)), ((), ())), preferred_element_type=F32)
-    top = jnp.max(scores, -1, keepdims=True)
-    expo = jnp.exp(scores - top)
-    total = jnp.sum(expo, -1, keepdims=True)
-    return dot(expo.astype(BF16), keys) / total, top + jnp.log(total)
+def softmax_part(queries, *parts):
+    scores = [
+        lax.dot_general(queries, keys, (((1,), (1,)), ((), ())), preferred_element_type=F32) for keys in parts
+    ]
+    top = functools.reduce(jnp.maximum, [jnp.max(score, -1, keepdims=True) for score in scores])
+    expos = [jnp.exp(score - top) for score in scores]
+    total = sum(jnp.sum(expo, -1, keepdims=True) for expo in expos)
+    summed = sum(dot(expo.astype(BF16), keys) for expo, keys in zip(expos, parts))
+    return summed * (1.0 / total), top + jnp.log(total)
 
 
 def attend_two_kernel(q1_ref, q2_ref, keys_ref, other_keys_ref, sent1_ref, sent2_ref):
-    keys = jnp.concatenate([keys_ref[...], other_keys_ref[...]], 0)
-    mixed, level = softmax_part(jnp.concatenate([q1_ref[...], q2_ref[...]], 0), keys)
+    keys = (keys_ref[...], other_keys_ref[...])
+    mixed, level = softmax_part(jnp.concatenate([q1_ref[...], q2_ref[...]], 0), *keys)
     sent1_ref[...] = packed(mixed[:128], level[:128])
     sent2_ref[...] = packed(mixed[128:], level[128:])
 
 
 def attend_last_kernel(q3_ref, mine_ref, keys_ref, other_keys_ref, sent3_ref, mixed_ref, level_ref):
-    keys = jnp.concatenate([keys_ref[...], other_keys_ref[...]], 0)
-    mixed, level = softmax_part(jnp.concatenate([q3_ref[...], mine_ref[...]], 0), keys)
+    keys = (keys_ref[...], other_keys_ref[...])
+    mixed, level = softmax_part(jnp.concatenate([q3_ref[...], mine_ref[...]], 0), *keys)
     sent3_ref[...] = packed(mixed[:128], level[:128])
     mixed_ref[...] = mixed[128:]
     level_ref[...] = jnp.broadcast_to(level[128:], (128, 128))

time: 76.9 us -> 76.9 us (level)
  no operation moved by 1% of the time
where the time goes in v9:
time: 76.9 us; the launch traced here: 76.6 us
  starting transfers between devices  32.8 us (43%)
  waiting for transfers between devices  22.3 us (29%)
  Pallas kernels  20.9 us (27%)
    ppermute x6, waiting for transfers between devices, turned(): return lax.ppermute(value, RING, [(i, (i + step) % 4) for i in range(4)])  12 us
    all_to_all x1, starting transfers between devices, per_device(): keys = lax.all_to_all(copies, 'y', 0, 0, tiled=True).reshape(512, 512)  9.09 us
    ppermute x5, starting transfers between devices, swapped(): return lax.ppermute(value, axis, pairs)  6.47 us
    ppermute x1, starting transfers between devices, per_device(): near = lax.ppermute(near, 'tm', [(i, i + 1) for i in range(7)])  5.6 us
    ppermute x1, starting transfers between devices, per_device(): got = lax.ppermute(sent, 'tm', [(i, i + 1) for i in range(7)])  5.17 us
    ppermute x6, starting transfers between devices, turned(): return lax.ppermute(value, RING, [(i, (i + step) % 4) for i in range(4)])  4.29 us
    pallas_call x2, Pallas kernels, compose(): call(functools.partial(compose_kernel, own), shape((16, 256, 256), BF16),...  3.83 us
    ppermute x5, waiting for transfers between devices, swapped(): return lax.ppermute(value, axis, pairs)  3.13 us
  transfers between devices with their start and end apart: 15, of which 11 were waited for; matrix products, arithmetic and copies ran while one was open for 0% of the time, Pallas kernels for 17%

profile of v9, /device:TPU:96, one launch (start us, length us, event | category | flops | bytes accessed | tf_op | source)
XLA Modules:
  0.0 76.6 jit_solution(13549030817935064211)
XLA Ops:
  0.0 1.0 %edges.1 = (bf16[2,3,64,128]{3,2,1,0:T(8,128)(2,1)S(1)}, bf16[2,3,64,128]{3,2,1,0:T(8,128)(2,1)S(1)}) custom-call(s32[1]{0:T(128)} %bitcast.3.odd_ref, bf16[2,32,64,128]{3,2,1,0:T(8,128)(2,1)} %x_ref.1), custom_call_target="tpu_custom_call" | custom-call | flops 1000 | bytes 4194304 | tf_op jit(solution)/shard_map/edges/pallas_call | solution.py:405
  1.0 0.7 collective-permute-start
  1.6 4.5 %collective-permute-start.1 = (bf16[2,3,64,128]{3,2,1,0:T(8,128)(2,1)S(1)}, bf16[2,3,64,128]{3,2,1,0:T(8,128)(2,1)S(1)}, u32[]{:S(2)}, u32[]{:S(2)}) collective-permute-start(bf16[2,3,64,128]{3,2,1,0:T(8,128)(2,1)S(1)} %get-tuple-element.48), channel_id=1, source_target_pairs={{0,8},{8,0},{16,24},{24,16},{1,9},{9,1},{17,25},{25,17},{2,10},{10... | collective-permute-start | bytes 294920 | tf_op jit(solution)/shard_map/ppermute | solution.py:395
  6.1 2.0 %prepare.1 = (f32[2,32,64,128]{3,2,1,0:T(8,128)S(1)}, bf16[2,32,4,128]{3,2,1,0:T(4,128)(2,1)S(1)}, bf16[2,32,4,128]{3,2,1,0:T(4,128)(2,1)S(1)}, bf16[3,3,3,128,1...) custom-call(bf16[2,32,64,128]{3,2,1,0:T(8,128)(2,1)} %x_ref.1, f32[1,128]{1,0:T(1,128)} %bitcast.25, ...), custom_call_target="tpu_custom_call" | custom-call | flops 10000000 | bytes 4194304 | tf_op jit(solution)/shard_map/prepare/pallas_call | solution.py:139
  8.1 0.0 copy-start.9
  8.1 0.1 pad_add_fusion.flag_ref
  8.3 0.1 broadcast_select_fusion.4
  8.4 0.7 collective-permute-start.2
  9.1 0.7 collective-permute-start.3
  9.7 1.9 %compose_next.1.weight_ref = bf16[16,256,256]{2,1,0:T(8,128)(2,1)S(1)} custom-call(s32[3]{0:T(128)S(1)} %pad_add_fusion.flag_ref, bf16[3,3,3,128,128]{4,3,2,1,0:T(8,128)(2,1)S(1)} %get-tuple-element.64.conv, bf16[1024,256]{1,0:T(8,128)(2,1)S(1)} %get-tuple-element.65.down.down_ref), custom_call_target="tpu_custom_call" | custom-call | flops 900000000 | bytes 4194304 | tf_op jit(solution)/shard_map/compose_next/pallas_call | solution.py:85
  11.6 1.2 %collective-permute-done.2 = bf16[2,38,4,128]{3,2,1,0:T(4,128)(2,1)S(1)} collective-permute-done((bf16[2,38,4,128]{3,2,1,0:T(4,128)(2,1)S(1)}, bf16[2,38,4,128]{3,2,1,0:T(4,128)(2,1)S(1)}, u32[]{:S(2)}, u32[]{:S(2)}) %collective-permute-start.2) | collective-permute-done | bytes 77856 | tf_op jit(solution)/shard_map/ppermute | solution.py:395
  12.9 0.0 copy-start.3
  12.9 0.0 copy-start.4
  12.9 0.0 copy-start.5
  12.9 0.0 copy-start.6
  13.0 2.4 %fine_next.1 = (bf16[624,256]{1,0:T(8,128)(2,1)S(1)}, bf16[2,4,19,48,256]{4,3,2,1,0:T(8,128)(2,1)S(1)}) custom-call(f32[2,32,64,128]{3,2,1,0:T(8,128)S(1)} %get-tuple-element.52.act_ref, bf16[2,3,64,128]{3,2,1,0:T(8,128)(2,1)S(1)} %get-tuple-element.53.up_ref, bf16[2,3,64,128]{3,2,1,0:T(8,128)(2,1)S(1)} %get-tuple-element.54.low_ref, ...), custom_call_target="tpu_custom_call" | custom-call | flops 1800000000 | bytes 4194304 | tf_op jit(solution)/shard_map/fine_next/pallas_call | solution.py:224
  15.4 0.0 copy-start.1
  15.4 5.2 %collective-permute-start.4 = (bf16[624,256]{1,0:T(8,128)(2,1)S(1)}, bf16[624,256]{1,0:T(8,128)(2,1)S(1)}, u32[]{:S(2)}, u32[]{:S(2)}) collective-permute-start(bf16[624,256]{1,0:T(8,128)(2,1)S(1)} %get-tuple-element.63), channel_id=1, source_target_pairs={{0,32},{32,64},{64,96},{96,128},{128,160},{160,192},{192,224},{1,3... | collective-permute-start | bytes 958472 | tf_op jit(solution)/shard_map/ppermute | solution.py:435
  20.6 0.7 mix.1
  21.4 1.9 %compose_own.1.weight_ref = bf16[16,256,256]{2,1,0:T(8,128)(2,1)S(1)} custom-call(s32[3]{0:T(128)S(1)} %pad_add_fusion.flag_ref, bf16[3,3,3,128,128]{4,3,2,1,0:T(8,128)(2,1)S(1)} %get-tuple-element.64.conv, bf16[1024,256]{1,0:T(8,128)(2,1)S(1)} %get-tuple-element.65.down.down_ref), custom_call_target="tpu_custom_call" | custom-call | flops 900000000 | bytes 4194304 | tf_op jit(solution)/shard_map/compose_own/pallas_call | solution.py:85
  23.3 0.0 copy-start
  23.3 0.0 copy-start.2
  23.3 0.0 copy-start.8
  23.3 2.6 %fine_own.1.own_ref = f32[18,48,256]{2,1,0:T(8,128)S(1)} custom-call(bf16[2,32,64,128]{3,2,1,0:T(8,128)(2,1)S(1)} %copy-done.1, bf16[2,3,64,128]{3,2,1,0:T(8,128)(2,1)S(1)} %get-tuple-element.53.up_ref, bf16[2,3,64,128]{3,2,1,0:T(8,128)(2,1)S(1)} %get-tuple-element.54.low_ref, bf16[2,38,4,128]{3,2,1,0:T(4,128)(2,1)S(1)} %bitcast.22, ...), custom_call_target="tpu_custom_call" | custom-call | flops 2200000000 | bytes 4194304 | tf_op jit(solution)/shard_map/fine_own/pallas_call | solution.py:235
  26.0 1.0 %collective-permute-done.4.got_ref = bf16[624,256]{1,0:T(8,128)(2,1)S(1)} collective-permute-done((bf16[624,256]{1,0:T(8,128)(2,1)S(1)}, bf16[624,256]{1,0:T(8,128)(2,1)S(1)}, u32[]{:S(2)}, u32[]{:S(2)}) %collective-permute-start.4) | collective-permute-done | bytes 319520 | tf_op jit(solution)/shard_map/ppermute | solution.py:435
  27.0 2.5 %coarse_sent.1 = (bf16[128,512]{1,0:T(8,128)(2,1)S(1)}, bf16[128,512]{1,0:T(8,128)(2,1)S(1)}, f32[512,256]{1,0:T(8,128)S(1)}, bf16[512,2304]{1,0:T(8,128)(2,1)S(1)}, f32[2,18,48,128]{3,2,1,0:T(8,128)S(1)}) custom-call(s32[3]{0:T(128)S(1)} %pad_add_fusion.flag_ref, f32[18,48,256]{2,1,0:T(8,128)S(1)} %fine_own.1.own_ref, ...), custom_call_target="tpu_custom_call" | custom-call | flops 1500000000 | bytes 4194304 | tf_op jit(solution)/shard_map/coarse_sent/pallas_call | solution.py:309
  29.5 5.6 %collective-permute-start.5 = (bf16[128,512]{1,0:T(8,128)(2,1)S(1)}, bf16[128,512]{1,0:T(8,128)(2,1)S(1)}, u32[]{:S(2)}, u32[]{:S(2)}) collective-permute-start(bf16[128,512]{1,0:T(8,128)(2,1)S(1)} %get-tuple-element.74), channel_id=1, source_target_pairs={{0,32},{32,64},{64,96},{96,128},{128,160},{160,192},{192,224},{1,3... | collective-permute-start | bytes 393224 | tf_op jit(solution)/shard_map/ppermute | solution.py:445
  35.1 2.2 %collective-permute-start.6 = (bf16[128,512]{1,0:T(8,128)(2,1)S(1)}, bf16[128,512]{1,0:T(8,128)(2,1)S(1)}, u32[]{:S(2)}, u32[]{:S(2)}) collective-permute-start(bf16[128,512]{1,0:T(8,128)(2,1)S(1)} %get-tuple-element.75), channel_id=1, source_target_pairs={{0,64},{32,96},{64,128},{96,160},{128,192},{160,224},{1,65},{33,97... | collective-permute-start | bytes 393224 | tf_op jit(solution)/shard_map/ppermute | solution.py:444
  37.3 1.8 %coarse_here.1.own_ref = f32[128,512]{1,0:T(8,128)S(1)} custom-call(s32[3]{0:T(128)S(1)} %pad_add_fusion.flag_ref, bf16[512,2304]{1,0:T(8,128)(2,1)S(1)} %get-tuple-element.71.windows, f32[2,18,48,128]{3,2,1,0:T(8,128)S(1)} %get-tuple-element.72.reduced, f32[512,256]{1,0:T(8,128)S(1)} %get-tuple-element.73.c1_ref, bf16[3,9,256,256]{3,2,1,0:T(8,128)(2,1)S(1)} %bitcast.15, ...), custom_call_target="tpu_custom_call" | custom-call | flops 1000 | bytes 1000 | tf_op jit(solution)/shard_map/coarse_here/pallas_call | solution.py:317
  39.0 1.7 %collective-permute-done.5.near_ref = bf16[128,512]{1,0:T(8,128)(2,1)S(1)} collective-permute-done((bf16[128,512]{1,0:T(8,128)(2,1)S(1)}, bf16[128,512]{1,0:T(8,128)(2,1)S(1)}, u32[]{:S(2)}, u32[]{:S(2)}) %collective-permute-start.5) | collective-permute-done | bytes 131104 | tf_op jit(solution)/shard_map/ppermute | solution.py:445
  40.7 2.3 %collective-permute-done.6.far_ref = bf16[128,512]{1,0:T(8,128)(2,1)S(1)} collective-permute-done((bf16[128,512]{1,0:T(8,128)(2,1)S(1)}, bf16[128,512]{1,0:T(8,128)(2,1)S(1)}, u32[]{:S(2)}, u32[]{:S(2)}) %collective-permute-start.6) | collective-permute-done | bytes 131104 | tf_op jit(solution)/shard_map/ppermute | solution.py:444
  43.0 1.0 %latent.1 = (bf16[128,512]{1,0:T(8,128)(2,1)S(1)}, bf16[128,512]{1,0:T(8,128)(2,1)S(1)}, bf16[4,128,512]{2,1,0:T(8,128)(2,1)}) custom-call(f32[128,512]{1,0:T(8,128)S(1)} %coarse_here.1.own_ref, bf16[128,512]{1,0:T(8,128)(2,1)S(1)} %collective-permute-done.5.near_ref, bf16[128,512]{1,0:T(8,128)(2,1)S(1)} %collective-permute-done.6.far_ref, ...), custom_call_target="tpu_custom_call" | custom-call | flops 80000000 | bytes 4194304 | tf_op jit(solution)/shard_map/latent/pallas_call | solution.py:446
  44.0 9.1 %all-to-all-start = ((bf16[4,128,512]{2,1,0:T(8,128)(2,1)}), bf16[4,128,512]{2,1,0:T(8,128)(2,1)S(1)}, u32[]{:S(2)}, u32[]{:S(2)}) async-start(bf16[4,128,512]{2,1,0:T(8,128)(2,1)} %get-tuple-element.78), calls=%async_computation | async-start | bytes 1048576 | tf_op jit(solution)/shard_map/all_to_all | solution.py:449
  53.1 0.6 collective-permute-start.8
  53.7 1.3 %collective-permute-start.9 = (bf16[128,512]{1,0:T(8,128)(2,1)S(1)}, bf16[128,512]{1,0:T(8,128)(2,1)S(1)}, u32[]{:S(2)}, u32[]{:S(2)}) collective-permute-start(bf16[128,512]{1,0:T(8,128)(2,1)S(1)} %get-tuple-element.77.mine_ref), channel_id=1, source_target_pairs={{0,17},{1,0},{16,1},{17,16},{2,19},{3,2},{18,3},{19,18},{4,21},{5,... | collective-permute-start | bytes 393224 | tf_op jit(solution)/shard_map/ppermute | solution.py:399
  55.0 4.5 %collective-permute-done.8.q1_ref = bf16[128,512]{1,0:T(8,128)(2,1)S(1)} collective-permute-done((bf16[128,512]{1,0:T(8,128)(2,1)S(1)}, bf16[128,512]{1,0:T(8,128)(2,1)S(1)}, u32[]{:S(2)}, u32[]{:S(2)}) %collective-permute-start.8) | collective-permute-done | bytes 131104 | tf_op jit(solution)/shard_map/ppermute | solution.py:399
  59.6 2.2 %all-to-all-done = bf16[4,128,512]{2,1,0:T(8,128)(2,1)S(1)} async-done(((bf16[4,128,512]{2,1,0:T(8,128)(2,1)}), bf16[4,128,512]{2,1,0:T(8,128)(2,1)S(1)}, u32[]{:S(2)}, u32[]{:S(2)}) %all-to-all-start) | async-done | bytes 524320 | tf_op jit(solution)/shard_map/all_to_all | solution.py:449
  61.8 1.9 %collective-permute-done.10.other_keys_ref = bf16[512,512]{1,0:T(8,128)(2,1)S(1)} collective-permute-done((bf16[512,512]{1,0:T(8,128)(2,1)S(1)}, bf16[512,512]{1,0:T(8,128)(2,1)S(1)}, u32[]{:S(2)}, u32[]{:S(2)}) %collective-permute-start.10) | collective-permute-done | bytes 524320 | tf_op jit(solution)/shard_map/ppermute | solution.py:395
  63.7 1.0 %attend_two.1 = (bf16[144,512]{1,0:T(8,128)(2,1)S(1)}, bf16[144,512]{1,0:T(8,128)(2,1)S(1)}) custom-call(bf16[128,512]{1,0:T(8,128)(2,1)S(1)} %collective-permute-done.8.q1_ref, bf16[128,512]{1,0:T(8,128)(2,1)S(1)} %collective-permute-done.9.q2_ref, bf16[512,512]{1,0:T(8,128)(2,1)S(1)} %bitcast.17, bf16[512,512]{1,0:T(8,128)(2,1)S(1)} %collective-permute-done.10.other_keys_ref), custom_call_target="tpu_custom_call" | custom-call | flops 550000000 | bytes 4194304 | tf_op jit(solution)/shard_map/attend_two/pallas_call | solution.py:454
  64.7 0.2 collective-permute-start.11
  64.9 2.1 %collective-permute-start.12 = (bf16[144,512]{1,0:T(8,128)(2,1)S(1)}, bf16[144,512]{1,0:T(8,128)(2,1)S(1)}, u32[]{:S(2)}, u32[]{:S(2)}) collective-permute-start(bf16[144,512]{1,0:T(8,128)(2,1)S(1)} %get-tuple-element.85), channel_id=1, source_target_pairs={{0,1},{1,16},{16,17},{17,0},{2,3},{3,18},{18,19},{19,2},{4,5},{5,2... | collective-permute-start | bytes 442376 | tf_op jit(solution)/shard_map/ppermute | solution.py:399
  67.0 2.0 %collective-permute-done.7.q3_ref = bf16[128,512]{1,0:T(8,128)(2,1)S(1)} collective-permute-done((bf16[128,512]{1,0:T(8,128)(2,1)S(1)}, bf16[128,512]{1,0:T(8,128)(2,1)S(1)}, u32[]{:S(2)}, u32[]{:S(2)}) %collective-permute-start.7) | collective-permute-done | bytes 131104 | tf_op jit(solution)/shard_map/ppermute | solution.py:399
  69.0 1.0 %attend_last.1 = (bf16[144,512]{1,0:T(8,128)(2,1)S(1)}, f32[128,512]{1,0:T(8,128)S(1)}, f32[128,128]{1,0:T(8,128)S(1)}) custom-call(bf16[128,512]{1,0:T(8,128)(2,1)S(1)} %collective-permute-done.7.q3_ref, bf16[128,512]{1,0:T(8,128)(2,1)S(1)} %get-tuple-element.77.mine_ref, bf16[512,512]{1,0:T(8,128)(2,1)S(1)} %bitcast.18, ...), custom_call_target="tpu_custom_call" | custom-call | flops 550000000 | bytes 4194304 | tf_op jit(solution)/shard_map/attend_last/pallas_call | solution.py:457
  70.0 0.1 collective-permute-start.13
  70.1 3.0 %collective-permute-done.11.got1_ref = bf16[144,512]{1,0:T(8,128)(2,1)S(1)} collective-permute-done((bf16[144,512]{1,0:T(8,128)(2,1)S(1)}, bf16[144,512]{1,0:T(8,128)(2,1)S(1)}, u32[]{:S(2)}, u32[]{:S(2)}) %collective-permute-start.11) | collective-permute-done | bytes 147488 | tf_op jit(solution)/shard_map/ppermute | solution.py:399
  73.0 2.2 %collective-permute-done.12.got2_ref = bf16[144,512]{1,0:T(8,128)(2,1)S(1)} collective-permute-done((bf16[144,512]{1,0:T(8,128)(2,1)S(1)}, bf16[144,512]{1,0:T(8,128)(2,1)S(1)}, u32[]{:S(2)}, u32[]{:S(2)}) %collective-permute-start.12) | collective-permute-done | bytes 147488 | tf_op jit(solution)/shard_map/ppermute | solution.py:399
  75.3 0.2 collective-permute-done.13.got3_ref
  75.5 1.1 %finish.1 = bf16[128,512]{1,0:T(8,128)(2,1)} custom-call(f32[128,512]{1,0:T(8,128)S(1)} %get-tuple-element.80.mixed_ref, f32[128,128]{1,0:T(8,128)S(1)} %get-tuple-element.81.level_ref, bf16[144,512]{1,0:T(8,128)(2,1)S(1)} %collective-permute-done.11.got1_ref, bf16[144,512]{1,0:T(8,128)(2,1)S(1)} %collective-permute-done.12.got2_ref, ...), custom_call_target="tpu_custom_call" | custom-call | flops 70000000 | bytes 4194304 | tf_op jit(solution)/shard_map/finish/pallas_call | solution.py:465
  (20 shorter events, 0.1 us)
Async XLA Ops:
  1.0 7.2 %collective-permute-start = (bf16[2,3,64,128]{3,2,1,0:T(8,128)(2,1)S(1)}, bf16[2,3,64,128]{3,2,1,0:T(8,128)(2,1)S(1)}, u32[]{:S(2)}, u32[]{:S(2)}) collective-permute-start(bf16[2,3,64,128]{3,2,1,0:T(8,128)(2,1)S(1)} %get-tuple-element.47), channel_id=1, source_target_pairs={{8,16},{16,8},{9,17},{17,9},{10,18},{18,10},{11,19},{19,11},{12,20... | collective-permute-start | bytes 294920 | tf_op jit(solution)/shard_map/ppermute | solution.py:395
  1.6 6.6 %collective-permute-start.1 = (bf16[2,3,64,128]{3,2,1,0:T(8,128)(2,1)S(1)}, bf16[2,3,64,128]{3,2,1,0:T(8,128)(2,1)S(1)}, u32[]{:S(2)}, u32[]{:S(2)}) collective-permute-start(bf16[2,3,64,128]{3,2,1,0:T(8,128)(2,1)S(1)} %get-tuple-element.48), channel_id=1, source_target_pairs={{0,8},{8,0},{16,24},{24,16},{1,9},{9,1},{17,25},{25,17},{2,10},{10... | collective-permute-start | bytes 294920 | tf_op jit(solution)/shard_map/ppermute | solution.py:395
  8.1 4.8 %copy-start.9 = (f32[128]{0:T(128)S(1)}, f32[128]{0:T(128)}, u32[]{:S(2)}) copy-start(f32[128]{0:T(128)} %param.13) | copy-start | bytes 1540
  8.4 4.5 %collective-permute-start.2 = (bf16[2,38,4,128]{3,2,1,0:T(4,128)(2,1)S(1)}, bf16[2,38,4,128]{3,2,1,0:T(4,128)(2,1)S(1)}, u32[]{:S(2)}, u32[]{:S(2)}) collective-permute-start(bf16[2,38,4,128]{3,2,1,0:T(4,128)(2,1)S(1)} %get-tuple-element.94), channel_id=1, source_target_pairs={{0,1},{1,0},{2,3},{3,2},{4,5},{5,4},{6,7},{7,6},{8,9},{9,8},{10,11... | collective-permute-start | bytes 233480 | tf_op jit(solution)/shard_map/ppermute | solution.py:395
  9.1 3.8 %collective-permute-start.3 = (bf16[2,38,4,128]{3,2,1,0:T(4,128)(2,1)S(1)}, bf16[2,38,4,128]{3,2,1,0:T(4,128)(2,1)S(1)}, u32[]{:S(2)}, u32[]{:S(2)}) collective-permute-start(bf16[2,38,4,128]{3,2,1,0:T(4,128)(2,1)S(1)} %get-tuple-element.93), channel_id=1, source_target_pairs={{1,2},{2,1},{3,4},{4,3},{5,6},{6,5},{9,10},{10,9},{11,12},{12,11},... | collective-permute-start | bytes 233480 | tf_op jit(solution)/shard_map/ppermute | solution.py:395
  12.9 7.7 %copy-start.3 = (bf16[512,512]{1,0:T(8,128)(2,1)S(1)}, bf16[512,512]{1,0:T(8,128)(2,1)}, u32[]{:S(2)}) copy-start(bf16[512,512]{1,0:T(8,128)(2,1)} %query_ref.1) | copy-start | bytes 1572868
  12.9 7.7 %copy-start.4 = (bf16[512,512]{1,0:T(8,128)(2,1)S(1)}, bf16[512,512]{1,0:T(8,128)(2,1)}, u32[]{:S(2)}) copy-start(bf16[512,512]{1,0:T(8,128)(2,1)} %key_ref.1) | copy-start | bytes 1572868
  12.9 7.7 %copy-start.5 = (bf16[512,512]{1,0:T(8,128)(2,1)S(1)}, bf16[512,512]{1,0:T(8,128)(2,1)}, u32[]{:S(2)}) copy-start(bf16[512,512]{1,0:T(8,128)(2,1)} %value_ref.1) | copy-start | bytes 1572868
  12.9 7.7 %copy-start.6 = (bf16[512,512]{1,0:T(8,128)(2,1)S(1)}, bf16[512,512]{1,0:T(8,128)(2,1)}, u32[]{:S(2)}) copy-start(bf16[512,512]{1,0:T(8,128)(2,1)} %out_ref.1) | copy-start | bytes 1572868
  15.4 7.9 %copy-start.1 = (bf16[2,32,64,128]{3,2,1,0:T(8,128)(2,1)S(1)}, bf16[2,32,64,128]{3,2,1,0:T(8,128)(2,1)}, u32[]{:S(2)}) copy-start(bf16[2,32,64,128]{3,2,1,0:T(8,128)(2,1)} %x_ref.1) | copy-start | bytes 3145732
  15.4 11.6 %collective-permute-start.4 = (bf16[624,256]{1,0:T(8,128)(2,1)S(1)}, bf16[624,256]{1,0:T(8,128)(2,1)S(1)}, u32[]{:S(2)}, u32[]{:S(2)}) collective-permute-start(bf16[624,256]{1,0:T(8,128)(2,1)S(1)} %get-tuple-element.63), channel_id=1, source_target_pairs={{0,32},{32,64},{64,96},{96,128},{128,160},{160,192},{192,224},{1,3... | collective-permute-start | bytes 958472 | tf_op jit(solution)/shard_map/ppermute | solution.py:435
  23.3 3.7 %copy-start = (bf16[3,3,3,256,256]{4,3,2,1,0:T(8,128)(2,1)S(1)}, bf16[3,3,3,256,256]{4,3,2,1,0:T(8,128)(2,1)}, u32[]{:S(2)}) copy-start(bf16[3,3,3,256,256]{4,3,2,1,0:T(8,128)(2,1)} %param.17) | copy-start | bytes 10616836
  23.3 3.7 %copy-start.2 = (bf16[1024,512]{1,0:T(8,128)(2,1)S(1)}, bf16[1024,512]{1,0:T(8,128)(2,1)}, u32[]{:S(2)}) copy-start(bf16[1024,512]{1,0:T(8,128)(2,1)} %down_ref.3) | copy-start | bytes 3145732
  23.3 3.6 %copy-start.8 = (f32[256]{0:T(256)S(1)}, f32[256]{0:T(256)}, u32[]{:S(2)}) copy-start(f32[256]{0:T(256)} %param.16) | copy-start | bytes 3076
  29.5 11.2 %collective-permute-start.5 = (bf16[128,512]{1,0:T(8,128)(2,1)S(1)}, bf16[128,512]{1,0:T(8,128)(2,1)S(1)}, u32[]{:S(2)}, u32[]{:S(2)}) collective-permute-start(bf16[128,512]{1,0:T(8,128)(2,1)S(1)} %get-tuple-element.74), channel_id=1, source_target_pairs={{0,32},{32,64},{64,96},{96,128},{128,160},{160,192},{192,224},{1,3... | collective-permute-start | bytes 393224 | tf_op jit(solution)/shard_map/ppermute | solution.py:445
  35.1 8.0 %collective-permute-start.6 = (bf16[128,512]{1,0:T(8,128)(2,1)S(1)}, bf16[128,512]{1,0:T(8,128)(2,1)S(1)}, u32[]{:S(2)}, u32[]{:S(2)}) collective-permute-start(bf16[128,512]{1,0:T(8,128)(2,1)S(1)} %get-tuple-element.75), channel_id=1, source_target_pairs={{0,64},{32,96},{64,128},{96,160},{128,192},{160,224},{1,65},{33,97... | collective-permute-start | bytes 393224 | tf_op jit(solution)/shard_map/ppermute | solution.py:444
  37.3 5.8 %copy-start.7 = (f32[512]{0:T(512)S(1)}, f32[512]{0:T(512)}, u32[]{:S(2)}) copy-start(f32[512]{0:T(512)} %param.19) | copy-start | bytes 6148
  44.0 17.8 %all-to-all-start = ((bf16[4,128,512]{2,1,0:T(8,128)(2,1)}), bf16[4,128,512]{2,1,0:T(8,128)(2,1)S(1)}, u32[]{:S(2)}, u32[]{:S(2)}) async-start(bf16[4,128,512]{2,1,0:T(8,128)(2,1)} %get-tuple-element.78), calls=%async_computation | async-start | bytes 1048576 | tf_op jit(solution)/shard_map/all_to_all | solution.py:449
  53.1 6.5 %collective-permute-start.8 = (bf16[128,512]{1,0:T(8,128)(2,1)S(1)}, bf16[128,512]{1,0:T(8,128)(2,1)S(1)}, u32[]{:S(2)}, u32[]{:S(2)}) collective-permute-start(bf16[128,512]{1,0:T(8,128)(2,1)S(1)} %get-tuple-element.77.mine_ref), channel_id=1, source_target_pairs={{0,16},{1,17},{16,0},{17,1},{2,18},{3,19},{18,2},{19,3},{4,20},{5,... | collective-permute-start | bytes 393224 | tf_op jit(solution)/shard_map/ppermute | solution.py:399
  53.7 5.9 %collective-permute-start.9 = (bf16[128,512]{1,0:T(8,128)(2,1)S(1)}, bf16[128,512]{1,0:T(8,128)(2,1)S(1)}, u32[]{:S(2)}, u32[]{:S(2)}) collective-permute-start(bf16[128,512]{1,0:T(8,128)(2,1)S(1)} %get-tuple-element.77.mine_ref), channel_id=1, source_target_pairs={{0,17},{1,0},{16,1},{17,16},{2,19},{3,2},{18,3},{19,18},{4,21},{5,... | collective-permute-start | bytes 393224 | tf_op jit(solution)/shard_map/ppermute | solution.py:399
  61.8 1.9 %collective-permute-start.10 = (bf16[512,512]{1,0:T(8,128)(2,1)S(1)}, bf16[512,512]{1,0:T(8,128)(2,1)S(1)}, u32[]{:S(2)}, u32[]{:S(2)}) collective-permute-start(bf16[512,512]{1,0:T(8,128)(2,1)S(1)} %bitcast.16), channel_id=1, source_target_pairs={{0,8},{8,0},{1,9},{9,1},{2,10},{10,2},{3,11},{11,3},{4,12},{12,4},... | collective-permute-start | bytes 1572872 | tf_op jit(solution)/shard_map/ppermute | solution.py:395
  61.8 7.2 %collective-permute-start.7 = (bf16[128,512]{1,0:T(8,128)(2,1)S(1)}, bf16[128,512]{1,0:T(8,128)(2,1)S(1)}, u32[]{:S(2)}, u32[]{:S(2)}) collective-permute-start(bf16[128,512]{1,0:T(8,128)(2,1)S(1)} %get-tuple-element.77.mine_ref), channel_id=1, source_target_pairs={{0,1},{1,16},{16,17},{17,0},{2,3},{3,18},{18,19},{19,2},{4,5},{5,2... | collective-permute-start | bytes 393224 | tf_op jit(solution)/shard_map/ppermute | solution.py:399
  64.7 8.3 %collective-permute-start.11 = (bf16[144,512]{1,0:T(8,128)(2,1)S(1)}, bf16[144,512]{1,0:T(8,128)(2,1)S(1)}, u32[]{:S(2)}, u32[]{:S(2)}) collective-permute-start(bf16[144,512]{1,0:T(8,128)(2,1)S(1)} %get-tuple-element.84), channel_id=1, source_target_pairs={{0,16},{1,17},{16,0},{17,1},{2,18},{3,19},{18,2},{19,3},{4,20},{5,... | collective-permute-start | bytes 442376 | tf_op jit(solution)/shard_map/ppermute | solution.py:399
  64.9 10.3 %collective-permute-start.12 = (bf16[144,512]{1,0:T(8,128)(2,1)S(1)}, bf16[144,512]{1,0:T(8,128)(2,1)S(1)}, u32[]{:S(2)}, u32[]{:S(2)}) collective-permute-start(bf16[144,512]{1,0:T(8,128)(2,1)S(1)} %get-tuple-element.85), channel_id=1, source_target_pairs={{0,1},{1,16},{16,17},{17,0},{2,3},{3,18},{18,19},{19,2},{4,5},{5,2... | collective-permute-start | bytes 442376 | tf_op jit(solution)/shard_map/ppermute | solution.py:399
  70.0 5.5 %collective-permute-start.13 = (bf16[144,512]{1,0:T(8,128)(2,1)S(1)}, bf16[144,512]{1,0:T(8,128)(2,1)S(1)}, u32[]{:S(2)}, u32[]{:S(2)}) collective-permute-start(bf16[144,512]{1,0:T(8,128)(2,1)S(1)} %get-tuple-element.86), channel_id=1, source_target_pairs={{0,17},{1,0},{16,1},{17,16},{2,19},{3,2},{18,3},{19,18},{4,21},{5,... | collective-permute-start | bytes 442376 | tf_op jit(solution)/shard_map/ppermute | solution.py:399

commit v10 on v9

--- a/solution.py
+++ b/solution.py
@@ -346,11 +346,6 @@
     return jnp.concatenate([values, last], 0).astype(BF16)
 
 
-def level_of(block):
-    across = jnp.sum(block[128:, :128].astype(F32), 0, keepdims=True)
-    return jnp.broadcast_to(across, (128, 128)).T[:, :1]
-
-
 def softmax_part(queries, *parts):
     scores = [
         lax.dot_general(queries, keys, (((1,), (1,)), ((), ())), preferred_element_type=F32) for keys in parts
@@ -379,7 +374,9 @@
 
 def finish_kernel(mixed_ref, level_ref, got1_ref, got2_ref, got3_ref, latent_ref, mix_ref, out_ref):
     blocks = [ref[...] for ref in (got1_ref, got2_ref, got3_ref)]
-    levels = [level_ref[:, :1]] + [level_of(block) for block in blocks]
+    across = [jnp.sum(block[128:, :128].astype(F32), 0, keepdims=True) for block in blocks]
+    turned_levels = jnp.concatenate(across + [jnp.zeros((125, 128), F32)], 0).T
+    levels = [level_ref[:, :1]] + [turned_levels[:, k : k + 1] for k in range(3)]
     values = [mixed_ref[...]] + [block[:128].astype(F32) for block in blocks]
     top = functools.reduce(jnp.maximum, levels)
     shares = [jnp.exp(level - top) for level in levels]

time: 76.9 us -> 77 us (level)
  no operation moved by 1% of the time
where the time goes in v10:
time: 77 us; the launch traced here: 76.7 us
  starting transfers between devices  32.8 us (43%)
  waiting for transfers between devices  22.3 us (29%)
  Pallas kernels  21 us (27%)
    ppermute x6, waiting for transfers between devices, turned(): return lax.ppermute(value, RING, [(i, (i + step) % 4) for i in range(4)])  12 us
    all_to_all x1, starting transfers between devices, per_device(): keys = lax.all_to_all(copies, 'y', 0, 0, tiled=True).reshape(512, 512)  9.09 us
    ppermute x5, starting transfers between devices, swapped(): return lax.ppermute(value, axis, pairs)  6.47 us
    ppermute x1, starting transfers between devices, per_device(): near = lax.ppermute(near, 'tm', [(i, i + 1) for i in range(7)])  5.6 us
    ppermute x1, starting transfers between devices, per_device(): got = lax.ppermute(sent, 'tm', [(i, i + 1) for i in range(7)])  5.17 us
    ppermute x6, starting transfers between devices, turned(): return lax.ppermute(value, RING, [(i, (i + step) % 4) for i in range(4)])  4.29 us
    pallas_call x2, Pallas kernels, compose(): call(functools.partial(compose_kernel, own), shape((16, 256, 256), BF16),...  3.83 us
    ppermute x5, waiting for transfers between devices, swapped(): return lax.ppermute(value, axis, pairs)  3.13 us
  transfers between devices with their start and end apart: 15, of which 11 were waited for; matrix products, arithmetic and copies ran while one was open for 0% of the time, Pallas kernels for 17%

profile of v10, /device:TPU:96, one launch (start us, length us, event | category | flops | bytes accessed | tf_op | source)
XLA Modules:
  0.0 76.7 jit_solution(16975227301751182726)
XLA Ops:
  0.0 1.0 %edges.1 = (bf16[2,3,64,128]{3,2,1,0:T(8,128)(2,1)S(1)}, bf16[2,3,64,128]{3,2,1,0:T(8,128)(2,1)S(1)}) custom-call(s32[1]{0:T(128)} %bitcast.3.odd_ref, bf16[2,32,64,128]{3,2,1,0:T(8,128)(2,1)} %x_ref.1), custom_call_target="tpu_custom_call" | custom-call | flops 1000 | bytes 4194304 | tf_op jit(solution)/shard_map/edges/pallas_call | solution.py:402
  1.0 0.7 collective-permute-start
  1.6 4.5 %collective-permute-start.1 = (bf16[2,3,64,128]{3,2,1,0:T(8,128)(2,1)S(1)}, bf16[2,3,64,128]{3,2,1,0:T(8,128)(2,1)S(1)}, u32[]{:S(2)}, u32[]{:S(2)}) collective-permute-start(bf16[2,3,64,128]{3,2,1,0:T(8,128)(2,1)S(1)} %get-tuple-element.48), channel_id=1, source_target_pairs={{0,8},{8,0},{16,24},{24,16},{1,9},{9,1},{17,25},{25,17},{2,10},{10... | collective-permute-start | bytes 294920 | tf_op jit(solution)/shard_map/ppermute | solution.py:392
  6.1 2.0 %prepare.1 = (f32[2,32,64,128]{3,2,1,0:T(8,128)S(1)}, bf16[2,32,4,128]{3,2,1,0:T(4,128)(2,1)S(1)}, bf16[2,32,4,128]{3,2,1,0:T(4,128)(2,1)S(1)}, bf16[3,3,3,128,1...) custom-call(bf16[2,32,64,128]{3,2,1,0:T(8,128)(2,1)} %x_ref.1, f32[1,128]{1,0:T(1,128)} %bitcast.25, ...), custom_call_target="tpu_custom_call" | custom-call | flops 10000000 | bytes 4194304 | tf_op jit(solution)/shard_map/prepare/pallas_call | solution.py:139
  8.1 0.0 copy-start.9
  8.1 0.1 pad_add_fusion.flag_ref
  8.3 0.1 broadcast_select_fusion.4
  8.4 0.7 collective-permute-start.2
  9.1 0.7 collective-permute-start.3
  9.7 1.9 %compose_next.1.weight_ref = bf16[16,256,256]{2,1,0:T(8,128)(2,1)S(1)} custom-call(s32[3]{0:T(128)S(1)} %pad_add_fusion.flag_ref, bf16[3,3,3,128,128]{4,3,2,1,0:T(8,128)(2,1)S(1)} %get-tuple-element.64.conv, bf16[1024,256]{1,0:T(8,128)(2,1)S(1)} %get-tuple-element.65.down.down_ref), custom_call_target="tpu_custom_call" | custom-call | flops 900000000 | bytes 4194304 | tf_op jit(solution)/shard_map/compose_next/pallas_call | solution.py:85
  11.6 1.2 %collective-permute-done.2 = bf16[2,38,4,128]{3,2,1,0:T(4,128)(2,1)S(1)} collective-permute-done((bf16[2,38,4,128]{3,2,1,0:T(4,128)(2,1)S(1)}, bf16[2,38,4,128]{3,2,1,0:T(4,128)(2,1)S(1)}, u32[]{:S(2)}, u32[]{:S(2)}) %collective-permute-start.2) | collective-permute-done | bytes 77856 | tf_op jit(solution)/shard_map/ppermute | solution.py:392
  12.9 0.0 copy-start.3
  12.9 0.0 copy-start.4
  12.9 0.0 copy-start.5
  12.9 0.0 copy-start.6
  13.0 2.4 %fine_next.1 = (bf16[624,256]{1,0:T(8,128)(2,1)S(1)}, bf16[2,4,19,48,256]{4,3,2,1,0:T(8,128)(2,1)S(1)}) custom-call(f32[2,32,64,128]{3,2,1,0:T(8,128)S(1)} %get-tuple-element.52.act_ref, bf16[2,3,64,128]{3,2,1,0:T(8,128)(2,1)S(1)} %get-tuple-element.53.up_ref, bf16[2,3,64,128]{3,2,1,0:T(8,128)(2,1)S(1)} %get-tuple-element.54.low_ref, ...), custom_call_target="tpu_custom_call" | custom-call | flops 1800000000 | bytes 4194304 | tf_op jit(solution)/shard_map/fine_next/pallas_call | solution.py:224
  15.4 0.0 copy-start.1
  15.4 5.2 %collective-permute-start.4 = (bf16[624,256]{1,0:T(8,128)(2,1)S(1)}, bf16[624,256]{1,0:T(8,128)(2,1)S(1)}, u32[]{:S(2)}, u32[]{:S(2)}) collective-permute-start(bf16[624,256]{1,0:T(8,128)(2,1)S(1)} %get-tuple-element.63), channel_id=1, source_target_pairs={{0,32},{32,64},{64,96},{96,128},{128,160},{160,192},{192,224},{1,3... | collective-permute-start | bytes 958472 | tf_op jit(solution)/shard_map/ppermute | solution.py:432
  20.6 0.7 mix.1
  21.4 1.9 %compose_own.1.weight_ref = bf16[16,256,256]{2,1,0:T(8,128)(2,1)S(1)} custom-call(s32[3]{0:T(128)S(1)} %pad_add_fusion.flag_ref, bf16[3,3,3,128,128]{4,3,2,1,0:T(8,128)(2,1)S(1)} %get-tuple-element.64.conv, bf16[1024,256]{1,0:T(8,128)(2,1)S(1)} %get-tuple-element.65.down.down_ref), custom_call_target="tpu_custom_call" | custom-call | flops 900000000 | bytes 4194304 | tf_op jit(solution)/shard_map/compose_own/pallas_call | solution.py:85
  23.3 0.0 copy-start
  23.3 0.0 copy-start.2
  23.3 2.6 %fine_own.1.own_ref = f32[18,48,256]{2,1,0:T(8,128)S(1)} custom-call(bf16[2,32,64,128]{3,2,1,0:T(8,128)(2,1)S(1)} %copy-done.1, bf16[2,3,64,128]{3,2,1,0:T(8,128)(2,1)S(1)} %get-tuple-element.53.up_ref, bf16[2,3,64,128]{3,2,1,0:T(8,128)(2,1)S(1)} %get-tuple-element.54.low_ref, bf16[2,38,4,128]{3,2,1,0:T(4,128)(2,1)S(1)} %bitcast.22, ...), custom_call_target="tpu_custom_call" | custom-call | flops 2200000000 | bytes 4194304 | tf_op jit(solution)/shard_map/fine_own/pallas_call | solution.py:235
  26.0 1.0 %collective-permute-done.4.got_ref = bf16[624,256]{1,0:T(8,128)(2,1)S(1)} collective-permute-done((bf16[624,256]{1,0:T(8,128)(2,1)S(1)}, bf16[624,256]{1,0:T(8,128)(2,1)S(1)}, u32[]{:S(2)}, u32[]{:S(2)}) %collective-permute-start.4) | collective-permute-done | bytes 319520 | tf_op jit(solution)/shard_map/ppermute | solution.py:432
  27.0 2.5 %coarse_sent.1 = (bf16[128,512]{1,0:T(8,128)(2,1)S(1)}, bf16[128,512]{1,0:T(8,128)(2,1)S(1)}, f32[512,256]{1,0:T(8,128)S(1)}, bf16[512,2304]{1,0:T(8,128)(2,1)S(1)}, f32[2,18,48,128]{3,2,1,0:T(8,128)S(1)}) custom-call(s32[3]{0:T(128)S(1)} %pad_add_fusion.flag_ref, f32[18,48,256]{2,1,0:T(8,128)S(1)} %fine_own.1.own_ref, ...), custom_call_target="tpu_custom_call" | custom-call | flops 1500000000 | bytes 4194304 | tf_op jit(solution)/shard_map/coarse_sent/pallas_call | solution.py:309
  29.5 5.6 %collective-permute-start.5 = (bf16[128,512]{1,0:T(8,128)(2,1)S(1)}, bf16[128,512]{1,0:T(8,128)(2,1)S(1)}, u32[]{:S(2)}, u32[]{:S(2)}) collective-permute-start(bf16[128,512]{1,0:T(8,128)(2,1)S(1)} %get-tuple-element.74), channel_id=1, source_target_pairs={{0,32},{32,64},{64,96},{96,128},{128,160},{160,192},{192,224},{1,3... | collective-permute-start | bytes 393224 | tf_op jit(solution)/shard_map/ppermute | solution.py:442
  35.1 2.2 %collective-permute-start.6 = (bf16[128,512]{1,0:T(8,128)(2,1)S(1)}, bf16[128,512]{1,0:T(8,128)(2,1)S(1)}, u32[]{:S(2)}, u32[]{:S(2)}) collective-permute-start(bf16[128,512]{1,0:T(8,128)(2,1)S(1)} %get-tuple-element.75), channel_id=1, source_target_pairs={{0,64},{32,96},{64,128},{96,160},{128,192},{160,224},{1,65},{33,97... | collective-permute-start | bytes 393224 | tf_op jit(solution)/shard_map/ppermute | solution.py:441
  37.3 0.0 copy-start.7
  37.3 1.8 %coarse_here.1.own_ref = f32[128,512]{1,0:T(8,128)S(1)} custom-call(s32[3]{0:T(128)S(1)} %pad_add_fusion.flag_ref, bf16[512,2304]{1,0:T(8,128)(2,1)S(1)} %get-tuple-element.71.windows, f32[2,18,48,128]{3,2,1,0:T(8,128)S(1)} %get-tuple-element.72.reduced, f32[512,256]{1,0:T(8,128)S(1)} %get-tuple-element.73.c1_ref, bf16[3,9,256,256]{3,2,1,0:T(8,128)(2,1)S(1)} %bitcast.15, ...), custom_call_target="tpu_custom_call" | custom-call | flops 1000 | bytes 1000 | tf_op jit(solution)/shard_map/coarse_here/pallas_call | solution.py:317
  39.0 1.7 %collective-permute-done.5.near_ref = bf16[128,512]{1,0:T(8,128)(2,1)S(1)} collective-permute-done((bf16[128,512]{1,0:T(8,128)(2,1)S(1)}, bf16[128,512]{1,0:T(8,128)(2,1)S(1)}, u32[]{:S(2)}, u32[]{:S(2)}) %collective-permute-start.5) | collective-permute-done | bytes 131104 | tf_op jit(solution)/shard_map/ppermute | solution.py:442
  40.7 2.3 %collective-permute-done.6.far_ref = bf16[128,512]{1,0:T(8,128)(2,1)S(1)} collective-permute-done((bf16[128,512]{1,0:T(8,128)(2,1)S(1)}, bf16[128,512]{1,0:T(8,128)(2,1)S(1)}, u32[]{:S(2)}, u32[]{:S(2)}) %collective-permute-start.6) | collective-permute-done | bytes 131104 | tf_op jit(solution)/shard_map/ppermute | solution.py:441
  43.0 1.0 %latent.1 = (bf16[128,512]{1,0:T(8,128)(2,1)S(1)}, bf16[128,512]{1,0:T(8,128)(2,1)S(1)}, bf16[4,128,512]{2,1,0:T(8,128)(2,1)}) custom-call(f32[128,512]{1,0:T(8,128)S(1)} %coarse_here.1.own_ref, bf16[128,512]{1,0:T(8,128)(2,1)S(1)} %collective-permute-done.5.near_ref, bf16[128,512]{1,0:T(8,128)(2,1)S(1)} %collective-permute-done.6.far_ref, ...), custom_call_target="tpu_custom_call" | custom-call | flops 80000000 | bytes 4194304 | tf_op jit(solution)/shard_map/latent/pallas_call | solution.py:443
  44.0 9.1 %all-to-all-start = ((bf16[4,128,512]{2,1,0:T(8,128)(2,1)}), bf16[4,128,512]{2,1,0:T(8,128)(2,1)S(1)}, u32[]{:S(2)}, u32[]{:S(2)}) async-start(bf16[4,128,512]{2,1,0:T(8,128)(2,1)} %get-tuple-element.78), calls=%async_computation | async-start | bytes 1048576 | tf_op jit(solution)/shard_map/all_to_all | solution.py:446
  53.1 0.6 collective-permute-start.8
  53.7 1.3 %collective-permute-start.9 = (bf16[128,512]{1,0:T(8,128)(2,1)S(1)}, bf16[128,512]{1,0:T(8,128)(2,1)S(1)}, u32[]{:S(2)}, u32[]{:S(2)}) collective-permute-start(bf16[128,512]{1,0:T(8,128)(2,1)S(1)} %get-tuple-element.77.mine_ref), channel_id=1, source_target_pairs={{0,17},{1,0},{16,1},{17,16},{2,19},{3,2},{18,3},{19,18},{4,21},{5,... | collective-permute-start | bytes 393224 | tf_op jit(solution)/shard_map/ppermute | solution.py:396
  55.0 4.5 %collective-permute-done.8.q1_ref = bf16[128,512]{1,0:T(8,128)(2,1)S(1)} collective-permute-done((bf16[128,512]{1,0:T(8,128)(2,1)S(1)}, bf16[128,512]{1,0:T(8,128)(2,1)S(1)}, u32[]{:S(2)}, u32[]{:S(2)}) %collective-permute-start.8) | collective-permute-done | bytes 131104 | tf_op jit(solution)/shard_map/ppermute | solution.py:396
  59.6 2.2 %all-to-all-done = bf16[4,128,512]{2,1,0:T(8,128)(2,1)S(1)} async-done(((bf16[4,128,512]{2,1,0:T(8,128)(2,1)}), bf16[4,128,512]{2,1,0:T(8,128)(2,1)S(1)}, u32[]{:S(2)}, u32[]{:S(2)}) %all-to-all-start) | async-done | bytes 524320 | tf_op jit(solution)/shard_map/all_to_all | solution.py:446
  61.8 1.9 %collective-permute-done.10.other_keys_ref = bf16[512,512]{1,0:T(8,128)(2,1)S(1)} collective-permute-done((bf16[512,512]{1,0:T(8,128)(2,1)S(1)}, bf16[512,512]{1,0:T(8,128)(2,1)S(1)}, u32[]{:S(2)}, u32[]{:S(2)}) %collective-permute-start.10) | collective-permute-done | bytes 524320 | tf_op jit(solution)/shard_map/ppermute | solution.py:392
  63.7 1.0 %attend_two.1 = (bf16[144,512]{1,0:T(8,128)(2,1)S(1)}, bf16[144,512]{1,0:T(8,128)(2,1)S(1)}) custom-call(bf16[128,512]{1,0:T(8,128)(2,1)S(1)} %collective-permute-done.8.q1_ref, bf16[128,512]{1,0:T(8,128)(2,1)S(1)} %collective-permute-done.9.q2_ref, bf16[512,512]{1,0:T(8,128)(2,1)S(1)} %bitcast.17, bf16[512,512]{1,0:T(8,128)(2,1)S(1)} %collective-permute-done.10.other_keys_ref), custom_call_target="tpu_custom_call" | custom-call | flops 550000000 | bytes 4194304 | tf_op jit(solution)/shard_map/attend_two/pallas_call | solution.py:451
  64.7 0.2 collective-permute-start.11
  64.9 2.1 %collective-permute-start.12 = (bf16[144,512]{1,0:T(8,128)(2,1)S(1)}, bf16[144,512]{1,0:T(8,128)(2,1)S(1)}, u32[]{:S(2)}, u32[]{:S(2)}) collective-permute-start(bf16[144,512]{1,0:T(8,128)(2,1)S(1)} %get-tuple-element.85), channel_id=1, source_target_pairs={{0,1},{1,16},{16,17},{17,0},{2,3},{3,18},{18,19},{19,2},{4,5},{5,2... | collective-permute-start | bytes 442376 | tf_op jit(solution)/shard_map/ppermute | solution.py:396
  67.0 2.0 %collective-permute-done.7.q3_ref = bf16[128,512]{1,0:T(8,128)(2,1)S(1)} collective-permute-done((bf16[128,512]{1,0:T(8,128)(2,1)S(1)}, bf16[128,512]{1,0:T(8,128)(2,1)S(1)}, u32[]{:S(2)}, u32[]{:S(2)}) %collective-permute-start.7) | collective-permute-done | bytes 131104 | tf_op jit(solution)/shard_map/ppermute | solution.py:396
  69.0 1.0 %attend_last.1 = (bf16[144,512]{1,0:T(8,128)(2,1)S(1)}, f32[128,512]{1,0:T(8,128)S(1)}, f32[128,128]{1,0:T(8,128)S(1)}) custom-call(bf16[128,512]{1,0:T(8,128)(2,1)S(1)} %collective-permute-done.7.q3_ref, bf16[128,512]{1,0:T(8,128)(2,1)S(1)} %get-tuple-element.77.mine_ref, bf16[512,512]{1,0:T(8,128)(2,1)S(1)} %bitcast.18, ...), custom_call_target="tpu_custom_call" | custom-call | flops 550000000 | bytes 4194304 | tf_op jit(solution)/shard_map/attend_last/pallas_call | solution.py:454
  70.0 0.1 collective-permute-start.13
  70.1 3.0 %collective-permute-done.11.got1_ref = bf16[144,512]{1,0:T(8,128)(2,1)S(1)} collective-permute-done((bf16[144,512]{1,0:T(8,128)(2,1)S(1)}, bf16[144,512]{1,0:T(8,128)(2,1)S(1)}, u32[]{:S(2)}, u32[]{:S(2)}) %collective-permute-start.11) | collective-permute-done | bytes 147488 | tf_op jit(solution)/shard_map/ppermute | solution.py:396
  73.0 2.2 %collective-permute-done.12.got2_ref = bf16[144,512]{1,0:T(8,128)(2,1)S(1)} collective-permute-done((bf16[144,512]{1,0:T(8,128)(2,1)S(1)}, bf16[144,512]{1,0:T(8,128)(2,1)S(1)}, u32[]{:S(2)}, u32[]{:S(2)}) %collective-permute-start.12) | collective-permute-done | bytes 147488 | tf_op jit(solution)/shard_map/ppermute | solution.py:396
  75.3 0.2 collective-permute-done.13.got3_ref
  75.5 1.3 %finish.1 = bf16[128,512]{1,0:T(8,128)(2,1)} custom-call(f32[128,512]{1,0:T(8,128)S(1)} %get-tuple-element.80.mixed_ref, f32[128,128]{1,0:T(8,128)S(1)} %get-tuple-element.81.level_ref, bf16[144,512]{1,0:T(8,128)(2,1)S(1)} %collective-permute-done.11.got1_ref, bf16[144,512]{1,0:T(8,128)(2,1)S(1)} %collective-permute-done.12.got2_ref, ...), custom_call_target="tpu_custom_call" | custom-call | flops 70000000 | bytes 4194304 | tf_op jit(solution)/shard_map/finish/pallas_call | solution.py:462
  (20 shorter events, 0.1 us)
Async XLA Ops:
  1.0 7.2 %collective-permute-start = (bf16[2,3,64,128]{3,2,1,0:T(8,128)(2,1)S(1)}, bf16[2,3,64,128]{3,2,1,0:T(8,128)(2,1)S(1)}, u32[]{:S(2)}, u32[]{:S(2)}) collective-permute-start(bf16[2,3,64,128]{3,2,1,0:T(8,128)(2,1)S(1)} %get-tuple-element.47), channel_id=1, source_target_pairs={{8,16},{16,8},{9,17},{17,9},{10,18},{18,10},{11,19},{19,11},{12,20... | collective-permute-start | bytes 294920 | tf_op jit(solution)/shard_map/ppermute | solution.py:392
  1.6 6.6 %collective-permute-start.1 = (bf16[2,3,64,128]{3,2,1,0:T(8,128)(2,1)S(1)}, bf16[2,3,64,128]{3,2,1,0:T(8,128)(2,1)S(1)}, u32[]{:S(2)}, u32[]{:S(2)}) collective-permute-start(bf16[2,3,64,128]{3,2,1,0:T(8,128)(2,1)S(1)} %get-tuple-element.48), channel_id=1, source_target_pairs={{0,8},{8,0},{16,24},{24,16},{1,9},{9,1},{17,25},{25,17},{2,10},{10... | collective-permute-start | bytes 294920 | tf_op jit(solution)/shard_map/ppermute | solution.py:392
  8.1 4.8 %copy-start.9 = (f32[128]{0:T(128)S(1)}, f32[128]{0:T(128)}, u32[]{:S(2)}) copy-start(f32[128]{0:T(128)} %param.13) | copy-start | bytes 1540
  8.4 4.5 %collective-permute-start.2 = (bf16[2,38,4,128]{3,2,1,0:T(4,128)(2,1)S(1)}, bf16[2,38,4,128]{3,2,1,0:T(4,128)(2,1)S(1)}, u32[]{:S(2)}, u32[]{:S(2)}) collective-permute-start(bf16[2,38,4,128]{3,2,1,0:T(4,128)(2,1)S(1)} %get-tuple-element.94), channel_id=1, source_target_pairs={{0,1},{1,0},{2,3},{3,2},{4,5},{5,4},{6,7},{7,6},{8,9},{9,8},{10,11... | collective-permute-start | bytes 233480 | tf_op jit(solution)/shard_map/ppermute | solution.py:392
  9.1 3.8 %collective-permute-start.3 = (bf16[2,38,4,128]{3,2,1,0:T(4,128)(2,1)S(1)}, bf16[2,38,4,128]{3,2,1,0:T(4,128)(2,1)S(1)}, u32[]{:S(2)}, u32[]{:S(2)}) collective-permute-start(bf16[2,38,4,128]{3,2,1,0:T(4,128)(2,1)S(1)} %get-tuple-element.93), channel_id=1, source_target_pairs={{1,2},{2,1},{3,4},{4,3},{5,6},{6,5},{9,10},{10,9},{11,12},{12,11},... | collective-permute-start | bytes 233480 | tf_op jit(solution)/shard_map/ppermute | solution.py:392
  12.9 7.7 %copy-start.3 = (bf16[512,512]{1,0:T(8,128)(2,1)S(1)}, bf16[512,512]{1,0:T(8,128)(2,1)}, u32[]{:S(2)}) copy-start(bf16[512,512]{1,0:T(8,128)(2,1)} %query_ref.1) | copy-start | bytes 1572868
  12.9 7.7 %copy-start.4 = (bf16[512,512]{1,0:T(8,128)(2,1)S(1)}, bf16[512,512]{1,0:T(8,128)(2,1)}, u32[]{:S(2)}) copy-start(bf16[512,512]{1,0:T(8,128)(2,1)} %key_ref.1) | copy-start | bytes 1572868
  12.9 7.7 %copy-start.5 = (bf16[512,512]{1,0:T(8,128)(2,1)S(1)}, bf16[512,512]{1,0:T(8,128)(2,1)}, u32[]{:S(2)}) copy-start(bf16[512,512]{1,0:T(8,128)(2,1)} %value_ref.1) | copy-start | bytes 1572868
  12.9 7.7 %copy-start.6 = (bf16[512,512]{1,0:T(8,128)(2,1)S(1)}, bf16[512,512]{1,0:T(8,128)(2,1)}, u32[]{:S(2)}) copy-start(bf16[512,512]{1,0:T(8,128)(2,1)} %out_ref.1) | copy-start | bytes 1572868
  15.4 7.9 %copy-start.1 = (bf16[2,32,64,128]{3,2,1,0:T(8,128)(2,1)S(1)}, bf16[2,32,64,128]{3,2,1,0:T(8,128)(2,1)}, u32[]{:S(2)}) copy-start(bf16[2,32,64,128]{3,2,1,0:T(8,128)(2,1)} %x_ref.1) | copy-start | bytes 3145732
  15.4 11.6 %collective-permute-start.4 = (bf16[624,256]{1,0:T(8,128)(2,1)S(1)}, bf16[624,256]{1,0:T(8,128)(2,1)S(1)}, u32[]{:S(2)}, u32[]{:S(2)}) collective-permute-start(bf16[624,256]{1,0:T(8,128)(2,1)S(1)} %get-tuple-element.63), channel_id=1, source_target_pairs={{0,32},{32,64},{64,96},{96,128},{128,160},{160,192},{192,224},{1,3... | collective-permute-start | bytes 958472 | tf_op jit(solution)/shard_map/ppermute | solution.py:432
  23.3 3.7 %copy-start = (bf16[3,3,3,256,256]{4,3,2,1,0:T(8,128)(2,1)S(1)}, bf16[3,3,3,256,256]{4,3,2,1,0:T(8,128)(2,1)}, u32[]{:S(2)}) copy-start(bf16[3,3,3,256,256]{4,3,2,1,0:T(8,128)(2,1)} %param.17) | copy-start | bytes 10616836
  23.3 3.7 %copy-start.2 = (bf16[1024,512]{1,0:T(8,128)(2,1)S(1)}, bf16[1024,512]{1,0:T(8,128)(2,1)}, u32[]{:S(2)}) copy-start(bf16[1024,512]{1,0:T(8,128)(2,1)} %down_ref.3) | copy-start | bytes 3145732
  23.3 3.6 %copy-start.8 = (f32[256]{0:T(256)S(1)}, f32[256]{0:T(256)}, u32[]{:S(2)}) copy-start(f32[256]{0:T(256)} %param.16) | copy-start | bytes 3076
  29.5 11.2 %collective-permute-start.5 = (bf16[128,512]{1,0:T(8,128)(2,1)S(1)}, bf16[128,512]{1,0:T(8,128)(2,1)S(1)}, u32[]{:S(2)}, u32[]{:S(2)}) collective-permute-start(bf16[128,512]{1,0:T(8,128)(2,1)S(1)} %get-tuple-element.74), channel_id=1, source_target_pairs={{0,32},{32,64},{64,96},{96,128},{128,160},{160,192},{192,224},{1,3... | collective-permute-start | bytes 393224 | tf_op jit(solution)/shard_map/ppermute | solution.py:442
  35.1 8.0 %collective-permute-start.6 = (bf16[128,512]{1,0:T(8,128)(2,1)S(1)}, bf16[128,512]{1,0:T(8,128)(2,1)S(1)}, u32[]{:S(2)}, u32[]{:S(2)}) collective-permute-start(bf16[128,512]{1,0:T(8,128)(2,1)S(1)} %get-tuple-element.75), channel_id=1, source_target_pairs={{0,64},{32,96},{64,128},{96,160},{128,192},{160,224},{1,65},{33,97... | collective-permute-start | bytes 393224 | tf_op jit(solution)/shard_map/ppermute | solution.py:441
  37.3 5.8 %copy-start.7 = (f32[512]{0:T(512)S(1)}, f32[512]{0:T(512)}, u32[]{:S(2)}) copy-start(f32[512]{0:T(512)} %param.19) | copy-start | bytes 6148
  44.0 17.8 %all-to-all-start = ((bf16[4,128,512]{2,1,0:T(8,128)(2,1)}), bf16[4,128,512]{2,1,0:T(8,128)(2,1)S(1)}, u32[]{:S(2)}, u32[]{:S(2)}) async-start(bf16[4,128,512]{2,1,0:T(8,128)(2,1)} %get-tuple-element.78), calls=%async_computation | async-start | bytes 1048576 | tf_op jit(solution)/shard_map/all_to_all | solution.py:446
  53.1 6.5 %collective-permute-start.8 = (bf16[128,512]{1,0:T(8,128)(2,1)S(1)}, bf16[128,512]{1,0:T(8,128)(2,1)S(1)}, u32[]{:S(2)}, u32[]{:S(2)}) collective-permute-start(bf16[128,512]{1,0:T(8,128)(2,1)S(1)} %get-tuple-element.77.mine_ref), channel_id=1, source_target_pairs={{0,16},{1,17},{16,0},{17,1},{2,18},{3,19},{18,2},{19,3},{4,20},{5,... | collective-permute-start | bytes 393224 | tf_op jit(solution)/shard_map/ppermute | solution.py:396
  53.7 5.9 %collective-permute-start.9 = (bf16[128,512]{1,0:T(8,128)(2,1)S(1)}, bf16[128,512]{1,0:T(8,128)(2,1)S(1)}, u32[]{:S(2)}, u32[]{:S(2)}) collective-permute-start(bf16[128,512]{1,0:T(8,128)(2,1)S(1)} %get-tuple-element.77.mine_ref), channel_id=1, source_target_pairs={{0,17},{1,0},{16,1},{17,16},{2,19},{3,2},{18,3},{19,18},{4,21},{5,... | collective-permute-start | bytes 393224 | tf_op jit(solution)/shard_map/ppermute | solution.py:396
  61.8 1.9 %collective-permute-start.10 = (bf16[512,512]{1,0:T(8,128)(2,1)S(1)}, bf16[512,512]{1,0:T(8,128)(2,1)S(1)}, u32[]{:S(2)}, u32[]{:S(2)}) collective-permute-start(bf16[512,512]{1,0:T(8,128)(2,1)S(1)} %bitcast.16), channel_id=1, source_target_pairs={{0,8},{8,0},{1,9},{9,1},{2,10},{10,2},{3,11},{11,3},{4,12},{12,4},... | collective-permute-start | bytes 1572872 | tf_op jit(solution)/shard_map/ppermute | solution.py:392
  61.8 7.2 %collective-permute-start.7 = (bf16[128,512]{1,0:T(8,128)(2,1)S(1)}, bf16[128,512]{1,0:T(8,128)(2,1)S(1)}, u32[]{:S(2)}, u32[]{:S(2)}) collective-permute-start(bf16[128,512]{1,0:T(8,128)(2,1)S(1)} %get-tuple-element.77.mine_ref), channel_id=1, source_target_pairs={{0,1},{1,16},{16,17},{17,0},{2,3},{3,18},{18,19},{19,2},{4,5},{5,2... | collective-permute-start | bytes 393224 | tf_op jit(solution)/shard_map/ppermute | solution.py:396
  64.7 8.3 %collective-permute-start.11 = (bf16[144,512]{1,0:T(8,128)(2,1)S(1)}, bf16[144,512]{1,0:T(8,128)(2,1)S(1)}, u32[]{:S(2)}, u32[]{:S(2)}) collective-permute-start(bf16[144,512]{1,0:T(8,128)(2,1)S(1)} %get-tuple-element.84), channel_id=1, source_target_pairs={{0,16},{1,17},{16,0},{17,1},{2,18},{3,19},{18,2},{19,3},{4,20},{5,... | collective-permute-start | bytes 442376 | tf_op jit(solution)/shard_map/ppermute | solution.py:396
  64.9 10.3 %collective-permute-start.12 = (bf16[144,512]{1,0:T(8,128)(2,1)S(1)}, bf16[144,512]{1,0:T(8,128)(2,1)S(1)}, u32[]{:S(2)}, u32[]{:S(2)}) collective-permute-start(bf16[144,512]{1,0:T(8,128)(2,1)S(1)} %get-tuple-element.85), channel_id=1, source_target_pairs={{0,1},{1,16},{16,17},{17,0},{2,3},{3,18},{18,19},{19,2},{4,5},{5,2... | collective-permute-start | bytes 442376 | tf_op jit(solution)/shard_map/ppermute | solution.py:396
  70.0 5.5 %collective-permute-start.13 = (bf16[144,512]{1,0:T(8,128)(2,1)S(1)}, bf16[144,512]{1,0:T(8,128)(2,1)S(1)}, u32[]{:S(2)}, u32[]{:S(2)}) collective-permute-start(bf16[144,512]{1,0:T(8,128)(2,1)S(1)} %get-tuple-element.86), channel_id=1, source_target_pairs={{0,17},{1,0},{16,1},{17,16},{2,19},{3,2},{18,3},{19,18},{4,21},{5,... | collective-permute-start | bytes 442376 | tf_op jit(solution)/shard_map/ppermute | solution.py:396
